TPU v7x, 32 devices: a whole 2x2x4 slice. The times are simulated.
32 devices in a mesh: slot: 8 (over z, y), space: 4 (over x, core).
Axes of the slice: x: 2, y: 2, z: 4, core: 2. Of those that a mesh axis runs over, the one named last changes fastest.
Arguments:
- queries: bfloat16 [2048, 1024], P('space'), may hold values from -150 to 150
- raw_clip: bfloat16 [8, 8, 64, 2048], P(None, 'space', None, 'slot'), may hold values from -60 to 60
- pool_weight: bfloat16 [27, 2048], P(None, 'slot'), may hold values from -1.25 to 1.25
- old_memory: bfloat16 [8, 4, 4, 32, 2048], P('slot', None, 'space'), may hold values from -6 to 6
- valid_columns: int32 [9], replicated, may hold values from 16 to 32, as said below
- out_weight: bfloat16 [1024, 1024], replicated, may hold values from -0.1875 to 0.1875
Outputs:
- attended: bfloat16 [2048, 1024], P('space')
- fresh_memory: bfloat16 [4, 4, 32, 2048], P(None, 'space', None, 'slot')
- aged_memory: bfloat16 [8, 4, 4, 32, 2048], P('slot', None, 'space')
Inputs may be any that keep to these rules, and one draw needn't show every extreme that they name: `valid_columns`: at least one entry equals 32.
All inputs are finite; a program needn't handle non-finite values.
Results may differ from a plain program's by a relative error of at most 0.0085.
Values may be sent and summed in bfloat16 or wider, within the bound.
No kernel may reach another device: no remote copies, remote signals or barrier semaphores. Data moves between devices by JAX's collectives and lax.ppermute only.
A program may use at most 128 MiB of HBM per device.

v0:
```python
from functools import partial

import jax
import jax.numpy as jnp
from jax import lax
from jax.sharding import PartitionSpec as P

H = 16
MC = 32


block_keys = 256
masked_score = -1e30


def from_behind(block, axis, distance):
    devices = range(lax.axis_size(axis))
    route = [(i - distance, i) for i in devices if i - distance in devices]
    return lax.ppermute(block, axis, route)


def combine_parts(first, second):
    peak_first, sum_first, weighted_first = first
    peak_second, sum_second, weighted_second = second
    peak_score = jnp.maximum(peak_first, peak_second)
    factor_first = jnp.exp(peak_first - peak_score)
    factor_second = jnp.exp(peak_second - peak_score)
    weight_sum = sum_first * factor_first + sum_second * factor_second
    weighted = weighted_first * factor_first[..., None] + weighted_second * factor_second[..., None]
    return (peak_score, weight_sum, weighted)


def block_scores(query_heads, memory_rows, first_row, valid_count, head_size):
    key_count = memory_rows.shape[0]
    head_count = query_heads.shape[1]
    unpacked = memory_rows.reshape(key_count, head_count, 2, head_size)
    key_rows = unpacked[:, :, 0, :]
    value_rows = unpacked[:, :, 1, :]
    scores = jnp.einsum(
        "qhd,khd->qhk", query_heads, key_rows, preferred_element_type=jnp.float32
    ) * head_size ** (-0.5)
    column = (first_row + jnp.arange(key_count, dtype=jnp.int32)) % MC
    usable = column < valid_count
    scores = jnp.where(usable[None, None, :], scores, masked_score)
    peak_score = jnp.max(scores, axis=2)
    weights = jnp.where(usable[None, None, :], jnp.exp(scores - peak_score[..., None]), 0.0)
    weight_sum = jnp.sum(weights, axis=2)
    weighted = jnp.einsum(
        "qhk,khd->qhd", weights.astype(jnp.bfloat16), value_rows, preferred_element_type=jnp.float32
    )
    return (peak_score, weight_sum, weighted)


def attend(running, shard_piece, first_row, query_heads, valid_count, head_size):
    key_count = shard_piece.shape[0]
    key_blocks = shard_piece.reshape(key_count // block_keys, block_keys, shard_piece.shape[1])
    offsets = block_keys * jnp.arange(key_count // block_keys, dtype=jnp.int32)

    def advance(state, item_pair):
        key_block, offset = item_pair
        return (
            combine_parts(
                state, block_scores(query_heads, key_block, offset, valid_count, head_size)
            ),
            None,
        )

    return lax.scan(advance, running, (key_blocks, offsets))[0]


def empty_parts(query_rows, head_count, head_size):
    return (
        jnp.full((query_rows, head_count), masked_score, jnp.float32),
        jnp.zeros((query_rows, head_count), jnp.float32),
        jnp.zeros((query_rows, head_count, head_size), jnp.float32),
    )


def pool_slab(raw_clip, pool_weight, head_size):
    upper_row = from_behind(raw_clip[:, -1:], "space", 1)
    stacked = jnp.concatenate([upper_row, raw_clip], axis=1).astype(jnp.float32)
    padded = jnp.pad(stacked, ((1, 0), (0, 0), (1, 0), (0, 0)))
    frames_out = raw_clip.shape[0] // 2
    columns_out = raw_clip.shape[2] // 2
    channels = raw_clip.shape[3]
    weight = pool_weight.astype(jnp.float32)
    pooled = jnp.zeros((frames_out, 1, columns_out, channels), jnp.float32)
    for frame_tap in range(3):
        for row_tap in range(3):
            for column_tap in range(3):
                tapped = padded[
                    frame_tap : frame_tap + 2 * frames_out : 2,
                    row_tap : row_tap + 1,
                    column_tap : column_tap + 2 * columns_out : 2,
                ]
                pooled = pooled + weight[9 * frame_tap + 3 * row_tap + column_tap] * tapped
    shaped = pooled.reshape(frames_out, 1, columns_out, channels // (2 * head_size), 2, head_size)
    center = jnp.mean(shaped, axis=-1, keepdims=True)
    centered = shaped - center
    spread = jnp.mean(centered * centered, axis=-1, keepdims=True)
    normed = centered * lax.rsqrt(spread + 1e-06)
    return normed.reshape(pooled.shape).astype(jnp.bfloat16)


def local(queries, raw_clip, pool_weight, old_memory, valid_columns, out_weight):
    model_width = queries.shape[1]
    head_size = model_width // H
    local_heads = H // lax.axis_size("slot")
    slot_index = lax.axis_index("slot")
    first_head = slot_index * local_heads
    query_rows = queries.shape[0]
    fresh_keys = pool_slab(raw_clip, pool_weight, head_size)
    aged_memory = from_behind(old_memory, "slot", 1)
    query_heads = queries.reshape(query_rows, H, head_size)
    resident = old_memory.reshape(-1, old_memory.shape[-1])
    resident_valid = lax.dynamic_index_in_dim(valid_columns, slot_index + 1, keepdims=False)
    fresh_valid = valid_columns[0]
    fold_slot = partial(
        attend, query_heads=query_heads, valid_count=resident_valid, head_size=head_size
    )
    peak_part, sum_part, weighted_part = fold_slot(
        empty_parts(query_rows, H, head_size),
        lax.all_gather(resident, "space", axis=0, tiled=True),
        jnp.int32(0),
    )
    fresh_rows = fresh_keys.reshape(-1, fresh_keys.shape[-1])
    fresh_queries = lax.dynamic_slice_in_dim(query_heads, first_head, local_heads, axis=1)
    fold_fresh = partial(
        attend, query_heads=fresh_queries, valid_count=fresh_valid, head_size=head_size
    )
    fresh_parts = fold_fresh(
        empty_parts(query_rows, local_heads, head_size),
        lax.all_gather(fresh_rows, "space", axis=0, tiled=True),
        jnp.int32(0),
    )
    window = (
        lax.dynamic_slice_in_dim(peak_part, first_head, local_heads, axis=1),
        lax.dynamic_slice_in_dim(sum_part, first_head, local_heads, axis=1),
        lax.dynamic_slice_in_dim(weighted_part, first_head, local_heads, axis=1),
    )
    joined = combine_parts(window, fresh_parts)
    peak_part = lax.dynamic_update_slice_in_dim(peak_part, joined[0], first_head, axis=1)
    sum_part = lax.dynamic_update_slice_in_dim(sum_part, joined[1], first_head, axis=1)
    weighted_part = lax.dynamic_update_slice_in_dim(weighted_part, joined[2], first_head, axis=1)
    peak_score = lax.pmax(peak_part, "slot")
    factor = jnp.exp(peak_part - peak_score)
    weight_sum, weighted = lax.psum((sum_part * factor, weighted_part * factor[..., None]), "slot")
    mixed_heads = (
        (weighted / weight_sum[..., None]).astype(jnp.bfloat16).reshape(query_rows, model_width)
    )
    attended = jnp.dot(mixed_heads, out_weight, preferred_element_type=jnp.float32).astype(
        jnp.bfloat16
    )
    return (attended, fresh_keys, aged_memory)


def solution(mesh):
    return jax.shard_map(
        local,
        mesh=mesh,
        in_specs=(
            P("space", None),
            P(None, "space", None, "slot"),
            P(None, "slot"),
            P("slot", None, "space", None, None),
            P(),
            P(),
        ),
        out_specs=(
            P("space", None),
            P(None, "space", None, "slot"),
            P("slot", None, "space", None, None),
        ),
        check_vma=False,
    )
```

profile of v0, /device:TPU:0, one launch (start us, length us, event | category | flops | bytes accessed | tf_op | source)
XLA Modules:
  0.0 324.8 jit_solution(5318807901764285021)
XLA Ops:
  9.7 3.1 collective-permute-start
  27.8 3.0 slice.241
  33.7 2.9 slice.237
  43.2 3.0 slice.229
  49.2 3.0 slice.225
  52.2 3.0 slice.223
  61.0 3.0 slice.217
  69.8 3.0 slice.211
  78.7 3.0 slice.205
  87.5 3.0 slice.199
  101.6 7.9 %all_gather.7 = bf16[512,256]{1,0:T(8,128)(2,1)} all-gather(bf16[128,256]{1,0:T(8,128)(2,1)S(1)} %bitcast.136), channel_id=1, replica_groups=mesh['slot'=8,'space'=4] {'space'}, dimensions={0}, use_global_device_ids=true | all-gather | bytes 327680 | tf_op jit(solution)/shard_map/all_gather | solution.py:133
  109.5 12.1 %while.35 = (s32[]{:T(128)}, f32[512,2]{0,1:T(2,128)S(1)}, f32[512,2]{0,1:T(2,128)S(1)}, f32[512,2,64]{0,2,1:T(8,128)S(1)}, s32[2]{0:T(128)}, /*index=5*/s32[]{:...) while((s32[]{:T(128)}, f32[512,2]{0,1:T(2,128)S(1)}, ...), condition=%wide.region_9.10_spmd.clone, body=%wide.region_6.9_spmd.clone.sunk | while | flops 69739776 | bytes 4516268 | solution.py:68
  121.6 42.8 %while.34 = (s32[]{:T(128)}, f32[512,16]{0,1:T(8,128)}, f32[512,16]{0,1:T(8,128)}, f32[512,16,64]{0,2,1:T(8,128)}, s32[2]{0:T(128)}, /*index=5*/s32[]{:T(128)}, ...) while((s32[]{:T(128)}, f32[512,16]{0,1:T(8,128)}, ...), condition=%wide.region_3.4_spmd.clone, body=%wide.region_0.3_spmd.clone.sunk | while | flops 566283520 | bytes 74385464 | solution.py:68
  126.8 3.3 %bitcast_reduce_fusion.2 = (f32[512,16]{0,1:T(8,128)S(1)}, f32[16,256,512]{2,1,0:T(8,128)S(1)}) fusion(pred[256]{0:T(512)(128)(4,1)S(1)} %fusion.65, bf16[512,16,64]{0,2,1:T(8,128)(2,1)} %get-tuple-element.515, bf16[256,16,2,64]{0,3,2,1:T(8,128)(2,1)} %bitcast.127), kind=kOutput, calls=%fused_computation.1.clone.1 | convolution fusion | flops 274718720 | bytes 9994496 | tf_op jit(solution)/shard_map/while/body/eval_jaxpr/qhd,khd->qhk/dot_general | solution.py:39
  130.2 3.2 copy-done.1
  135.8 7.0 %fusion.68 = f32[512,16,64]{0,2,1:T(8,128)} fusion(f32[512,16,64]{0,2,1:T(8,128)} %get-tuple-element.501, f32[16,256,512]{2,1,0:T(8,128)} %copy-done.1, f32[512,16]{0,1:T(8,128)S(1)} %get-tuple-element.469, pred[256]{0:T(512)(128)(4,1)S(1)} %fusion.65, f32[512,16]{0,1:T(8,128)S(1)} %get-tuple-element.472, f32[512,16]{0,1:T(8,128)S(1)} %get-tuple-element.473, ...), kind=kOutput, calls=%fused_computation.11.clone.1 | convolution fusion | flops 281018368 | bytes 13206529 | tf_op jit(solution)/shard_map/while/body/eval_jaxpr/qhk,khd->qhd/dot_general | solution.py:48
  147.9 3.3 %bitcast_reduce_fusion.2 = (f32[512,16]{0,1:T(8,128)S(1)}, f32[16,256,512]{2,1,0:T(8,128)S(1)}) fusion(pred[256]{0:T(512)(128)(4,1)S(1)} %fusion.65, bf16[512,16,64]{0,2,1:T(8,128)(2,1)} %get-tuple-element.515, bf16[256,16,2,64]{0,3,2,1:T(8,128)(2,1)} %bitcast.127), kind=kOutput, calls=%fused_computation.1.clone.1 | convolution fusion | flops 274718720 | bytes 9994496 | tf_op jit(solution)/shard_map/while/body/eval_jaxpr/qhd,khd->qhk/dot_general | solution.py:39
  151.3 3.2 copy-done.1
  156.9 7.6 %fusion.68 = f32[512,16,64]{0,2,1:T(8,128)} fusion(f32[512,16,64]{0,2,1:T(8,128)} %get-tuple-element.501, f32[16,256,512]{2,1,0:T(8,128)} %copy-done.1, f32[512,16]{0,1:T(8,128)S(1)} %get-tuple-element.469, pred[256]{0:T(512)(128)(4,1)S(1)} %fusion.65, f32[512,16]{0,1:T(8,128)S(1)} %get-tuple-element.472, f32[512,16]{0,1:T(8,128)S(1)} %get-tuple-element.473, ...), kind=kOutput, calls=%fused_computation.11.clone.1 | convolution fusion | flops 281018368 | bytes 13206529 | tf_op jit(solution)/shard_map/while/body/eval_jaxpr/qhk,khd->qhd/dot_general | solution.py:48
  165.8 38.0 %pmax.7 = f32[512,16]{0,1:T(8,128)S(1)} all-reduce(f32[512,16]{0,1:T(8,128)} %get-tuple-element.336), channel_id=1, replica_groups=mesh['slot'=8,'space'=4] {'slot'}, use_global_device_ids=true, to_apply=%region_10.11 | all-reduce | flops 8192 | bytes 65536 | tf_op jit(solution)/shard_map/pmax | solution.py:145
  206.4 3.2 broadcast_multiply_fusion
  211.9 13.7 %collective-permute-done.1 = bf16[1,4,1,32,2048]{4,3,2,1,0:T(8,128)(2,1)S(1)} collective-permute-done((bf16[1,4,1,32,2048]{4,3,2,1,0:T(8,128)(2,1)S(1)}, bf16[1,4,1,32,2048]{4,3,2,1,0:T(8,128)(2,1)S(1)}, u32[]{:S(2)}, u32[]{:S(2)}) %collective-permute-start.1) | collective-permute-done | bytes 524320 | tf_op jit(solution)/shard_map/ppermute | solution.py:19
  225.6 41.6 %psum.15 = f32[512,16]{0,1:T(8,128)S(1)} all-reduce(f32[512,16]{0,1:T(8,128)S(1)} %get-tuple-element.327), channel_id=1, replica_groups=mesh['slot'=8,'space'=4] {'slot'}, use_global_device_ids=true, to_apply=%region_12.13 | all-reduce | flops 8192 | bytes 65536 | tf_op jit(solution)/shard_map/psum | solution.py:147
  267.2 45.7 %all-reduce.3.cloned.1.call-done = f32[512,16,64]{0,2,1:T(8,128)} async-done(((f32[512,16,64]{0,2,1:T(8,128)}), f32[512,16,64]{0,2,1:T(8,128)}) %all-reduce.3.cloned.1.call-update) | async-done | bytes 2097168 | tf_op jit(solution)/shard_map/psum | solution.py:147
  (133 shorter events, 102.3 us)
Async XLA Ops:
  7.2 307.7 %copy-start = (bf16[1024,1024]{1,0:T(8,128)(2,1)S(1)}, bf16[1024,1024]{1,0:T(8,128)(2,1)}, u32[]{:S(2)}) copy-start(bf16[1024,1024]{1,0:T(8,128)(2,1)} %param.15) | copy-start | bytes 6291460
  7.2 7.1 %copy-start.16 = (bf16[27,256]{1,0:T(8,128)(2,1)S(1)}, bf16[27,256]{1,0:T(8,128)(2,1)}, u32[]{:S(2)}) copy-start(bf16[27,256]{1,0:T(8,128)(2,1)} %param.12) | copy-start | bytes 41476
  7.2 7.7 %copy-start.17 = (s32[9]{0:T(128)S(1)}, s32[9]{0:T(128)}, u32[]{:S(2)}) copy-start(s32[9]{0:T(128)} %param.14) | copy-start | bytes 112
  7.2 114.4 %all-gather.2.cloned.1.call-start = ((), (), s32[]{:S(2)}) async-start(), calls=%async_computation | async-start | bytes 2621440 | tf_op jit(solution)/shard_map/all_gather | solution.py:123
  7.9 305.0 %all-reduce.3.cloned.1.call-start = ((), (), s32[]{:S(2)}) async-start(), calls=%async_computation.1 | async-start | bytes 4194304 | tf_op jit(solution)/shard_map/psum | solution.py:147
  9.7 7.8 %collective-permute-start = (bf16[8,1,64,256]{3,2,1,0:T(8,128)(2,1)}, bf16[8,1,64,256]{3,2,1,0:T(8,128)(2,1)}, u32[]{:S(2)}, u32[]{:S(2)}) collective-permute-start(bf16[8,1,64,256]{3,2,1,0:T(8,128)(2,1)} %slice.194), channel_id=1, source_target_pairs={{0,1},{1,2},{2,3},{4,5},{5,6},{6,7},{8,9},{9,10},{10,11},{12,13},{... | collective-permute-start | bytes 786440 | tf_op jit(solution)/shard_map/ppermute | solution.py:19
  14.2 19.5 %copy-start.3 = (bf16[512,1024]{0,1:T(8,128)(2,1)}, bf16[512,1024]{0,1:T(8,128)(2,1)S(1)}, u32[]{:S(2)}) copy-start(bf16[512,1024]{0,1:T(8,128)(2,1)S(1)} %copy.25) | copy-start | bytes 3145732
  49.1 47.2 %copy-start.9 = (f32[4,1,32,256]{3,2,1,0:T(8,128)S(1)}, f32[4,1,32,256]{3,2,1,0:T(8,128)}, u32[]{:S(2)}) copy-start(f32[4,1,32,256]{3,2,1,0:T(8,128)} %slice.245) | copy-start | bytes 393220
  49.1 47.2 %copy-start.10 = (f32[4,1,32,256]{3,2,1,0:T(8,128)S(1)}, f32[4,1,32,256]{3,2,1,0:T(8,128)}, u32[]{:S(2)}) copy-start(f32[4,1,32,256]{3,2,1,0:T(8,128)} %slice.243) | copy-start | bytes 393220
  49.1 47.2 %copy-start.11 = (f32[4,1,32,256]{3,2,1,0:T(8,128)S(1)}, f32[4,1,32,256]{3,2,1,0:T(8,128)}, u32[]{:S(2)}) copy-start(f32[4,1,32,256]{3,2,1,0:T(8,128)} %slice.241) | copy-start | bytes 393220
  49.2 47.2 %copy-start.12 = (f32[4,1,32,256]{3,2,1,0:T(8,128)S(1)}, f32[4,1,32,256]{3,2,1,0:T(8,128)}, u32[]{:S(2)}) copy-start(f32[4,1,32,256]{3,2,1,0:T(8,128)} %slice.239) | copy-start | bytes 393220
  49.2 47.2 %copy-start.13 = (f32[4,1,32,256]{3,2,1,0:T(8,128)S(1)}, f32[4,1,32,256]{3,2,1,0:T(8,128)}, u32[]{:S(2)}) copy-start(f32[4,1,32,256]{3,2,1,0:T(8,128)} %slice.237) | copy-start | bytes 393220
  101.6 7.9 %copy-start.14 = (bf16[4,1,32,256]{3,2,1,0:T(8,128)(2,1)}, bf16[4,1,32,256]{3,2,1,0:T(8,128)(2,1)S(1)}, u32[]{:S(2)}) copy-start(bf16[4,1,32,256]{3,2,1,0:T(8,128)(2,1)S(1)} %multiply_convert_fusion) | copy-start | bytes 196612
  130.2 3.2 copy-start.1
  133.4 2.3 copy-start.6
  133.4 2.4 copy-start.2
  135.7 7.0 %copy-start.5 = (f32[512,16]{0,1:T(8,128)}, f32[512,16]{0,1:T(8,128)S(1)}, u32[]{:S(2)}) copy-start(f32[512,16]{0,1:T(8,128)S(1)} %get-tuple-element.509) | copy-start | bytes 98308 | tf_op jit(solution)/shard_map/while
  135.8 7.0 %copy-start.7 = (f32[512,16]{0,1:T(8,128)}, f32[512,16]{0,1:T(8,128)S(1)}, u32[]{:S(2)}) copy-start(f32[512,16]{0,1:T(8,128)S(1)} %get-tuple-element.510) | copy-start | bytes 98308 | tf_op jit(solution)/shard_map/while
  151.3 3.2 copy-start.1
  154.5 2.3 copy-start.6
  154.5 2.4 copy-start.2
  156.9 7.6 %copy-start.5 = (f32[512,16]{0,1:T(8,128)}, f32[512,16]{0,1:T(8,128)S(1)}, u32[]{:S(2)}) copy-start(f32[512,16]{0,1:T(8,128)S(1)} %get-tuple-element.509) | copy-start | bytes 98308 | tf_op jit(solution)/shard_map/while
  156.9 7.6 %copy-start.7 = (f32[512,16]{0,1:T(8,128)}, f32[512,16]{0,1:T(8,128)S(1)}, u32[]{:S(2)}) copy-start(f32[512,16]{0,1:T(8,128)S(1)} %get-tuple-element.510) | copy-start | bytes 98308 | tf_op jit(solution)/shard_map/while
  210.6 15.0 %collective-permute-start.1 = (bf16[1,4,1,32,2048]{4,3,2,1,0:T(8,128)(2,1)S(1)}, bf16[1,4,1,32,2048]{4,3,2,1,0:T(8,128)(2,1)S(1)}, u32[]{:S(2)}, u32[]{:S(2)}) collective-permute-start(bf16[1,4,1,32,2048]{4,3,2,1,0:T(8,128)(2,1)S(1)} %copy-done.8), channel_id=1, source_target_pairs={{0,4},{4,8},{8,12},{12,16},{16,20},{20,24},{24,28},{1,5},{5,9},{9,... | collective-permute-start | bytes 1572872 | tf_op jit(solution)/shard_map/ppermute | solution.py:19
  (5 other events, 8.2 us)
Sparse Core Ops, SparseCore 0:
  9.6 25.2 all-gather.1
  209.7 103.2 all-reduce.2
where the time goes:
time: 329 us; the launch traced here: 325 us
  local copies, waits for them, and re-layouts  104 us (32%)
  blocking collectives  87.5 us (27%)
  waiting for transfers between devices  60.2 us (18%)
  matrix products  27.9 us (8%)
  other arithmetic  26.1 us (8%)
  between operations  14.3 us (4%)
  starting transfers between devices  4.45 us (1%)
    slice x27, local copies, waits for them, and re-layouts, pool_slab(): padded[frame_tap:frame_tap + 2 * frames_out:2, row_tap:row_tap + 1, colum...  76.2 us
    psum x1, waiting for transfers between devices, local(): lax.psum((sum_part * factor, weighted_part * factor[..., None]), 'slot')  45.7 us
    psum x1, blocking collectives, local(): lax.psum((sum_part * factor, weighted_part * factor[..., None]), 'slot')  41.6 us
    pmax x1, blocking collectives, local(): peak_score = lax.pmax(peak_part, 'slot')  38 us
    dot_general x4, matrix products, block_scores(): jnp.einsum('qhk,khd->qhd', weights.astype(jnp.bfloat16), value_rows, pref...  16.5 us
    ppermute x2, waiting for transfers between devices, from_behind(): return lax.ppermute(block, axis, route)  13.7 us
    dynamic_slice x12, local copies, waits for them, and re-layouts, attend(): return lax.scan(advance, running, (key_blocks, offsets))[0]  12.1 us
    dot_general x4, matrix products, block_scores(): jnp.einsum('qhd,khd->qhk', query_heads, key_rows, preferred_element_type=...  9.19 us
  transfers between devices with their start and end apart: 4, of which 2 were waited for; matrix products, arithmetic and copies ran while one was open for 32% of the time, Pallas kernels for 0%

commit v1 on v0

v1 whole, which is shorter than its diff:
```python
from functools import partial

import jax
import jax.numpy as jnp
from jax import lax
from jax.experimental import pallas as pl
from jax.experimental.pallas import tpu as pltpu
from jax.sharding import PartitionSpec as P

H = 16
MASKED = -1e30
VMEM_LIMIT = 48 * 1024 * 1024
VMEM = pltpu.VMEM
SMEM = pltpu.SMEM


def params(**more):
    return pltpu.CompilerParams(vmem_limit_bytes=VMEM_LIMIT, **more)


def lanes_of(shape):
    return lax.broadcasted_iota(jnp.int32, shape, len(shape) - 1)


def exchange(block, axis, distance):
    size = lax.axis_size(axis)
    return lax.ppermute(block, axis, [(i, i ^ distance) for i in range(size)])


def from_behind(block, axis, distance):
    devices = range(lax.axis_size(axis))
    return lax.ppermute(block, axis, [(i - distance, i) for i in devices if i - distance in devices])


def pool_kernel(head_size, raw_ref, halo_ref, weight_ref, out_ref, slabs):
    frames, rows, columns, channels = raw_ref.shape
    frames_out, columns_out = frames // 2, columns // 2
    pieces, _, _, wide = slabs.shape
    group = lax.broadcasted_iota(jnp.int32, (wide, wide), 0) // head_size
    averaging = jnp.where(
        group == lanes_of((wide, wide)) // head_size, 1.0 / head_size, 0.0
    ).astype(jnp.float32)
    first_row = lax.broadcasted_iota(jnp.int32, (columns_out, wide), 0) == 0
    mean = partial(
        jnp.dot, precision=lax.Precision.HIGHEST, preferred_element_type=jnp.float32
    )
    for piece in range(pieces):
        lanes = slice(piece * wide, (piece + 1) * wide)
        for f in range(frames):
            slabs[piece, 3 * f] = halo_ref[f, 0, :, lanes].astype(jnp.float32)
            slabs[piece, 3 * f + 1] = raw_ref[f, 0, :, lanes].astype(jnp.float32)
            slabs[piece, 3 * f + 2] = raw_ref[f, 1, :, lanes].astype(jnp.float32)
        weight = weight_ref[:, lanes].astype(jnp.float32)
        for f in range(frames_out):
            sums = [jnp.zeros((columns_out, wide), jnp.float32) for _ in range(3)]
            for a in range(3):
                frame = 2 * f + a - 1
                if frame < 0:
                    continue
                for b in range(3):
                    even = slabs[piece, 3 * frame + b, pl.ds(0, columns_out, stride=2), :]
                    odd = slabs[piece, 3 * frame + b, pl.ds(1, columns_out, stride=2), :]
                    for g, tapped in enumerate((odd, even, odd)):
                        tap = 9 * a + 3 * b + g
                        sums[g] = sums[g] + weight[tap : tap + 1] * tapped
            behind = jnp.where(first_row, 0.0, pltpu.roll(sums[0], 1, 0))
            pooled = behind + sums[1] + sums[2]
            centered = pooled - mean(pooled, averaging)
            spread = mean(centered * centered, averaging)
            out_ref[f, 0, :, lanes] = (centered * lax.rsqrt(spread + 1e-06)).astype(jnp.bfloat16)


def pool(raw_clip, halo, pool_weight, head_size):
    frames, rows, columns, channels = raw_clip.shape
    return pl.pallas_call(
        partial(pool_kernel, head_size),
        out_shape=jax.ShapeDtypeStruct((frames // 2, 1, columns // 2, channels), jnp.bfloat16),
        in_specs=[pl.BlockSpec(memory_space=VMEM)] * 3,
        out_specs=pl.BlockSpec(memory_space=VMEM),
        scratch_shapes=[VMEM((channels // 128, 3 * frames, columns, 128), jnp.float32)],
        compiler_params=params(),
        name="pool",
    )(raw_clip, halo, pool_weight)


def cut_kernel(width, place_ref, memory_ref, *out_refs):
    place = place_ref[0]
    for distance, out_ref in enumerate(out_refs):
        start = pl.multiple_of((place ^ distance) * width, 128)
        out_ref[...] = memory_ref[:, pl.ds(start, width)]


def cut(place, memory, pieces):
    tokens, channels = memory.shape
    width = channels // pieces
    return pl.pallas_call(
        partial(cut_kernel, width),
        out_shape=[jax.ShapeDtypeStruct((tokens, width), memory.dtype)] * pieces,
        in_specs=[pl.BlockSpec(memory_space=SMEM), pl.BlockSpec(memory_space=VMEM)],
        out_specs=[pl.BlockSpec(memory_space=VMEM)] * pieces,
        compiler_params=params(),
        name="cut",
    )(place, memory)


def attend_kernel(
    head_size, columns, distances, final, has_state, place_ref, valid_ref, query_ref, *refs
):
    refs = list(refs)
    sources = [refs.pop(0), refs.pop(0)]
    state_ref = refs.pop(0) if has_state else None
    if final:
        value_ref, level_ref = refs.pop(0), refs.pop(0)
    else:
        state_out_ref = refs.pop(0)
    key_scratch, value_scratch = refs
    heads, key_count, wide = key_scratch.shape
    tokens = key_count // (2 * len(distances))

    @pl.when(pl.program_id(0) == 0)
    def _():
        lane = lanes_of((tokens, wide))
        column = lax.broadcasted_iota(jnp.int32, (tokens, wide), 0) % columns
        place = place_ref[0]
        for b, distance in enumerate(distances):
            valid = valid_ref[0] if distance is None else valid_ref[1 + (place ^ distance)]
            extra = jnp.where((lane == head_size) & (column >= valid), MASKED, 0.0)
            for c, source in enumerate(sources):
                row = (c * len(distances) + b) * tokens
                for h in range(heads):
                    tile = source[b * tokens : (b + 1) * tokens, h * wide : (h + 1) * wide]
                    tile = tile.astype(jnp.float32)
                    key_scratch[h, row : row + tokens] = jnp.where(
                        lane < head_size, tile, extra
                    ).astype(jnp.bfloat16)
                    value_scratch[h, row : row + tokens] = jnp.where(
                        lane < head_size, 1.0, tile
                    ).astype(jnp.bfloat16)

    block = query_ref.shape[0]
    lane = lanes_of((block, wide))
    queries = query_ref[...].astype(jnp.float32) * head_size ** (-0.5)
    values, levels = [], []
    for h in range(heads):
        rows = queries if h == 0 else pltpu.roll(queries, wide - h * head_size, 1)
        if rows.shape[1] < wide:
            rows = jnp.concatenate([rows, rows], axis=1)
        rows = jnp.where(lane < head_size, rows, jnp.where(lane == head_size, 1.0, 0.0))
        scores = lax.dot_general(
            rows.astype(jnp.bfloat16),
            key_scratch[h],
            (((1,), (1,)), ((), ())),
            preferred_element_type=jnp.float32,
        )
        peak = jnp.max(scores, axis=1, keepdims=True)
        if has_state:
            state = state_ref[h]
            old_peak = state[:, head_size // 2 : head_size // 2 + 1]
            peak = jnp.maximum(peak, old_peak)
        weights = jnp.exp(scores - peak).astype(jnp.bfloat16)
        total = jnp.dot(weights, value_scratch[h], preferred_element_type=jnp.float32)
        if has_state:
            total = total + state * jnp.exp(old_peak - peak)
        if final:
            weight_sum = total[:, :1]
            values.append(total[:, head_size:] / weight_sum)
            levels.append(jnp.broadcast_to(peak + jnp.log(weight_sum), (block, head_size)))
        else:
            keep = (lane >= head_size // 2) & (lane < head_size)
            state_out_ref[h] = jnp.where(keep, peak, total)
    if final:
        value_ref[...] = jnp.concatenate(values, axis=1).astype(value_ref.dtype)
        level = jnp.concatenate(levels, axis=1)
        if level.shape[1] < wide:
            level = jnp.concatenate([level, level], axis=1)
        turned = level.T
        for h in range(heads):
            level_ref[h : h + 1, :] = turned[h * head_size : h * head_size + 1, :]


def attend(
    place, valid, queries, sources, state, state_start, distances, columns, head_size, final, dtype
):
    rows, width = queries.shape
    heads = width // head_size
    wide = 2 * head_size
    key_count = 2 * sources[0].shape[0]
    block = min(256, rows)
    start = state_start // block
    whole = pl.BlockSpec(memory_space=VMEM)
    in_specs = [
        pl.BlockSpec(memory_space=SMEM),
        pl.BlockSpec(memory_space=SMEM),
        pl.BlockSpec((block, width), lambda i: (i, 0)),
        whole,
        whole,
    ]
    operands = [place, valid, queries, *sources]
    if state is not None:
        in_specs.append(pl.BlockSpec((heads, block, wide), lambda i: (0, i + start, 0)))
        operands.append(state)
    if final:
        out_shape = [
            jax.ShapeDtypeStruct((rows, width), dtype),
            jax.ShapeDtypeStruct((8, rows), jnp.float32),
        ]
        out_specs = [
            pl.BlockSpec((block, width), lambda i: (i, 0)),
            pl.BlockSpec((8, block), lambda i: (0, i)),
        ]
    else:
        out_shape = jax.ShapeDtypeStruct((heads, rows, wide), jnp.float32)
        out_specs = pl.BlockSpec((heads, block, wide), lambda i: (0, i, 0))
    return pl.pallas_call(
        partial(attend_kernel, head_size, columns, distances, final, state is not None),
        grid=(rows // block,),
        out_shape=out_shape,
        in_specs=in_specs,
        out_specs=out_specs,
        scratch_shapes=[VMEM((heads, key_count, wide), jnp.bfloat16)] * 2,
        compiler_params=params(),
        cost_estimate=pl.CostEstimate(
            flops=4 * rows * key_count * wide * heads,
            bytes_accessed=4 * key_count * wide * heads + 8 * rows * wide * heads,
            transcendentals=rows * key_count * heads,
        ),
        name="attend",
    )(*operands)


def merge_kernel(head_size, *refs):
    out_ref = refs[-1]
    refs = refs[:-1]
    values = [ref[...].astype(jnp.float32) for ref in refs[0::2]]
    rows, width = values[0].shape
    heads = width // head_size
    levels = []
    for ref in refs[1::2]:
        turned = jnp.concatenate(
            [jnp.broadcast_to(ref[h : h + 1, :], (head_size, rows)) for h in range(heads)], axis=0
        )
        levels.append(turned.T)
    top = levels[0]
    for level in levels[1:]:
        top = jnp.maximum(top, level)
    total = jnp.zeros((rows, width), jnp.float32)
    share = jnp.zeros((rows, width), jnp.float32)
    for value, level in zip(values, levels):
        factor = jnp.exp(level - top)
        total = total + value * factor
        share = share + factor
    out_ref[...] = (total / share).astype(out_ref.dtype)


def merge(parts, head_size):
    rows, width = parts[0][0].shape
    flat = [array for part in parts for array in part]
    return pl.pallas_call(
        partial(merge_kernel, head_size),
        out_shape=jax.ShapeDtypeStruct((rows, width), jnp.bfloat16),
        in_specs=[pl.BlockSpec(memory_space=VMEM)] * len(flat),
        out_specs=pl.BlockSpec(memory_space=VMEM),
        compiler_params=params(),
        name="merge",
    )(*flat)


def project_kernel(place_ref, weight_ref, *refs):
    out_ref = refs[-1]
    place = place_ref[0]
    total = None
    for distance, ref in enumerate(refs[:-1]):
        width = ref.shape[1]
        start = pl.multiple_of((place ^ distance) * width, width)
        term = jnp.dot(
            ref[...], weight_ref[pl.ds(start, width), :], preferred_element_type=jnp.float32
        )
        total = term if total is None else total + term
    out_ref[...] = total.astype(out_ref.dtype)


def project(place, out_weight, blocks):
    rows = blocks[0].shape[0]
    return pl.pallas_call(
        project_kernel,
        out_shape=jax.ShapeDtypeStruct((rows, out_weight.shape[1]), jnp.bfloat16),
        in_specs=[pl.BlockSpec(memory_space=SMEM)]
        + [pl.BlockSpec(memory_space=VMEM)] * (1 + len(blocks)),
        out_specs=pl.BlockSpec(memory_space=VMEM),
        compiler_params=params(),
        name="project",
    )(place, out_weight, *blocks)


def local(queries, raw_clip, pool_weight, old_memory, valid_columns, out_weight):
    query_rows, model_width = queries.shape
    head_size = model_width // H
    slots = lax.axis_size("slot")
    spaces = lax.axis_size("space")
    columns = old_memory.shape[3]
    width = model_width // slots
    slot_index = lax.axis_index("slot")
    place = slot_index.astype(jnp.int32).reshape(1)

    halo = from_behind(raw_clip[:, -1:], "space", 1)
    own_queries = lax.dynamic_slice_in_dim(queries, slot_index * width, width, axis=1)
    space_partners = range(2, spaces, 2)
    all_queries = [own_queries] + [exchange(own_queries, "space", d) for d in space_partners]

    resident = old_memory.reshape(-1, old_memory.shape[-1])
    pieces = cut(place, resident, slots)
    received = [pieces[0]] + [exchange(pieces[d], "slot", d) for d in range(1, slots)]

    fresh = pool(raw_clip, halo, pool_weight, head_size)
    fresh_rows = fresh.reshape(-1, fresh.shape[-1])

    half = slots // 2
    first = jnp.concatenate([fresh_rows] + received[:half], axis=0)
    first_other = exchange(first, "space", 1)
    second = jnp.concatenate(received[half:], axis=0)
    second_other = exchange(second, "space", 1)

    call = partial(attend, place, valid_columns, columns=columns, head_size=head_size)
    state = call(
        jnp.concatenate(all_queries, axis=0),
        (first, first_other),
        None,
        0,
        distances=(None,) + tuple(range(half)),
        final=False,
        dtype=None,
    )
    parts = []
    for k in list(range(1, len(all_queries))) + [0]:
        value, level = call(
            all_queries[k],
            (second, second_other),
            state,
            k * query_rows,
            distances=tuple(range(half, slots)),
            final=True,
            dtype=jnp.bfloat16 if k else jnp.float32,
        )
        if k:
            value = exchange(value, "space", 2 * k)
            level = exchange(level, "space", 2 * k)
        parts.append((value, level))
    mixed = merge(parts, head_size)

    blocks = {0: mixed}
    for d in range(2, slots, 2):
        blocks[d] = exchange(mixed, "slot", d)
    for d in range(0, slots, 2):
        blocks[d + 1] = exchange(blocks[d], "slot", 1)
    attended = project(place, out_weight, [blocks[d] for d in range(slots)])
    aged_memory = from_behind(old_memory, "slot", 1)
    return (attended, fresh, aged_memory)


def solution(mesh):
    return jax.shard_map(
        local,
        mesh=mesh,
        in_specs=(
            P("space", None),
            P(None, "space", None, "slot"),
            P(None, "slot"),
            P("slot", None, "space", None, None),
            P(),
            P(),
        ),
        out_specs=(
            P("space", None),
            P(None, "space", None, "slot"),
            P("slot", None, "space", None, None),
        ),
        check_vma=False,
    )
```

time: 329 us -> 82 us (0.25); the launches traced: 325 us -> 81.6 us
  local copies, waits for them, and re-layouts: 104 us -> 5.63 us
  blocking collectives: 87.5 us -> 0 us
  waiting for transfers between devices: 60.2 us -> 23.2 us
  starting transfers between devices: 4.45 us -> 32.7 us
  matrix products: 27.9 us -> 0 us
  other arithmetic: 26.1 us -> 0.02 us
  Pallas kernels: 0 us -> 19.2 us
  between operations: 14.3 us -> 0.88 us
    slice x31 -> x1, local copies, waits for them, and re-layouts: 79.9 us -> 1.09 us  [local(): halo = from_behind(raw_clip[:, -1:], 'space', 1)]
    psum x1 -> x0, waiting for transfers between devices: 45.7 us -> none  [local(): lax.psum((sum_part * factor, weighted_part * factor[..., None]), 'slot')]
    psum x1 -> x0, blocking collectives: 41.6 us -> none  [local(): lax.psum((sum_part * factor, weighted_part * factor[..., None]), 'slot')]
    pmax x1 -> x0, blocking collectives: 38 us -> none  [local(): peak_score = lax.pmax(peak_part, 'slot')]
    ppermute x2 -> x21, starting transfers between devices: 4.37 us -> 32.7 us  [the longest x19 26.8 us: exchange(): return lax.ppermute(block, axis, [(i, i ^ distance) for i in range(size)])]
    dot_general x9 -> x0, matrix products: 27.9 us -> none  [the longest x4 16.5 us: block_scores(): jnp.einsum('qhk,khd->qhd', weights.astype(jnp.bfloat16), value_rows, pref...]
    pallas_call x0 -> x7, Pallas kernels: none -> 19.2 us  [the longest x3 13.8 us: attend(): pl.pallas_call(partial(attend_kernel, head_size, columns, distances, fina...]
    dynamic_slice x13 -> x1, local copies, waits for them, and re-layouts: 12.8 us -> 0.04 us  [local(): lax.dynamic_slice_in_dim(queries, slot_index * width, width, axis=1)]
  transfers between devices with their start and end apart: 4 -> 21, of which waited for: 2 -> 7; matrix products, arithmetic and copies ran while one was open for 32% -> 1% of each run, Pallas kernels for 0% -> 20%
where the time goes in v1:
time: 82 us; the launch traced here: 81.6 us
  starting transfers between devices  32.7 us (40%)
  waiting for transfers between devices  23.2 us (28%)
  Pallas kernels  19.2 us (23%)
  local copies, waits for them, and re-layouts  5.63 us (7%)
  between operations  0.88 us (1%)
    ppermute x19, starting transfers between devices, exchange(): return lax.ppermute(block, axis, [(i, i ^ distance) for i in range(size)])  26.8 us
    ppermute x19, waiting for transfers between devices, exchange(): return lax.ppermute(block, axis, [(i, i ^ distance) for i in range(size)])  23.2 us
    pallas_call x3, Pallas kernels, attend(): pl.pallas_call(partial(attend_kernel, head_size, columns, distances, fina...  13.8 us
    ppermute x2, starting transfers between devices, from_behind(): lax.ppermute(block, axis, [(i - distance, i) for i in devices if i - dist...  5.83 us
    unnamed x22, local copies, waits for them, and re-layouts  4.49 us
    pallas_call x1, Pallas kernels, project(): pl.pallas_call(project_kernel, out_shape=jax.ShapeDtypeStruct((rows, out_...  3.28 us
    pallas_call x1, Pallas kernels, pool(): pl.pallas_call(partial(pool_kernel, head_size), out_shape=jax.ShapeDtypeS...  1.82 us
  transfers between devices with their start and end apart: 21, of which 7 were waited for; matrix products, arithmetic and copies ran while one was open for 1% of the time, Pallas kernels for 20%

profile of v1, /device:TPU:0, one launch (start us, length us, event | category | flops | bytes accessed | tf_op | source)
XLA Modules:
  0.0 81.6 jit_solution(7900442621657953891)
XLA Ops:
  0.7 1.1 %slice.3 = bf16[8,1,64,256]{3,2,1,0:T(8,128)(2,1)S(1)} slice(bf16[8,2,64,256]{3,2,1,0:T(8,128)(2,1)} %raw_ref.1), slice={[0:8], [1:2], [0:64], [0:256]} | slice | bytes 524288 | tf_op jit(solution)/shard_map/slice | solution.py:305
  1.8 2.4 %collective-permute-start.6 = (bf16[8,1,64,256]{3,2,1,0:T(8,128)(2,1)S(1)}, bf16[8,1,64,256]{3,2,1,0:T(8,128)(2,1)S(1)}, u32[]{:S(2)}, u32[]{:S(2)}) collective-permute-start(bf16[8,1,64,256]{3,2,1,0:T(8,128)(2,1)S(1)} %slice.3), channel_id=1, source_target_pairs={{0,1},{1,2},{2,3},{4,5},{5,6},{6,7},{8,9},{9,10},{10,11},{12,13},{... | collective-permute-start | bytes 786440 | tf_op jit(solution)/shard_map/ppermute | solution.py:32
  5.3 2.4 %collective-permute-start.7 = (bf16[128,256]{1,0:T(8,128)(2,1)S(1)}, bf16[128,256]{1,0:T(8,128)(2,1)S(1)}, u32[]{:S(2)}, u32[]{:S(2)}) collective-permute-start(bf16[128,256]{1,0:T(8,128)(2,1)S(1)} %get-tuple-element.20), channel_id=1, source_target_pairs={{0,4},{4,0},{8,12},{12,8},{16,20},{20,16},{24,28},{28,24},{1,5},{5... | collective-permute-start | bytes 196616 | tf_op jit(solution)/shard_map/ppermute | solution.py:27
  7.7 1.6 %collective-permute-start.8 = (bf16[128,256]{1,0:T(8,128)(2,1)S(1)}, bf16[128,256]{1,0:T(8,128)(2,1)S(1)}, u32[]{:S(2)}, u32[]{:S(2)}) collective-permute-start(bf16[128,256]{1,0:T(8,128)(2,1)S(1)} %get-tuple-element.21), channel_id=1, source_target_pairs={{0,8},{4,12},{8,0},{12,4},{16,24},{20,28},{24,16},{28,20},{1,9},{5... | collective-permute-start | bytes 196616 | tf_op jit(solution)/shard_map/ppermute | solution.py:27
  9.3 3.0 %collective-permute-start.1 = (bf16[128,256]{1,0:T(8,128)(2,1)S(1)}, bf16[128,256]{1,0:T(8,128)(2,1)S(1)}, u32[]{:S(2)}, u32[]{:S(2)}) collective-permute-start(bf16[128,256]{1,0:T(8,128)(2,1)S(1)} %get-tuple-element.15), channel_id=1, source_target_pairs={{0,16},{4,20},{8,24},{12,28},{16,0},{20,4},{24,8},{28,12},{1,17},{... | collective-permute-start | bytes 196616 | tf_op jit(solution)/shard_map/ppermute | solution.py:27
  12.3 2.7 %collective-permute-done.1 = bf16[128,256]{1,0:T(8,128)(2,1)S(1)} collective-permute-done((bf16[128,256]{1,0:T(8,128)(2,1)S(1)}, bf16[128,256]{1,0:T(8,128)(2,1)S(1)}, u32[]{:S(2)}, u32[]{:S(2)}) %collective-permute-start.1) | collective-permute-done | bytes 65568 | tf_op jit(solution)/shard_map/ppermute | solution.py:27
  15.0 4.1 %collective-permute-start.2 = (bf16[128,256]{1,0:T(8,128)(2,1)S(1)}, bf16[128,256]{1,0:T(8,128)(2,1)S(1)}, u32[]{:S(2)}, u32[]{:S(2)}) collective-permute-start(bf16[128,256]{1,0:T(8,128)(2,1)S(1)} %get-tuple-element.16), channel_id=1, source_target_pairs={{0,20},{4,16},{8,28},{12,24},{16,4},{20,0},{24,12},{28,8},{1,21},{... | collective-permute-start | bytes 196616 | tf_op jit(solution)/shard_map/ppermute | solution.py:27
  19.1 2.2 %collective-permute-done.2 = bf16[128,256]{1,0:T(8,128)(2,1)S(1)} collective-permute-done((bf16[128,256]{1,0:T(8,128)(2,1)S(1)}, bf16[128,256]{1,0:T(8,128)(2,1)S(1)}, u32[]{:S(2)}, u32[]{:S(2)}) %collective-permute-start.2) | collective-permute-done | bytes 65568 | tf_op jit(solution)/shard_map/ppermute | solution.py:27
  21.3 1.4 %collective-permute-start = (bf16[512,128]{1,0:T(8,128)(2,1)S(1)}, bf16[512,128]{1,0:T(8,128)(2,1)S(1)}, u32[]{:S(2)}, u32[]{:S(2)}) collective-permute-start(bf16[512,128]{1,0:T(8,128)(2,1)S(1)} %constant_dynamic-slice_fusion.query_ref), channel_id=1, source_target_pairs={{0,2},{1,3},{2,0},{3,1},{4,6},{5,7},{6,4},{7,5},{8,10},{9,11},{10,... | collective-permute-start | bytes 393224 | tf_op jit(solution)/shard_map/ppermute | solution.py:27
  22.7 4.1 %collective-permute-start.3 = (bf16[128,256]{1,0:T(8,128)(2,1)S(1)}, bf16[128,256]{1,0:T(8,128)(2,1)S(1)}, u32[]{:S(2)}, u32[]{:S(2)}) collective-permute-start(bf16[128,256]{1,0:T(8,128)(2,1)S(1)} %get-tuple-element.17), channel_id=1, source_target_pairs={{0,24},{4,28},{8,16},{12,20},{16,8},{20,12},{24,0},{28,4},{1,25},{... | collective-permute-start | bytes 196616 | tf_op jit(solution)/shard_map/ppermute | solution.py:27
  28.6 1.8 %pool.1 = bf16[4,1,32,256]{3,2,1,0:T(8,128)(2,1)} custom-call(bf16[8,2,64,256]{3,2,1,0:T(8,128)(2,1)S(1)} %copy-done.2, bf16[8,1,64,256]{3,2,1,0:T(8,128)(2,1)S(1)} %collective-permute-done.6.halo_ref, bf16[27,256]{1,0:T(8,128)(2,1)S(1)} %copy-done.5), custom_call_target="tpu_custom_call" | custom-call | tf_op jit(solution)/shard_map/pool/pallas_call | solution.py:75
  32.5 5.8 %collective-permute-done.4 = bf16[128,256]{1,0:T(8,128)(2,1)S(1)} collective-permute-done((bf16[128,256]{1,0:T(8,128)(2,1)S(1)}, bf16[128,256]{1,0:T(8,128)(2,1)S(1)}, u32[]{:S(2)}, u32[]{:S(2)}) %collective-permute-start.4) | collective-permute-done | bytes 65568 | tf_op jit(solution)/shard_map/ppermute | solution.py:27
  38.4 3.5 %collective-permute-start.20 = (bf16[1,4,1,32,2048]{4,3,2,1,0:T(8,128)(2,1)S(1)}, bf16[1,4,1,32,2048]{4,3,2,1,0:T(8,128)(2,1)S(1)}, u32[]{:S(2)}, u32[]{:S(2)}) collective-permute-start(bf16[1,4,1,32,2048]{4,3,2,1,0:T(8,128)(2,1)S(1)} %copy-done.4), channel_id=1, source_target_pairs={{0,4},{4,8},{8,12},{12,16},{16,20},{20,24},{24,28},{1,5},{5,9},{9,... | collective-permute-start | bytes 1572872 | tf_op jit(solution)/shard_map/ppermute | solution.py:32
  41.9 6.0 %attend.3.refs_2_ = f32[2,1024,128]{2,1,0:T(8,128)S(1)} custom-call(s32[1]{0:T(128)} %bitcast.place_ref, s32[9]{0:T(128)S(1)} %copy-done.6, bf16[1024,128]{1,0:T(8,128)(2,1)S(1)} %pad_maximum_fusion.query_ref, bf16[640,256]{1,0:T(8,128)(2,1)S(1)} %constant_dynamic-update-slice_fusion.4.refs_0_, bf16[640,256]{1,0:T(8,128)(2,1)S(1)} %collective-permute-done.10.refs_1_), custom_call_target="tpu_custom_call" | custom-call | flops 1342177280 | bytes 3407872 | tf_op jit(solution)/shard_map/attend/pallas_call | solution.py:214
  47.9 3.9 %attend.4 = (bf16[512,128]{1,0:T(8,128)(2,1)S(1)}, f32[8,512]{1,0:T(8,128)S(1)}) custom-call(s32[1]{0:T(128)} %bitcast.place_ref, s32[9]{0:T(128)S(1)} %copy-done.6, bf16[512,128]{1,0:T(8,128)(2,1)S(1)} %collective-permute-done.query_ref, bf16[512,256]{1,0:T(8,128)(2,1)S(1)} %constant_dynamic-update-slice_fusion.refs_0_, ...), custom_call_target="tpu_custom_call" | custom-call | flops 536870912 | bytes 2097152 | tf_op jit(solution)/shard_map/attend/pallas_call | solution.py:214
  51.8 1.8 %collective-permute-start.11 = (bf16[512,128]{1,0:T(8,128)(2,1)S(1)}, bf16[512,128]{1,0:T(8,128)(2,1)S(1)}, u32[]{:S(2)}, u32[]{:S(2)}) collective-permute-start(bf16[512,128]{1,0:T(8,128)(2,1)S(1)} %get-tuple-element.23), channel_id=1, source_target_pairs={{0,2},{1,3},{2,0},{3,1},{4,6},{5,7},{6,4},{7,5},{8,10},{9,11},{10,... | collective-permute-start | bytes 393224 | tf_op jit(solution)/shard_map/ppermute | solution.py:27
  53.9 3.9 %attend.5 = (f32[512,128]{1,0:T(8,128)S(1)}, f32[8,512]{1,0:T(8,128)S(1)}) custom-call(s32[1]{0:T(128)} %bitcast.place_ref, s32[9]{0:T(128)S(1)} %copy-done.6, bf16[512,128]{1,0:T(8,128)(2,1)S(1)} %constant_dynamic-slice_fusion.query_ref, bf16[512,256]{1,0:T(8,128)(2,1)S(1)} %constant_dynamic-update-slice_fusion.refs_0_, ...), custom_call_target="tpu_custom_call" | custom-call | flops 536870912 | bytes 2097152 | tf_op jit(solution)/shard_map/attend/pallas_call | solution.py:214
  58.7 3.8 %collective-permute-start.18 = (bf16[512,128]{1,0:T(8,128)(2,1)S(1)}, bf16[512,128]{1,0:T(8,128)(2,1)S(1)}, u32[]{:S(2)}, u32[]{:S(2)}) collective-permute-start(bf16[512,128]{1,0:T(8,128)(2,1)S(1)} %merge.1.refs_0_), channel_id=1, source_target_pairs={{0,24},{4,28},{8,16},{12,20},{16,8},{20,12},{24,0},{28,4},{1,25},{... | collective-permute-start | bytes 393224 | tf_op jit(solution)/shard_map/ppermute | solution.py:27
  62.8 2.2 %collective-permute-done.14.refs_2_ = bf16[512,128]{1,0:T(8,128)(2,1)S(1)} collective-permute-done((bf16[512,128]{1,0:T(8,128)(2,1)S(1)}, bf16[512,128]{1,0:T(8,128)(2,1)S(1)}, u32[]{:S(2)}, u32[]{:S(2)}) %collective-permute-start.14) | collective-permute-done | bytes 131104 | tf_op jit(solution)/shard_map/ppermute | solution.py:27
  65.3 5.8 %collective-permute-done.16.refs_4_ = bf16[512,128]{1,0:T(8,128)(2,1)S(1)} collective-permute-done((bf16[512,128]{1,0:T(8,128)(2,1)S(1)}, bf16[512,128]{1,0:T(8,128)(2,1)S(1)}, u32[]{:S(2)}, u32[]{:S(2)}) %collective-permute-start.16) | collective-permute-done | bytes 131104 | tf_op jit(solution)/shard_map/ppermute | solution.py:27
  71.4 1.8 %collective-permute-start.19 = (bf16[512,128]{1,0:T(8,128)(2,1)S(1)}, bf16[512,128]{1,0:T(8,128)(2,1)S(1)}, u32[]{:S(2)}, u32[]{:S(2)}) collective-permute-start(bf16[512,128]{1,0:T(8,128)(2,1)S(1)} %collective-permute-done.18.refs_6_), channel_id=1, source_target_pairs={{0,4},{4,0},{8,12},{12,8},{16,20},{20,16},{24,28},{28,24},{1,5},{5... | collective-permute-start | bytes 393224 | tf_op jit(solution)/shard_map/ppermute | solution.py:27
  73.2 2.9 %collective-permute-done.17.refs_5_ = bf16[512,128]{1,0:T(8,128)(2,1)S(1)} collective-permute-done((bf16[512,128]{1,0:T(8,128)(2,1)S(1)}, bf16[512,128]{1,0:T(8,128)(2,1)S(1)}, u32[]{:S(2)}, u32[]{:S(2)}) %collective-permute-start.17) | collective-permute-done | bytes 131104 | tf_op jit(solution)/shard_map/ppermute | solution.py:27
  76.1 1.4 %collective-permute-done.19.refs_7_ = bf16[512,128]{1,0:T(8,128)(2,1)S(1)} collective-permute-done((bf16[512,128]{1,0:T(8,128)(2,1)S(1)}, bf16[512,128]{1,0:T(8,128)(2,1)S(1)}, u32[]{:S(2)}, u32[]{:S(2)}) %collective-permute-start.19) | collective-permute-done | bytes 131104 | tf_op jit(solution)/shard_map/ppermute | solution.py:27
  77.5 3.3 %project.1 = bf16[512,1024]{1,0:T(8,128)(2,1)} custom-call(s32[1]{0:T(128)} %bitcast.place_ref, bf16[1024,1024]{1,0:T(8,128)(2,1)S(1)} %copy-done.1, bf16[512,128]{1,0:T(8,128)(2,1)S(1)} %merge.1.refs_0_, bf16[512,128]{1,0:T(8,128)(2,1)S(1)} %collective-permute-done.13.refs_1_, bf16[512,128]{1,0:T(8,128)(2,1)S(1)} %collective-permute-done.14.refs_2_, ...), custom_call_target="tpu_custom_call" | custom-call | tf_op jit(solution)/shard_map/project/pallas_call | solution.py:284
  (52 shorter events, 7.8 us)
Async XLA Ops:
  0.6 37.7 %copy-start.4 = (bf16[1,4,1,32,2048]{4,3,2,1,0:T(8,128)(2,1)S(1)}, bf16[1,4,1,32,2048]{4,3,2,1,0:T(8,128)(2,1)}, u32[]{:S(2)}) copy-start(bf16[1,4,1,32,2048]{4,3,2,1,0:T(8,128)(2,1)} %param.9) | copy-start | bytes 1572868
  0.7 41.2 %copy-start.6 = (s32[9]{0:T(128)S(1)}, s32[9]{0:T(128)}, u32[]{:S(2)}) copy-start(s32[9]{0:T(128)} %valid_ref.5) | copy-start | bytes 112
  1.8 21.0 %collective-permute-start.6 = (bf16[8,1,64,256]{3,2,1,0:T(8,128)(2,1)S(1)}, bf16[8,1,64,256]{3,2,1,0:T(8,128)(2,1)S(1)}, u32[]{:S(2)}, u32[]{:S(2)}) collective-permute-start(bf16[8,1,64,256]{3,2,1,0:T(8,128)(2,1)S(1)} %slice.3), channel_id=1, source_target_pairs={{0,1},{1,2},{2,3},{4,5},{5,6},{6,7},{8,9},{9,10},{10,11},{12,13},{... | collective-permute-start | bytes 786440 | tf_op jit(solution)/shard_map/ppermute | solution.py:32
  5.3 26.0 %collective-permute-start.7 = (bf16[128,256]{1,0:T(8,128)(2,1)S(1)}, bf16[128,256]{1,0:T(8,128)(2,1)S(1)}, u32[]{:S(2)}, u32[]{:S(2)}) collective-permute-start(bf16[128,256]{1,0:T(8,128)(2,1)S(1)} %get-tuple-element.20), channel_id=1, source_target_pairs={{0,4},{4,0},{8,12},{12,8},{16,20},{20,16},{24,28},{28,24},{1,5},{5... | collective-permute-start | bytes 196616 | tf_op jit(solution)/shard_map/ppermute | solution.py:27
  7.7 24.7 %collective-permute-start.8 = (bf16[128,256]{1,0:T(8,128)(2,1)S(1)}, bf16[128,256]{1,0:T(8,128)(2,1)S(1)}, u32[]{:S(2)}, u32[]{:S(2)}) collective-permute-start(bf16[128,256]{1,0:T(8,128)(2,1)S(1)} %get-tuple-element.21), channel_id=1, source_target_pairs={{0,8},{4,12},{8,0},{12,4},{16,24},{20,28},{24,16},{28,20},{1,9},{5... | collective-permute-start | bytes 196616 | tf_op jit(solution)/shard_map/ppermute | solution.py:27
  9.3 23.1 %collective-permute-start.9 = (bf16[128,256]{1,0:T(8,128)(2,1)S(1)}, bf16[128,256]{1,0:T(8,128)(2,1)S(1)}, u32[]{:S(2)}, u32[]{:S(2)}) collective-permute-start(bf16[128,256]{1,0:T(8,128)(2,1)S(1)} %get-tuple-element.22), channel_id=1, source_target_pairs={{0,12},{4,8},{8,4},{12,0},{16,28},{20,24},{24,20},{28,16},{1,13},{... | collective-permute-start | bytes 196616 | tf_op jit(solution)/shard_map/ppermute | solution.py:27
  9.3 5.7 %collective-permute-start.1 = (bf16[128,256]{1,0:T(8,128)(2,1)S(1)}, bf16[128,256]{1,0:T(8,128)(2,1)S(1)}, u32[]{:S(2)}, u32[]{:S(2)}) collective-permute-start(bf16[128,256]{1,0:T(8,128)(2,1)S(1)} %get-tuple-element.15), channel_id=1, source_target_pairs={{0,16},{4,20},{8,24},{12,28},{16,0},{20,4},{24,8},{28,12},{1,17},{... | collective-permute-start | bytes 196616 | tf_op jit(solution)/shard_map/ppermute | solution.py:27
  15.0 6.4 %collective-permute-start.2 = (bf16[128,256]{1,0:T(8,128)(2,1)S(1)}, bf16[128,256]{1,0:T(8,128)(2,1)S(1)}, u32[]{:S(2)}, u32[]{:S(2)}) collective-permute-start(bf16[128,256]{1,0:T(8,128)(2,1)S(1)} %get-tuple-element.16), channel_id=1, source_target_pairs={{0,20},{4,16},{8,28},{12,24},{16,4},{20,0},{24,12},{28,8},{1,21},{... | collective-permute-start | bytes 196616 | tf_op jit(solution)/shard_map/ppermute | solution.py:27
  21.3 20.5 %collective-permute-start = (bf16[512,128]{1,0:T(8,128)(2,1)S(1)}, bf16[512,128]{1,0:T(8,128)(2,1)S(1)}, u32[]{:S(2)}, u32[]{:S(2)}) collective-permute-start(bf16[512,128]{1,0:T(8,128)(2,1)S(1)} %constant_dynamic-slice_fusion.query_ref), channel_id=1, source_target_pairs={{0,2},{1,3},{2,0},{3,1},{4,6},{5,7},{6,4},{7,5},{8,10},{9,11},{10,... | collective-permute-start | bytes 393224 | tf_op jit(solution)/shard_map/ppermute | solution.py:27
  22.7 9.7 %collective-permute-start.3 = (bf16[128,256]{1,0:T(8,128)(2,1)S(1)}, bf16[128,256]{1,0:T(8,128)(2,1)S(1)}, u32[]{:S(2)}, u32[]{:S(2)}) collective-permute-start(bf16[128,256]{1,0:T(8,128)(2,1)S(1)} %get-tuple-element.17), channel_id=1, source_target_pairs={{0,24},{4,28},{8,16},{12,20},{16,8},{20,12},{24,0},{28,4},{1,25},{... | collective-permute-start | bytes 196616 | tf_op jit(solution)/shard_map/ppermute | solution.py:27
  31.3 7.0 %collective-permute-start.4 = (bf16[128,256]{1,0:T(8,128)(2,1)S(1)}, bf16[128,256]{1,0:T(8,128)(2,1)S(1)}, u32[]{:S(2)}, u32[]{:S(2)}) collective-permute-start(bf16[128,256]{1,0:T(8,128)(2,1)S(1)} %get-tuple-element.18), channel_id=1, source_target_pairs={{0,28},{4,24},{8,20},{12,16},{16,12},{20,8},{24,4},{28,0},{1,29},{... | collective-permute-start | bytes 196616 | tf_op jit(solution)/shard_map/ppermute | solution.py:27
  32.4 9.5 %collective-permute-start.10 = (bf16[640,256]{1,0:T(8,128)(2,1)S(1)}, bf16[640,256]{1,0:T(8,128)(2,1)S(1)}, u32[]{:S(2)}, u32[]{:S(2)}) collective-permute-start(bf16[640,256]{1,0:T(8,128)(2,1)S(1)} %constant_dynamic-update-slice_fusion.4.refs_0_), channel_id=1, source_target_pairs={{0,1},{1,0},{2,3},{3,2},{4,5},{5,4},{6,7},{7,6},{8,9},{9,8},{10,11... | collective-permute-start | bytes 983048 | tf_op jit(solution)/shard_map/ppermute | solution.py:27
  38.3 9.5 %collective-permute-start.5 = (bf16[512,256]{1,0:T(8,128)(2,1)S(1)}, bf16[512,256]{1,0:T(8,128)(2,1)S(1)}, u32[]{:S(2)}, u32[]{:S(2)}) collective-permute-start(bf16[512,256]{1,0:T(8,128)(2,1)S(1)} %constant_dynamic-update-slice_fusion.refs_0_), channel_id=1, source_target_pairs={{0,1},{1,0},{2,3},{3,2},{4,5},{5,4},{6,7},{7,6},{8,9},{9,8},{10,11... | collective-permute-start | bytes 786440 | tf_op jit(solution)/shard_map/ppermute | solution.py:27
  38.4 34.8 %collective-permute-start.20 = (bf16[1,4,1,32,2048]{4,3,2,1,0:T(8,128)(2,1)S(1)}, bf16[1,4,1,32,2048]{4,3,2,1,0:T(8,128)(2,1)S(1)}, u32[]{:S(2)}, u32[]{:S(2)}) collective-permute-start(bf16[1,4,1,32,2048]{4,3,2,1,0:T(8,128)(2,1)S(1)} %copy-done.4), channel_id=1, source_target_pairs={{0,4},{4,8},{8,12},{12,16},{16,20},{20,24},{24,28},{1,5},{5,9},{9,... | collective-permute-start | bytes 1572872 | tf_op jit(solution)/shard_map/ppermute | solution.py:32
  47.9 29.7 %copy-start.1 = (bf16[1024,1024]{1,0:T(8,128)(2,1)S(1)}, bf16[1024,1024]{1,0:T(8,128)(2,1)}, u32[]{:S(2)}) copy-start(bf16[1024,1024]{1,0:T(8,128)(2,1)} %weight_ref.3) | copy-start | bytes 6291460
  51.8 6.0 %collective-permute-start.11 = (bf16[512,128]{1,0:T(8,128)(2,1)S(1)}, bf16[512,128]{1,0:T(8,128)(2,1)S(1)}, u32[]{:S(2)}, u32[]{:S(2)}) collective-permute-start(bf16[512,128]{1,0:T(8,128)(2,1)S(1)} %get-tuple-element.23), channel_id=1, source_target_pairs={{0,2},{1,3},{2,0},{3,1},{4,6},{5,7},{6,4},{7,5},{8,10},{9,11},{10,... | collective-permute-start | bytes 393224 | tf_op jit(solution)/shard_map/ppermute | solution.py:27
  53.6 4.2 %collective-permute-start.12 = (f32[8,512]{1,0:T(8,128)S(1)}, f32[8,512]{1,0:T(8,128)S(1)}, u32[]{:S(2)}, u32[]{:S(2)}) collective-permute-start(f32[8,512]{1,0:T(8,128)S(1)} %get-tuple-element.24), channel_id=1, source_target_pairs={{0,2},{1,3},{2,0},{3,1},{4,6},{5,7},{6,4},{7,5},{8,10},{9,11},{10,... | collective-permute-start | bytes 49160 | tf_op jit(solution)/shard_map/ppermute | solution.py:27
  58.1 6.9 %collective-permute-start.14 = (bf16[512,128]{1,0:T(8,128)(2,1)S(1)}, bf16[512,128]{1,0:T(8,128)(2,1)S(1)}, u32[]{:S(2)}, u32[]{:S(2)}) collective-permute-start(bf16[512,128]{1,0:T(8,128)(2,1)S(1)} %merge.1.refs_0_), channel_id=1, source_target_pairs={{0,8},{4,12},{8,0},{12,4},{16,24},{20,28},{24,16},{28,20},{1,9},{5... | collective-permute-start | bytes 393224 | tf_op jit(solution)/shard_map/ppermute | solution.py:27
  58.2 12.9 %collective-permute-start.16 = (bf16[512,128]{1,0:T(8,128)(2,1)S(1)}, bf16[512,128]{1,0:T(8,128)(2,1)S(1)}, u32[]{:S(2)}, u32[]{:S(2)}) collective-permute-start(bf16[512,128]{1,0:T(8,128)(2,1)S(1)} %merge.1.refs_0_), channel_id=1, source_target_pairs={{0,16},{4,20},{8,24},{12,28},{16,0},{20,4},{24,8},{28,12},{1,17},{... | collective-permute-start | bytes 393224 | tf_op jit(solution)/shard_map/ppermute | solution.py:27
  58.7 12.7 %collective-permute-start.18 = (bf16[512,128]{1,0:T(8,128)(2,1)S(1)}, bf16[512,128]{1,0:T(8,128)(2,1)S(1)}, u32[]{:S(2)}, u32[]{:S(2)}) collective-permute-start(bf16[512,128]{1,0:T(8,128)(2,1)S(1)} %merge.1.refs_0_), channel_id=1, source_target_pairs={{0,24},{4,28},{8,16},{12,20},{16,8},{20,12},{24,0},{28,4},{1,25},{... | collective-permute-start | bytes 393224 | tf_op jit(solution)/shard_map/ppermute | solution.py:27
  62.6 10.6 %collective-permute-start.13 = (bf16[512,128]{1,0:T(8,128)(2,1)S(1)}, bf16[512,128]{1,0:T(8,128)(2,1)S(1)}, u32[]{:S(2)}, u32[]{:S(2)}) collective-permute-start(bf16[512,128]{1,0:T(8,128)(2,1)S(1)} %merge.1.refs_0_), channel_id=1, source_target_pairs={{0,4},{4,0},{8,12},{12,8},{16,20},{20,16},{24,28},{28,24},{1,5},{5... | collective-permute-start | bytes 393224 | tf_op jit(solution)/shard_map/ppermute | solution.py:27
  65.0 8.2 %collective-permute-start.15 = (bf16[512,128]{1,0:T(8,128)(2,1)S(1)}, bf16[512,128]{1,0:T(8,128)(2,1)S(1)}, u32[]{:S(2)}, u32[]{:S(2)}) collective-permute-start(bf16[512,128]{1,0:T(8,128)(2,1)S(1)} %collective-permute-done.14.refs_2_), channel_id=1, source_target_pairs={{0,4},{4,0},{8,12},{12,8},{16,20},{20,16},{24,28},{28,24},{1,5},{5... | collective-permute-start | bytes 393224 | tf_op jit(solution)/shard_map/ppermute | solution.py:27
  71.1 5.0 %collective-permute-start.17 = (bf16[512,128]{1,0:T(8,128)(2,1)S(1)}, bf16[512,128]{1,0:T(8,128)(2,1)S(1)}, u32[]{:S(2)}, u32[]{:S(2)}) collective-permute-start(bf16[512,128]{1,0:T(8,128)(2,1)S(1)} %collective-permute-done.16.refs_4_), channel_id=1, source_target_pairs={{0,4},{4,0},{8,12},{12,8},{16,20},{20,16},{24,28},{28,24},{1,5},{5... | collective-permute-start | bytes 393224 | tf_op jit(solution)/shard_map/ppermute | solution.py:27
  71.4 6.1 %collective-permute-start.19 = (bf16[512,128]{1,0:T(8,128)(2,1)S(1)}, bf16[512,128]{1,0:T(8,128)(2,1)S(1)}, u32[]{:S(2)}, u32[]{:S(2)}) collective-permute-start(bf16[512,128]{1,0:T(8,128)(2,1)S(1)} %collective-permute-done.18.refs_6_), channel_id=1, source_target_pairs={{0,4},{4,0},{8,12},{12,8},{16,20},{20,16},{24,28},{28,24},{1,5},{5... | collective-permute-start | bytes 393224 | tf_op jit(solution)/shard_map/ppermute | solution.py:27
  (4 other events, 14.4 us)

commit v2 on v1

--- a/solution.py
+++ b/solution.py
@@ -47,7 +47,7 @@
     for piece in range(pieces):
         lanes = slice(piece * wide, (piece + 1) * wide)
         for f in range(frames):
-            slabs[piece, 3 * f] = halo_ref[f, 0, :, lanes].astype(jnp.float32)
+            slabs[piece, 3 * f] = halo_ref[f, rows - 1, :, lanes].astype(jnp.float32)
             slabs[piece, 3 * f + 1] = raw_ref[f, 0, :, lanes].astype(jnp.float32)
             slabs[piece, 3 * f + 2] = raw_ref[f, 1, :, lanes].astype(jnp.float32)
         weight = weight_ref[:, lanes].astype(jnp.float32)
@@ -107,74 +107,71 @@
     head_size, columns, distances, final, has_state, place_ref, valid_ref, query_ref, *refs
 ):
     refs = list(refs)
-    sources = [refs.pop(0), refs.pop(0)]
+    sources = [refs.pop(0) for _ in distances]
     state_ref = refs.pop(0) if has_state else None
-    if final:
-        value_ref, level_ref = refs.pop(0), refs.pop(0)
-    else:
-        state_out_ref = refs.pop(0)
-    key_scratch, value_scratch = refs
-    heads, key_count, wide = key_scratch.shape
-    tokens = key_count // (2 * len(distances))
-
-    @pl.when(pl.program_id(0) == 0)
-    def _():
-        lane = lanes_of((tokens, wide))
-        column = lax.broadcasted_iota(jnp.int32, (tokens, wide), 0) % columns
-        place = place_ref[0]
-        for b, distance in enumerate(distances):
-            valid = valid_ref[0] if distance is None else valid_ref[1 + (place ^ distance)]
-            extra = jnp.where((lane == head_size) & (column >= valid), MASKED, 0.0)
-            for c, source in enumerate(sources):
-                row = (c * len(distances) + b) * tokens
-                for h in range(heads):
-                    tile = source[b * tokens : (b + 1) * tokens, h * wide : (h + 1) * wide]
-                    tile = tile.astype(jnp.float32)
-                    key_scratch[h, row : row + tokens] = jnp.where(
-                        lane < head_size, tile, extra
-                    ).astype(jnp.bfloat16)
-                    value_scratch[h, row : row + tokens] = jnp.where(
-                        lane < head_size, 1.0, tile
-                    ).astype(jnp.bfloat16)
-
-    block = query_ref.shape[0]
-    lane = lanes_of((block, wide))
+    rows, width = query_ref.shape
+    heads = width // head_size
+    wide = 2 * head_size
+    place = place_ref[0]
+    biases, tokens = [], 0
+    for source, distance in zip(sources, distances):
+        column = lanes_of((1, source.shape[0])) % columns
+        valid = valid_ref[0] if distance is None else valid_ref[1 + (place ^ distance)]
+        biases.append(jnp.where(column < valid, 0.0, MASKED))
+        tokens += source.shape[0]
+    bias = jnp.concatenate(biases, axis=1)
+    lane = lanes_of((rows, wide))
     queries = query_ref[...].astype(jnp.float32) * head_size ** (-0.5)
+    memory, scores = [], []
+    for h in range(heads):
+        own = queries if h == 0 else pltpu.roll(queries, width - h * head_size, 1)
+        if own.shape[1] < wide:
+            own = jnp.concatenate([own, own], axis=1)
+        own = jnp.where(lane < head_size, own, 0.0).astype(jnp.bfloat16)
+        memory.append(
+            jnp.concatenate([source[:, h * wide : (h + 1) * wide] for source in sources], axis=0)
+        )
+        product = lax.dot_general(
+            own, memory[h], (((1,), (1,)), ((), ())), preferred_element_type=jnp.float32
+        )
+        scores.append(product + bias)
+    weights, peaks = [], []
+    for h in range(heads):
+        peak = jnp.max(scores[h], axis=1, keepdims=True)
+        if has_state:
+            peak = jnp.maximum(peak, state_ref[h, :, head_size // 2 : head_size // 2 + 1])
+        peaks.append(peak)
+        weights.append(jnp.exp(scores[h] - peak).astype(jnp.bfloat16))
     values, levels = [], []
+    memory_lane = lanes_of((tokens, wide))
     for h in range(heads):
-        rows = queries if h == 0 else pltpu.roll(queries, wide - h * head_size, 1)
-        if rows.shape[1] < wide:
-            rows = jnp.concatenate([rows, rows], axis=1)
-        rows = jnp.where(lane < head_size, rows, jnp.where(lane == head_size, 1.0, 0.0))
-        scores = lax.dot_general(
-            rows.astype(jnp.bfloat16),
-            key_scratch[h],
-            (((1,), (1,)), ((), ())),
-            preferred_element_type=jnp.float32,
-        )
-        peak = jnp.max(scores, axis=1, keepdims=True)
+        ones_and_values = jnp.where(memory_lane < head_size, 1.0, memory[h].astype(jnp.float32))
+        total = jnp.dot(
+            weights[h], ones_and_values.astype(jnp.bfloat16), preferred_element_type=jnp.float32
+        )
         if has_state:
             state = state_ref[h]
             old_peak = state[:, head_size // 2 : head_size // 2 + 1]
-            peak = jnp.maximum(peak, old_peak)
-        weights = jnp.exp(scores - peak).astype(jnp.bfloat16)
-        total = jnp.dot(weights, value_scratch[h], preferred_element_type=jnp.float32)
-        if has_state:
-            total = total + state * jnp.exp(old_peak - peak)
+            total = total + state * jnp.exp(old_peak - peaks[h])
         if final:
             weight_sum = total[:, :1]
-            values.append(total[:, head_size:] / weight_sum)
-            levels.append(jnp.broadcast_to(peak + jnp.log(weight_sum), (block, head_size)))
+            values.append(total[:, head_size:] * (1.0 / weight_sum))
+            level = peaks[h] + jnp.log(weight_sum)
+            levels.append(jnp.broadcast_to(level, (rows, head_size)))
         else:
             keep = (lane >= head_size // 2) & (lane < head_size)
-            state_out_ref[h] = jnp.where(keep, peak, total)
+            refs[0][h] = jnp.where(keep, peaks[h], total)
     if final:
-        value_ref[...] = jnp.concatenate(values, axis=1).astype(value_ref.dtype)
-        level = jnp.concatenate(levels, axis=1)
-        if level.shape[1] < wide:
-            level = jnp.concatenate([level, level], axis=1)
-        turned = level.T
-        for h in range(heads):
+        refs[0][...] = jnp.concatenate(values, axis=1).astype(refs[0].dtype)
+        write_levels(refs[1], jnp.concatenate(levels, axis=1), head_size)
+
+
+def write_levels(level_ref, level, head_size):
+    if level.shape[1] < 128:
+        level = jnp.concatenate([level, level], axis=1)
+    turned = level.T
+    for h in range(H):
+        if (h + 1) * head_size <= level.shape[1]:
             level_ref[h : h + 1, :] = turned[h * head_size : h * head_size + 1, :]
 
 
@@ -184,17 +181,15 @@
     rows, width = queries.shape
     heads = width // head_size
     wide = 2 * head_size
-    key_count = 2 * sources[0].shape[0]
-    block = min(256, rows)
+    key_count = sum(source.shape[0] for source in sources)
+    block = min(512, rows)
     start = state_start // block
     whole = pl.BlockSpec(memory_space=VMEM)
     in_specs = [
         pl.BlockSpec(memory_space=SMEM),
         pl.BlockSpec(memory_space=SMEM),
         pl.BlockSpec((block, width), lambda i: (i, 0)),
-        whole,
-        whole,
-    ]
+    ] + [whole] * len(sources)
     operands = [place, valid, queries, *sources]
     if state is not None:
         in_specs.append(pl.BlockSpec((heads, block, wide), lambda i: (0, i + start, 0)))
@@ -217,7 +212,6 @@
         out_shape=out_shape,
         in_specs=in_specs,
         out_specs=out_specs,
-        scratch_shapes=[VMEM((heads, key_count, wide), jnp.bfloat16)] * 2,
         compiler_params=params(),
         cost_estimate=pl.CostEstimate(
             flops=4 * rows * key_count * wide * heads,
@@ -228,18 +222,15 @@
     )(*operands)
 
 
-def merge_kernel(head_size, *refs):
-    out_ref = refs[-1]
-    refs = refs[:-1]
-    values = [ref[...].astype(jnp.float32) for ref in refs[0::2]]
+def merge_kernel(head_size, count, final, *refs):
+    parts, outs = refs[: 2 * count], refs[2 * count :]
+    values = [ref[...].astype(jnp.float32) for ref in parts[0::2]]
     rows, width = values[0].shape
     heads = width // head_size
     levels = []
-    for ref in refs[1::2]:
-        turned = jnp.concatenate(
-            [jnp.broadcast_to(ref[h : h + 1, :], (head_size, rows)) for h in range(heads)], axis=0
-        )
-        levels.append(turned.T)
+    for ref in parts[1::2]:
+        spread = [jnp.broadcast_to(ref[h : h + 1, :], (head_size, rows)) for h in range(heads)]
+        levels.append(jnp.concatenate(spread, axis=0).T)
     top = levels[0]
     for level in levels[1:]:
         top = jnp.maximum(top, level)
@@ -249,20 +240,38 @@
         factor = jnp.exp(level - top)
         total = total + value * factor
         share = share + factor
-    out_ref[...] = (total / share).astype(out_ref.dtype)
-
-
-def merge(parts, head_size):
-    rows, width = parts[0][0].shape
-    flat = [array for part in parts for array in part]
-    return pl.pallas_call(
-        partial(merge_kernel, head_size),
-        out_shape=jax.ShapeDtypeStruct((rows, width), jnp.bfloat16),
-        in_specs=[pl.BlockSpec(memory_space=VMEM)] * len(flat),
-        out_specs=pl.BlockSpec(memory_space=VMEM),
+    outs[0][...] = (total / share).astype(outs[0].dtype)
+    if not final:
+        write_levels(outs[1], top + jnp.log(share), head_size)
+
+
+def merge(parts, rows, head_size, final):
+    width = parts[0][0].shape[1]
+    operands, in_specs = [], []
+    for value, level, block in parts:
+        operands += [value, level]
+        in_specs += [
+            pl.BlockSpec((rows, width), lambda i, block=block: (block, 0)),
+            pl.BlockSpec((8, rows), lambda i, block=block: (0, block)),
+        ]
+    out_shape = [
+        jax.ShapeDtypeStruct((rows, width), jnp.bfloat16),
+        jax.ShapeDtypeStruct((8, rows), jnp.float32),
+    ]
+    out_specs = [
+        pl.BlockSpec((rows, width), lambda i: (0, 0)),
+        pl.BlockSpec((8, rows), lambda i: (0, 0)),
+    ]
+    keep = 1 if final else 2
+    return pl.pallas_call(
+        partial(merge_kernel, head_size, len(parts), final),
+        grid=(1,),
+        out_shape=out_shape[:keep],
+        in_specs=in_specs,
+        out_specs=out_specs[:keep],
         compiler_params=params(),
         name="merge",
-    )(*flat)
+    )(*operands)
 
 
 def project_kernel(place_ref, weight_ref, *refs):
@@ -302,53 +311,58 @@
     slot_index = lax.axis_index("slot")
     place = slot_index.astype(jnp.int32).reshape(1)
 
-    halo = from_behind(raw_clip[:, -1:], "space", 1)
-    own_queries = lax.dynamic_slice_in_dim(queries, slot_index * width, width, axis=1)
-    space_partners = range(2, spaces, 2)
-    all_queries = [own_queries] + [exchange(own_queries, "space", d) for d in space_partners]
-
     resident = old_memory.reshape(-1, old_memory.shape[-1])
     pieces = cut(place, resident, slots)
-    received = [pieces[0]] + [exchange(pieces[d], "slot", d) for d in range(1, slots)]
-
-    fresh = pool(raw_clip, halo, pool_weight, head_size)
+    received = {0: pieces[0]}
+    for d in reversed(range(1, slots)):
+        received[d] = exchange(pieces[d], "slot", d)
+
+    own_queries = lax.dynamic_slice_in_dim(queries, slot_index * width, width, axis=1)
+    evens = range(2, spaces, 2)
+    near = jnp.concatenate([exchange(own_queries, "space", e) for e in evens] + [own_queries], 0)
+    far = exchange(near, "space", 1)
+
+    behind = from_behind(raw_clip, "space", 1)
+    fresh = pool(raw_clip, behind, pool_weight, head_size)
     fresh_rows = fresh.reshape(-1, fresh.shape[-1])
 
     half = slots // 2
-    first = jnp.concatenate([fresh_rows] + received[:half], axis=0)
-    first_other = exchange(first, "space", 1)
-    second = jnp.concatenate(received[half:], axis=0)
-    second_other = exchange(second, "space", 1)
-
+    first = (0,) + tuple(range(half, slots))
+    second = tuple(range(1, half))
     call = partial(attend, place, valid_columns, columns=columns, head_size=head_size)
     state = call(
-        jnp.concatenate(all_queries, axis=0),
-        (first, first_other),
+        jnp.concatenate([far, near], axis=0),
+        [received[d] for d in first],
         None,
         0,
-        distances=(None,) + tuple(range(half)),
+        distances=first,
         final=False,
         dtype=None,
     )
+    sources = [fresh_rows] + [received[d] for d in second]
+    call = partial(call, sources=sources, state=state, distances=(None,) + second, final=True)
+    far_value, far_level = call(queries=far, state_start=0, dtype=jnp.bfloat16)
+    core_value = exchange(far_value, "space", 1)
+    core_level = exchange(far_level, "space", 1)
     parts = []
-    for k in list(range(1, len(all_queries))) + [0]:
+    for k, e in enumerate(evens):
+        rows = slice(k * query_rows, (k + 1) * query_rows)
         value, level = call(
-            all_queries[k],
-            (second, second_other),
-            state,
-            k * query_rows,
-            distances=tuple(range(half, slots)),
-            final=True,
-            dtype=jnp.bfloat16 if k else jnp.float32,
-        )
-        if k:
-            value = exchange(value, "space", 2 * k)
-            level = exchange(level, "space", 2 * k)
-        parts.append((value, level))
-    mixed = merge(parts, head_size)
+            queries=near[rows], state_start=far.shape[0] + k * query_rows, dtype=jnp.float32
+        )
+        value, level = merge(
+            [(value, level, 0), (core_value, core_level, k)], query_rows, head_size, False
+        )
+        parts.append((exchange(value, "space", e), exchange(level, "space", e), 0))
+    last = len(evens)
+    value, level = call(
+        queries=own_queries, state_start=far.shape[0] + last * query_rows, dtype=jnp.float32
+    )
+    parts = [(value, level, 0), (core_value, core_level, last)] + parts
+    (mixed,) = merge(parts, query_rows, head_size, True)
 
     blocks = {0: mixed}
-    for d in range(2, slots, 2):
+    for d in reversed(range(2, slots, 2)):
         blocks[d] = exchange(mixed, "slot", d)
     for d in range(0, slots, 2):
         blocks[d + 1] = exchange(blocks[d], "slot", 1)

time: 82 us -> 80.9 us (0.987)
  waiting for transfers between devices: 23.2 us -> 18.6 us
  Pallas kernels: 19.2 us -> 22.7 us
  starting transfers between devices: 32.7 us -> 34.4 us
  local copies, waits for them, and re-layouts: 5.63 us -> 3.94 us
    ppermute x19 -> x20, waiting for transfers between devices: 23.2 us -> 18.6 us  [exchange(): return lax.ppermute(block, axis, [(i, i ^ distance) for i in range(size)])]
    pallas_call x3 -> x4, Pallas kernels: 13.8 us -> 16.8 us  [attend(): pl.pallas_call(partial(attend_kernel, head_size, columns, distances, fina...]
    ppermute x19 -> x20, starting transfers between devices: 26.8 us -> 29.6 us  [exchange(): return lax.ppermute(block, axis, [(i, i ^ distance) for i in range(size)])]
    slice x1 -> x0, local copies, waits for them, and re-layouts: 1.09 us -> none  [local(): halo = from_behind(raw_clip[:, -1:], 'space', 1)]
    ppermute x2, starting transfers between devices: 5.83 us -> 4.86 us  [from_behind(): lax.ppermute(block, axis, [(i - distance, i) for i in devices if i - dist...]
    unnamed x22 -> x19, local copies, waits for them, and re-layouts: 4.49 us -> 3.9 us
  transfers between devices with their start and end apart: 21 -> 22, of which waited for: 7 -> 6; matrix products, arithmetic and copies ran while one was open for 1% -> 0% of each run, Pallas kernels for 20% -> 17%
where the time goes in v2:
time: 80.9 us; the launch traced here: 80.6 us
  starting transfers between devices  34.4 us (43%)
  Pallas kernels  22.7 us (28%)
  waiting for transfers between devices  18.6 us (23%)
  local copies, waits for them, and re-layouts  3.94 us (5%)
  between operations  0.87 us (1%)
    ppermute x20, starting transfers between devices, exchange(): return lax.ppermute(block, axis, [(i, i ^ distance) for i in range(size)])  29.6 us
    ppermute x20, waiting for transfers between devices, exchange(): return lax.ppermute(block, axis, [(i, i ^ distance) for i in range(size)])  18.6 us
    pallas_call x4, Pallas kernels, attend(): pl.pallas_call(partial(attend_kernel, head_size, columns, distances, fina...  16.8 us
    ppermute x2, starting transfers between devices, from_behind(): lax.ppermute(block, axis, [(i - distance, i) for i in devices if i - dist...  4.86 us
    unnamed x19, local copies, waits for them, and re-layouts  3.9 us
    pallas_call x1, Pallas kernels, project(): pl.pallas_call(project_kernel, out_shape=jax.ShapeDtypeStruct((rows, out_...  3.29 us
    pallas_call x1, Pallas kernels, pool(): pl.pallas_call(partial(pool_kernel, head_size), out_shape=jax.ShapeDtypeS...  1.84 us
  transfers between devices with their start and end apart: 22, of which 6 were waited for; matrix products, arithmetic and copies ran while one was open for 0% of the time, Pallas kernels for 17%

profile of v2, /device:TPU:0, one launch (start us, length us, event | category | flops | bytes accessed | tf_op | source)
XLA Modules:
  0.0 80.6 jit_solution(974946002994330113)
XLA Ops:
  1.9 3.0 %collective-permute-start.4 = (bf16[512,128]{1,0:T(8,128)(2,1)S(1)}, bf16[512,128]{1,0:T(8,128)(2,1)S(1)}, u32[]{:S(2)}, u32[]{:S(2)}) collective-permute-start(bf16[512,128]{1,0:T(8,128)(2,1)S(1)} %constant_dynamic-slice_fusion.query_ref), channel_id=1, source_target_pairs={{0,2},{1,3},{2,0},{3,1},{4,6},{5,7},{6,4},{7,5},{8,10},{9,11},{10,... | collective-permute-start | bytes 393224 | tf_op jit(solution)/shard_map/ppermute | solution.py:27
  4.9 3.5 %collective-permute-done.4.query_ref = bf16[512,128]{1,0:T(8,128)(2,1)S(1)} collective-permute-done((bf16[512,128]{1,0:T(8,128)(2,1)S(1)}, bf16[512,128]{1,0:T(8,128)(2,1)S(1)}, u32[]{:S(2)}, u32[]{:S(2)}) %collective-permute-start.4) | collective-permute-done | bytes 131104 | tf_op jit(solution)/shard_map/ppermute | solution.py:27
  8.5 2.4 %collective-permute-start = (bf16[8,2,64,256]{3,2,1,0:T(8,128)(2,1)}, bf16[8,2,64,256]{3,2,1,0:T(8,128)(2,1)S(1)}, u32[]{:S(2)}, u32[]{:S(2)}) collective-permute-start(bf16[8,2,64,256]{3,2,1,0:T(8,128)(2,1)} %raw_ref.1), channel_id=1, source_target_pairs={{0,1},{1,2},{2,3},{4,5},{5,6},{6,7},{8,9},{9,10},{10,11},{12,13},{... | collective-permute-start | bytes 1572872 | tf_op jit(solution)/shard_map/ppermute | solution.py:32
  12.0 2.9 %collective-permute-start.6 = (bf16[128,256]{1,0:T(8,128)(2,1)S(1)}, bf16[128,256]{1,0:T(8,128)(2,1)S(1)}, u32[]{:S(2)}, u32[]{:S(2)}) collective-permute-start(bf16[128,256]{1,0:T(8,128)(2,1)S(1)} %get-tuple-element.23), channel_id=1, source_target_pairs={{0,16},{4,20},{8,24},{12,28},{16,0},{20,4},{24,8},{28,12},{1,17},{... | collective-permute-start | bytes 196616 | tf_op jit(solution)/shard_map/ppermute | solution.py:27
  16.2 3.6 %collective-permute-start.8 = (bf16[128,256]{1,0:T(8,128)(2,1)S(1)}, bf16[128,256]{1,0:T(8,128)(2,1)S(1)}, u32[]{:S(2)}, u32[]{:S(2)}) collective-permute-start(bf16[128,256]{1,0:T(8,128)(2,1)S(1)} %get-tuple-element.25), channel_id=1, source_target_pairs={{0,24},{4,28},{8,16},{12,20},{16,8},{20,12},{24,0},{28,4},{1,25},{... | collective-permute-start | bytes 196616 | tf_op jit(solution)/shard_map/ppermute | solution.py:27
  19.9 1.7 %collective-permute-start.1 = (bf16[128,256]{1,0:T(8,128)(2,1)S(1)}, bf16[128,256]{1,0:T(8,128)(2,1)S(1)}, u32[]{:S(2)}, u32[]{:S(2)}) collective-permute-start(bf16[128,256]{1,0:T(8,128)(2,1)S(1)} %get-tuple-element.19), channel_id=1, source_target_pairs={{0,4},{4,0},{8,12},{12,8},{16,20},{20,16},{24,28},{28,24},{1,5},{5... | collective-permute-start | bytes 196616 | tf_op jit(solution)/shard_map/ppermute | solution.py:27
  21.7 3.1 %collective-permute-done.7.refs_2_ = bf16[128,256]{1,0:T(8,128)(2,1)S(1)} collective-permute-done((bf16[128,256]{1,0:T(8,128)(2,1)S(1)}, bf16[128,256]{1,0:T(8,128)(2,1)S(1)}, u32[]{:S(2)}, u32[]{:S(2)}) %collective-permute-start.7) | collective-permute-done | bytes 65568 | tf_op jit(solution)/shard_map/ppermute | solution.py:27
  25.9 3.0 %collective-permute-start.3 = (bf16[128,256]{1,0:T(8,128)(2,1)S(1)}, bf16[128,256]{1,0:T(8,128)(2,1)S(1)}, u32[]{:S(2)}, u32[]{:S(2)}) collective-permute-start(bf16[128,256]{1,0:T(8,128)(2,1)S(1)} %get-tuple-element.21), channel_id=1, source_target_pairs={{0,12},{4,8},{8,4},{12,0},{16,28},{20,24},{24,20},{28,16},{1,13},{... | collective-permute-start | bytes 196616 | tf_op jit(solution)/shard_map/ppermute | solution.py:27
  28.9 5.2 %attend.4.refs_4_ = f32[2,2048,128]{2,1,0:T(8,128)S(1)} custom-call(s32[1]{0:T(128)} %bitcast.place_ref, s32[9]{0:T(128)S(1)} %copy-done.8, bf16[2048,128]{1,0:T(8,128)(2,1)S(1)} %pad_maximum_fusion.query_ref, bf16[128,256]{1,0:T(8,128)(2,1)S(1)} %get-tuple-element.22.refs_0_, bf16[128,256]{1,0:T(8,128)(2,1)S(1)} %collective-permute-done.6.refs_1_, ...), custom_call_target="tpu_custom_call" | custom-call | flops 1342177280 | bytes 4849664 | tf_op jit(solution)/shard_map/attend/pallas_call | solution.py:209
  34.2 1.8 %pool.1 = bf16[4,1,32,256]{3,2,1,0:T(8,128)(2,1)} custom-call(bf16[8,2,64,256]{3,2,1,0:T(8,128)(2,1)S(1)} %copy-done.6, bf16[8,2,64,256]{3,2,1,0:T(8,128)(2,1)S(1)} %collective-permute-done.halo_ref, bf16[27,256]{1,0:T(8,128)(2,1)S(1)} %copy-done.7), custom_call_target="tpu_custom_call" | custom-call | tf_op jit(solution)/shard_map/pool/pallas_call | solution.py:75
  36.9 5.5 %attend.6 = (bf16[1024,128]{1,0:T(8,128)(2,1)S(1)}, f32[8,1024]{1,0:T(8,128)S(1)}) custom-call(s32[1]{0:T(128)} %bitcast.place_ref, s32[9]{0:T(128)S(1)} %copy-done.8, bf16[1024,128]{1,0:T(8,128)(2,1)S(1)} %collective-permute-done.5.query_ref, bf16[128,256]{1,0:T(8,128)(2,1)S(1)} %bitcast.3, bf16[128,256]{1,0:T(8,128)(2,1)S(1)} %collective-permute-done.1.refs_1_, ...), custom_call_target="tpu_custom_call" | custom-call | flops 536870912 | bytes 2621440 | tf_op jit(solution)/shard_map/attend/pallas_call | solution.py:209
  42.5 2.4 %collective-permute-start.21 = (bf16[1,4,1,32,2048]{4,3,2,1,0:T(8,128)(2,1)S(1)}, bf16[1,4,1,32,2048]{4,3,2,1,0:T(8,128)(2,1)S(1)}, u32[]{:S(2)}, u32[]{:S(2)}) collective-permute-start(bf16[1,4,1,32,2048]{4,3,2,1,0:T(8,128)(2,1)S(1)} %copy-done.5), channel_id=1, source_target_pairs={{0,4},{4,8},{8,12},{12,16},{16,20},{20,24},{24,28},{1,5},{5,9},{9,... | collective-permute-start | bytes 1572872 | tf_op jit(solution)/shard_map/ppermute | solution.py:32
  45.2 3.0 %attend.7 = (f32[512,128]{1,0:T(8,128)S(1)}, f32[8,512]{1,0:T(8,128)S(1)}) custom-call(s32[1]{0:T(128)} %bitcast.place_ref, s32[9]{0:T(128)S(1)} %copy-done.8, bf16[512,128]{1,0:T(8,128)(2,1)S(1)} %collective-permute-done.4.query_ref, bf16[128,256]{1,0:T(8,128)(2,1)S(1)} %bitcast.4, bf16[128,256]{1,0:T(8,128)(2,1)S(1)} %collective-permute-done.1.refs_1_, ...), custom_call_target="tpu_custom_call" | custom-call | flops 268435456 | bytes 1572864 | tf_op jit(solution)/shard_map/attend/pallas_call | solution.py:209
  49.1 1.7 %collective-permute-start.13 = (f32[8,512]{1,0:T(8,128)S(1)}, f32[8,512]{1,0:T(8,128)S(1)}, u32[]{:S(2)}, u32[]{:S(2)}) collective-permute-start(f32[8,512]{1,0:T(8,128)S(1)} %get-tuple-element.34), channel_id=1, source_target_pairs={{0,2},{1,3},{2,0},{3,1},{4,6},{5,7},{6,4},{7,5},{8,10},{9,11},{10,... | collective-permute-start | bytes 49160 | tf_op jit(solution)/shard_map/ppermute | solution.py:27
  50.7 3.0 %attend.5 = (f32[512,128]{1,0:T(8,128)S(1)}, f32[8,512]{1,0:T(8,128)S(1)}) custom-call(s32[1]{0:T(128)} %bitcast.place_ref, s32[9]{0:T(128)S(1)} %copy-done.8, bf16[512,128]{1,0:T(8,128)(2,1)S(1)} %constant_dynamic-slice_fusion.query_ref, bf16[128,256]{1,0:T(8,128)(2,1)S(1)} %bitcast.5, bf16[128,256]{1,0:T(8,128)(2,1)S(1)} %collective-permute-done.1.refs_1_, ...), custom_call_target="tpu_custom_call" | custom-call | flops 268435456 | bytes 1572864 | tf_op jit(solution)/shard_map/attend/pallas_call | solution.py:209
  55.2 1.4 %collective-permute-start.15 = (bf16[512,128]{1,0:T(8,128)(2,1)S(1)}, bf16[512,128]{1,0:T(8,128)(2,1)S(1)}, u32[]{:S(2)}, u32[]{:S(2)}) collective-permute-start(bf16[512,128]{1,0:T(8,128)(2,1)S(1)} %merge.3.refs_0_), channel_id=1, source_target_pairs={{0,8},{4,12},{8,0},{12,4},{16,24},{20,28},{24,16},{28,20},{1,9},{5... | collective-permute-start | bytes 393224 | tf_op jit(solution)/shard_map/ppermute | solution.py:27
  56.6 3.0 %collective-permute-start.17 = (bf16[512,128]{1,0:T(8,128)(2,1)S(1)}, bf16[512,128]{1,0:T(8,128)(2,1)S(1)}, u32[]{:S(2)}, u32[]{:S(2)}) collective-permute-start(bf16[512,128]{1,0:T(8,128)(2,1)S(1)} %merge.3.refs_0_), channel_id=1, source_target_pairs={{0,16},{4,20},{8,24},{12,28},{16,0},{20,4},{24,8},{28,12},{1,17},{... | collective-permute-start | bytes 393224 | tf_op jit(solution)/shard_map/ppermute | solution.py:27
  59.6 2.3 %collective-permute-start.14 = (bf16[512,128]{1,0:T(8,128)(2,1)S(1)}, bf16[512,128]{1,0:T(8,128)(2,1)S(1)}, u32[]{:S(2)}, u32[]{:S(2)}) collective-permute-start(bf16[512,128]{1,0:T(8,128)(2,1)S(1)} %merge.3.refs_0_), channel_id=1, source_target_pairs={{0,4},{4,0},{8,12},{12,8},{16,20},{20,16},{24,28},{28,24},{1,5},{5... | collective-permute-start | bytes 393224 | tf_op jit(solution)/shard_map/ppermute | solution.py:27
  61.9 1.5 %collective-permute-start.16 = (bf16[512,128]{1,0:T(8,128)(2,1)S(1)}, bf16[512,128]{1,0:T(8,128)(2,1)S(1)}, u32[]{:S(2)}, u32[]{:S(2)}) collective-permute-start(bf16[512,128]{1,0:T(8,128)(2,1)S(1)} %collective-permute-done.15.refs_2_), channel_id=1, source_target_pairs={{0,4},{4,0},{8,12},{12,8},{16,20},{20,16},{24,28},{28,24},{1,5},{5... | collective-permute-start | bytes 393224 | tf_op jit(solution)/shard_map/ppermute | solution.py:27
  63.4 6.0 %collective-permute-done.17.refs_4_ = bf16[512,128]{1,0:T(8,128)(2,1)S(1)} collective-permute-done((bf16[512,128]{1,0:T(8,128)(2,1)S(1)}, bf16[512,128]{1,0:T(8,128)(2,1)S(1)}, u32[]{:S(2)}, u32[]{:S(2)}) %collective-permute-start.17) | collective-permute-done | bytes 131104 | tf_op jit(solution)/shard_map/ppermute | solution.py:27
  69.5 2.1 %collective-permute-start.18 = (bf16[512,128]{1,0:T(8,128)(2,1)S(1)}, bf16[512,128]{1,0:T(8,128)(2,1)S(1)}, u32[]{:S(2)}, u32[]{:S(2)}) collective-permute-start(bf16[512,128]{1,0:T(8,128)(2,1)S(1)} %collective-permute-done.17.refs_4_), channel_id=1, source_target_pairs={{0,4},{4,0},{8,12},{12,8},{16,20},{20,16},{24,28},{28,24},{1,5},{5... | collective-permute-start | bytes 393224 | tf_op jit(solution)/shard_map/ppermute | solution.py:27
  71.6 3.4 %collective-permute-done.18.refs_5_ = bf16[512,128]{1,0:T(8,128)(2,1)S(1)} collective-permute-done((bf16[512,128]{1,0:T(8,128)(2,1)S(1)}, bf16[512,128]{1,0:T(8,128)(2,1)S(1)}, u32[]{:S(2)}, u32[]{:S(2)}) %collective-permute-start.18) | collective-permute-done | bytes 131104 | tf_op jit(solution)/shard_map/ppermute | solution.py:27
  75.0 1.5 %collective-permute-done.20.refs_7_ = bf16[512,128]{1,0:T(8,128)(2,1)S(1)} collective-permute-done((bf16[512,128]{1,0:T(8,128)(2,1)S(1)}, bf16[512,128]{1,0:T(8,128)(2,1)S(1)}, u32[]{:S(2)}, u32[]{:S(2)}) %collective-permute-start.20) | collective-permute-done | bytes 131104 | tf_op jit(solution)/shard_map/ppermute | solution.py:27
  76.6 3.3 %project.1 = bf16[512,1024]{1,0:T(8,128)(2,1)} custom-call(s32[1]{0:T(128)} %bitcast.place_ref, bf16[1024,1024]{1,0:T(8,128)(2,1)S(1)} %copy-done.1, bf16[512,128]{1,0:T(8,128)(2,1)S(1)} %merge.3.refs_0_, bf16[512,128]{1,0:T(8,128)(2,1)S(1)} %collective-permute-done.14.refs_1_, bf16[512,128]{1,0:T(8,128)(2,1)S(1)} %collective-permute-done.15.refs_2_, ...), custom_call_target="tpu_custom_call" | custom-call | tf_op jit(solution)/shard_map/project/pallas_call | solution.py:293
  (51 shorter events, 9.2 us)
Async XLA Ops:
  0.6 28.3 %copy-start.8 = (s32[9]{0:T(128)S(1)}, s32[9]{0:T(128)}, u32[]{:S(2)}) copy-start(s32[9]{0:T(128)} %valid_ref.7) | copy-start | bytes 112
  1.9 6.5 %collective-permute-start.4 = (bf16[512,128]{1,0:T(8,128)(2,1)S(1)}, bf16[512,128]{1,0:T(8,128)(2,1)S(1)}, u32[]{:S(2)}, u32[]{:S(2)}) collective-permute-start(bf16[512,128]{1,0:T(8,128)(2,1)S(1)} %constant_dynamic-slice_fusion.query_ref), channel_id=1, source_target_pairs={{0,2},{1,3},{2,0},{3,1},{4,6},{5,7},{6,4},{7,5},{8,10},{9,11},{10,... | collective-permute-start | bytes 393224 | tf_op jit(solution)/shard_map/ppermute | solution.py:27
  8.4 11.4 %collective-permute-start.5 = (bf16[1024,128]{1,0:T(8,128)(2,1)S(1)}, bf16[1024,128]{1,0:T(8,128)(2,1)S(1)}, u32[]{:S(2)}, u32[]{:S(2)}) collective-permute-start(bf16[1024,128]{1,0:T(8,128)(2,1)S(1)} %pad_maximum_fusion.1), channel_id=1, source_target_pairs={{0,1},{1,0},{2,3},{3,2},{4,5},{5,4},{6,7},{7,6},{8,9},{9,8},{10,11... | collective-permute-start | bytes 786440 | tf_op jit(solution)/shard_map/ppermute | solution.py:27
  8.5 25.7 %collective-permute-start = (bf16[8,2,64,256]{3,2,1,0:T(8,128)(2,1)}, bf16[8,2,64,256]{3,2,1,0:T(8,128)(2,1)S(1)}, u32[]{:S(2)}, u32[]{:S(2)}) collective-permute-start(bf16[8,2,64,256]{3,2,1,0:T(8,128)(2,1)} %raw_ref.1), channel_id=1, source_target_pairs={{0,1},{1,2},{2,3},{4,5},{5,6},{6,7},{8,9},{9,10},{10,11},{12,13},{... | collective-permute-start | bytes 1572872 | tf_op jit(solution)/shard_map/ppermute | solution.py:32
  12.0 7.8 %collective-permute-start.6 = (bf16[128,256]{1,0:T(8,128)(2,1)S(1)}, bf16[128,256]{1,0:T(8,128)(2,1)S(1)}, u32[]{:S(2)}, u32[]{:S(2)}) collective-permute-start(bf16[128,256]{1,0:T(8,128)(2,1)S(1)} %get-tuple-element.23), channel_id=1, source_target_pairs={{0,16},{4,20},{8,24},{12,28},{16,0},{20,4},{24,8},{28,12},{1,17},{... | collective-permute-start | bytes 196616 | tf_op jit(solution)/shard_map/ppermute | solution.py:27
  15.0 9.8 %collective-permute-start.7 = (bf16[128,256]{1,0:T(8,128)(2,1)S(1)}, bf16[128,256]{1,0:T(8,128)(2,1)S(1)}, u32[]{:S(2)}, u32[]{:S(2)}) collective-permute-start(bf16[128,256]{1,0:T(8,128)(2,1)S(1)} %get-tuple-element.24), channel_id=1, source_target_pairs={{0,20},{4,16},{8,28},{12,24},{16,4},{20,0},{24,12},{28,8},{1,21},{... | collective-permute-start | bytes 196616 | tf_op jit(solution)/shard_map/ppermute | solution.py:27
  16.2 9.7 %collective-permute-start.8 = (bf16[128,256]{1,0:T(8,128)(2,1)S(1)}, bf16[128,256]{1,0:T(8,128)(2,1)S(1)}, u32[]{:S(2)}, u32[]{:S(2)}) collective-permute-start(bf16[128,256]{1,0:T(8,128)(2,1)S(1)} %get-tuple-element.25), channel_id=1, source_target_pairs={{0,24},{4,28},{8,16},{12,20},{16,8},{20,12},{24,0},{28,4},{1,25},{... | collective-permute-start | bytes 196616 | tf_op jit(solution)/shard_map/ppermute | solution.py:27
  19.9 9.1 %collective-permute-start.9 = (bf16[128,256]{1,0:T(8,128)(2,1)S(1)}, bf16[128,256]{1,0:T(8,128)(2,1)S(1)}, u32[]{:S(2)}, u32[]{:S(2)}) collective-permute-start(bf16[128,256]{1,0:T(8,128)(2,1)S(1)} %get-tuple-element.26), channel_id=1, source_target_pairs={{0,28},{4,24},{8,20},{12,16},{16,12},{20,8},{24,4},{28,0},{1,29},{... | collective-permute-start | bytes 196616 | tf_op jit(solution)/shard_map/ppermute | solution.py:27
  19.9 16.1 %collective-permute-start.1 = (bf16[128,256]{1,0:T(8,128)(2,1)S(1)}, bf16[128,256]{1,0:T(8,128)(2,1)S(1)}, u32[]{:S(2)}, u32[]{:S(2)}) collective-permute-start(bf16[128,256]{1,0:T(8,128)(2,1)S(1)} %get-tuple-element.19), channel_id=1, source_target_pairs={{0,4},{4,0},{8,12},{12,8},{16,20},{20,16},{24,28},{28,24},{1,5},{5... | collective-permute-start | bytes 196616 | tf_op jit(solution)/shard_map/ppermute | solution.py:27
  24.8 11.3 %collective-permute-start.2 = (bf16[128,256]{1,0:T(8,128)(2,1)S(1)}, bf16[128,256]{1,0:T(8,128)(2,1)S(1)}, u32[]{:S(2)}, u32[]{:S(2)}) collective-permute-start(bf16[128,256]{1,0:T(8,128)(2,1)S(1)} %get-tuple-element.20), channel_id=1, source_target_pairs={{0,8},{4,12},{8,0},{12,4},{16,24},{20,28},{24,16},{28,20},{1,9},{5... | collective-permute-start | bytes 196616 | tf_op jit(solution)/shard_map/ppermute | solution.py:27
  25.9 10.1 %collective-permute-start.3 = (bf16[128,256]{1,0:T(8,128)(2,1)S(1)}, bf16[128,256]{1,0:T(8,128)(2,1)S(1)}, u32[]{:S(2)}, u32[]{:S(2)}) collective-permute-start(bf16[128,256]{1,0:T(8,128)(2,1)S(1)} %get-tuple-element.21), channel_id=1, source_target_pairs={{0,12},{4,8},{8,4},{12,0},{16,28},{20,24},{24,20},{28,16},{1,13},{... | collective-permute-start | bytes 196616 | tf_op jit(solution)/shard_map/ppermute | solution.py:27
  42.4 5.9 %collective-permute-start.10 = (bf16[1024,128]{1,0:T(8,128)(2,1)S(1)}, bf16[1024,128]{1,0:T(8,128)(2,1)S(1)}, u32[]{:S(2)}, u32[]{:S(2)}) collective-permute-start(bf16[1024,128]{1,0:T(8,128)(2,1)S(1)} %get-tuple-element.29), channel_id=1, source_target_pairs={{0,1},{1,0},{2,3},{3,2},{4,5},{5,4},{6,7},{7,6},{8,9},{9,8},{10,11... | collective-permute-start | bytes 786440 | tf_op jit(solution)/shard_map/ppermute | solution.py:27
  42.5 29.1 %collective-permute-start.21 = (bf16[1,4,1,32,2048]{4,3,2,1,0:T(8,128)(2,1)S(1)}, bf16[1,4,1,32,2048]{4,3,2,1,0:T(8,128)(2,1)S(1)}, u32[]{:S(2)}, u32[]{:S(2)}) collective-permute-start(bf16[1,4,1,32,2048]{4,3,2,1,0:T(8,128)(2,1)S(1)} %copy-done.5), channel_id=1, source_target_pairs={{0,4},{4,8},{8,12},{12,16},{16,20},{20,24},{24,28},{1,5},{5,9},{9,... | collective-permute-start | bytes 1572872 | tf_op jit(solution)/shard_map/ppermute | solution.py:32
  45.0 3.3 %collective-permute-start.11 = (f32[8,1024]{1,0:T(8,128)S(1)}, f32[8,1024]{1,0:T(8,128)S(1)}, u32[]{:S(2)}, u32[]{:S(2)}) collective-permute-start(f32[8,1024]{1,0:T(8,128)S(1)} %get-tuple-element.30), channel_id=1, source_target_pairs={{0,1},{1,0},{2,3},{3,2},{4,5},{5,4},{6,7},{7,6},{8,9},{9,8},{10,11... | collective-permute-start | bytes 98312 | tf_op jit(solution)/shard_map/ppermute | solution.py:27
  48.3 28.3 %copy-start.1 = (bf16[1024,1024]{1,0:T(8,128)(2,1)S(1)}, bf16[1024,1024]{1,0:T(8,128)(2,1)}, u32[]{:S(2)}) copy-start(bf16[1024,1024]{1,0:T(8,128)(2,1)} %weight_ref.3) | copy-start | bytes 6291460
  48.7 6.1 %collective-permute-start.12 = (bf16[512,128]{1,0:T(8,128)(2,1)S(1)}, bf16[512,128]{1,0:T(8,128)(2,1)S(1)}, u32[]{:S(2)}, u32[]{:S(2)}) collective-permute-start(bf16[512,128]{1,0:T(8,128)(2,1)S(1)} %get-tuple-element.33), channel_id=1, source_target_pairs={{0,2},{1,3},{2,0},{3,1},{4,6},{5,7},{6,4},{7,5},{8,10},{9,11},{10,... | collective-permute-start | bytes 393224 | tf_op jit(solution)/shard_map/ppermute | solution.py:27
  49.1 5.7 %collective-permute-start.13 = (f32[8,512]{1,0:T(8,128)S(1)}, f32[8,512]{1,0:T(8,128)S(1)}, u32[]{:S(2)}, u32[]{:S(2)}) collective-permute-start(f32[8,512]{1,0:T(8,128)S(1)} %get-tuple-element.34), channel_id=1, source_target_pairs={{0,2},{1,3},{2,0},{3,1},{4,6},{5,7},{6,4},{7,5},{8,10},{9,11},{10,... | collective-permute-start | bytes 49160 | tf_op jit(solution)/shard_map/ppermute | solution.py:27
  55.2 6.7 %collective-permute-start.15 = (bf16[512,128]{1,0:T(8,128)(2,1)S(1)}, bf16[512,128]{1,0:T(8,128)(2,1)S(1)}, u32[]{:S(2)}, u32[]{:S(2)}) collective-permute-start(bf16[512,128]{1,0:T(8,128)(2,1)S(1)} %merge.3.refs_0_), channel_id=1, source_target_pairs={{0,8},{4,12},{8,0},{12,4},{16,24},{20,28},{24,16},{28,20},{1,9},{5... | collective-permute-start | bytes 393224 | tf_op jit(solution)/shard_map/ppermute | solution.py:27
  56.6 12.9 %collective-permute-start.17 = (bf16[512,128]{1,0:T(8,128)(2,1)S(1)}, bf16[512,128]{1,0:T(8,128)(2,1)S(1)}, u32[]{:S(2)}, u32[]{:S(2)}) collective-permute-start(bf16[512,128]{1,0:T(8,128)(2,1)S(1)} %merge.3.refs_0_), channel_id=1, source_target_pairs={{0,16},{4,20},{8,24},{12,28},{16,0},{20,4},{24,8},{28,12},{1,17},{... | collective-permute-start | bytes 393224 | tf_op jit(solution)/shard_map/ppermute | solution.py:27
  59.6 12.0 %collective-permute-start.19 = (bf16[512,128]{1,0:T(8,128)(2,1)S(1)}, bf16[512,128]{1,0:T(8,128)(2,1)S(1)}, u32[]{:S(2)}, u32[]{:S(2)}) collective-permute-start(bf16[512,128]{1,0:T(8,128)(2,1)S(1)} %merge.3.refs_0_), channel_id=1, source_target_pairs={{0,24},{4,28},{8,16},{12,20},{16,8},{20,12},{24,0},{28,4},{1,25},{... | collective-permute-start | bytes 393224 | tf_op jit(solution)/shard_map/ppermute | solution.py:27
  59.6 12.0 %collective-permute-start.14 = (bf16[512,128]{1,0:T(8,128)(2,1)S(1)}, bf16[512,128]{1,0:T(8,128)(2,1)S(1)}, u32[]{:S(2)}, u32[]{:S(2)}) collective-permute-start(bf16[512,128]{1,0:T(8,128)(2,1)S(1)} %merge.3.refs_0_), channel_id=1, source_target_pairs={{0,4},{4,0},{8,12},{12,8},{16,20},{20,16},{24,28},{28,24},{1,5},{5... | collective-permute-start | bytes 393224 | tf_op jit(solution)/shard_map/ppermute | solution.py:27
  61.9 9.7 %collective-permute-start.16 = (bf16[512,128]{1,0:T(8,128)(2,1)S(1)}, bf16[512,128]{1,0:T(8,128)(2,1)S(1)}, u32[]{:S(2)}, u32[]{:S(2)}) collective-permute-start(bf16[512,128]{1,0:T(8,128)(2,1)S(1)} %collective-permute-done.15.refs_2_), channel_id=1, source_target_pairs={{0,4},{4,0},{8,12},{12,8},{16,20},{20,16},{24,28},{28,24},{1,5},{5... | collective-permute-start | bytes 393224 | tf_op jit(solution)/shard_map/ppermute | solution.py:27
  69.5 5.5 %collective-permute-start.18 = (bf16[512,128]{1,0:T(8,128)(2,1)S(1)}, bf16[512,128]{1,0:T(8,128)(2,1)S(1)}, u32[]{:S(2)}, u32[]{:S(2)}) collective-permute-start(bf16[512,128]{1,0:T(8,128)(2,1)S(1)} %collective-permute-done.17.refs_4_), channel_id=1, source_target_pairs={{0,4},{4,0},{8,12},{12,8},{16,20},{20,16},{24,28},{28,24},{1,5},{5... | collective-permute-start | bytes 393224 | tf_op jit(solution)/shard_map/ppermute | solution.py:27
  71.6 5.0 %collective-permute-start.20 = (bf16[512,128]{1,0:T(8,128)(2,1)S(1)}, bf16[512,128]{1,0:T(8,128)(2,1)S(1)}, u32[]{:S(2)}, u32[]{:S(2)}) collective-permute-start(bf16[512,128]{1,0:T(8,128)(2,1)S(1)} %collective-permute-done.19.refs_6_), channel_id=1, source_target_pairs={{0,4},{4,0},{8,12},{12,8},{16,20},{20,16},{24,28},{28,24},{1,5},{5... | collective-permute-start | bytes 393224 | tf_op jit(solution)/shard_map/ppermute | solution.py:27
  (7 other events, 30.3 us)

commit v3 on v2

--- a/solution.py
+++ b/solution.py
@@ -83,42 +83,41 @@
     )(raw_clip, halo, pool_weight)
 
 
-def cut_kernel(width, place_ref, memory_ref, *out_refs):
+def cut_kernel(width, place_ref, memory_ref, raw_ref, weight_ref, raw_out, weight_out, *out_refs):
     place = place_ref[0]
     for distance, out_ref in enumerate(out_refs):
         start = pl.multiple_of((place ^ distance) * width, 128)
         out_ref[...] = memory_ref[:, pl.ds(start, width)]
-
-
-def cut(place, memory, pieces):
+    raw_out[...] = raw_ref[...]
+    weight_out[...] = weight_ref[...]
+
+
+def cut(place, memory, raw_clip, pool_weight, pieces):
     tokens, channels = memory.shape
     width = channels // pieces
+    out = [raw_clip, pool_weight]
+    out += [jax.ShapeDtypeStruct((tokens, width), memory.dtype)] * pieces
     return pl.pallas_call(
         partial(cut_kernel, width),
-        out_shape=[jax.ShapeDtypeStruct((tokens, width), memory.dtype)] * pieces,
-        in_specs=[pl.BlockSpec(memory_space=SMEM), pl.BlockSpec(memory_space=VMEM)],
-        out_specs=[pl.BlockSpec(memory_space=VMEM)] * pieces,
+        out_shape=[jax.ShapeDtypeStruct(o.shape, o.dtype) for o in out],
+        in_specs=[pl.BlockSpec(memory_space=SMEM)] + [pl.BlockSpec(memory_space=VMEM)] * 3,
+        out_specs=[pl.BlockSpec(memory_space=VMEM)] * len(out),
         compiler_params=params(),
         name="cut",
-    )(place, memory)
-
-
-def attend_kernel(
-    head_size, columns, distances, final, has_state, place_ref, valid_ref, query_ref, *refs
-):
-    refs = list(refs)
-    sources = [refs.pop(0) for _ in distances]
-    state_ref = refs.pop(0) if has_state else None
+    )(place, memory, raw_clip, pool_weight)
+
+
+def attend_kernel(head_size, columns, distances, place_ref, valid_ref, query_ref, *refs):
+    sources, (value_ref, level_ref) = refs[: len(distances)], refs[len(distances) :]
     rows, width = query_ref.shape
     heads = width // head_size
     wide = 2 * head_size
     place = place_ref[0]
-    biases, tokens = [], 0
+    biases = []
     for source, distance in zip(sources, distances):
         column = lanes_of((1, source.shape[0])) % columns
         valid = valid_ref[0] if distance is None else valid_ref[1 + (place ^ distance)]
         biases.append(jnp.where(column < valid, 0.0, MASKED))
-        tokens += source.shape[0]
     bias = jnp.concatenate(biases, axis=1)
     lane = lanes_of((rows, wide))
     queries = query_ref[...].astype(jnp.float32) * head_size ** (-0.5)
@@ -137,81 +136,60 @@
         scores.append(product + bias)
     weights, peaks = [], []
     for h in range(heads):
-        peak = jnp.max(scores[h], axis=1, keepdims=True)
-        if has_state:
-            peak = jnp.maximum(peak, state_ref[h, :, head_size // 2 : head_size // 2 + 1])
-        peaks.append(peak)
-        weights.append(jnp.exp(scores[h] - peak).astype(jnp.bfloat16))
+        peaks.append(jnp.max(scores[h], axis=1, keepdims=True))
+        weights.append(jnp.exp(scores[h] - peaks[h]).astype(jnp.bfloat16))
     values, levels = [], []
-    memory_lane = lanes_of((tokens, wide))
+    memory_lane = lanes_of(memory[0].shape)
     for h in range(heads):
         ones_and_values = jnp.where(memory_lane < head_size, 1.0, memory[h].astype(jnp.float32))
         total = jnp.dot(
             weights[h], ones_and_values.astype(jnp.bfloat16), preferred_element_type=jnp.float32
         )
-        if has_state:
-            state = state_ref[h]
-            old_peak = state[:, head_size // 2 : head_size // 2 + 1]
-            total = total + state * jnp.exp(old_peak - peaks[h])
-        if final:
-            weight_sum = total[:, :1]
-            values.append(total[:, head_size:] * (1.0 / weight_sum))
-            level = peaks[h] + jnp.log(weight_sum)
-            levels.append(jnp.broadcast_to(level, (rows, head_size)))
+        turned = pltpu.roll(total, head_size, 1)
+        if h % 2:
+            values.append(total / turned)
+            levels.append(jnp.log(turned) + peaks[h])
         else:
-            keep = (lane >= head_size // 2) & (lane < head_size)
-            refs[0][h] = jnp.where(keep, peaks[h], total)
-    if final:
-        refs[0][...] = jnp.concatenate(values, axis=1).astype(refs[0].dtype)
-        write_levels(refs[1], jnp.concatenate(levels, axis=1), head_size)
-
-
-def write_levels(level_ref, level, head_size):
-    if level.shape[1] < 128:
-        level = jnp.concatenate([level, level], axis=1)
+            values.append(turned / total)
+            levels.append(jnp.log(total) + peaks[h])
+    if heads == 1:
+        value_ref[...] = values[0][:, :head_size].astype(value_ref.dtype)
+        level = levels[0]
+    else:
+        value_ref[...] = jnp.where(lane < head_size, *values).astype(value_ref.dtype)
+        level = jnp.where(lane < head_size, *levels)
+    write_levels(level_ref, level, heads, head_size)
+
+
+def write_levels(level_ref, level, heads, head_size):
     turned = level.T
-    for h in range(H):
-        if (h + 1) * head_size <= level.shape[1]:
-            level_ref[h : h + 1, :] = turned[h * head_size : h * head_size + 1, :]
-
-
-def attend(
-    place, valid, queries, sources, state, state_start, distances, columns, head_size, final, dtype
-):
+    for h in range(heads):
+        level_ref[h : h + 1, :] = turned[h * head_size : h * head_size + 1, :]
+
+
+def attend(place, valid, queries, sources, distances, columns, head_size, dtype):
     rows, width = queries.shape
     heads = width // head_size
     wide = 2 * head_size
     key_count = sum(source.shape[0] for source in sources)
     block = min(512, rows)
-    start = state_start // block
-    whole = pl.BlockSpec(memory_space=VMEM)
-    in_specs = [
-        pl.BlockSpec(memory_space=SMEM),
-        pl.BlockSpec(memory_space=SMEM),
-        pl.BlockSpec((block, width), lambda i: (i, 0)),
-    ] + [whole] * len(sources)
-    operands = [place, valid, queries, *sources]
-    if state is not None:
-        in_specs.append(pl.BlockSpec((heads, block, wide), lambda i: (0, i + start, 0)))
-        operands.append(state)
-    if final:
-        out_shape = [
+    return pl.pallas_call(
+        partial(attend_kernel, head_size, columns, distances),
+        grid=(rows // block,),
+        out_shape=[
             jax.ShapeDtypeStruct((rows, width), dtype),
             jax.ShapeDtypeStruct((8, rows), jnp.float32),
+        ],
+        in_specs=[
+            pl.BlockSpec(memory_space=SMEM),
+            pl.BlockSpec(memory_space=SMEM),
+            pl.BlockSpec((block, width), lambda i: (i, 0)),
         ]
-        out_specs = [
+        + [pl.BlockSpec(memory_space=VMEM)] * len(sources),
+        out_specs=[
             pl.BlockSpec((block, width), lambda i: (i, 0)),
             pl.BlockSpec((8, block), lambda i: (0, i)),
-        ]
-    else:
-        out_shape = jax.ShapeDtypeStruct((heads, rows, wide), jnp.float32)
-        out_specs = pl.BlockSpec((heads, block, wide), lambda i: (0, i, 0))
-    return pl.pallas_call(
-        partial(attend_kernel, head_size, columns, distances, final, state is not None),
-        grid=(rows // block,),
-        out_shape=out_shape,
-        in_specs=in_specs,
-        out_specs=out_specs,
+        ],
         compiler_params=params(),
         cost_estimate=pl.CostEstimate(
             flops=4 * rows * key_count * wide * heads,
@@ -219,7 +197,7 @@
             transcendentals=rows * key_count * heads,
         ),
         name="attend",
-    )(*operands)
+    )(place, valid, queries, *sources)
 
 
 def merge_kernel(head_size, count, final, *refs):
@@ -242,7 +220,10 @@
         share = share + factor
     outs[0][...] = (total / share).astype(outs[0].dtype)
     if not final:
-        write_levels(outs[1], top + jnp.log(share), head_size)
+        level = top + jnp.log(share)
+        if width < 128:
+            level = jnp.concatenate([level, level], axis=1)
+        write_levels(outs[1], level, heads, head_size)
 
 
 def merge(parts, rows, head_size, final):
@@ -274,31 +255,70 @@
     )(*operands)
 
 
-def project_kernel(place_ref, weight_ref, *refs):
-    out_ref = refs[-1]
+def project_kernel(distances, has_total, aged, place_ref, weight_ref, *refs):
+    refs = list(refs)
+    blocks = [refs.pop(0) for _ in distances]
+    total_ref = refs.pop(0) if has_total else None
+    if aged:
+        aged_ref, out_ref, aged_out, semaphore = refs
+        copy = pltpu.make_async_copy(aged_ref, aged_out, semaphore)
+        copy.start()
+    else:
+        (out_ref,) = refs
     place = place_ref[0]
-    total = None
-    for distance, ref in enumerate(refs[:-1]):
-        width = ref.shape[1]
+    width = blocks[0].shape[1]
+    weights = []
+    for distance in distances:
         start = pl.multiple_of((place ^ distance) * width, width)
-        term = jnp.dot(
-            ref[...], weight_ref[pl.ds(start, width), :], preferred_element_type=jnp.float32
-        )
-        total = term if total is None else total + term
+        weights.append(weight_ref[pl.ds(start, width), :])
+    total = jnp.dot(
+        jnp.concatenate([block[...] for block in blocks], axis=1),
+        jnp.concatenate(weights, axis=0),
+        preferred_element_type=jnp.float32,
+    )
+    if has_total:
+        total = total + total_ref[...]
     out_ref[...] = total.astype(out_ref.dtype)
-
-
-def project(place, out_weight, blocks):
-    rows = blocks[0].shape[0]
+    if aged:
+        copy.wait()
+
+
+def project(place, out_weight, blocks, distances, total=None, aged=None):
+    rows, columns = blocks[0].shape[0], out_weight.shape[1]
+    operands = [place, out_weight, *blocks]
+    in_specs = [pl.BlockSpec(memory_space=SMEM)]
+    in_specs += [pl.BlockSpec(memory_space=VMEM)] * (1 + len(blocks))
+    dtype = jnp.float32 if total is None else jnp.bfloat16
+    out_shape = [jax.ShapeDtypeStruct((rows, columns), dtype)]
+    out_specs = [pl.BlockSpec(memory_space=VMEM)]
+    scratch = []
+    if total is not None:
+        operands.append(total)
+        in_specs.append(pl.BlockSpec(memory_space=VMEM))
+    if aged is not None:
+        operands.append(aged)
+        in_specs.append(pl.BlockSpec(memory_space=pl.ANY))
+        out_shape.append(jax.ShapeDtypeStruct(aged.shape, aged.dtype))
+        out_specs.append(pl.BlockSpec(memory_space=pl.ANY))
+        scratch.append(pltpu.SemaphoreType.DMA)
     return pl.pallas_call(
-        project_kernel,
-        out_shape=jax.ShapeDtypeStruct((rows, out_weight.shape[1]), jnp.bfloat16),
-        in_specs=[pl.BlockSpec(memory_space=SMEM)]
-        + [pl.BlockSpec(memory_space=VMEM)] * (1 + len(blocks)),
-        out_specs=pl.BlockSpec(memory_space=VMEM),
+        partial(project_kernel, distances, total is not None, aged is not None),
+        out_shape=out_shape,
+        in_specs=in_specs,
+        out_specs=out_specs,
+        scratch_shapes=scratch,
         compiler_params=params(),
+        cost_estimate=pl.CostEstimate(
+            flops=2 * rows * columns * blocks[0].shape[1] * len(blocks),
+            bytes_accessed=4 * rows * columns,
+            transcendentals=0,
+        ),
         name="project",
-    )(place, out_weight, *blocks)
+    )(*operands)
+
+
+def after(array, *others):
+    return lax.optimization_barrier((array, *others))[0]
 
 
 def local(queries, raw_clip, pool_weight, old_memory, valid_columns, out_weight):
@@ -311,54 +331,45 @@
     slot_index = lax.axis_index("slot")
     place = slot_index.astype(jnp.int32).reshape(1)
 
+    own_queries = lax.dynamic_slice_in_dim(queries, slot_index * width, width, axis=1)
+    evens = range(2, spaces, 2)
+    near = jnp.concatenate([exchange(own_queries, "space", e) for e in evens] + [own_queries], 0)
+
     resident = old_memory.reshape(-1, old_memory.shape[-1])
-    pieces = cut(place, resident, slots)
+    raw_clip, pool_weight, *pieces = cut(place, resident, raw_clip, pool_weight, slots)
     received = {0: pieces[0]}
     for d in reversed(range(1, slots)):
         received[d] = exchange(pieces[d], "slot", d)
 
-    own_queries = lax.dynamic_slice_in_dim(queries, slot_index * width, width, axis=1)
-    evens = range(2, spaces, 2)
-    near = jnp.concatenate([exchange(own_queries, "space", e) for e in evens] + [own_queries], 0)
-    far = exchange(near, "space", 1)
-
-    behind = from_behind(raw_clip, "space", 1)
+    far = exchange(after(near, received[slots - 1]), "space", 1)
+    behind = from_behind(after(raw_clip, received[slots - 1]), "space", 1)
     fresh = pool(raw_clip, behind, pool_weight, head_size)
     fresh_rows = fresh.reshape(-1, fresh.shape[-1])
-
-    half = slots // 2
-    first = (0,) + tuple(range(half, slots))
-    second = tuple(range(1, half))
-    call = partial(attend, place, valid_columns, columns=columns, head_size=head_size)
-    state = call(
-        jnp.concatenate([far, near], axis=0),
-        [received[d] for d in first],
-        None,
-        0,
-        distances=first,
-        final=False,
-        dtype=None,
+    aged_memory = from_behind(after(old_memory, *received.values()), "slot", 1)
+
+    distances = tuple(range(slots))
+    call = partial(
+        attend,
+        place,
+        valid_columns,
+        sources=[fresh_rows] + [received[d] for d in distances],
+        distances=(None,) + distances,
+        columns=columns,
+        head_size=head_size,
     )
-    sources = [fresh_rows] + [received[d] for d in second]
-    call = partial(call, sources=sources, state=state, distances=(None,) + second, final=True)
-    far_value, far_level = call(queries=far, state_start=0, dtype=jnp.bfloat16)
+    far_value, far_level = call(queries=far, dtype=jnp.bfloat16)
     core_value = exchange(far_value, "space", 1)
     core_level = exchange(far_level, "space", 1)
     parts = []
     for k, e in enumerate(evens):
         rows = slice(k * query_rows, (k + 1) * query_rows)
-        value, level = call(
-            queries=near[rows], state_start=far.shape[0] + k * query_rows, dtype=jnp.float32
-        )
+        value, level = call(queries=near[rows], dtype=jnp.float32)
         value, level = merge(
             [(value, level, 0), (core_value, core_level, k)], query_rows, head_size, False
         )
         parts.append((exchange(value, "space", e), exchange(level, "space", e), 0))
-    last = len(evens)
-    value, level = call(
-        queries=own_queries, state_start=far.shape[0] + last * query_rows, dtype=jnp.float32
-    )
-    parts = [(value, level, 0), (core_value, core_level, last)] + parts
+    value, level = call(queries=own_queries, dtype=jnp.float32)
+    parts = [(value, level, 0), (core_value, core_level, len(evens))] + parts
     (mixed,) = merge(parts, query_rows, head_size, True)
 
     blocks = {0: mixed}
@@ -366,8 +377,12 @@
         blocks[d] = exchange(mixed, "slot", d)
     for d in range(0, slots, 2):
         blocks[d + 1] = exchange(blocks[d], "slot", 1)
-    attended = project(place, out_weight, [blocks[d] for d in range(slots)])
-    aged_memory = from_behind(old_memory, "slot", 1)
+    half = slots // 2
+    first, second = distances[:half], distances[half:]
+    (total,) = project(place, out_weight, [blocks[d] for d in first], first)
+    attended, aged_memory = project(
+        place, out_weight, [blocks[d] for d in second], second, total, aged_memory
+    )
     return (attended, fresh, aged_memory)
 
 

time: 80.9 us -> 80.9 us (level)
  Pallas kernels: 22.7 us -> 14.8 us
  starting transfers between devices: 34.4 us -> 40.1 us
  waiting for transfers between devices: 18.6 us -> 21 us
    pallas_call x5, Pallas kernels: 20.1 us -> 12.2 us  [the longest x3 9.59 us: attend(): pl.pallas_call(partial(attend_kernel, head_size, columns, distances), gri...]
    ppermute x20, starting transfers between devices: 29.6 us -> 36.2 us  [exchange(): return lax.ppermute(block, axis, [(i, i ^ distance) for i in range(size)])]
    ppermute x20, waiting for transfers between devices: 18.6 us -> 21 us  [exchange(): return lax.ppermute(block, axis, [(i, i ^ distance) for i in range(size)])]
    ppermute x2, starting transfers between devices: 4.86 us -> 3.96 us  [from_behind(): lax.ppermute(block, axis, [(i - distance, i) for i in devices if i - dist...]
    unnamed x19 -> x16, local copies, waits for them, and re-layouts: 3.9 us -> 3.74 us
  transfers between devices with their start and end apart: 22 -> 22, of which waited for: 6 -> 10; matrix products, arithmetic and copies ran while one was open for 0% -> 0% of each run, Pallas kernels for 17% -> 10%
where the time goes in v3:
time: 80.9 us; the launch traced here: 80.6 us
  starting transfers between devices  40.1 us (50%)
  waiting for transfers between devices  21 us (26%)
  Pallas kernels  14.8 us (18%)
  local copies, waits for them, and re-layouts  3.78 us (5%)
  between operations  0.83 us (1%)
    ppermute x20, starting transfers between devices, exchange(): return lax.ppermute(block, axis, [(i, i ^ distance) for i in range(size)])  36.2 us
    ppermute x20, waiting for transfers between devices, exchange(): return lax.ppermute(block, axis, [(i, i ^ distance) for i in range(size)])  21 us
    pallas_call x3, Pallas kernels, attend(): pl.pallas_call(partial(attend_kernel, head_size, columns, distances), gri...  9.59 us
    ppermute x2, starting transfers between devices, from_behind(): lax.ppermute(block, axis, [(i - distance, i) for i in devices if i - dist...  3.96 us
    unnamed x16, local copies, waits for them, and re-layouts  3.74 us
    pallas_call x2, Pallas kernels, project(): pl.pallas_call(partial(project_kernel, distances, total is not None, aged...  2.57 us
    pallas_call x1, Pallas kernels, pool(): pl.pallas_call(partial(pool_kernel, head_size), out_shape=jax.ShapeDtypeS...  1.82 us
  transfers between devices with their start and end apart: 22, of which 10 were waited for; matrix products, arithmetic and copies ran while one was open for 0% of the time, Pallas kernels for 10%

profile of v3, /device:TPU:0, one launch (start us, length us, event | category | flops | bytes accessed | tf_op | source)
XLA Modules:
  0.0 80.6 jit_solution(3796417455881332607)
XLA Ops:
  3.6 6.1 %collective-permute-start = (bf16[128,256]{1,0:T(8,128)(2,1)S(1)}, bf16[128,256]{1,0:T(8,128)(2,1)S(1)}, u32[]{:S(2)}, u32[]{:S(2)}) collective-permute-start(bf16[128,256]{1,0:T(8,128)(2,1)S(1)} %get-tuple-element.27), channel_id=1, source_target_pairs={{0,28},{4,24},{8,20},{12,16},{16,12},{20,8},{24,4},{28,0},{1,29},{... | collective-permute-start | bytes 196616 | tf_op jit(solution)/shard_map/ppermute | solution.py:27
  9.7 2.2 %collective-permute-done.refs_8_ = bf16[128,256]{1,0:T(8,128)(2,1)S(1)} collective-permute-done((bf16[128,256]{1,0:T(8,128)(2,1)S(1)}, bf16[128,256]{1,0:T(8,128)(2,1)S(1)}, u32[]{:S(2)}, u32[]{:S(2)}) %collective-permute-start) | collective-permute-done | bytes 65568 | tf_op jit(solution)/shard_map/ppermute | solution.py:27
  13.3 2.3 %collective-permute-start.8 = (bf16[512,128]{1,0:T(8,128)(2,1)S(1)}, bf16[512,128]{1,0:T(8,128)(2,1)S(1)}, u32[]{:S(2)}, u32[]{:S(2)}) collective-permute-start(bf16[512,128]{1,0:T(8,128)(2,1)S(1)} %constant_dynamic-slice_fusion.query_ref), channel_id=1, source_target_pairs={{0,2},{1,3},{2,0},{3,1},{4,6},{5,7},{6,4},{7,5},{8,10},{9,11},{10,... | collective-permute-start | bytes 393224 | tf_op jit(solution)/shard_map/ppermute | solution.py:27
  15.7 3.8 %collective-permute-done.8.query_ref = bf16[512,128]{1,0:T(8,128)(2,1)S(1)} collective-permute-done((bf16[512,128]{1,0:T(8,128)(2,1)S(1)}, bf16[512,128]{1,0:T(8,128)(2,1)S(1)}, u32[]{:S(2)}, u32[]{:S(2)}) %collective-permute-start.8) | collective-permute-done | bytes 131104 | tf_op jit(solution)/shard_map/ppermute | solution.py:27
  19.5 5.1 %collective-permute-start.9 = (bf16[1024,128]{1,0:T(8,128)(2,1)S(1)}, bf16[1024,128]{1,0:T(8,128)(2,1)S(1)}, u32[]{:S(2)}, u32[]{:S(2)}) collective-permute-start(bf16[1024,128]{1,0:T(8,128)(2,1)S(1)} %pad_maximum_fusion), channel_id=1, source_target_pairs={{0,1},{1,0},{2,3},{3,2},{4,5},{5,4},{6,7},{7,6},{8,9},{9,8},{10,11... | collective-permute-start | bytes 786440 | tf_op jit(solution)/shard_map/ppermute | solution.py:27
  24.6 1.5 %collective-permute-start.2 = (bf16[128,256]{1,0:T(8,128)(2,1)S(1)}, bf16[128,256]{1,0:T(8,128)(2,1)S(1)}, u32[]{:S(2)}, u32[]{:S(2)}) collective-permute-start(bf16[128,256]{1,0:T(8,128)(2,1)S(1)} %get-tuple-element.31), channel_id=1, source_target_pairs={{0,4},{4,0},{8,12},{12,8},{16,20},{20,16},{24,28},{28,24},{1,5},{5... | collective-permute-start | bytes 196616 | tf_op jit(solution)/shard_map/ppermute | solution.py:27
  28.9 1.4 %collective-permute-start.5 = (bf16[128,256]{1,0:T(8,128)(2,1)S(1)}, bf16[128,256]{1,0:T(8,128)(2,1)S(1)}, u32[]{:S(2)}, u32[]{:S(2)}) collective-permute-start(bf16[128,256]{1,0:T(8,128)(2,1)S(1)} %get-tuple-element.34), channel_id=1, source_target_pairs={{0,16},{4,20},{8,24},{12,28},{16,0},{20,4},{24,8},{28,12},{1,17},{... | collective-permute-start | bytes 196616 | tf_op jit(solution)/shard_map/ppermute | solution.py:27
  30.7 2.1 %collective-permute-start.6 = (bf16[128,256]{1,0:T(8,128)(2,1)S(1)}, bf16[128,256]{1,0:T(8,128)(2,1)S(1)}, u32[]{:S(2)}, u32[]{:S(2)}) collective-permute-start(bf16[128,256]{1,0:T(8,128)(2,1)S(1)} %get-tuple-element.35), channel_id=1, source_target_pairs={{0,20},{4,16},{8,28},{12,24},{16,4},{20,0},{24,12},{28,8},{1,21},{... | collective-permute-start | bytes 196616 | tf_op jit(solution)/shard_map/ppermute | solution.py:27
  32.8 3.6 %collective-permute-start.7 = (bf16[128,256]{1,0:T(8,128)(2,1)S(1)}, bf16[128,256]{1,0:T(8,128)(2,1)S(1)}, u32[]{:S(2)}, u32[]{:S(2)}) collective-permute-start(bf16[128,256]{1,0:T(8,128)(2,1)S(1)} %get-tuple-element.36), channel_id=1, source_target_pairs={{0,24},{4,28},{8,16},{12,20},{16,8},{20,12},{24,0},{28,4},{1,25},{... | collective-permute-start | bytes 196616 | tf_op jit(solution)/shard_map/ppermute | solution.py:27
  36.4 1.8 %pool.1 = bf16[4,1,32,256]{3,2,1,0:T(8,128)(2,1)} custom-call(bf16[8,2,64,256]{3,2,1,0:T(8,128)(2,1)S(1)} %get-tuple-element.28.raw_ref, bf16[8,2,64,256]{3,2,1,0:T(8,128)(2,1)S(1)} %collective-permute-done.1.halo_ref, bf16[27,256]{1,0:T(8,128)(2,1)S(1)} %get-tuple-element.29.weight_ref), custom_call_target="tpu_custom_call" | custom-call | tf_op jit(solution)/shard_map/pool/pallas_call | solution.py:75
  38.2 2.3 %collective-permute-done.6.refs_6_ = bf16[128,256]{1,0:T(8,128)(2,1)S(1)} collective-permute-done((bf16[128,256]{1,0:T(8,128)(2,1)S(1)}, bf16[128,256]{1,0:T(8,128)(2,1)S(1)}, u32[]{:S(2)}, u32[]{:S(2)}) %collective-permute-start.6) | collective-permute-done | bytes 65568 | tf_op jit(solution)/shard_map/ppermute | solution.py:27
  41.4 4.5 %attend.4 = (bf16[1024,128]{1,0:T(8,128)(2,1)S(1)}, f32[8,1024]{1,0:T(8,128)S(1)}) custom-call(s32[1]{0:T(128)} %bitcast.place_ref, s32[9]{0:T(128)S(1)} %copy-done.7, bf16[1024,128]{1,0:T(8,128)(2,1)S(1)} %collective-permute-done.9.query_ref, bf16[128,256]{1,0:T(8,128)(2,1)S(1)} %bitcast.4, bf16[128,256]{1,0:T(8,128)(2,1)S(1)} %get-tuple-element.30.refs_1_, ...), custom_call_target="tpu_custom_call" | custom-call | flops 1207959552 | bytes 3276800 | tf_op jit(solution)/shard_map/attend/pallas_call | solution.py:176
  46.0 2.7 %collective-permute-start.21 = (bf16[1,4,1,32,2048]{4,3,2,1,0:T(8,128)(2,1)S(1)}, bf16[1,4,1,32,2048]{4,3,2,1,0:T(8,128)(2,1)S(1)}, u32[]{:S(2)}, u32[]{:S(2)}) collective-permute-start(bf16[1,4,1,32,2048]{4,3,2,1,0:T(8,128)(2,1)S(1)} %copy-done.4), channel_id=1, source_target_pairs={{0,4},{4,8},{8,12},{12,16},{16,20},{20,24},{24,28},{1,5},{5,9},{9,... | collective-permute-start | bytes 1572872 | tf_op jit(solution)/shard_map/ppermute | solution.py:32
  48.9 2.5 %attend.5 = (f32[512,128]{1,0:T(8,128)S(1)}, f32[8,512]{1,0:T(8,128)S(1)}) custom-call(s32[1]{0:T(128)} %bitcast.place_ref, s32[9]{0:T(128)S(1)} %copy-done.7, bf16[512,128]{1,0:T(8,128)(2,1)S(1)} %collective-permute-done.8.query_ref, bf16[128,256]{1,0:T(8,128)(2,1)S(1)} %bitcast.5, bf16[128,256]{1,0:T(8,128)(2,1)S(1)} %get-tuple-element.30.refs_1_, ...), custom_call_target="tpu_custom_call" | custom-call | flops 603979776 | bytes 2228224 | tf_op jit(solution)/shard_map/attend/pallas_call | solution.py:176
  51.8 2.3 %collective-permute-start.12 = (bf16[512,128]{1,0:T(8,128)(2,1)S(1)}, bf16[512,128]{1,0:T(8,128)(2,1)S(1)}, u32[]{:S(2)}, u32[]{:S(2)}) collective-permute-start(bf16[512,128]{1,0:T(8,128)(2,1)S(1)} %get-tuple-element.44), channel_id=1, source_target_pairs={{0,2},{1,3},{2,0},{3,1},{4,6},{5,7},{6,4},{7,5},{8,10},{9,11},{10,... | collective-permute-start | bytes 393224 | tf_op jit(solution)/shard_map/ppermute | solution.py:27
  54.2 2.5 %attend.3 = (f32[512,128]{1,0:T(8,128)S(1)}, f32[8,512]{1,0:T(8,128)S(1)}) custom-call(s32[1]{0:T(128)} %bitcast.place_ref, s32[9]{0:T(128)S(1)} %copy-done.7, bf16[512,128]{1,0:T(8,128)(2,1)S(1)} %constant_dynamic-slice_fusion.query_ref, bf16[128,256]{1,0:T(8,128)(2,1)S(1)} %bitcast.6, bf16[128,256]{1,0:T(8,128)(2,1)S(1)} %get-tuple-element.30.refs_1_, ...), custom_call_target="tpu_custom_call" | custom-call | flops 603979776 | bytes 2228224 | tf_op jit(solution)/shard_map/attend/pallas_call | solution.py:176
  56.7 1.7 %collective-permute-done.13.refs_5_ = f32[8,512]{1,0:T(8,128)S(1)} collective-permute-done((f32[8,512]{1,0:T(8,128)S(1)}, f32[8,512]{1,0:T(8,128)S(1)}, u32[]{:S(2)}, u32[]{:S(2)}) %collective-permute-start.13) | collective-permute-done | bytes 16416 | tf_op jit(solution)/shard_map/ppermute | solution.py:27
  60.0 2.4 %collective-permute-start.16 = (bf16[512,128]{1,0:T(8,128)(2,1)S(1)}, bf16[512,128]{1,0:T(8,128)(2,1)S(1)}, u32[]{:S(2)}, u32[]{:S(2)}) collective-permute-start(bf16[512,128]{1,0:T(8,128)(2,1)S(1)} %merge.3.refs_0_), channel_id=1, source_target_pairs={{0,24},{4,28},{8,16},{12,20},{16,8},{20,12},{24,0},{28,4},{1,25},{... | collective-permute-start | bytes 393224 | tf_op jit(solution)/shard_map/ppermute | solution.py:27
  62.4 1.7 %collective-permute-start.18 = (bf16[512,128]{1,0:T(8,128)(2,1)S(1)}, bf16[512,128]{1,0:T(8,128)(2,1)S(1)}, u32[]{:S(2)}, u32[]{:S(2)}) collective-permute-start(bf16[512,128]{1,0:T(8,128)(2,1)S(1)} %merge.3.refs_0_), channel_id=1, source_target_pairs={{0,4},{4,0},{8,12},{12,8},{16,20},{20,16},{24,28},{28,24},{1,5},{5... | collective-permute-start | bytes 393224 | tf_op jit(solution)/shard_map/ppermute | solution.py:27
  65.3 4.3 %collective-permute-done.16.refs_2_ = bf16[512,128]{1,0:T(8,128)(2,1)S(1)} collective-permute-done((bf16[512,128]{1,0:T(8,128)(2,1)S(1)}, bf16[512,128]{1,0:T(8,128)(2,1)S(1)}, u32[]{:S(2)}, u32[]{:S(2)}) %collective-permute-start.16) | collective-permute-done | bytes 131104 | tf_op jit(solution)/shard_map/ppermute | solution.py:27
  69.6 1.7 %collective-permute-start.17 = (bf16[512,128]{1,0:T(8,128)(2,1)S(1)}, bf16[512,128]{1,0:T(8,128)(2,1)S(1)}, u32[]{:S(2)}, u32[]{:S(2)}) collective-permute-start(bf16[512,128]{1,0:T(8,128)(2,1)S(1)} %collective-permute-done.16.refs_2_), channel_id=1, source_target_pairs={{0,4},{4,0},{8,12},{12,8},{16,20},{20,16},{24,28},{28,24},{1,5},{5... | collective-permute-start | bytes 393224 | tf_op jit(solution)/shard_map/ppermute | solution.py:27
  71.3 2.4 %collective-permute-done.14.refs_0_ = bf16[512,128]{1,0:T(8,128)(2,1)S(1)} collective-permute-done((bf16[512,128]{1,0:T(8,128)(2,1)S(1)}, bf16[512,128]{1,0:T(8,128)(2,1)S(1)}, u32[]{:S(2)}, u32[]{:S(2)}) %collective-permute-start.14) | collective-permute-done | bytes 131104 | tf_op jit(solution)/shard_map/ppermute | solution.py:27
  75.7 3.0 %collective-permute-done.15.refs_1_ = bf16[512,128]{1,0:T(8,128)(2,1)S(1)} collective-permute-done((bf16[512,128]{1,0:T(8,128)(2,1)S(1)}, bf16[512,128]{1,0:T(8,128)(2,1)S(1)}, u32[]{:S(2)}, u32[]{:S(2)}) %collective-permute-start.15) | collective-permute-done | bytes 131104 | tf_op jit(solution)/shard_map/ppermute | solution.py:27
  78.7 1.9 %project.3 = (bf16[512,1024]{1,0:T(8,128)(2,1)}, bf16[1,4,1,32,2048]{4,3,2,1,0:T(8,128)(2,1)}) custom-call(s32[1]{0:T(128)} %bitcast.place_ref, bf16[1024,1024]{1,0:T(8,128)(2,1)S(1)} %copy-done.1, bf16[512,128]{1,0:T(8,128)(2,1)S(1)} %collective-permute-done.14.refs_0_, bf16[512,128]{1,0:T(8,128)(2,1)S(1)} %collective-permute-done.15.refs_1_, ...), custom_call_target="tpu_custom_call" | custom-call | flops 536870912 | bytes 2097152 | tf_op jit(solution)/shard_map/project/pallas_call | solution.py:304
  (47 shorter events, 13.8 us)
Async XLA Ops:
  0.6 39.9 %copy-start.7 = (s32[9]{0:T(128)S(1)}, s32[9]{0:T(128)}, u32[]{:S(2)}) copy-start(s32[9]{0:T(128)} %valid_ref.5) | copy-start | bytes 112
  3.6 8.3 %collective-permute-start = (bf16[128,256]{1,0:T(8,128)(2,1)S(1)}, bf16[128,256]{1,0:T(8,128)(2,1)S(1)}, u32[]{:S(2)}, u32[]{:S(2)}) collective-permute-start(bf16[128,256]{1,0:T(8,128)(2,1)S(1)} %get-tuple-element.27), channel_id=1, source_target_pairs={{0,28},{4,24},{8,20},{12,16},{16,12},{20,8},{24,4},{28,0},{1,29},{... | collective-permute-start | bytes 196616 | tf_op jit(solution)/shard_map/ppermute | solution.py:27
  12.0 20.8 %collective-permute-start.1 = (bf16[8,2,64,256]{3,2,1,0:T(8,128)(2,1)S(1)}, bf16[8,2,64,256]{3,2,1,0:T(8,128)(2,1)S(1)}, u32[]{:S(2)}, u32[]{:S(2)}) collective-permute-start(bf16[8,2,64,256]{3,2,1,0:T(8,128)(2,1)S(1)} %get-tuple-element.28.raw_ref), channel_id=1, source_target_pairs={{0,1},{1,2},{2,3},{4,5},{5,6},{6,7},{8,9},{9,10},{10,11},{12,13},{... | collective-permute-start | bytes 1572872 | tf_op jit(solution)/shard_map/ppermute | solution.py:32
  13.3 6.2 %collective-permute-start.8 = (bf16[512,128]{1,0:T(8,128)(2,1)S(1)}, bf16[512,128]{1,0:T(8,128)(2,1)S(1)}, u32[]{:S(2)}, u32[]{:S(2)}) collective-permute-start(bf16[512,128]{1,0:T(8,128)(2,1)S(1)} %constant_dynamic-slice_fusion.query_ref), channel_id=1, source_target_pairs={{0,2},{1,3},{2,0},{3,1},{4,6},{5,7},{6,4},{7,5},{8,10},{9,11},{10,... | collective-permute-start | bytes 393224 | tf_op jit(solution)/shard_map/ppermute | solution.py:27
  19.5 21.0 %collective-permute-start.9 = (bf16[1024,128]{1,0:T(8,128)(2,1)S(1)}, bf16[1024,128]{1,0:T(8,128)(2,1)S(1)}, u32[]{:S(2)}, u32[]{:S(2)}) collective-permute-start(bf16[1024,128]{1,0:T(8,128)(2,1)S(1)} %pad_maximum_fusion), channel_id=1, source_target_pairs={{0,1},{1,0},{2,3},{3,2},{4,5},{5,4},{6,7},{7,6},{8,9},{9,8},{10,11... | collective-permute-start | bytes 786440 | tf_op jit(solution)/shard_map/ppermute | solution.py:27
  24.6 4.3 %collective-permute-start.2 = (bf16[128,256]{1,0:T(8,128)(2,1)S(1)}, bf16[128,256]{1,0:T(8,128)(2,1)S(1)}, u32[]{:S(2)}, u32[]{:S(2)}) collective-permute-start(bf16[128,256]{1,0:T(8,128)(2,1)S(1)} %get-tuple-element.31), channel_id=1, source_target_pairs={{0,4},{4,0},{8,12},{12,8},{16,20},{20,16},{24,28},{28,24},{1,5},{5... | collective-permute-start | bytes 196616 | tf_op jit(solution)/shard_map/ppermute | solution.py:27
  26.2 4.5 %collective-permute-start.3 = (bf16[128,256]{1,0:T(8,128)(2,1)S(1)}, bf16[128,256]{1,0:T(8,128)(2,1)S(1)}, u32[]{:S(2)}, u32[]{:S(2)}) collective-permute-start(bf16[128,256]{1,0:T(8,128)(2,1)S(1)} %get-tuple-element.32), channel_id=1, source_target_pairs={{0,8},{4,12},{8,0},{12,4},{16,24},{20,28},{24,16},{28,20},{1,9},{5... | collective-permute-start | bytes 196616 | tf_op jit(solution)/shard_map/ppermute | solution.py:27
  27.0 11.2 %collective-permute-start.4 = (bf16[128,256]{1,0:T(8,128)(2,1)S(1)}, bf16[128,256]{1,0:T(8,128)(2,1)S(1)}, u32[]{:S(2)}, u32[]{:S(2)}) collective-permute-start(bf16[128,256]{1,0:T(8,128)(2,1)S(1)} %get-tuple-element.33), channel_id=1, source_target_pairs={{0,12},{4,8},{8,4},{12,0},{16,28},{20,24},{24,20},{28,16},{1,13},{... | collective-permute-start | bytes 196616 | tf_op jit(solution)/shard_map/ppermute | solution.py:27
  28.9 9.3 %collective-permute-start.5 = (bf16[128,256]{1,0:T(8,128)(2,1)S(1)}, bf16[128,256]{1,0:T(8,128)(2,1)S(1)}, u32[]{:S(2)}, u32[]{:S(2)}) collective-permute-start(bf16[128,256]{1,0:T(8,128)(2,1)S(1)} %get-tuple-element.34), channel_id=1, source_target_pairs={{0,16},{4,20},{8,24},{12,28},{16,0},{20,4},{24,8},{28,12},{1,17},{... | collective-permute-start | bytes 196616 | tf_op jit(solution)/shard_map/ppermute | solution.py:27
  30.7 9.8 %collective-permute-start.6 = (bf16[128,256]{1,0:T(8,128)(2,1)S(1)}, bf16[128,256]{1,0:T(8,128)(2,1)S(1)}, u32[]{:S(2)}, u32[]{:S(2)}) collective-permute-start(bf16[128,256]{1,0:T(8,128)(2,1)S(1)} %get-tuple-element.35), channel_id=1, source_target_pairs={{0,20},{4,16},{8,28},{12,24},{16,4},{20,0},{24,12},{28,8},{1,21},{... | collective-permute-start | bytes 196616 | tf_op jit(solution)/shard_map/ppermute | solution.py:27
  32.8 7.7 %collective-permute-start.7 = (bf16[128,256]{1,0:T(8,128)(2,1)S(1)}, bf16[128,256]{1,0:T(8,128)(2,1)S(1)}, u32[]{:S(2)}, u32[]{:S(2)}) collective-permute-start(bf16[128,256]{1,0:T(8,128)(2,1)S(1)} %get-tuple-element.36), channel_id=1, source_target_pairs={{0,24},{4,28},{8,16},{12,20},{16,8},{20,12},{24,0},{28,4},{1,25},{... | collective-permute-start | bytes 196616 | tf_op jit(solution)/shard_map/ppermute | solution.py:27
  45.9 5.6 %collective-permute-start.10 = (bf16[1024,128]{1,0:T(8,128)(2,1)S(1)}, bf16[1024,128]{1,0:T(8,128)(2,1)S(1)}, u32[]{:S(2)}, u32[]{:S(2)}) collective-permute-start(bf16[1024,128]{1,0:T(8,128)(2,1)S(1)} %get-tuple-element.40), channel_id=1, source_target_pairs={{0,1},{1,0},{2,3},{3,2},{4,5},{5,4},{6,7},{7,6},{8,9},{9,8},{10,11... | collective-permute-start | bytes 786440 | tf_op jit(solution)/shard_map/ppermute | solution.py:27
  46.0 29.7 %collective-permute-start.21 = (bf16[1,4,1,32,2048]{4,3,2,1,0:T(8,128)(2,1)S(1)}, bf16[1,4,1,32,2048]{4,3,2,1,0:T(8,128)(2,1)S(1)}, u32[]{:S(2)}, u32[]{:S(2)}) collective-permute-start(bf16[1,4,1,32,2048]{4,3,2,1,0:T(8,128)(2,1)S(1)} %copy-done.4), channel_id=1, source_target_pairs={{0,4},{4,8},{8,12},{12,16},{16,20},{20,24},{24,28},{1,5},{5,9},{9,... | collective-permute-start | bytes 1572872 | tf_op jit(solution)/shard_map/ppermute | solution.py:32
  48.6 2.8 %collective-permute-start.11 = (f32[8,1024]{1,0:T(8,128)S(1)}, f32[8,1024]{1,0:T(8,128)S(1)}, u32[]{:S(2)}, u32[]{:S(2)}) collective-permute-start(f32[8,1024]{1,0:T(8,128)S(1)} %get-tuple-element.41), channel_id=1, source_target_pairs={{0,1},{1,0},{2,3},{3,2},{4,5},{5,4},{6,7},{7,6},{8,9},{9,8},{10,11... | collective-permute-start | bytes 98312 | tf_op jit(solution)/shard_map/ppermute | solution.py:27
  51.4 23.5 %copy-start.1 = (bf16[1024,1024]{1,0:T(8,128)(2,1)S(1)}, bf16[1024,1024]{1,0:T(8,128)(2,1)}, u32[]{:S(2)}) copy-start(bf16[1024,1024]{1,0:T(8,128)(2,1)} %weight_ref.5) | copy-start | bytes 6291460
  51.8 6.6 %collective-permute-start.12 = (bf16[512,128]{1,0:T(8,128)(2,1)S(1)}, bf16[512,128]{1,0:T(8,128)(2,1)S(1)}, u32[]{:S(2)}, u32[]{:S(2)}) collective-permute-start(bf16[512,128]{1,0:T(8,128)(2,1)S(1)} %get-tuple-element.44), channel_id=1, source_target_pairs={{0,2},{1,3},{2,0},{3,1},{4,6},{5,7},{6,4},{7,5},{8,10},{9,11},{10,... | collective-permute-start | bytes 393224 | tf_op jit(solution)/shard_map/ppermute | solution.py:27
  54.1 4.3 %collective-permute-start.13 = (f32[8,512]{1,0:T(8,128)S(1)}, f32[8,512]{1,0:T(8,128)S(1)}, u32[]{:S(2)}, u32[]{:S(2)}) collective-permute-start(f32[8,512]{1,0:T(8,128)S(1)} %get-tuple-element.45), channel_id=1, source_target_pairs={{0,2},{1,3},{2,0},{3,1},{4,6},{5,7},{6,4},{7,5},{8,10},{9,11},{10,... | collective-permute-start | bytes 49160 | tf_op jit(solution)/shard_map/ppermute | solution.py:27
  58.8 5.3 %collective-permute-start.19 = (bf16[512,128]{1,0:T(8,128)(2,1)S(1)}, bf16[512,128]{1,0:T(8,128)(2,1)S(1)}, u32[]{:S(2)}, u32[]{:S(2)}) collective-permute-start(bf16[512,128]{1,0:T(8,128)(2,1)S(1)} %merge.3.refs_0_), channel_id=1, source_target_pairs={{0,8},{4,12},{8,0},{12,4},{16,24},{20,28},{24,16},{28,20},{1,9},{5... | collective-permute-start | bytes 393224 | tf_op jit(solution)/shard_map/ppermute | solution.py:27
  60.0 9.7 %collective-permute-start.16 = (bf16[512,128]{1,0:T(8,128)(2,1)S(1)}, bf16[512,128]{1,0:T(8,128)(2,1)S(1)}, u32[]{:S(2)}, u32[]{:S(2)}) collective-permute-start(bf16[512,128]{1,0:T(8,128)(2,1)S(1)} %merge.3.refs_0_), channel_id=1, source_target_pairs={{0,24},{4,28},{8,16},{12,20},{16,8},{20,12},{24,0},{28,4},{1,25},{... | collective-permute-start | bytes 393224 | tf_op jit(solution)/shard_map/ppermute | solution.py:27
  62.4 11.4 %collective-permute-start.14 = (bf16[512,128]{1,0:T(8,128)(2,1)S(1)}, bf16[512,128]{1,0:T(8,128)(2,1)S(1)}, u32[]{:S(2)}, u32[]{:S(2)}) collective-permute-start(bf16[512,128]{1,0:T(8,128)(2,1)S(1)} %merge.3.refs_0_), channel_id=1, source_target_pairs={{0,16},{4,20},{8,24},{12,28},{16,0},{20,4},{24,8},{28,12},{1,17},{... | collective-permute-start | bytes 393224 | tf_op jit(solution)/shard_map/ppermute | solution.py:27
  62.4 12.6 %collective-permute-start.18 = (bf16[512,128]{1,0:T(8,128)(2,1)S(1)}, bf16[512,128]{1,0:T(8,128)(2,1)S(1)}, u32[]{:S(2)}, u32[]{:S(2)}) collective-permute-start(bf16[512,128]{1,0:T(8,128)(2,1)S(1)} %merge.3.refs_0_), channel_id=1, source_target_pairs={{0,4},{4,0},{8,12},{12,8},{16,20},{20,16},{24,28},{28,24},{1,5},{5... | collective-permute-start | bytes 393224 | tf_op jit(solution)/shard_map/ppermute | solution.py:27
  64.1 10.9 %collective-permute-start.20 = (bf16[512,128]{1,0:T(8,128)(2,1)S(1)}, bf16[512,128]{1,0:T(8,128)(2,1)S(1)}, u32[]{:S(2)}, u32[]{:S(2)}) collective-permute-start(bf16[512,128]{1,0:T(8,128)(2,1)S(1)} %collective-permute-done.19.refs_2_), channel_id=1, source_target_pairs={{0,4},{4,0},{8,12},{12,8},{16,20},{20,16},{24,28},{28,24},{1,5},{5... | collective-permute-start | bytes 393224 | tf_op jit(solution)/shard_map/ppermute | solution.py:27
  69.6 6.1 %collective-permute-start.17 = (bf16[512,128]{1,0:T(8,128)(2,1)S(1)}, bf16[512,128]{1,0:T(8,128)(2,1)S(1)}, u32[]{:S(2)}, u32[]{:S(2)}) collective-permute-start(bf16[512,128]{1,0:T(8,128)(2,1)S(1)} %collective-permute-done.16.refs_2_), channel_id=1, source_target_pairs={{0,4},{4,0},{8,12},{12,8},{16,20},{20,16},{24,28},{28,24},{1,5},{5... | collective-permute-start | bytes 393224 | tf_op jit(solution)/shard_map/ppermute | solution.py:27
  73.7 5.0 %collective-permute-start.15 = (bf16[512,128]{1,0:T(8,128)(2,1)S(1)}, bf16[512,128]{1,0:T(8,128)(2,1)S(1)}, u32[]{:S(2)}, u32[]{:S(2)}) collective-permute-start(bf16[512,128]{1,0:T(8,128)(2,1)S(1)} %collective-permute-done.14.refs_0_), channel_id=1, source_target_pairs={{0,4},{4,0},{8,12},{12,8},{16,20},{20,16},{24,28},{28,24},{1,5},{5... | collective-permute-start | bytes 393224 | tf_op jit(solution)/shard_map/ppermute | solution.py:27
  (6 other events, 21.0 us)

commit v4 on v3

--- a/solution.py
+++ b/solution.py
@@ -83,39 +83,39 @@
     )(raw_clip, halo, pool_weight)
 
 
-def cut_kernel(width, place_ref, memory_ref, raw_ref, weight_ref, raw_out, weight_out, *out_refs):
+def cut_kernel(width, groups, place_ref, memory_ref, *out_refs):
     place = place_ref[0]
-    for distance, out_ref in enumerate(out_refs):
-        start = pl.multiple_of((place ^ distance) * width, 128)
-        out_ref[...] = memory_ref[:, pl.ds(start, width)]
-    raw_out[...] = raw_ref[...]
-    weight_out[...] = weight_ref[...]
-
-
-def cut(place, memory, raw_clip, pool_weight, pieces):
+    tokens = memory_ref.shape[0]
+    for group, out_ref in zip(groups, out_refs):
+        for k, distance in enumerate(group):
+            start = pl.multiple_of((place ^ distance) * width, 128)
+            out_ref[k * tokens : (k + 1) * tokens] = memory_ref[:, pl.ds(start, width)]
+
+
+def cut(place, memory, pieces, groups):
     tokens, channels = memory.shape
     width = channels // pieces
-    out = [raw_clip, pool_weight]
-    out += [jax.ShapeDtypeStruct((tokens, width), memory.dtype)] * pieces
     return pl.pallas_call(
-        partial(cut_kernel, width),
-        out_shape=[jax.ShapeDtypeStruct(o.shape, o.dtype) for o in out],
-        in_specs=[pl.BlockSpec(memory_space=SMEM)] + [pl.BlockSpec(memory_space=VMEM)] * 3,
-        out_specs=[pl.BlockSpec(memory_space=VMEM)] * len(out),
+        partial(cut_kernel, width, groups),
+        out_shape=[jax.ShapeDtypeStruct((len(g) * tokens, width), memory.dtype) for g in groups],
+        in_specs=[pl.BlockSpec(memory_space=SMEM), pl.BlockSpec(memory_space=VMEM)],
+        out_specs=[pl.BlockSpec(memory_space=VMEM)] * len(groups),
         compiler_params=params(),
         name="cut",
-    )(place, memory, raw_clip, pool_weight)
-
-
-def attend_kernel(head_size, columns, distances, place_ref, valid_ref, query_ref, *refs):
-    sources, (value_ref, level_ref) = refs[: len(distances)], refs[len(distances) :]
+    )(place, memory)
+
+
+def attend_kernel(
+    head_size, columns, tokens, distances, place_ref, valid_ref, query_ref, *refs
+):
+    sources, (value_ref, level_ref) = refs[:-2], refs[-2:]
     rows, width = query_ref.shape
     heads = width // head_size
     wide = 2 * head_size
     place = place_ref[0]
     biases = []
-    for source, distance in zip(sources, distances):
-        column = lanes_of((1, source.shape[0])) % columns
+    column = lanes_of((1, tokens)) % columns
+    for distance in distances:
         valid = valid_ref[0] if distance is None else valid_ref[1 + (place ^ distance)]
         biases.append(jnp.where(column < valid, 0.0, MASKED))
     bias = jnp.concatenate(biases, axis=1)
@@ -167,14 +167,14 @@
         level_ref[h : h + 1, :] = turned[h * head_size : h * head_size + 1, :]
 
 
-def attend(place, valid, queries, sources, distances, columns, head_size, dtype):
+def attend(place, valid, queries, sources, tokens, distances, columns, head_size, dtype):
     rows, width = queries.shape
     heads = width // head_size
     wide = 2 * head_size
     key_count = sum(source.shape[0] for source in sources)
     block = min(512, rows)
     return pl.pallas_call(
-        partial(attend_kernel, head_size, columns, distances),
+        partial(attend_kernel, head_size, columns, tokens, distances),
         grid=(rows // block,),
         out_shape=[
             jax.ShapeDtypeStruct((rows, width), dtype),
@@ -336,24 +336,38 @@
     near = jnp.concatenate([exchange(own_queries, "space", e) for e in evens] + [own_queries], 0)
 
     resident = old_memory.reshape(-1, old_memory.shape[-1])
-    raw_clip, pool_weight, *pieces = cut(place, resident, raw_clip, pool_weight, slots)
-    received = {0: pieces[0]}
-    for d in reversed(range(1, slots)):
-        received[d] = exchange(pieces[d], "slot", d)
-
-    far = exchange(after(near, received[slots - 1]), "space", 1)
-    behind = from_behind(after(raw_clip, received[slots - 1]), "space", 1)
+    tokens = resident.shape[0]
+    half = slots // 2
+    pairs = [tuple(range(d, d + 2)) for d in range(0, slots, 2)]
+    odd_far = tuple(range(half + 1, slots, 2))
+    odd_near = tuple(range(1, half, 2))
+    far_out, near_out, *kept = cut(
+        place, resident, slots, (odd_far, odd_near) + tuple((d,) for d in range(0, slots, 2))
+    )
+    far_in = exchange(far_out, "slot", 1)
+    near_in = exchange(near_out, "slot", 1)
+    sources = [kept[0], near_in[:tokens]]
+    distances = [0, 1]
+    for d in list(range(half, slots, 2))[::-1] + list(range(2, half, 2)):
+        passed, row = (far_in, d - half) if d >= half else (near_in, d)
+        row = row // 2 * tokens
+        both = jnp.concatenate([kept[d // 2], passed[row : row + tokens]], axis=0)
+        sources.append(exchange(both, "slot", d))
+        distances += [d, d + 1]
+
+    far = exchange(near, "space", 1)
+    behind = from_behind(raw_clip, "space", 1)
     fresh = pool(raw_clip, behind, pool_weight, head_size)
     fresh_rows = fresh.reshape(-1, fresh.shape[-1])
-    aged_memory = from_behind(after(old_memory, *received.values()), "slot", 1)
-
-    distances = tuple(range(slots))
+    aged_memory = from_behind(after(old_memory, *sources), "slot", 1)
+
     call = partial(
         attend,
         place,
         valid_columns,
-        sources=[fresh_rows] + [received[d] for d in distances],
-        distances=(None,) + distances,
+        sources=[fresh_rows] + sources,
+        tokens=tokens,
+        distances=(None,) + tuple(distances),
         columns=columns,
         head_size=head_size,
     )
@@ -369,6 +383,7 @@
         )
         parts.append((exchange(value, "space", e), exchange(level, "space", e), 0))
     value, level = call(queries=own_queries, dtype=jnp.float32)
+    value, _ = lax.optimization_barrier((value, aged_memory))
     parts = [(value, level, 0), (core_value, core_level, len(evens))] + parts
     (mixed,) = merge(parts, query_rows, head_size, True)
 
@@ -377,8 +392,7 @@
         blocks[d] = exchange(mixed, "slot", d)
     for d in range(0, slots, 2):
         blocks[d + 1] = exchange(blocks[d], "slot", 1)
-    half = slots // 2
-    first, second = distances[:half], distances[half:]
+    first, second = tuple(range(half)), tuple(range(half, slots))
     (total,) = project(place, out_weight, [blocks[d] for d in first], first)
     attended, aged_memory = project(
         place, out_weight, [blocks[d] for d in second], second, total, aged_memory

time: 80.9 us -> 69.4 us (0.86)
  starting transfers between devices: 40.1 us -> 25.3 us
  waiting for transfers between devices: 21 us -> 25 us
  local copies, waits for them, and re-layouts: 3.78 us -> 2.1 us
  Pallas kernels: 14.8 us -> 15.9 us
    ppermute x20 -> x18, starting transfers between devices: 36.2 us -> 20.5 us  [exchange(): return lax.ppermute(block, axis, [(i, i ^ distance) for i in range(size)])]
    ppermute x20 -> x18, waiting for transfers between devices: 21 us -> 25 us  [exchange(): return lax.ppermute(block, axis, [(i, i ^ distance) for i in range(size)])]
    unnamed x16 -> x12, local copies, waits for them, and re-layouts: 3.74 us -> 2.05 us
    pallas_call x4, Pallas kernels: 9.68 us -> 10.7 us  [the longest x3 9.62 us: attend(): pl.pallas_call(partial(attend_kernel, head_size, columns, tokens, distanc...]
  transfers between devices with their start and end apart: 22 -> 20, of which waited for: 10 -> 9; matrix products, arithmetic and copies ran while one was open for 0% -> 0% of each run, Pallas kernels for 10% -> 20%
where the time goes in v4:
time: 69.4 us; the launch traced here: 69.2 us
  starting transfers between devices  25.3 us (36%)
  waiting for transfers between devices  25 us (36%)
  Pallas kernels  15.9 us (23%)
  local copies, waits for them, and re-layouts  2.1 us (3%)
  between operations  0.88 us (1%)
    ppermute x18, waiting for transfers between devices, exchange(): return lax.ppermute(block, axis, [(i, i ^ distance) for i in range(size)])  25 us
    ppermute x18, starting transfers between devices, exchange(): return lax.ppermute(block, axis, [(i, i ^ distance) for i in range(size)])  20.5 us
    pallas_call x3, Pallas kernels, attend(): pl.pallas_call(partial(attend_kernel, head_size, columns, tokens, distanc...  9.62 us
    ppermute x2, starting transfers between devices, from_behind(): lax.ppermute(block, axis, [(i - distance, i) for i in devices if i - dist...  4.76 us
    pallas_call x2, Pallas kernels, project(): pl.pallas_call(partial(project_kernel, distances, total is not None, aged...  2.58 us
    unnamed x12, local copies, waits for them, and re-layouts  2.05 us
    pallas_call x1, Pallas kernels, pool(): pl.pallas_call(partial(pool_kernel, head_size), out_shape=jax.ShapeDtypeS...  1.82 us
  transfers between devices with their start and end apart: 20, of which 9 were waited for; matrix products, arithmetic and copies ran while one was open for 0% of the time, Pallas kernels for 20%

profile of v4, /device:TPU:0, one launch (start us, length us, event | category | flops | bytes accessed | tf_op | source)
XLA Modules:
  0.0 69.2 jit_solution(9498049694445969596)
XLA Ops:
  0.7 1.2 %copy-done = bf16[512,1024]{1,0:T(8,128)(2,1)S(1)} copy-done((bf16[512,1024]{1,0:T(8,128)(2,1)S(1)}, bf16[512,1024]{1,0:T(8,128)(2,1)}, u32[]{:S(2)}) %copy-start) | copy-done | bytes 1048600
  1.9 3.0 %collective-permute-start.7 = (bf16[512,128]{1,0:T(8,128)(2,1)S(1)}, bf16[512,128]{1,0:T(8,128)(2,1)S(1)}, u32[]{:S(2)}, u32[]{:S(2)}) collective-permute-start(bf16[512,128]{1,0:T(8,128)(2,1)S(1)} %constant_dynamic-slice_fusion.query_ref), channel_id=1, source_target_pairs={{0,2},{1,3},{2,0},{3,1},{4,6},{5,7},{6,4},{7,5},{8,10},{9,11},{10,... | collective-permute-start | bytes 393224 | tf_op jit(solution)/shard_map/ppermute | solution.py:27
  6.0 1.6 %collective-permute-start.1 = (bf16[256,256]{1,0:T(8,128)(2,1)S(1)}, bf16[256,256]{1,0:T(8,128)(2,1)S(1)}, u32[]{:S(2)}, u32[]{:S(2)}) collective-permute-start(bf16[256,256]{1,0:T(8,128)(2,1)S(1)} %get-tuple-element.22), channel_id=1, source_target_pairs={{0,4},{4,0},{8,12},{12,8},{16,20},{20,16},{24,28},{28,24},{1,5},{5... | collective-permute-start | bytes 393224 | tf_op jit(solution)/shard_map/ppermute | solution.py:27
  8.1 1.3 %collective-permute-start = (bf16[8,2,64,256]{3,2,1,0:T(8,128)(2,1)}, bf16[8,2,64,256]{3,2,1,0:T(8,128)(2,1)S(1)}, u32[]{:S(2)}, u32[]{:S(2)}) collective-permute-start(bf16[8,2,64,256]{3,2,1,0:T(8,128)(2,1)} %raw_ref.1), channel_id=1, source_target_pairs={{0,1},{1,2},{2,3},{4,5},{5,6},{6,7},{8,9},{9,10},{10,11},{12,13},{... | collective-permute-start | bytes 1572872 | tf_op jit(solution)/shard_map/ppermute | solution.py:32
  10.3 2.1 %collective-permute-done.1 = bf16[256,256]{1,0:T(8,128)(2,1)S(1)} collective-permute-done((bf16[256,256]{1,0:T(8,128)(2,1)S(1)}, bf16[256,256]{1,0:T(8,128)(2,1)S(1)}, u32[]{:S(2)}, u32[]{:S(2)}) %collective-permute-start.1) | collective-permute-done | bytes 131104 | tf_op jit(solution)/shard_map/ppermute | solution.py:27
  12.5 1.6 %collective-permute-start.5 = (bf16[256,256]{1,0:T(8,128)(2,1)S(1)}, bf16[256,256]{1,0:T(8,128)(2,1)S(1)}, u32[]{:S(2)}, u32[]{:S(2)}) collective-permute-start(bf16[256,256]{1,0:T(8,128)(2,1)S(1)} %pad_maximum_fusion.3), channel_id=1, source_target_pairs={{0,8},{4,12},{8,0},{12,4},{16,24},{20,28},{24,16},{28,20},{1,9},{5... | collective-permute-start | bytes 393224 | tf_op jit(solution)/shard_map/ppermute | solution.py:27
  14.2 3.4 %collective-permute-start.3 = (bf16[256,256]{1,0:T(8,128)(2,1)S(1)}, bf16[256,256]{1,0:T(8,128)(2,1)S(1)}, u32[]{:S(2)}, u32[]{:S(2)}) collective-permute-start(bf16[256,256]{1,0:T(8,128)(2,1)S(1)} %pad_maximum_fusion.1), channel_id=1, source_target_pairs={{0,24},{4,28},{8,16},{12,20},{16,8},{20,12},{24,0},{28,4},{1,25},{... | collective-permute-start | bytes 393224 | tf_op jit(solution)/shard_map/ppermute | solution.py:27
  17.6 1.3 %collective-permute-done.5.refs_5_ = bf16[256,256]{1,0:T(8,128)(2,1)S(1)} collective-permute-done((bf16[256,256]{1,0:T(8,128)(2,1)S(1)}, bf16[256,256]{1,0:T(8,128)(2,1)S(1)}, u32[]{:S(2)}, u32[]{:S(2)}) %collective-permute-start.5) | collective-permute-done | bytes 131104 | tf_op jit(solution)/shard_map/ppermute | solution.py:27
  18.9 3.8 %collective-permute-done.3.refs_3_ = bf16[256,256]{1,0:T(8,128)(2,1)S(1)} collective-permute-done((bf16[256,256]{1,0:T(8,128)(2,1)S(1)}, bf16[256,256]{1,0:T(8,128)(2,1)S(1)}, u32[]{:S(2)}, u32[]{:S(2)}) %collective-permute-start.3) | collective-permute-done | bytes 131104 | tf_op jit(solution)/shard_map/ppermute | solution.py:27
  22.7 4.7 %collective-permute-done.4.refs_4_ = bf16[256,256]{1,0:T(8,128)(2,1)S(1)} collective-permute-done((bf16[256,256]{1,0:T(8,128)(2,1)S(1)}, bf16[256,256]{1,0:T(8,128)(2,1)S(1)}, u32[]{:S(2)}, u32[]{:S(2)}) %collective-permute-start.4) | collective-permute-done | bytes 131104 | tf_op jit(solution)/shard_map/ppermute | solution.py:27
  27.4 3.4 %collective-permute-start.6 = (bf16[1,4,1,32,2048]{4,3,2,1,0:T(8,128)(2,1)}, bf16[1,4,1,32,2048]{4,3,2,1,0:T(8,128)(2,1)S(1)}, u32[]{:S(2)}, u32[]{:S(2)}) collective-permute-start(bf16[1,4,1,32,2048]{4,3,2,1,0:T(8,128)(2,1)} %param.9), channel_id=1, source_target_pairs={{0,4},{4,8},{8,12},{12,16},{16,20},{20,24},{24,28},{1,5},{5,9},{9,... | collective-permute-start | bytes 1572872 | tf_op jit(solution)/shard_map/ppermute | solution.py:32
  30.9 1.8 %pool.1 = bf16[4,1,32,256]{3,2,1,0:T(8,128)(2,1)} custom-call(bf16[8,2,64,256]{3,2,1,0:T(8,128)(2,1)S(1)} %copy-done.2, bf16[8,2,64,256]{3,2,1,0:T(8,128)(2,1)S(1)} %collective-permute-done.halo_ref, bf16[27,256]{1,0:T(8,128)(2,1)S(1)} %copy-done.4), custom_call_target="tpu_custom_call" | custom-call | tf_op jit(solution)/shard_map/pool/pallas_call | solution.py:75
  33.6 4.6 %attend.4 = (bf16[1024,128]{1,0:T(8,128)(2,1)S(1)}, f32[8,1024]{1,0:T(8,128)S(1)}) custom-call(s32[1]{0:T(128)} %bitcast.place_ref, s32[9]{0:T(128)S(1)} %copy-done.5, bf16[1024,128]{1,0:T(8,128)(2,1)S(1)} %collective-permute-done.8.query_ref, bf16[128,256]{1,0:T(8,128)(2,1)S(1)} %bitcast.3, bf16[128,256]{1,0:T(8,128)(2,1)S(1)} %get-tuple-element.21.refs_1_, ...), custom_call_target="tpu_custom_call" | custom-call | flops 1207959552 | bytes 3276800 | tf_op jit(solution)/shard_map/attend/pallas_call | solution.py:176
  38.7 2.5 %attend.5 = (f32[512,128]{1,0:T(8,128)S(1)}, f32[8,512]{1,0:T(8,128)S(1)}) custom-call(s32[1]{0:T(128)} %bitcast.place_ref, s32[9]{0:T(128)S(1)} %copy-done.5, bf16[512,128]{1,0:T(8,128)(2,1)S(1)} %collective-permute-done.7.query_ref, bf16[128,256]{1,0:T(8,128)(2,1)S(1)} %bitcast.4, bf16[128,256]{1,0:T(8,128)(2,1)S(1)} %get-tuple-element.21.refs_1_, ...), custom_call_target="tpu_custom_call" | custom-call | flops 603979776 | bytes 2228224 | tf_op jit(solution)/shard_map/attend/pallas_call | solution.py:176
  42.3 1.5 %collective-permute-start.12 = (f32[8,512]{1,0:T(8,128)S(1)}, f32[8,512]{1,0:T(8,128)S(1)}, u32[]{:S(2)}, u32[]{:S(2)}) collective-permute-start(f32[8,512]{1,0:T(8,128)S(1)} %get-tuple-element.36), channel_id=1, source_target_pairs={{0,2},{1,3},{2,0},{3,1},{4,6},{5,7},{6,4},{7,5},{8,10},{9,11},{10,... | collective-permute-start | bytes 49160 | tf_op jit(solution)/shard_map/ppermute | solution.py:27
  43.8 2.5 %attend.3 = (f32[512,128]{1,0:T(8,128)S(1)}, f32[8,512]{1,0:T(8,128)S(1)}) custom-call(s32[1]{0:T(128)} %bitcast.place_ref, s32[9]{0:T(128)S(1)} %copy-done.5, bf16[512,128]{1,0:T(8,128)(2,1)S(1)} %constant_dynamic-slice_fusion.query_ref, bf16[128,256]{1,0:T(8,128)(2,1)S(1)} %bitcast.5, bf16[128,256]{1,0:T(8,128)(2,1)S(1)} %get-tuple-element.21.refs_1_, ...), custom_call_target="tpu_custom_call" | custom-call | flops 603979776 | bytes 2228224 | tf_op jit(solution)/shard_map/attend/pallas_call | solution.py:176
  46.3 1.3 %collective-permute-done.12.refs_5_ = f32[8,512]{1,0:T(8,128)S(1)} collective-permute-done((f32[8,512]{1,0:T(8,128)S(1)}, f32[8,512]{1,0:T(8,128)S(1)}, u32[]{:S(2)}, u32[]{:S(2)}) %collective-permute-start.12) | collective-permute-done | bytes 16416 | tf_op jit(solution)/shard_map/ppermute | solution.py:27
  48.0 2.6 %collective-permute-start.15 = (bf16[512,128]{1,0:T(8,128)(2,1)S(1)}, bf16[512,128]{1,0:T(8,128)(2,1)S(1)}, u32[]{:S(2)}, u32[]{:S(2)}) collective-permute-start(bf16[512,128]{1,0:T(8,128)(2,1)S(1)} %merge.3.refs_0_), channel_id=1, source_target_pairs={{0,24},{4,28},{8,16},{12,20},{16,8},{20,12},{24,0},{28,4},{1,25},{... | collective-permute-start | bytes 393224 | tf_op jit(solution)/shard_map/ppermute | solution.py:27
  52.5 2.4 %collective-permute-done.18.refs_2_ = bf16[512,128]{1,0:T(8,128)(2,1)S(1)} collective-permute-done((bf16[512,128]{1,0:T(8,128)(2,1)S(1)}, bf16[512,128]{1,0:T(8,128)(2,1)S(1)}, u32[]{:S(2)}, u32[]{:S(2)}) %collective-permute-start.18) | collective-permute-done | bytes 131104 | tf_op jit(solution)/shard_map/ppermute | solution.py:27
  54.9 2.8 %collective-permute-done.15.refs_2_ = bf16[512,128]{1,0:T(8,128)(2,1)S(1)} collective-permute-done((bf16[512,128]{1,0:T(8,128)(2,1)S(1)}, bf16[512,128]{1,0:T(8,128)(2,1)S(1)}, u32[]{:S(2)}, u32[]{:S(2)}) %collective-permute-start.15) | collective-permute-done | bytes 131104 | tf_op jit(solution)/shard_map/ppermute | solution.py:27
  57.6 1.7 %collective-permute-start.16 = (bf16[512,128]{1,0:T(8,128)(2,1)S(1)}, bf16[512,128]{1,0:T(8,128)(2,1)S(1)}, u32[]{:S(2)}, u32[]{:S(2)}) collective-permute-start(bf16[512,128]{1,0:T(8,128)(2,1)S(1)} %collective-permute-done.15.refs_2_), channel_id=1, source_target_pairs={{0,4},{4,0},{8,12},{12,8},{16,20},{20,16},{24,28},{28,24},{1,5},{5... | collective-permute-start | bytes 393224 | tf_op jit(solution)/shard_map/ppermute | solution.py:27
  59.3 3.0 %collective-permute-done.13.refs_0_ = bf16[512,128]{1,0:T(8,128)(2,1)S(1)} collective-permute-done((bf16[512,128]{1,0:T(8,128)(2,1)S(1)}, bf16[512,128]{1,0:T(8,128)(2,1)S(1)}, u32[]{:S(2)}, u32[]{:S(2)}) %collective-permute-start.13) | collective-permute-done | bytes 131104 | tf_op jit(solution)/shard_map/ppermute | solution.py:27
  63.6 3.7 %collective-permute-done.14.refs_1_ = bf16[512,128]{1,0:T(8,128)(2,1)S(1)} collective-permute-done((bf16[512,128]{1,0:T(8,128)(2,1)S(1)}, bf16[512,128]{1,0:T(8,128)(2,1)S(1)}, u32[]{:S(2)}, u32[]{:S(2)}) %collective-permute-start.14) | collective-permute-done | bytes 131104 | tf_op jit(solution)/shard_map/ppermute | solution.py:27
  67.3 1.9 %project.3 = (bf16[512,1024]{1,0:T(8,128)(2,1)}, bf16[1,4,1,32,2048]{4,3,2,1,0:T(8,128)(2,1)}) custom-call(s32[1]{0:T(128)} %bitcast.place_ref, bf16[1024,1024]{1,0:T(8,128)(2,1)S(1)} %copy-done.1, bf16[512,128]{1,0:T(8,128)(2,1)S(1)} %collective-permute-done.13.refs_0_, bf16[512,128]{1,0:T(8,128)(2,1)S(1)} %collective-permute-done.14.refs_1_, ...), custom_call_target="tpu_custom_call" | custom-call | flops 536870912 | bytes 2097152 | tf_op jit(solution)/shard_map/project/pallas_call | solution.py:304
  (44 shorter events, 8.7 us)
Async XLA Ops:
  0.6 30.3 %copy-start.2 = (bf16[8,2,64,256]{3,2,1,0:T(8,128)(2,1)S(1)}, bf16[8,2,64,256]{3,2,1,0:T(8,128)(2,1)}, u32[]{:S(2)}) copy-start(bf16[8,2,64,256]{3,2,1,0:T(8,128)(2,1)} %raw_ref.1) | copy-start | bytes 1572868
  0.7 30.3 %copy-start.4 = (bf16[27,256]{1,0:T(8,128)(2,1)S(1)}, bf16[27,256]{1,0:T(8,128)(2,1)}, u32[]{:S(2)}) copy-start(bf16[27,256]{1,0:T(8,128)(2,1)} %weight_ref.3) | copy-start | bytes 41476
  0.7 32.1 %copy-start.5 = (s32[9]{0:T(128)S(1)}, s32[9]{0:T(128)}, u32[]{:S(2)}) copy-start(s32[9]{0:T(128)} %valid_ref.5) | copy-start | bytes 112
  1.9 7.5 %collective-permute-start.7 = (bf16[512,128]{1,0:T(8,128)(2,1)S(1)}, bf16[512,128]{1,0:T(8,128)(2,1)S(1)}, u32[]{:S(2)}, u32[]{:S(2)}) collective-permute-start(bf16[512,128]{1,0:T(8,128)(2,1)S(1)} %constant_dynamic-slice_fusion.query_ref), channel_id=1, source_target_pairs={{0,2},{1,3},{2,0},{3,1},{4,6},{5,7},{6,4},{7,5},{8,10},{9,11},{10,... | collective-permute-start | bytes 393224 | tf_op jit(solution)/shard_map/ppermute | solution.py:27
  6.0 6.4 %collective-permute-start.1 = (bf16[256,256]{1,0:T(8,128)(2,1)S(1)}, bf16[256,256]{1,0:T(8,128)(2,1)S(1)}, u32[]{:S(2)}, u32[]{:S(2)}) collective-permute-start(bf16[256,256]{1,0:T(8,128)(2,1)S(1)} %get-tuple-element.22), channel_id=1, source_target_pairs={{0,4},{4,0},{8,12},{12,8},{16,20},{20,16},{24,28},{28,24},{1,5},{5... | collective-permute-start | bytes 393224 | tf_op jit(solution)/shard_map/ppermute | solution.py:27
  7.6 6.5 %collective-permute-start.2 = (bf16[256,256]{1,0:T(8,128)(2,1)S(1)}, bf16[256,256]{1,0:T(8,128)(2,1)S(1)}, u32[]{:S(2)}, u32[]{:S(2)}) collective-permute-start(bf16[256,256]{1,0:T(8,128)(2,1)S(1)} %get-tuple-element.24), channel_id=1, source_target_pairs={{0,4},{4,0},{8,12},{12,8},{16,20},{20,16},{24,28},{28,24},{1,5},{5... | collective-permute-start | bytes 393224 | tf_op jit(solution)/shard_map/ppermute | solution.py:27
  8.1 22.8 %collective-permute-start = (bf16[8,2,64,256]{3,2,1,0:T(8,128)(2,1)}, bf16[8,2,64,256]{3,2,1,0:T(8,128)(2,1)S(1)}, u32[]{:S(2)}, u32[]{:S(2)}) collective-permute-start(bf16[8,2,64,256]{3,2,1,0:T(8,128)(2,1)} %raw_ref.1), channel_id=1, source_target_pairs={{0,1},{1,2},{2,3},{4,5},{5,6},{6,7},{8,9},{9,10},{10,11},{12,13},{... | collective-permute-start | bytes 1572872 | tf_op jit(solution)/shard_map/ppermute | solution.py:32
  9.5 23.3 %collective-permute-start.8 = (bf16[1024,128]{1,0:T(8,128)(2,1)S(1)}, bf16[1024,128]{1,0:T(8,128)(2,1)S(1)}, u32[]{:S(2)}, u32[]{:S(2)}) collective-permute-start(bf16[1024,128]{1,0:T(8,128)(2,1)S(1)} %pad_maximum_fusion), channel_id=1, source_target_pairs={{0,1},{1,0},{2,3},{3,2},{4,5},{5,4},{6,7},{7,6},{8,9},{9,8},{10,11... | collective-permute-start | bytes 786440 | tf_op jit(solution)/shard_map/ppermute | solution.py:27
  12.5 6.4 %collective-permute-start.5 = (bf16[256,256]{1,0:T(8,128)(2,1)S(1)}, bf16[256,256]{1,0:T(8,128)(2,1)S(1)}, u32[]{:S(2)}, u32[]{:S(2)}) collective-permute-start(bf16[256,256]{1,0:T(8,128)(2,1)S(1)} %pad_maximum_fusion.3), channel_id=1, source_target_pairs={{0,8},{4,12},{8,0},{12,4},{16,24},{20,28},{24,16},{28,20},{1,9},{5... | collective-permute-start | bytes 393224 | tf_op jit(solution)/shard_map/ppermute | solution.py:27
  14.2 8.6 %collective-permute-start.3 = (bf16[256,256]{1,0:T(8,128)(2,1)S(1)}, bf16[256,256]{1,0:T(8,128)(2,1)S(1)}, u32[]{:S(2)}, u32[]{:S(2)}) collective-permute-start(bf16[256,256]{1,0:T(8,128)(2,1)S(1)} %pad_maximum_fusion.1), channel_id=1, source_target_pairs={{0,24},{4,28},{8,16},{12,20},{16,8},{20,12},{24,0},{28,4},{1,25},{... | collective-permute-start | bytes 393224 | tf_op jit(solution)/shard_map/ppermute | solution.py:27
  17.6 9.9 %collective-permute-start.4 = (bf16[256,256]{1,0:T(8,128)(2,1)S(1)}, bf16[256,256]{1,0:T(8,128)(2,1)S(1)}, u32[]{:S(2)}, u32[]{:S(2)}) collective-permute-start(bf16[256,256]{1,0:T(8,128)(2,1)S(1)} %pad_maximum_fusion.2), channel_id=1, source_target_pairs={{0,16},{4,20},{8,24},{12,28},{16,0},{20,4},{24,8},{28,12},{1,17},{... | collective-permute-start | bytes 393224 | tf_op jit(solution)/shard_map/ppermute | solution.py:27
  27.4 18.9 %collective-permute-start.6 = (bf16[1,4,1,32,2048]{4,3,2,1,0:T(8,128)(2,1)}, bf16[1,4,1,32,2048]{4,3,2,1,0:T(8,128)(2,1)S(1)}, u32[]{:S(2)}, u32[]{:S(2)}) collective-permute-start(bf16[1,4,1,32,2048]{4,3,2,1,0:T(8,128)(2,1)} %param.9), channel_id=1, source_target_pairs={{0,4},{4,8},{8,12},{12,16},{16,20},{20,24},{24,28},{1,5},{5,9},{9,... | collective-permute-start | bytes 1572872 | tf_op jit(solution)/shard_map/ppermute | solution.py:32
  38.2 3.1 %collective-permute-start.9 = (bf16[1024,128]{1,0:T(8,128)(2,1)S(1)}, bf16[1024,128]{1,0:T(8,128)(2,1)S(1)}, u32[]{:S(2)}, u32[]{:S(2)}) collective-permute-start(bf16[1024,128]{1,0:T(8,128)(2,1)S(1)} %get-tuple-element.31), channel_id=1, source_target_pairs={{0,1},{1,0},{2,3},{3,2},{4,5},{5,4},{6,7},{7,6},{8,9},{9,8},{10,11... | collective-permute-start | bytes 786440 | tf_op jit(solution)/shard_map/ppermute | solution.py:27
  38.2 3.1 %collective-permute-start.10 = (f32[8,1024]{1,0:T(8,128)S(1)}, f32[8,1024]{1,0:T(8,128)S(1)}, u32[]{:S(2)}, u32[]{:S(2)}) collective-permute-start(f32[8,1024]{1,0:T(8,128)S(1)} %get-tuple-element.32), channel_id=1, source_target_pairs={{0,1},{1,0},{2,3},{3,2},{4,5},{5,4},{6,7},{7,6},{8,9},{9,8},{10,11... | collective-permute-start | bytes 98312 | tf_op jit(solution)/shard_map/ppermute | solution.py:27
  41.3 21.6 %copy-start.1 = (bf16[1024,1024]{1,0:T(8,128)(2,1)S(1)}, bf16[1024,1024]{1,0:T(8,128)(2,1)}, u32[]{:S(2)}) copy-start(bf16[1024,1024]{1,0:T(8,128)(2,1)} %weight_ref.5) | copy-start | bytes 6291460
  41.7 5.9 %collective-permute-start.11 = (bf16[512,128]{1,0:T(8,128)(2,1)S(1)}, bf16[512,128]{1,0:T(8,128)(2,1)S(1)}, u32[]{:S(2)}, u32[]{:S(2)}) collective-permute-start(bf16[512,128]{1,0:T(8,128)(2,1)S(1)} %get-tuple-element.35), channel_id=1, source_target_pairs={{0,2},{1,3},{2,0},{3,1},{4,6},{5,7},{6,4},{7,5},{8,10},{9,11},{10,... | collective-permute-start | bytes 393224 | tf_op jit(solution)/shard_map/ppermute | solution.py:27
  42.3 5.3 %collective-permute-start.12 = (f32[8,512]{1,0:T(8,128)S(1)}, f32[8,512]{1,0:T(8,128)S(1)}, u32[]{:S(2)}, u32[]{:S(2)}) collective-permute-start(f32[8,512]{1,0:T(8,128)S(1)} %get-tuple-element.36), channel_id=1, source_target_pairs={{0,2},{1,3},{2,0},{3,1},{4,6},{5,7},{6,4},{7,5},{8,10},{9,11},{10,... | collective-permute-start | bytes 49160 | tf_op jit(solution)/shard_map/ppermute | solution.py:27
  48.0 6.9 %collective-permute-start.18 = (bf16[512,128]{1,0:T(8,128)(2,1)S(1)}, bf16[512,128]{1,0:T(8,128)(2,1)S(1)}, u32[]{:S(2)}, u32[]{:S(2)}) collective-permute-start(bf16[512,128]{1,0:T(8,128)(2,1)S(1)} %merge.3.refs_0_), channel_id=1, source_target_pairs={{0,8},{4,12},{8,0},{12,4},{16,24},{20,28},{24,16},{28,20},{1,9},{5... | collective-permute-start | bytes 393224 | tf_op jit(solution)/shard_map/ppermute | solution.py:27
  48.0 9.6 %collective-permute-start.15 = (bf16[512,128]{1,0:T(8,128)(2,1)S(1)}, bf16[512,128]{1,0:T(8,128)(2,1)S(1)}, u32[]{:S(2)}, u32[]{:S(2)}) collective-permute-start(bf16[512,128]{1,0:T(8,128)(2,1)S(1)} %merge.3.refs_0_), channel_id=1, source_target_pairs={{0,24},{4,28},{8,16},{12,20},{16,8},{20,12},{24,0},{28,4},{1,25},{... | collective-permute-start | bytes 393224 | tf_op jit(solution)/shard_map/ppermute | solution.py:27
  50.6 11.7 %collective-permute-start.13 = (bf16[512,128]{1,0:T(8,128)(2,1)S(1)}, bf16[512,128]{1,0:T(8,128)(2,1)S(1)}, u32[]{:S(2)}, u32[]{:S(2)}) collective-permute-start(bf16[512,128]{1,0:T(8,128)(2,1)S(1)} %merge.3.refs_0_), channel_id=1, source_target_pairs={{0,16},{4,20},{8,24},{12,28},{16,0},{20,4},{24,8},{28,12},{1,17},{... | collective-permute-start | bytes 393224 | tf_op jit(solution)/shard_map/ppermute | solution.py:27
  51.5 11.4 %collective-permute-start.17 = (bf16[512,128]{1,0:T(8,128)(2,1)S(1)}, bf16[512,128]{1,0:T(8,128)(2,1)S(1)}, u32[]{:S(2)}, u32[]{:S(2)}) collective-permute-start(bf16[512,128]{1,0:T(8,128)(2,1)S(1)} %merge.3.refs_0_), channel_id=1, source_target_pairs={{0,4},{4,0},{8,12},{12,8},{16,20},{20,16},{24,28},{28,24},{1,5},{5... | collective-permute-start | bytes 393224 | tf_op jit(solution)/shard_map/ppermute | solution.py:27
  54.9 8.0 %collective-permute-start.19 = (bf16[512,128]{1,0:T(8,128)(2,1)S(1)}, bf16[512,128]{1,0:T(8,128)(2,1)S(1)}, u32[]{:S(2)}, u32[]{:S(2)}) collective-permute-start(bf16[512,128]{1,0:T(8,128)(2,1)S(1)} %collective-permute-done.18.refs_2_), channel_id=1, source_target_pairs={{0,4},{4,0},{8,12},{12,8},{16,20},{20,16},{24,28},{28,24},{1,5},{5... | collective-permute-start | bytes 393224 | tf_op jit(solution)/shard_map/ppermute | solution.py:27
  57.6 6.0 %collective-permute-start.16 = (bf16[512,128]{1,0:T(8,128)(2,1)S(1)}, bf16[512,128]{1,0:T(8,128)(2,1)S(1)}, u32[]{:S(2)}, u32[]{:S(2)}) collective-permute-start(bf16[512,128]{1,0:T(8,128)(2,1)S(1)} %collective-permute-done.15.refs_2_), channel_id=1, source_target_pairs={{0,4},{4,0},{8,12},{12,8},{16,20},{20,16},{24,28},{28,24},{1,5},{5... | collective-permute-start | bytes 393224 | tf_op jit(solution)/shard_map/ppermute | solution.py:27
  62.3 5.0 %collective-permute-start.14 = (bf16[512,128]{1,0:T(8,128)(2,1)S(1)}, bf16[512,128]{1,0:T(8,128)(2,1)S(1)}, u32[]{:S(2)}, u32[]{:S(2)}) collective-permute-start(bf16[512,128]{1,0:T(8,128)(2,1)S(1)} %collective-permute-done.13.refs_0_), channel_id=1, source_target_pairs={{0,4},{4,0},{8,12},{12,8},{16,20},{20,16},{24,28},{28,24},{1,5},{5... | collective-permute-start | bytes 393224 | tf_op jit(solution)/shard_map/ppermute | solution.py:27
  (2 other events, 2.1 us)

commit v5 on v4

v5 whole, which is shorter than its diff:
```python
from functools import partial

import jax
import jax.numpy as jnp
from jax import lax
from jax.experimental import pallas as pl
from jax.experimental.pallas import tpu as pltpu
from jax.sharding import PartitionSpec as P

H = 16
MASKED = -1e30
BLOCK = 512
VMEM_LIMIT = 48 * 1024 * 1024
VMEM = pltpu.VMEM
SMEM = pltpu.SMEM


def params(**more):
    return pltpu.CompilerParams(vmem_limit_bytes=VMEM_LIMIT, **more)


def lanes_of(shape):
    return lax.broadcasted_iota(jnp.int32, shape, len(shape) - 1)


def exchange(block, axis, distance):
    size = lax.axis_size(axis)
    return lax.ppermute(block, axis, [(i, i ^ distance) for i in range(size)])


def from_behind(block, axis, distance):
    devices = range(lax.axis_size(axis))
    return lax.ppermute(block, axis, [(i - distance, i) for i in devices if i - distance in devices])


def pool_kernel(head_size, raw_ref, halo_ref, weight_ref, out_ref, rows_ref, slabs):
    frames, rows, columns, channels = raw_ref.shape
    frames_out, columns_out = frames // 2, columns // 2
    pieces, _, _, wide = slabs.shape
    group = lax.broadcasted_iota(jnp.int32, (wide, wide), 0) // head_size
    averaging = jnp.where(
        group == lanes_of((wide, wide)) // head_size, 1.0 / head_size, 0.0
    ).astype(jnp.float32)
    first_row = lax.broadcasted_iota(jnp.int32, (columns_out, wide), 0) == 0
    mean = partial(
        jnp.dot, precision=lax.Precision.HIGHEST, preferred_element_type=jnp.float32
    )
    for piece in range(pieces):
        lanes = slice(piece * wide, (piece + 1) * wide)
        for f in range(frames):
            slabs[piece, 3 * f] = halo_ref[f, 0, :, lanes].astype(jnp.float32)
            slabs[piece, 3 * f + 1] = raw_ref[f, 0, :, lanes].astype(jnp.float32)
            slabs[piece, 3 * f + 2] = raw_ref[f, 1, :, lanes].astype(jnp.float32)
        weight = weight_ref[:, lanes].astype(jnp.float32)
        for f in range(frames_out):
            sums = [jnp.zeros((columns_out, wide), jnp.float32) for _ in range(3)]
            for a in range(3):
                frame = 2 * f + a - 1
                if frame < 0:
                    continue
                for b in range(3):
                    even = slabs[piece, 3 * frame + b, pl.ds(0, columns_out, stride=2), :]
                    odd = slabs[piece, 3 * frame + b, pl.ds(1, columns_out, stride=2), :]
                    for g, tapped in enumerate((odd, even, odd)):
                        tap = 9 * a + 3 * b + g
                        sums[g] = sums[g] + weight[tap : tap + 1] * tapped
            behind = jnp.where(first_row, 0.0, pltpu.roll(sums[0], 1, 0))
            pooled = behind + sums[1] + sums[2]
            centered = pooled - mean(pooled, averaging)
            spread = mean(centered * centered, averaging)
            normed = (centered * lax.rsqrt(spread + 1e-06)).astype(jnp.bfloat16)
            out_ref[f, 0, :, lanes] = normed
            rows_ref[f * columns_out : (f + 1) * columns_out, lanes] = normed


def edge_kernel(raw_ref, out_ref, semaphore):
    rows = raw_ref.shape[1]
    copy = pltpu.make_async_copy(raw_ref.at[:, pl.ds(rows - 1, 1)], out_ref, semaphore)
    copy.start()
    copy.wait()


def edge(raw_clip):
    frames, rows, columns, channels = raw_clip.shape
    return pl.pallas_call(
        edge_kernel,
        out_shape=jax.ShapeDtypeStruct((frames, 1, columns, channels), raw_clip.dtype),
        in_specs=[pl.BlockSpec(memory_space=pl.ANY)],
        out_specs=pl.BlockSpec(memory_space=VMEM),
        scratch_shapes=[pltpu.SemaphoreType.DMA],
        compiler_params=params(),
        name="edge",
    )(raw_clip)


def pool(raw_clip, halo, pool_weight, head_size):
    frames, rows, columns, channels = raw_clip.shape
    return pl.pallas_call(
        partial(pool_kernel, head_size),
        out_shape=[
            jax.ShapeDtypeStruct((frames // 2, 1, columns // 2, channels), jnp.bfloat16),
            jax.ShapeDtypeStruct((frames // 2 * columns // 2, channels), jnp.bfloat16),
        ],
        in_specs=[pl.BlockSpec(memory_space=VMEM)] * 3,
        out_specs=[pl.BlockSpec(memory_space=VMEM)] * 2,
        scratch_shapes=[VMEM((channels // 128, 3 * frames, columns, 128), jnp.float32)],
        compiler_params=params(),
        name="pool",
    )(raw_clip, halo, pool_weight)


def cut_kernel(width, groups, place_ref, memory_ref, *refs):
    out_refs, semaphores = refs[:-1], refs[-1]
    place = place_ref[0]
    tokens = memory_ref.shape[0]
    copies = []
    for group, out_ref in zip(groups, out_refs):
        for k, distance in enumerate(group):
            start = pl.multiple_of((place ^ distance) * width, 128)
            copy = pltpu.make_async_copy(
                memory_ref.at[:, pl.ds(start, width)],
                out_ref.at[pl.ds(k * tokens, tokens)],
                semaphores.at[len(copies)],
            )
            copy.start()
            copies.append(copy)
    for copy in copies:
        copy.wait()


def cut(place, memory, pieces, groups):
    tokens, channels = memory.shape
    width = channels // pieces
    return pl.pallas_call(
        partial(cut_kernel, width, groups),
        out_shape=[jax.ShapeDtypeStruct((len(g) * tokens, width), memory.dtype) for g in groups],
        in_specs=[pl.BlockSpec(memory_space=SMEM), pl.BlockSpec(memory_space=pl.ANY)],
        out_specs=[pl.BlockSpec(memory_space=VMEM)] * len(groups),
        scratch_shapes=[pltpu.SemaphoreType.DMA((pieces,))],
        compiler_params=params(),
        name="cut",
    )(place, memory)


def attend_kernel(
    head_size, columns, tokens, distances, travels, place_ref, valid_ref, query_ref, *refs
):
    outs = 1 if travels else 2
    sources, out_refs = refs[:-outs], refs[-outs:]
    rows, width = query_ref.shape
    heads = width // head_size
    wide = 2 * head_size
    place = place_ref[0]
    biases = []
    column = lanes_of((1, tokens)) % columns
    for distance in distances:
        valid = valid_ref[0] if distance is None else valid_ref[1 + (place ^ distance)]
        biases.append(jnp.where(column < valid, 0.0, MASKED))
    bias = jnp.concatenate(biases, axis=1)
    lane = lanes_of((rows, wide))
    queries = query_ref[...].astype(jnp.float32) * head_size ** (-0.5)
    memory, scores = [], []
    for h in range(heads):
        own = queries if h == 0 else pltpu.roll(queries, width - h * head_size, 1)
        if own.shape[1] < wide:
            own = jnp.concatenate([own, own], axis=1)
        own = jnp.where(lane < head_size, own, 0.0).astype(jnp.bfloat16)
        memory.append(
            jnp.concatenate([source[:, h * wide : (h + 1) * wide] for source in sources], axis=0)
        )
        product = lax.dot_general(
            own, memory[h], (((1,), (1,)), ((), ())), preferred_element_type=jnp.float32
        )
        scores.append(product + bias)
    weights, peaks = [], []
    for h in range(heads):
        peaks.append(jnp.max(scores[h], axis=1, keepdims=True))
        weights.append(jnp.exp(scores[h] - peaks[h]).astype(jnp.bfloat16))
    values, levels = [], []
    memory_lane = lanes_of(memory[0].shape)
    for h in range(heads):
        ones_and_values = jnp.where(memory_lane < head_size, 1.0, memory[h].astype(jnp.float32))
        total = jnp.dot(
            weights[h], ones_and_values.astype(jnp.bfloat16), preferred_element_type=jnp.float32
        )
        turned = pltpu.roll(total, head_size, 1)
        if h % 2:
            values.append(total / turned)
            levels.append(jnp.log(turned) + peaks[h])
        else:
            values.append(turned / total)
            levels.append(jnp.log(total) + peaks[h])
    if heads == 1:
        value, level = values[0][:, :head_size], levels[0]
    else:
        value = jnp.where(lane < head_size, *values)
        level = jnp.where(lane < head_size, *levels)
    if travels:
        pack(out_refs[0], value, level, head_size)
    else:
        out_refs[0][...] = value
        out_refs[1][...] = level[:, :width]


def packed_rows(rows, width, head_size):
    return -(-3 * (width // head_size) * rows // width // 16) * 16


def pack(out_ref, value, level, head_size):
    rows, width = value.shape
    out_ref[:rows] = value.astype(out_ref.dtype)
    turned = level.T
    lines = []
    for h in range(width // head_size):
        rest = turned[h * head_size : h * head_size + 1, :]
        for _ in range(3):
            term = rest.astype(jnp.bfloat16).astype(jnp.float32)
            rest = rest - term
            lines += [term[:, j : j + width] for j in range(0, rows, width)]
    below = packed_rows(rows, width, head_size)
    if len(lines) < below:
        lines.append(jnp.zeros((below - len(lines), width), jnp.float32))
    out_ref[rows:] = jnp.concatenate(lines, axis=0).astype(out_ref.dtype)


def unpack(ref, rows, head_size):
    width = ref.shape[1]
    packed = ref[rows:].astype(jnp.float32)
    count = rows // width
    spread = []
    for h in range(width // head_size):
        first = 3 * h * count
        line = [
            packed[j : j + 1] + packed[j + count : j + count + 1] + packed[j + 2 * count : j + 2 * count + 1]
            for j in range(first, first + count)
        ]
        spread.append(jnp.broadcast_to(jnp.concatenate(line, axis=1), (head_size, rows)))
    return ref[:rows].astype(jnp.float32), jnp.concatenate(spread, axis=0).T


def attend(
    place, valid, queries, sources, tokens, distances, columns, head_size, travels, weight=1
):
    rows, width = queries.shape
    heads = width // head_size
    wide = 2 * head_size
    key_count = sum(source.shape[0] for source in sources)
    block = min(BLOCK, rows)
    if travels:
        held = block + packed_rows(block, width, head_size)
        out_shape = [jax.ShapeDtypeStruct((rows // block * held, width), jnp.bfloat16)]
        out_specs = [pl.BlockSpec((held, width), lambda i: (i, 0))]
    else:
        out_shape = [jax.ShapeDtypeStruct((rows, width), jnp.float32)] * 2
        out_specs = [pl.BlockSpec((block, width), lambda i: (i, 0))] * 2
    return pl.pallas_call(
        partial(attend_kernel, head_size, columns, tokens, distances, travels),
        grid=(rows // block,),
        out_shape=out_shape,
        in_specs=[
            pl.BlockSpec(memory_space=SMEM),
            pl.BlockSpec(memory_space=SMEM),
            pl.BlockSpec((block, width), lambda i: (i, 0)),
        ]
        + [pl.BlockSpec(memory_space=VMEM)] * len(sources),
        out_specs=out_specs,
        compiler_params=params(),
        cost_estimate=pl.CostEstimate(
            flops=weight * 4 * rows * key_count * wide * heads,
            bytes_accessed=4 * key_count * wide * heads + 8 * rows * wide * heads,
            transcendentals=rows * key_count * heads,
        ),
        name="attend",
    )(place, valid, queries, *sources)


def merge_kernel(head_size, travels, value_ref, level_ref, *refs):
    parts, out_ref = refs[:-1], refs[-1]
    rows, width = value_ref.shape
    values, levels = [value_ref[...]], [level_ref[...]]
    for ref in parts:
        value, level = unpack(ref, rows, head_size)
        values.append(value)
        levels.append(level)
    top = levels[0]
    for level in levels[1:]:
        top = jnp.maximum(top, level)
    total = jnp.zeros((rows, width), jnp.float32)
    share = jnp.zeros((rows, width), jnp.float32)
    for value, level in zip(values, levels):
        factor = jnp.exp(level - top)
        total = total + value * factor
        share = share + factor
    mixed = total / share
    if travels:
        level = top + jnp.log(share)
        if width < 128:
            level = jnp.concatenate([level, level], axis=1)
        pack(out_ref, mixed, level, head_size)
    else:
        out_ref[...] = mixed.astype(out_ref.dtype)


def merge(value, level, parts, head_size, travels):
    rows, width = value.shape
    held = rows + packed_rows(rows, width, head_size)
    whole = pl.BlockSpec((rows, width), lambda i: (0, 0))
    part_specs = [pl.BlockSpec((held, width), lambda i, k=k: (k, 0)) for _, k in parts]
    out_rows = held if travels else rows
    return pl.pallas_call(
        partial(merge_kernel, head_size, travels),
        grid=(1,),
        out_shape=jax.ShapeDtypeStruct((out_rows, width), jnp.bfloat16),
        in_specs=[whole, whole] + part_specs,
        out_specs=pl.BlockSpec((out_rows, width), lambda i: (0, 0)),
        compiler_params=params(),
        name="merge",
    )(value, level, *[part for part, _ in parts])


def weight_rows(weight_ref, place, distances, width):
    starts = [pl.multiple_of((place ^ d) * width, width) for d in distances]
    return jnp.concatenate([weight_ref[pl.ds(start, width), :] for start in starts], axis=0)


def project_early_kernel(distances, place_ref, weight_ref, *refs):
    blocks, (aged_ref, out_ref, aged_out, semaphore) = refs[:-4], refs[-4:]
    copy = pltpu.make_async_copy(aged_ref, aged_out, semaphore)
    copy.start()
    out_ref[...] = jnp.dot(
        jnp.concatenate([block[...] for block in blocks], axis=1),
        weight_rows(weight_ref, place_ref[0], distances, blocks[0].shape[1]),
        preferred_element_type=jnp.float32,
    )
    copy.wait()


def project_late_kernel(distances, place_ref, weight_ref, *refs):
    blocks, (total_ref, out_ref, held, semaphores) = refs[:-4], refs[-4:]
    weights = weight_rows(weight_ref, place_ref[0], distances, blocks[0].shape[1])
    rows = total_ref.shape[0]
    step = rows // semaphores.shape[0]
    copies = []
    for k in range(semaphores.shape[0]):
        here = slice(k * step, (k + 1) * step)
        total = total_ref[here] + jnp.dot(
            jnp.concatenate([block[here] for block in blocks], axis=1),
            weights,
            preferred_element_type=jnp.float32,
        )
        held[here] = total.astype(held.dtype)
        copy = pltpu.make_async_copy(
            held.at[pl.ds(k * step, step)], out_ref.at[pl.ds(k * step, step)], semaphores.at[k]
        )
        copy.start()
        copies.append(copy)
    for copy in copies:
        copy.wait()


def project_cost(rows, columns, depth):
    return pl.CostEstimate(
        flops=2 * rows * columns * depth, bytes_accessed=4 * rows * columns, transcendentals=0
    )


def project_early(place, out_weight, blocks, distances, aged):
    rows, columns = blocks[0].shape[0], out_weight.shape[1]
    return pl.pallas_call(
        partial(project_early_kernel, distances),
        out_shape=[
            jax.ShapeDtypeStruct((rows, columns), jnp.float32),
            jax.ShapeDtypeStruct(aged.shape, aged.dtype),
        ],
        in_specs=[pl.BlockSpec(memory_space=SMEM)]
        + [pl.BlockSpec(memory_space=VMEM)] * (1 + len(blocks))
        + [pl.BlockSpec(memory_space=pl.ANY)],
        out_specs=[pl.BlockSpec(memory_space=VMEM), pl.BlockSpec(memory_space=pl.ANY)],
        scratch_shapes=[pltpu.SemaphoreType.DMA],
        compiler_params=params(),
        cost_estimate=project_cost(rows, columns, blocks[0].shape[1] * len(blocks)),
        name="project_early",
    )(place, out_weight, *blocks, aged)


def project_late(place, out_weight, blocks, distances, total):
    rows, columns = total.shape
    return pl.pallas_call(
        partial(project_late_kernel, distances),
        out_shape=jax.ShapeDtypeStruct((rows, columns), jnp.bfloat16),
        in_specs=[pl.BlockSpec(memory_space=SMEM)]
        + [pl.BlockSpec(memory_space=VMEM)] * (2 + len(blocks)),
        out_specs=pl.BlockSpec(memory_space=pl.ANY),
        scratch_shapes=[VMEM((rows, columns), jnp.bfloat16), pltpu.SemaphoreType.DMA((4,))],
        compiler_params=params(),
        cost_estimate=project_cost(rows, columns, blocks[0].shape[1] * len(blocks)),
        name="project_late",
    )(place, out_weight, *blocks, total)


def after(array, *others):
    return lax.optimization_barrier((array, *others))[0]


def gather(mixed, slots, aged):
    half, top = slots // 2, slots - 2
    blocks = {0: mixed, top: exchange(mixed, "slot", top)}
    late = after(mixed, aged)
    blocks[2] = exchange(late, "slot", 2)
    blocks[1] = exchange(late, "slot", 1)
    for d in range(3, half):
        blocks[d] = exchange(blocks[d ^ 1] if d % 2 else late, "slot", 1 if d % 2 else d)
    for d in range(1, half):
        blocks[top ^ d] = exchange(blocks[top], "slot", d)
    return blocks


def local(queries, raw_clip, pool_weight, old_memory, valid_columns, out_weight):
    query_rows, model_width = queries.shape
    head_size = model_width // H
    slots = lax.axis_size("slot")
    spaces = lax.axis_size("space")
    columns = old_memory.shape[3]
    width = model_width // slots
    slot_index = lax.axis_index("slot")
    place = slot_index.astype(jnp.int32).reshape(1)
    half = slots // 2

    own_queries = lax.dynamic_slice_in_dim(queries, slot_index * width, width, axis=1)
    evens = range(2, spaces, 2)
    crossed = {e: exchange(own_queries, "space", e) for e in evens}
    near = jnp.concatenate([crossed[e] for e in evens] + [own_queries], axis=0)

    resident = old_memory.reshape(-1, old_memory.shape[-1])
    tokens = resident.shape[0]
    odd_far = tuple(range(half + 1, slots, 2))
    odd_near = tuple(range(1, half, 2))
    far_out, near_out, *kept = cut(
        place, resident, slots, (odd_far, odd_near) + tuple((d,) for d in range(0, slots, 2))
    )
    far_in = exchange(far_out, "slot", 1)
    near_in = exchange(near_out, "slot", 1)
    sources = {0: kept[0], 1: near_in[:tokens]}
    for d in list(range(half, slots, 2))[::-1]:
        row = (d - half) // 2 * tokens
        both = jnp.concatenate([kept[d // 2], far_in[row : row + tokens]], axis=0)
        both = exchange(both, "slot", d)
        sources[d], sources[d + 1] = both[:tokens], both[tokens:]
    far = exchange(near, "space", 1)
    behind = from_behind(edge(raw_clip), "space", 1)
    fresh, fresh_rows = pool(raw_clip, behind, pool_weight, head_size)
    for d in range(2, half, 2):
        row = d // 2 * tokens
        both = jnp.concatenate([kept[d // 2], near_in[row : row + tokens]], axis=0)
        both = exchange(after(both, fresh_rows), "slot", d)
        sources[d], sources[d + 1] = both[:tokens], both[tokens:]
    call = partial(
        attend,
        place,
        valid_columns,
        sources=[fresh_rows] + [sources[d] for d in range(slots)],
        tokens=tokens,
        distances=(None,) + tuple(range(slots)),
        columns=columns,
        head_size=head_size,
    )
    aged_memory = from_behind(after(old_memory, *sources.values()), "slot", 1)
    parts = []
    for k, e in enumerate(evens):
        rows = slice(k * query_rows, (k + 1) * query_rows)
        (part,) = call(queries=far[rows], travels=True)
        core_part = exchange(part, "space", 1)
        value, level = call(queries=near[rows], travels=False)
        part = merge(value, level, [(core_part, 0)], head_size, True)
        parts.append((exchange(part, "space", e), 0))
        sent_part = part
    (part,) = call(queries=after(far[len(evens) * query_rows :], sent_part), travels=True)
    parts.append((exchange(part, "space", 1), 0))
    value, level = call(queries=own_queries, travels=False, weight=4)
    mixed = merge(value, level, parts, head_size, False)

    blocks = gather(mixed, slots, aged_memory)
    first, second = tuple(range(half)), tuple(range(half, slots))
    total, aged_memory = project_early(
        place, out_weight, [blocks[d] for d in first], first, aged_memory
    )
    attended = project_late(place, out_weight, [blocks[d] for d in second], second, total)
    return (attended, fresh, aged_memory)


def solution(mesh):
    return jax.shard_map(
        local,
        mesh=mesh,
        in_specs=(
            P("space", None),
            P(None, "space", None, "slot"),
            P(None, "slot"),
            P("slot", None, "space", None, None),
            P(),
            P(),
        ),
        out_specs=(
            P("space", None),
            P(None, "space", None, "slot"),
            P("slot", None, "space", None, None),
        ),
        check_vma=False,
    )
```

time: 69.4 us -> 62.6 us (0.902)
  waiting for transfers between devices: 25 us -> 14.3 us
  starting transfers between devices: 25.3 us -> 28.8 us
  local copies, waits for them, and re-layouts: 2.1 us -> 3.41 us
  Pallas kernels: 15.9 us -> 14.9 us
    ppermute x18 -> x17, waiting for transfers between devices: 25 us -> 14.3 us  [exchange(): return lax.ppermute(block, axis, [(i, i ^ distance) for i in range(size)])]
    ppermute x18 -> x17, starting transfers between devices: 20.5 us -> 23.8 us  [exchange(): return lax.ppermute(block, axis, [(i, i ^ distance) for i in range(size)])]
    unnamed x12 -> x14, local copies, waits for them, and re-layouts: 2.05 us -> 3.31 us
    pallas_call x1, Pallas kernels: 1.11 us -> 0.17 us  [cut(): pl.pallas_call(partial(cut_kernel, width, groups), out_shape=[jax.ShapeDt...]
    pallas_call x5 -> x6, Pallas kernels: 5.15 us -> 4.81 us  [the longest x1 1.83 us: pool(): pl.pallas_call(partial(pool_kernel, head_size), out_shape=[jax.ShapeDtype...]
    pallas_call x3 -> x4, Pallas kernels: 9.62 us -> 9.89 us  [attend(): pl.pallas_call(partial(attend_kernel, head_size, columns, tokens, distanc...]
  transfers between devices with their start and end apart: 20 -> 19, of which waited for: 9 -> 7; matrix products, arithmetic and copies ran while one was open for 0% -> 0% of each run, Pallas kernels for 20% -> 21%
where the time goes in v5:
time: 62.6 us; the launch traced here: 62.3 us
  starting transfers between devices  28.8 us (46%)
  Pallas kernels  14.9 us (24%)
  waiting for transfers between devices  14.3 us (23%)
  local copies, waits for them, and re-layouts  3.41 us (5%)
  between operations  0.9 us (1%)
    ppermute x17, starting transfers between devices, exchange(): return lax.ppermute(block, axis, [(i, i ^ distance) for i in range(size)])  23.8 us
    ppermute x17, waiting for transfers between devices, exchange(): return lax.ppermute(block, axis, [(i, i ^ distance) for i in range(size)])  14.3 us
    pallas_call x4, Pallas kernels, attend(): pl.pallas_call(partial(attend_kernel, head_size, columns, tokens, distanc...  9.89 us
    ppermute x2, starting transfers between devices, from_behind(): lax.ppermute(block, axis, [(i - distance, i) for i in devices if i - dist...  4.94 us
    unnamed x14, local copies, waits for them, and re-layouts  3.31 us
    pallas_call x1, Pallas kernels, pool(): pl.pallas_call(partial(pool_kernel, head_size), out_shape=[jax.ShapeDtype...  1.83 us
    pallas_call x1, Pallas kernels, project_late(): pl.pallas_call(partial(project_late_kernel, distances), out_shape=jax.Sha...  1.51 us
  transfers between devices with their start and end apart: 19, of which 7 were waited for; matrix products, arithmetic and copies ran while one was open for 0% of the time, Pallas kernels for 21%

profile of v5, /device:TPU:0, one launch (start us, length us, event | category | flops | bytes accessed | tf_op | source)
XLA Modules:
  0.0 62.3 jit_solution(3405136538789925213)
XLA Ops:
  0.7 1.2 %copy-done = bf16[512,1024]{1,0:T(8,128)(2,1)S(1)} copy-done((bf16[512,1024]{1,0:T(8,128)(2,1)S(1)}, bf16[512,1024]{1,0:T(8,128)(2,1)}, u32[]{:S(2)}) %copy-start) | copy-done | bytes 1048600
  1.9 3.0 %collective-permute-start.6 = (bf16[512,128]{1,0:T(8,128)(2,1)S(1)}, bf16[512,128]{1,0:T(8,128)(2,1)S(1)}, u32[]{:S(2)}, u32[]{:S(2)}) collective-permute-start(bf16[512,128]{1,0:T(8,128)(2,1)S(1)} %constant_dynamic-slice_fusion.query_ref), channel_id=1, source_target_pairs={{0,2},{1,3},{2,0},{3,1},{4,6},{5,7},{6,4},{7,5},{8,10},{9,11},{10,... | collective-permute-start | bytes 393224 | tf_op jit(solution)/shard_map/ppermute | solution.py:28
  4.9 1.0 %copy-done.3 = bf16[1,4,1,32,2048]{4,3,2,1,0:T(8,128)(2,1)S(1)} copy-done((bf16[1,4,1,32,2048]{4,3,2,1,0:T(8,128)(2,1)S(1)}, bf16[1,4,1,32,2048]{4,3,2,1,0:T(8,128)(2,1)}, u32[]{:S(2)}) %copy-start.3) | copy-done | bytes 524312
  6.1 1.6 %collective-permute-start.3 = (bf16[256,256]{1,0:T(8,128)(2,1)S(1)}, bf16[256,256]{1,0:T(8,128)(2,1)S(1)}, u32[]{:S(2)}, u32[]{:S(2)}) collective-permute-start(bf16[256,256]{1,0:T(8,128)(2,1)S(1)} %get-tuple-element.27), channel_id=1, source_target_pairs={{0,4},{4,0},{8,12},{12,8},{16,20},{20,16},{24,28},{28,24},{1,5},{5... | collective-permute-start | bytes 393224 | tf_op jit(solution)/shard_map/ppermute | solution.py:28
  7.7 1.0 %copy-done.2 = bf16[8,2,64,256]{3,2,1,0:T(8,128)(2,1)S(1)} copy-done((bf16[8,2,64,256]{3,2,1,0:T(8,128)(2,1)S(1)}, bf16[8,2,64,256]{3,2,1,0:T(8,128)(2,1)}, u32[]{:S(2)}) %copy-start.2) | copy-done | bytes 524312
  8.8 1.4 %collective-permute-start = (bf16[8,1,64,256]{3,2,1,0:T(8,128)(2,1)S(1)}, bf16[8,1,64,256]{3,2,1,0:T(8,128)(2,1)S(1)}, u32[]{:S(2)}, u32[]{:S(2)}) collective-permute-start(bf16[8,1,64,256]{3,2,1,0:T(8,128)(2,1)S(1)} %edge.1), channel_id=1, source_target_pairs={{0,1},{1,2},{2,3},{4,5},{5,6},{6,7},{8,9},{9,10},{10,11},{12,13},{... | collective-permute-start | bytes 786440 | tf_op jit(solution)/shard_map/ppermute | solution.py:33
  11.7 2.9 %collective-permute-start.4 = (bf16[256,256]{1,0:T(8,128)(2,1)S(1)}, bf16[256,256]{1,0:T(8,128)(2,1)S(1)}, u32[]{:S(2)}, u32[]{:S(2)}) collective-permute-start(bf16[256,256]{1,0:T(8,128)(2,1)S(1)} %pad_maximum_fusion.2), channel_id=1, source_target_pairs={{0,16},{4,20},{8,24},{12,28},{16,0},{20,4},{24,8},{28,12},{1,17},{... | collective-permute-start | bytes 393224 | tf_op jit(solution)/shard_map/ppermute | solution.py:28
  14.6 1.4 %collective-permute-start.5 = (bf16[256,256]{1,0:T(8,128)(2,1)S(1)}, bf16[256,256]{1,0:T(8,128)(2,1)S(1)}, u32[]{:S(2)}, u32[]{:S(2)}) collective-permute-start(bf16[256,256]{1,0:T(8,128)(2,1)S(1)} %pad_maximum_fusion.3), channel_id=1, source_target_pairs={{0,24},{4,28},{8,16},{12,20},{16,8},{20,12},{24,0},{28,4},{1,25},{... | collective-permute-start | bytes 393224 | tf_op jit(solution)/shard_map/ppermute | solution.py:28
  16.5 1.8 %pool.1 = (bf16[4,1,32,256]{3,2,1,0:T(8,128)(2,1)}, bf16[128,256]{1,0:T(8,128)(2,1)S(1)}) custom-call(bf16[8,2,64,256]{3,2,1,0:T(8,128)(2,1)S(1)} %copy-done.2, bf16[8,1,64,256]{3,2,1,0:T(8,128)(2,1)S(1)} %collective-permute-done.halo_ref, bf16[27,256]{1,0:T(8,128)(2,1)S(1)} %copy-done.5), custom_call_target="tpu_custom_call" | custom-call | tf_op jit(solution)/shard_map/pool/pallas_call | solution.py:98
  18.3 1.6 %collective-permute-start.2 = (bf16[256,256]{1,0:T(8,128)(2,1)S(1)}, bf16[256,256]{1,0:T(8,128)(2,1)S(1)}, u32[]{:S(2)}, u32[]{:S(2)}) collective-permute-start(bf16[256,256]{1,0:T(8,128)(2,1)S(1)} %pad_maximum_fusion.1), channel_id=1, source_target_pairs={{0,8},{4,12},{8,0},{12,4},{16,24},{20,28},{24,16},{28,20},{1,9},{5... | collective-permute-start | bytes 393224 | tf_op jit(solution)/shard_map/ppermute | solution.py:28
  19.9 4.8 %collective-permute-done.4 = bf16[256,256]{1,0:T(8,128)(2,1)S(1)} collective-permute-done((bf16[256,256]{1,0:T(8,128)(2,1)S(1)}, bf16[256,256]{1,0:T(8,128)(2,1)S(1)}, u32[]{:S(2)}, u32[]{:S(2)}) %collective-permute-start.4) | collective-permute-done | bytes 131104 | tf_op jit(solution)/shard_map/ppermute | solution.py:28
  24.7 2.0 %collective-permute-done.2 = bf16[256,256]{1,0:T(8,128)(2,1)S(1)} collective-permute-done((bf16[256,256]{1,0:T(8,128)(2,1)S(1)}, bf16[256,256]{1,0:T(8,128)(2,1)S(1)}, u32[]{:S(2)}, u32[]{:S(2)}) %collective-permute-start.2) | collective-permute-done | bytes 131104 | tf_op jit(solution)/shard_map/ppermute | solution.py:28
  26.7 3.5 %collective-permute-start.15 = (bf16[1,4,1,32,2048]{4,3,2,1,0:T(8,128)(2,1)S(1)}, bf16[1,4,1,32,2048]{4,3,2,1,0:T(8,128)(2,1)S(1)}, u32[]{:S(2)}, u32[]{:S(2)}) collective-permute-start(bf16[1,4,1,32,2048]{4,3,2,1,0:T(8,128)(2,1)S(1)} %copy-done.4), channel_id=1, source_target_pairs={{0,4},{4,8},{8,12},{12,16},{16,20},{20,24},{24,28},{1,5},{5,9},{9,... | collective-permute-start | bytes 1572872 | tf_op jit(solution)/shard_map/ppermute | solution.py:33
  30.3 2.5 %attend.6 = bf16[544,128]{1,0:T(8,128)(2,1)S(1)} custom-call(s32[1]{0:T(128)} %bitcast.place_ref, s32[9]{0:T(128)S(1)} %copy-done.6, bf16[512,128]{1,0:T(8,128)(2,1)S(1)} %get-tuple-element.40.query_ref, bf16[128,256]{1,0:T(8,128)(2,1)S(1)} %get-tuple-element.21.refs_0_, bf16[128,256]{1,0:T(8,128)(2,1)S(1)} %get-tuple-element.22.refs_1_, ...), custom_call_target="tpu_custom_call" | custom-call | flops 603979776 | bytes 2228224 | tf_op jit(solution)/shard_map/attend/pallas_call | solution.py:256
  32.9 2.4 %attend.5 = (f32[512,128]{1,0:T(8,128)S(1)}, f32[512,128]{1,0:T(8,128)S(1)}) custom-call(s32[1]{0:T(128)} %bitcast.place_ref, s32[9]{0:T(128)S(1)} %copy-done.6, bf16[512,128]{1,0:T(8,128)(2,1)S(1)} %collective-permute-done.6.query_ref, bf16[128,256]{1,0:T(8,128)(2,1)S(1)} %get-tuple-element.21.refs_0_, bf16[128,256]{1,0:T(8,128)(2,1)S(1)} %get-tuple-element.22.refs_1_, ...), custom_call_target="tpu_custom_call" | custom-call | flops 603979776 | bytes 2228224 | tf_op jit(solution)/shard_map/attend/pallas_call | solution.py:256
  36.4 2.5 %attend.7 = bf16[544,128]{1,0:T(8,128)(2,1)S(1)} custom-call(s32[1]{0:T(128)} %bitcast.place_ref, s32[9]{0:T(128)S(1)} %copy-done.6, bf16[512,128]{1,0:T(8,128)(2,1)S(1)} %get-tuple-element.33.query_ref, bf16[128,256]{1,0:T(8,128)(2,1)S(1)} %get-tuple-element.21.refs_0_, bf16[128,256]{1,0:T(8,128)(2,1)S(1)} %get-tuple-element.22.refs_1_, ...), custom_call_target="tpu_custom_call" | custom-call | flops 603979776 | bytes 2228224 | tf_op jit(solution)/shard_map/attend/pallas_call | solution.py:256
  39.2 2.4 %attend.4 = (f32[512,128]{1,0:T(8,128)S(1)}, f32[512,128]{1,0:T(8,128)S(1)}) custom-call(s32[1]{0:T(128)} %bitcast.place_ref, s32[9]{0:T(128)S(1)} %copy-done.6, bf16[512,128]{1,0:T(8,128)(2,1)S(1)} %constant_dynamic-slice_fusion.query_ref, bf16[128,256]{1,0:T(8,128)(2,1)S(1)} %get-tuple-element.21.refs_0_, bf16[128,256]{1,0:T(8,128)(2,1)S(1)} %get-tuple-element.22.refs_1_, ...), custom_call_target="tpu_custom_call" | custom-call | flops 2415919104 | bytes 2228224 | tf_op jit(solution)/shard_map/attend/pallas_call | solution.py:256
  42.1 2.0 %collective-permute-start.17 = (bf16[512,128]{1,0:T(8,128)(2,1)S(1)}, bf16[512,128]{1,0:T(8,128)(2,1)S(1)}, u32[]{:S(2)}, u32[]{:S(2)}) collective-permute-start(bf16[512,128]{1,0:T(8,128)(2,1)S(1)} %merge.3.refs_0_), channel_id=1, source_target_pairs={{0,8},{4,12},{8,0},{12,4},{16,24},{20,28},{24,16},{28,20},{1,9},{5... | collective-permute-start | bytes 393224 | tf_op jit(solution)/shard_map/ppermute | solution.py:28
  44.2 3.4 %collective-permute-start.11 = (bf16[512,128]{1,0:T(8,128)(2,1)S(1)}, bf16[512,128]{1,0:T(8,128)(2,1)S(1)}, u32[]{:S(2)}, u32[]{:S(2)}) collective-permute-start(bf16[512,128]{1,0:T(8,128)(2,1)S(1)} %merge.3.refs_0_), channel_id=1, source_target_pairs={{0,24},{4,28},{8,16},{12,20},{16,8},{20,12},{24,0},{28,4},{1,25},{... | collective-permute-start | bytes 393224 | tf_op jit(solution)/shard_map/ppermute | solution.py:28
  48.2 1.4 %collective-permute-start.18 = (bf16[512,128]{1,0:T(8,128)(2,1)S(1)}, bf16[512,128]{1,0:T(8,128)(2,1)S(1)}, u32[]{:S(2)}, u32[]{:S(2)}) collective-permute-start(bf16[512,128]{1,0:T(8,128)(2,1)S(1)} %collective-permute-done.17.refs_2_), channel_id=1, source_target_pairs={{0,4},{4,0},{8,12},{12,8},{16,20},{20,16},{24,28},{28,24},{1,5},{5... | collective-permute-start | bytes 393224 | tf_op jit(solution)/shard_map/ppermute | solution.py:28
  49.6 3.4 %collective-permute-done.11.refs_2_ = bf16[512,128]{1,0:T(8,128)(2,1)S(1)} collective-permute-done((bf16[512,128]{1,0:T(8,128)(2,1)S(1)}, bf16[512,128]{1,0:T(8,128)(2,1)S(1)}, u32[]{:S(2)}, u32[]{:S(2)}) %collective-permute-start.11) | collective-permute-done | bytes 131104 | tf_op jit(solution)/shard_map/ppermute | solution.py:28
  54.2 2.2 %collective-permute-start.12 = (bf16[512,128]{1,0:T(8,128)(2,1)S(1)}, bf16[512,128]{1,0:T(8,128)(2,1)S(1)}, u32[]{:S(2)}, u32[]{:S(2)}) collective-permute-start(bf16[512,128]{1,0:T(8,128)(2,1)S(1)} %collective-permute-done.11.refs_2_), channel_id=1, source_target_pairs={{0,8},{4,12},{8,0},{12,4},{16,24},{20,28},{24,16},{28,20},{1,9},{5... | collective-permute-start | bytes 393224 | tf_op jit(solution)/shard_map/ppermute | solution.py:28
  57.2 2.7 %collective-permute-done.14.refs_3_ = bf16[512,128]{1,0:T(8,128)(2,1)S(1)} collective-permute-done((bf16[512,128]{1,0:T(8,128)(2,1)S(1)}, bf16[512,128]{1,0:T(8,128)(2,1)S(1)}, u32[]{:S(2)}, u32[]{:S(2)}) %collective-permute-start.14) | collective-permute-done | bytes 131104 | tf_op jit(solution)/shard_map/ppermute | solution.py:28
  60.8 1.5 %project_late.1 = bf16[512,1024]{1,0:T(8,128)(2,1)} custom-call(s32[1]{0:T(128)} %bitcast.place_ref, bf16[1024,1024]{1,0:T(8,128)(2,1)S(1)} %copy-done.1, bf16[512,128]{1,0:T(8,128)(2,1)S(1)} %collective-permute-done.12.refs_0_, bf16[512,128]{1,0:T(8,128)(2,1)S(1)} %collective-permute-done.13.refs_1_, bf16[512,128]{1,0:T(8,128)(2,1)S(1)} %collective-permute-done.11.refs_2_, ...), custom_call_target="tpu_custom_call" | custom-call | flops 536870912 | bytes 2097152 | tf_op jit(solution)/shard_map/project_late/pallas_call | solution.py:388
  (50 shorter events, 7.6 us)
Async XLA Ops:
  0.6 1.2 %copy-start = (bf16[512,1024]{1,0:T(8,128)(2,1)S(1)}, bf16[512,1024]{1,0:T(8,128)(2,1)}, u32[]{:S(2)}) copy-start(bf16[512,1024]{1,0:T(8,128)(2,1)} %param.6) | copy-start | bytes 3145732
  0.6 15.8 %copy-start.5 = (bf16[27,256]{1,0:T(8,128)(2,1)S(1)}, bf16[27,256]{1,0:T(8,128)(2,1)}, u32[]{:S(2)}) copy-start(bf16[27,256]{1,0:T(8,128)(2,1)} %weight_ref.3) | copy-start | bytes 41476
  1.9 8.9 %collective-permute-start.6 = (bf16[512,128]{1,0:T(8,128)(2,1)S(1)}, bf16[512,128]{1,0:T(8,128)(2,1)S(1)}, u32[]{:S(2)}, u32[]{:S(2)}) collective-permute-start(bf16[512,128]{1,0:T(8,128)(2,1)S(1)} %constant_dynamic-slice_fusion.query_ref), channel_id=1, source_target_pairs={{0,2},{1,3},{2,0},{3,1},{4,6},{5,7},{6,4},{7,5},{8,10},{9,11},{10,... | collective-permute-start | bytes 393224 | tf_op jit(solution)/shard_map/ppermute | solution.py:28
  6.1 5.6 %collective-permute-start.3 = (bf16[256,256]{1,0:T(8,128)(2,1)S(1)}, bf16[256,256]{1,0:T(8,128)(2,1)S(1)}, u32[]{:S(2)}, u32[]{:S(2)}) collective-permute-start(bf16[256,256]{1,0:T(8,128)(2,1)S(1)} %get-tuple-element.27), channel_id=1, source_target_pairs={{0,4},{4,0},{8,12},{12,8},{16,20},{20,16},{24,28},{28,24},{1,5},{5... | collective-permute-start | bytes 393224 | tf_op jit(solution)/shard_map/ppermute | solution.py:28
  8.8 18.0 %copy-start.4 = (bf16[1,4,1,32,2048]{4,3,2,1,0:T(8,128)(2,1)S(1)}, bf16[1,4,1,32,2048]{4,3,2,1,0:T(8,128)(2,1)}, u32[]{:S(2)}) copy-start(bf16[1,4,1,32,2048]{4,3,2,1,0:T(8,128)(2,1)} %param.9) | copy-start | bytes 1572868
  8.8 21.5 %copy-start.6 = (s32[9]{0:T(128)S(1)}, s32[9]{0:T(128)}, u32[]{:S(2)}) copy-start(s32[9]{0:T(128)} %valid_ref.7) | copy-start | bytes 112
  8.8 7.6 %collective-permute-start = (bf16[8,1,64,256]{3,2,1,0:T(8,128)(2,1)S(1)}, bf16[8,1,64,256]{3,2,1,0:T(8,128)(2,1)S(1)}, u32[]{:S(2)}, u32[]{:S(2)}) collective-permute-start(bf16[8,1,64,256]{3,2,1,0:T(8,128)(2,1)S(1)} %edge.1), channel_id=1, source_target_pairs={{0,1},{1,2},{2,3},{4,5},{5,6},{6,7},{8,9},{9,10},{10,11},{12,13},{... | collective-permute-start | bytes 786440 | tf_op jit(solution)/shard_map/ppermute | solution.py:33
  10.3 6.2 %collective-permute-start.1 = (bf16[256,256]{1,0:T(8,128)(2,1)S(1)}, bf16[256,256]{1,0:T(8,128)(2,1)S(1)}, u32[]{:S(2)}, u32[]{:S(2)}) collective-permute-start(bf16[256,256]{1,0:T(8,128)(2,1)S(1)} %get-tuple-element.23), channel_id=1, source_target_pairs={{0,4},{4,0},{8,12},{12,8},{16,20},{20,16},{24,28},{28,24},{1,5},{5... | collective-permute-start | bytes 393224 | tf_op jit(solution)/shard_map/ppermute | solution.py:28
  10.8 19.4 %collective-permute-start.7 = (bf16[1024,128]{1,0:T(8,128)(2,1)S(1)}, bf16[1024,128]{1,0:T(8,128)(2,1)S(1)}, u32[]{:S(2)}, u32[]{:S(2)}) collective-permute-start(bf16[1024,128]{1,0:T(8,128)(2,1)S(1)} %pad_maximum_fusion), channel_id=1, source_target_pairs={{0,1},{1,0},{2,3},{3,2},{4,5},{5,4},{6,7},{7,6},{8,9},{9,8},{10,11... | collective-permute-start | bytes 786440 | tf_op jit(solution)/shard_map/ppermute | solution.py:28
  11.7 13.0 %collective-permute-start.4 = (bf16[256,256]{1,0:T(8,128)(2,1)S(1)}, bf16[256,256]{1,0:T(8,128)(2,1)S(1)}, u32[]{:S(2)}, u32[]{:S(2)}) collective-permute-start(bf16[256,256]{1,0:T(8,128)(2,1)S(1)} %pad_maximum_fusion.2), channel_id=1, source_target_pairs={{0,16},{4,20},{8,24},{12,28},{16,0},{20,4},{24,8},{28,12},{1,17},{... | collective-permute-start | bytes 393224 | tf_op jit(solution)/shard_map/ppermute | solution.py:28
  14.6 10.1 %collective-permute-start.5 = (bf16[256,256]{1,0:T(8,128)(2,1)S(1)}, bf16[256,256]{1,0:T(8,128)(2,1)S(1)}, u32[]{:S(2)}, u32[]{:S(2)}) collective-permute-start(bf16[256,256]{1,0:T(8,128)(2,1)S(1)} %pad_maximum_fusion.3), channel_id=1, source_target_pairs={{0,24},{4,28},{8,16},{12,20},{16,8},{20,12},{24,0},{28,4},{1,25},{... | collective-permute-start | bytes 393224 | tf_op jit(solution)/shard_map/ppermute | solution.py:28
  18.3 8.4 %collective-permute-start.2 = (bf16[256,256]{1,0:T(8,128)(2,1)S(1)}, bf16[256,256]{1,0:T(8,128)(2,1)S(1)}, u32[]{:S(2)}, u32[]{:S(2)}) collective-permute-start(bf16[256,256]{1,0:T(8,128)(2,1)S(1)} %pad_maximum_fusion.1), channel_id=1, source_target_pairs={{0,8},{4,12},{8,0},{12,4},{16,24},{20,28},{24,16},{28,20},{1,9},{5... | collective-permute-start | bytes 393224 | tf_op jit(solution)/shard_map/ppermute | solution.py:28
  26.7 15.4 %collective-permute-start.15 = (bf16[1,4,1,32,2048]{4,3,2,1,0:T(8,128)(2,1)S(1)}, bf16[1,4,1,32,2048]{4,3,2,1,0:T(8,128)(2,1)S(1)}, u32[]{:S(2)}, u32[]{:S(2)}) collective-permute-start(bf16[1,4,1,32,2048]{4,3,2,1,0:T(8,128)(2,1)S(1)} %copy-done.4), channel_id=1, source_target_pairs={{0,4},{4,8},{8,12},{12,16},{16,20},{20,24},{24,28},{1,5},{5,9},{9,... | collective-permute-start | bytes 1572872 | tf_op jit(solution)/shard_map/ppermute | solution.py:33
  32.8 2.5 %collective-permute-start.8 = (bf16[544,128]{1,0:T(8,128)(2,1)S(1)}, bf16[544,128]{1,0:T(8,128)(2,1)S(1)}, u32[]{:S(2)}, u32[]{:S(2)}) collective-permute-start(bf16[544,128]{1,0:T(8,128)(2,1)S(1)} %attend.6), channel_id=1, source_target_pairs={{0,1},{1,0},{2,3},{3,2},{4,5},{5,4},{6,7},{7,6},{8,9},{9,8},{10,11... | collective-permute-start | bytes 417800 | tf_op jit(solution)/shard_map/ppermute | solution.py:28
  35.6 6.1 %collective-permute-start.9 = (bf16[544,128]{1,0:T(8,128)(2,1)S(1)}, bf16[544,128]{1,0:T(8,128)(2,1)S(1)}, u32[]{:S(2)}, u32[]{:S(2)}) collective-permute-start(bf16[544,128]{1,0:T(8,128)(2,1)S(1)} %merge.2), channel_id=1, source_target_pairs={{0,2},{1,3},{2,0},{3,1},{4,6},{5,7},{6,4},{7,5},{8,10},{9,11},{10,... | collective-permute-start | bytes 417800 | tf_op jit(solution)/shard_map/ppermute | solution.py:28
  38.9 2.7 %collective-permute-start.10 = (bf16[544,128]{1,0:T(8,128)(2,1)S(1)}, bf16[544,128]{1,0:T(8,128)(2,1)S(1)}, u32[]{:S(2)}, u32[]{:S(2)}) collective-permute-start(bf16[544,128]{1,0:T(8,128)(2,1)S(1)} %attend.7), channel_id=1, source_target_pairs={{0,1},{1,0},{2,3},{3,2},{4,5},{5,4},{6,7},{7,6},{8,9},{9,8},{10,11... | collective-permute-start | bytes 417800 | tf_op jit(solution)/shard_map/ppermute | solution.py:28
  39.2 17.2 %copy-start.1 = (bf16[1024,1024]{1,0:T(8,128)(2,1)S(1)}, bf16[1024,1024]{1,0:T(8,128)(2,1)}, u32[]{:S(2)}) copy-start(bf16[1024,1024]{1,0:T(8,128)(2,1)} %weight_ref.5) | copy-start | bytes 6291460
  42.1 6.0 %collective-permute-start.17 = (bf16[512,128]{1,0:T(8,128)(2,1)S(1)}, bf16[512,128]{1,0:T(8,128)(2,1)S(1)}, u32[]{:S(2)}, u32[]{:S(2)}) collective-permute-start(bf16[512,128]{1,0:T(8,128)(2,1)S(1)} %merge.3.refs_0_), channel_id=1, source_target_pairs={{0,8},{4,12},{8,0},{12,4},{16,24},{20,28},{24,16},{28,20},{1,9},{5... | collective-permute-start | bytes 393224 | tf_op jit(solution)/shard_map/ppermute | solution.py:28
  44.2 8.8 %collective-permute-start.11 = (bf16[512,128]{1,0:T(8,128)(2,1)S(1)}, bf16[512,128]{1,0:T(8,128)(2,1)S(1)}, u32[]{:S(2)}, u32[]{:S(2)}) collective-permute-start(bf16[512,128]{1,0:T(8,128)(2,1)S(1)} %merge.3.refs_0_), channel_id=1, source_target_pairs={{0,24},{4,28},{8,16},{12,20},{16,8},{20,12},{24,0},{28,4},{1,25},{... | collective-permute-start | bytes 393224 | tf_op jit(solution)/shard_map/ppermute | solution.py:28
  47.5 8.9 %collective-permute-start.16 = (bf16[512,128]{1,0:T(8,128)(2,1)S(1)}, bf16[512,128]{1,0:T(8,128)(2,1)S(1)}, u32[]{:S(2)}, u32[]{:S(2)}) collective-permute-start(bf16[512,128]{1,0:T(8,128)(2,1)S(1)} %merge.3.refs_0_), channel_id=1, source_target_pairs={{0,4},{4,0},{8,12},{12,8},{16,20},{20,16},{24,28},{28,24},{1,5},{5... | collective-permute-start | bytes 393224 | tf_op jit(solution)/shard_map/ppermute | solution.py:28
  48.2 8.3 %collective-permute-start.18 = (bf16[512,128]{1,0:T(8,128)(2,1)S(1)}, bf16[512,128]{1,0:T(8,128)(2,1)S(1)}, u32[]{:S(2)}, u32[]{:S(2)}) collective-permute-start(bf16[512,128]{1,0:T(8,128)(2,1)S(1)} %collective-permute-done.17.refs_2_), channel_id=1, source_target_pairs={{0,4},{4,0},{8,12},{12,8},{16,20},{20,16},{24,28},{28,24},{1,5},{5... | collective-permute-start | bytes 393224 | tf_op jit(solution)/shard_map/ppermute | solution.py:28
  52.9 7.1 %collective-permute-start.14 = (bf16[512,128]{1,0:T(8,128)(2,1)S(1)}, bf16[512,128]{1,0:T(8,128)(2,1)S(1)}, u32[]{:S(2)}, u32[]{:S(2)}) collective-permute-start(bf16[512,128]{1,0:T(8,128)(2,1)S(1)} %collective-permute-done.11.refs_2_), channel_id=1, source_target_pairs={{0,4},{4,0},{8,12},{12,8},{16,20},{20,16},{24,28},{28,24},{1,5},{5... | collective-permute-start | bytes 393224 | tf_op jit(solution)/shard_map/ppermute | solution.py:28
  53.9 6.0 %collective-permute-start.13 = (bf16[512,128]{1,0:T(8,128)(2,1)S(1)}, bf16[512,128]{1,0:T(8,128)(2,1)S(1)}, u32[]{:S(2)}, u32[]{:S(2)}) collective-permute-start(bf16[512,128]{1,0:T(8,128)(2,1)S(1)} %collective-permute-done.11.refs_2_), channel_id=1, source_target_pairs={{0,12},{4,8},{8,4},{12,0},{16,28},{20,24},{24,20},{28,16},{1,13},{... | collective-permute-start | bytes 393224 | tf_op jit(solution)/shard_map/ppermute | solution.py:28
  54.2 6.6 %collective-permute-start.12 = (bf16[512,128]{1,0:T(8,128)(2,1)S(1)}, bf16[512,128]{1,0:T(8,128)(2,1)S(1)}, u32[]{:S(2)}, u32[]{:S(2)}) collective-permute-start(bf16[512,128]{1,0:T(8,128)(2,1)S(1)} %collective-permute-done.11.refs_2_), channel_id=1, source_target_pairs={{0,8},{4,12},{8,0},{12,4},{16,24},{20,28},{24,16},{28,20},{1,9},{5... | collective-permute-start | bytes 393224 | tf_op jit(solution)/shard_map/ppermute | solution.py:28
  (2 other events, 2.1 us)

commit v6 on v5

--- a/solution.py
+++ b/solution.py
@@ -142,21 +142,34 @@
     )(place, memory)
 
 
+def mask_kernel(columns, tokens, distances, place_ref, valid_ref, out_ref):
+    place = place_ref[0]
+    column = lanes_of((out_ref.shape[0], tokens)) % columns
+    for k, distance in enumerate(distances):
+        valid = valid_ref[0] if distance is None else valid_ref[1 + (place ^ distance)]
+        bias = jnp.where(column < valid, 0.0, MASKED)
+        out_ref[:, k * tokens : (k + 1) * tokens] = bias
+
+
+def mask(place, valid, columns, tokens, distances):
+    return pl.pallas_call(
+        partial(mask_kernel, columns, tokens, distances),
+        out_shape=jax.ShapeDtypeStruct((8, tokens * len(distances)), jnp.float32),
+        in_specs=[pl.BlockSpec(memory_space=SMEM)] * 2,
+        out_specs=pl.BlockSpec(memory_space=VMEM),
+        compiler_params=params(),
+        name="mask",
+    )(place, valid)
+
+
 def attend_kernel(
-    head_size, columns, tokens, distances, travels, place_ref, valid_ref, query_ref, *refs
+    head_size, travels, bias_ref, query_ref, *refs
 ):
     outs = 1 if travels else 2
     sources, out_refs = refs[:-outs], refs[-outs:]
     rows, width = query_ref.shape
     heads = width // head_size
     wide = 2 * head_size
-    place = place_ref[0]
-    biases = []
-    column = lanes_of((1, tokens)) % columns
-    for distance in distances:
-        valid = valid_ref[0] if distance is None else valid_ref[1 + (place ^ distance)]
-        biases.append(jnp.where(column < valid, 0.0, MASKED))
-    bias = jnp.concatenate(biases, axis=1)
     lane = lanes_of((rows, wide))
     queries = query_ref[...].astype(jnp.float32) * head_size ** (-0.5)
     memory, scores = [], []
@@ -171,30 +184,28 @@
         product = lax.dot_general(
             own, memory[h], (((1,), (1,)), ((), ())), preferred_element_type=jnp.float32
         )
-        scores.append(product + bias)
+        scores.append(product + bias_ref[:1])
     weights, peaks = [], []
     for h in range(heads):
         peaks.append(jnp.max(scores[h], axis=1, keepdims=True))
         weights.append(jnp.exp(scores[h] - peaks[h]).astype(jnp.bfloat16))
-    values, levels = [], []
+    totals = []
     memory_lane = lanes_of(memory[0].shape)
     for h in range(heads):
         ones_and_values = jnp.where(memory_lane < head_size, 1.0, memory[h].astype(jnp.float32))
         total = jnp.dot(
             weights[h], ones_and_values.astype(jnp.bfloat16), preferred_element_type=jnp.float32
         )
-        turned = pltpu.roll(total, head_size, 1)
-        if h % 2:
-            values.append(total / turned)
-            levels.append(jnp.log(turned) + peaks[h])
-        else:
-            values.append(turned / total)
-            levels.append(jnp.log(total) + peaks[h])
+        totals.append(total)
     if heads == 1:
-        value, level = values[0][:, :head_size], levels[0]
+        turned = pltpu.roll(totals[0], head_size, 1)
+        value = (turned / totals[0])[:, :head_size]
+        level = jnp.log(totals[0]) + peaks[0]
     else:
-        value = jnp.where(lane < head_size, *values)
-        level = jnp.where(lane < head_size, *levels)
+        first = lane < head_size
+        sums = jnp.where(first, totals[0], pltpu.roll(totals[1], head_size, 1))
+        value = jnp.where(first, pltpu.roll(totals[0], head_size, 1), totals[1]) / sums
+        level = jnp.log(sums) + jnp.where(first, peaks[0], peaks[1])
     if travels:
         pack(out_refs[0], value, level, head_size)
     else:
@@ -239,7 +250,7 @@
 
 
 def attend(
-    place, valid, queries, sources, tokens, distances, columns, head_size, travels, weight=1
+    bias, queries, sources, head_size, travels, weight=1
 ):
     rows, width = queries.shape
     heads = width // head_size
@@ -254,12 +265,11 @@
         out_shape = [jax.ShapeDtypeStruct((rows, width), jnp.float32)] * 2
         out_specs = [pl.BlockSpec((block, width), lambda i: (i, 0))] * 2
     return pl.pallas_call(
-        partial(attend_kernel, head_size, columns, tokens, distances, travels),
+        partial(attend_kernel, head_size, travels),
         grid=(rows // block,),
         out_shape=out_shape,
         in_specs=[
-            pl.BlockSpec(memory_space=SMEM),
-            pl.BlockSpec(memory_space=SMEM),
+            pl.BlockSpec(memory_space=VMEM),
             pl.BlockSpec((block, width), lambda i: (i, 0)),
         ]
         + [pl.BlockSpec(memory_space=VMEM)] * len(sources),
@@ -271,7 +281,7 @@
             transcendentals=rows * key_count * heads,
         ),
         name="attend",
-    )(place, valid, queries, *sources)
+    )(bias, queries, *sources)
 
 
 def merge_kernel(head_size, travels, value_ref, level_ref, *refs):
@@ -318,26 +328,53 @@
     )(value, level, *[part for part, _ in parts])
 
 
-def weight_rows(weight_ref, place, distances, width):
-    starts = [pl.multiple_of((place ^ d) * width, width) for d in distances]
-    return jnp.concatenate([weight_ref[pl.ds(start, width), :] for start in starts], axis=0)
-
-
-def project_early_kernel(distances, place_ref, weight_ref, *refs):
+def arrange_kernel(place_ref, weight_ref, early_ref, late_ref, semaphores):
+    place = place_ref[0]
+    count = semaphores.shape[0]
+    width = weight_ref.shape[0] // count
+    half = count // 2
+    copies = []
+    for distance in range(count):
+        start = pl.multiple_of((place ^ distance) * width, width)
+        out_ref = early_ref if distance < half else late_ref
+        copy = pltpu.make_async_copy(
+            weight_ref.at[pl.ds(start, width)],
+            out_ref.at[pl.ds(distance % half * width, width)],
+            semaphores.at[distance],
+        )
+        copy.start()
+        copies.append(copy)
+    for copy in copies:
+        copy.wait()
+
+
+def arrange(place, out_weight, count):
+    depth, columns = out_weight.shape
+    return pl.pallas_call(
+        arrange_kernel,
+        out_shape=[jax.ShapeDtypeStruct((depth // 2, columns), out_weight.dtype)] * 2,
+        in_specs=[pl.BlockSpec(memory_space=SMEM), pl.BlockSpec(memory_space=pl.ANY)],
+        out_specs=[pl.BlockSpec(memory_space=VMEM)] * 2,
+        scratch_shapes=[pltpu.SemaphoreType.DMA((count,))],
+        compiler_params=params(),
+        name="arrange",
+    )(place, out_weight)
+
+
+def project_early_kernel(weight_ref, *refs):
     blocks, (aged_ref, out_ref, aged_out, semaphore) = refs[:-4], refs[-4:]
     copy = pltpu.make_async_copy(aged_ref, aged_out, semaphore)
     copy.start()
     out_ref[...] = jnp.dot(
         jnp.concatenate([block[...] for block in blocks], axis=1),
-        weight_rows(weight_ref, place_ref[0], distances, blocks[0].shape[1]),
+        weight_ref[...],
         preferred_element_type=jnp.float32,
     )
     copy.wait()
 
 
-def project_late_kernel(distances, place_ref, weight_ref, *refs):
+def project_late_kernel(weight_ref, *refs):
     blocks, (total_ref, out_ref, held, semaphores) = refs[:-4], refs[-4:]
-    weights = weight_rows(weight_ref, place_ref[0], distances, blocks[0].shape[1])
     rows = total_ref.shape[0]
     step = rows // semaphores.shape[0]
     copies = []
@@ -345,7 +382,7 @@
         here = slice(k * step, (k + 1) * step)
         total = total_ref[here] + jnp.dot(
             jnp.concatenate([block[here] for block in blocks], axis=1),
-            weights,
+            weight_ref[...],
             preferred_element_type=jnp.float32,
         )
         held[here] = total.astype(held.dtype)
@@ -364,38 +401,36 @@
     )
 
 
-def project_early(place, out_weight, blocks, distances, aged):
+def project_early(out_weight, blocks, aged):
     rows, columns = blocks[0].shape[0], out_weight.shape[1]
     return pl.pallas_call(
-        partial(project_early_kernel, distances),
+        project_early_kernel,
         out_shape=[
             jax.ShapeDtypeStruct((rows, columns), jnp.float32),
             jax.ShapeDtypeStruct(aged.shape, aged.dtype),
         ],
-        in_specs=[pl.BlockSpec(memory_space=SMEM)]
-        + [pl.BlockSpec(memory_space=VMEM)] * (1 + len(blocks))
+        in_specs=[pl.BlockSpec(memory_space=VMEM)] * (1 + len(blocks))
         + [pl.BlockSpec(memory_space=pl.ANY)],
         out_specs=[pl.BlockSpec(memory_space=VMEM), pl.BlockSpec(memory_space=pl.ANY)],
         scratch_shapes=[pltpu.SemaphoreType.DMA],
         compiler_params=params(),
         cost_estimate=project_cost(rows, columns, blocks[0].shape[1] * len(blocks)),
         name="project_early",
-    )(place, out_weight, *blocks, aged)
-
-
-def project_late(place, out_weight, blocks, distances, total):
+    )(out_weight, *blocks, aged)
+
+
+def project_late(out_weight, blocks, total):
     rows, columns = total.shape
     return pl.pallas_call(
-        partial(project_late_kernel, distances),
+        project_late_kernel,
         out_shape=jax.ShapeDtypeStruct((rows, columns), jnp.bfloat16),
-        in_specs=[pl.BlockSpec(memory_space=SMEM)]
-        + [pl.BlockSpec(memory_space=VMEM)] * (2 + len(blocks)),
+        in_specs=[pl.BlockSpec(memory_space=VMEM)] * (2 + len(blocks)),
         out_specs=pl.BlockSpec(memory_space=pl.ANY),
         scratch_shapes=[VMEM((rows, columns), jnp.bfloat16), pltpu.SemaphoreType.DMA((4,))],
         compiler_params=params(),
         cost_estimate=project_cost(rows, columns, blocks[0].shape[1] * len(blocks)),
         name="project_late",
-    )(place, out_weight, *blocks, total)
+    )(out_weight, *blocks, total)
 
 
 def after(array, *others):
@@ -409,7 +444,7 @@
     blocks[2] = exchange(late, "slot", 2)
     blocks[1] = exchange(late, "slot", 1)
     for d in range(3, half):
-        blocks[d] = exchange(blocks[d ^ 1] if d % 2 else late, "slot", 1 if d % 2 else d)
+        blocks[d] = exchange(late, "slot", d)
     for d in range(1, half):
         blocks[top ^ d] = exchange(blocks[top], "slot", d)
     return blocks
@@ -439,32 +474,30 @@
         place, resident, slots, (odd_far, odd_near) + tuple((d,) for d in range(0, slots, 2))
     )
     far_in = exchange(far_out, "slot", 1)
-    near_in = exchange(near_out, "slot", 1)
+    near_in = exchange(after(near_out, far_in), "slot", 1)
     sources = {0: kept[0], 1: near_in[:tokens]}
     for d in list(range(half, slots, 2))[::-1]:
         row = (d - half) // 2 * tokens
         both = jnp.concatenate([kept[d // 2], far_in[row : row + tokens]], axis=0)
         both = exchange(both, "slot", d)
         sources[d], sources[d + 1] = both[:tokens], both[tokens:]
-    far = exchange(near, "space", 1)
-    behind = from_behind(edge(raw_clip), "space", 1)
+    behind = from_behind(edge(after(raw_clip, near_in)), "space", 1)
     fresh, fresh_rows = pool(raw_clip, behind, pool_weight, head_size)
     for d in range(2, half, 2):
         row = d // 2 * tokens
         both = jnp.concatenate([kept[d // 2], near_in[row : row + tokens]], axis=0)
-        both = exchange(after(both, fresh_rows), "slot", d)
+        both = exchange(both, "slot", d)
         sources[d], sources[d + 1] = both[:tokens], both[tokens:]
+    order = (None,) + tuple(range(slots))
+    bias = mask(place, after(valid_columns, fresh_rows), columns, tokens, order)
+    far = exchange(after(near, bias), "space", 1)
+    aged_memory = from_behind(after(old_memory, *sources.values(), bias), "slot", 1)
     call = partial(
         attend,
-        place,
-        valid_columns,
+        bias,
         sources=[fresh_rows] + [sources[d] for d in range(slots)],
-        tokens=tokens,
-        distances=(None,) + tuple(range(slots)),
-        columns=columns,
         head_size=head_size,
     )
-    aged_memory = from_behind(after(old_memory, *sources.values()), "slot", 1)
     parts = []
     for k, e in enumerate(evens):
         rows = slice(k * query_rows, (k + 1) * query_rows)
@@ -480,11 +513,9 @@
     mixed = merge(value, level, parts, head_size, False)
 
     blocks = gather(mixed, slots, aged_memory)
-    first, second = tuple(range(half)), tuple(range(half, slots))
-    total, aged_memory = project_early(
-        place, out_weight, [blocks[d] for d in first], first, aged_memory
-    )
-    attended = project_late(place, out_weight, [blocks[d] for d in second], second, total)
+    early_weight, late_weight = arrange(place, out_weight, slots)
+    total, aged_memory = project_early(early_weight, [blocks[d] for d in range(half)], aged_memory)
+    attended = project_late(late_weight, [blocks[d] for d in range(half, slots)], total)
     return (attended, fresh, aged_memory)
 
 

time: 62.6 us -> 59.6 us (0.952)
  starting transfers between devices: 28.8 us -> 32.8 us
  waiting for transfers between devices: 14.3 us -> 10.8 us
  local copies, waits for them, and re-layouts: 3.41 us -> 1.29 us
  Pallas kernels: 14.9 us -> 13.4 us
    ppermute x17, starting transfers between devices: 23.8 us -> 28.5 us  [exchange(): return lax.ppermute(block, axis, [(i, i ^ distance) for i in range(size)])]
    ppermute x17, waiting for transfers between devices: 14.3 us -> 10.8 us  [exchange(): return lax.ppermute(block, axis, [(i, i ^ distance) for i in range(size)])]
    unnamed x14, local copies, waits for them, and re-layouts: 3.31 us -> 1.18 us
    pallas_call x6 -> x8, Pallas kernels: 12.2 us -> 10.7 us  [the longest x4 7.62 us: attend(): pl.pallas_call(partial(attend_kernel, head_size, travels), grid=(rows //...]
    ppermute x2, starting transfers between devices: 4.94 us -> 4.3 us  [from_behind(): lax.ppermute(block, axis, [(i - distance, i) for i in devices if i - dist...]
  transfers between devices with their start and end apart: 19 -> 19, of which waited for: 7 -> 8; matrix products, arithmetic and copies ran while one was open for 0% -> 0% of each run, Pallas kernels for 21% -> 20%
where the time goes in v6:
time: 59.6 us; the launch traced here: 59.3 us
  starting transfers between devices  32.8 us (55%)
  Pallas kernels  13.4 us (22%)
  waiting for transfers between devices  10.8 us (18%)
  local copies, waits for them, and re-layouts  1.29 us (2%)
  between operations  0.94 us (2%)
    ppermute x17, starting transfers between devices, exchange(): return lax.ppermute(block, axis, [(i, i ^ distance) for i in range(size)])  28.5 us
    ppermute x17, waiting for transfers between devices, exchange(): return lax.ppermute(block, axis, [(i, i ^ distance) for i in range(size)])  10.8 us
    pallas_call x4, Pallas kernels, attend(): pl.pallas_call(partial(attend_kernel, head_size, travels), grid=(rows //...  7.62 us
    ppermute x2, starting transfers between devices, from_behind(): lax.ppermute(block, axis, [(i - distance, i) for i in devices if i - dist...  4.3 us
    pallas_call x1, Pallas kernels, pool(): pl.pallas_call(partial(pool_kernel, head_size), out_shape=[jax.ShapeDtype...  1.83 us
    pallas_call x1, Pallas kernels, project_late(): pl.pallas_call(project_late_kernel, out_shape=jax.ShapeDtypeStruct((rows,...  1.51 us
  transfers between devices with their start and end apart: 19, of which 8 were waited for; matrix products, arithmetic and copies ran while one was open for 0% of the time, Pallas kernels for 20%

profile of v6, /device:TPU:0, one launch (start us, length us, event | category | flops | bytes accessed | tf_op | source)
XLA Modules:
  0.0 59.3 jit_solution(13892132853536478103)
XLA Ops:
  0.7 1.1 %copy-done.3 = bf16[1,4,1,32,2048]{4,3,2,1,0:T(8,128)(2,1)S(1)} copy-done((bf16[1,4,1,32,2048]{4,3,2,1,0:T(8,128)(2,1)S(1)}, bf16[1,4,1,32,2048]{4,3,2,1,0:T(8,128)(2,1)}, u32[]{:S(2)}) %copy-start.3) | copy-done | bytes 524312
  2.0 3.0 %collective-permute-start = (bf16[256,256]{1,0:T(8,128)(2,1)S(1)}, bf16[256,256]{1,0:T(8,128)(2,1)S(1)}, u32[]{:S(2)}, u32[]{:S(2)}) collective-permute-start(bf16[256,256]{1,0:T(8,128)(2,1)S(1)} %get-tuple-element.28), channel_id=1, source_target_pairs={{0,4},{4,0},{8,12},{12,8},{16,20},{20,16},{24,28},{28,24},{1,5},{5... | collective-permute-start | bytes 393224 | tf_op jit(solution)/shard_map/ppermute | solution.py:28
  5.1 1.6 %collective-permute-start.6 = (bf16[512,128]{1,0:T(8,128)(2,1)S(1)}, bf16[512,128]{1,0:T(8,128)(2,1)S(1)}, u32[]{:S(2)}, u32[]{:S(2)}) collective-permute-start(bf16[512,128]{1,0:T(8,128)(2,1)S(1)} %constant_dynamic-slice_fusion.query_ref), channel_id=1, source_target_pairs={{0,2},{1,3},{2,0},{3,1},{4,6},{5,7},{6,4},{7,5},{8,10},{9,11},{10,... | collective-permute-start | bytes 393224 | tf_op jit(solution)/shard_map/ppermute | solution.py:28
  6.6 1.9 %collective-permute-done = bf16[256,256]{1,0:T(8,128)(2,1)S(1)} collective-permute-done((bf16[256,256]{1,0:T(8,128)(2,1)S(1)}, bf16[256,256]{1,0:T(8,128)(2,1)S(1)}, u32[]{:S(2)}, u32[]{:S(2)}) %collective-permute-start) | collective-permute-done | bytes 131104 | tf_op jit(solution)/shard_map/ppermute | solution.py:28
  8.5 1.7 %collective-permute-start.1 = (bf16[256,256]{1,0:T(8,128)(2,1)S(1)}, bf16[256,256]{1,0:T(8,128)(2,1)S(1)}, u32[]{:S(2)}, u32[]{:S(2)}) collective-permute-start(bf16[256,256]{1,0:T(8,128)(2,1)S(1)} %get-tuple-element.29), channel_id=1, source_target_pairs={{0,4},{4,0},{8,12},{12,8},{16,20},{20,16},{24,28},{28,24},{1,5},{5... | collective-permute-start | bytes 393224 | tf_op jit(solution)/shard_map/ppermute | solution.py:28
  10.3 3.7 %collective-permute-start.5 = (bf16[256,256]{1,0:T(8,128)(2,1)S(1)}, bf16[256,256]{1,0:T(8,128)(2,1)S(1)}, u32[]{:S(2)}, u32[]{:S(2)}) collective-permute-start(bf16[256,256]{1,0:T(8,128)(2,1)S(1)} %pad_maximum_fusion.3), channel_id=1, source_target_pairs={{0,24},{4,28},{8,16},{12,20},{16,8},{20,12},{24,0},{28,4},{1,25},{... | collective-permute-start | bytes 393224 | tf_op jit(solution)/shard_map/ppermute | solution.py:28
  14.2 1.3 %collective-permute-start.2 = (bf16[8,1,64,256]{3,2,1,0:T(8,128)(2,1)S(1)}, bf16[8,1,64,256]{3,2,1,0:T(8,128)(2,1)S(1)}, u32[]{:S(2)}, u32[]{:S(2)}) collective-permute-start(bf16[8,1,64,256]{3,2,1,0:T(8,128)(2,1)S(1)} %edge.1), channel_id=1, source_target_pairs={{0,1},{1,2},{2,3},{4,5},{5,6},{6,7},{8,9},{9,10},{10,11},{12,13},{... | collective-permute-start | bytes 786440 | tf_op jit(solution)/shard_map/ppermute | solution.py:33
  15.5 1.2 %collective-permute-start.3 = (bf16[256,256]{1,0:T(8,128)(2,1)S(1)}, bf16[256,256]{1,0:T(8,128)(2,1)S(1)}, u32[]{:S(2)}, u32[]{:S(2)}) collective-permute-start(bf16[256,256]{1,0:T(8,128)(2,1)S(1)} %pad_maximum_fusion.1), channel_id=1, source_target_pairs={{0,8},{4,12},{8,0},{12,4},{16,24},{20,28},{24,16},{28,20},{1,9},{5... | collective-permute-start | bytes 393224 | tf_op jit(solution)/shard_map/ppermute | solution.py:28
  17.9 1.8 %pool.1 = (bf16[4,1,32,256]{3,2,1,0:T(8,128)(2,1)}, bf16[128,256]{1,0:T(8,128)(2,1)S(1)}) custom-call(bf16[8,2,64,256]{3,2,1,0:T(8,128)(2,1)S(1)} %copy-done.2, bf16[8,1,64,256]{3,2,1,0:T(8,128)(2,1)S(1)} %collective-permute-done.2.halo_ref, bf16[27,256]{1,0:T(8,128)(2,1)S(1)} %copy-done.5), custom_call_target="tpu_custom_call" | custom-call | tf_op jit(solution)/shard_map/pool/pallas_call | solution.py:98
  20.3 3.2 %collective-permute-start.7 = (bf16[1024,128]{1,0:T(8,128)(2,1)S(1)}, bf16[1024,128]{1,0:T(8,128)(2,1)S(1)}, u32[]{:S(2)}, u32[]{:S(2)}) collective-permute-start(bf16[1024,128]{1,0:T(8,128)(2,1)S(1)} %pad_maximum_fusion), channel_id=1, source_target_pairs={{0,1},{1,0},{2,3},{3,2},{4,5},{5,4},{6,7},{7,6},{8,9},{9,8},{10,11... | collective-permute-start | bytes 786440 | tf_op jit(solution)/shard_map/ppermute | solution.py:28
  24.1 3.0 %collective-permute-start.15 = (bf16[1,4,1,32,2048]{4,3,2,1,0:T(8,128)(2,1)S(1)}, bf16[1,4,1,32,2048]{4,3,2,1,0:T(8,128)(2,1)S(1)}, u32[]{:S(2)}, u32[]{:S(2)}) collective-permute-start(bf16[1,4,1,32,2048]{4,3,2,1,0:T(8,128)(2,1)S(1)} %copy-done.4), channel_id=1, source_target_pairs={{0,4},{4,8},{8,12},{12,16},{16,20},{20,24},{24,28},{1,5},{5,9},{9,... | collective-permute-start | bytes 1572872 | tf_op jit(solution)/shard_map/ppermute | solution.py:33
  27.1 2.0 %attend.6 = bf16[544,128]{1,0:T(8,128)(2,1)S(1)} custom-call(f32[8,1152]{1,0:T(8,128)S(1)} %mask.1.bias_ref, bf16[512,128]{1,0:T(8,128)(2,1)S(1)} %get-tuple-element.50.query_ref, bf16[128,256]{1,0:T(8,128)(2,1)S(1)} %get-tuple-element.31.refs_0_, bf16[128,256]{1,0:T(8,128)(2,1)S(1)} %get-tuple-element.33.refs_1_, ...), custom_call_target="tpu_custom_call" | custom-call | flops 603979776 | bytes 2228224 | tf_op jit(solution)/shard_map/attend/pallas_call | solution.py:267
  29.5 1.8 %attend.5 = (f32[512,128]{1,0:T(8,128)S(1)}, f32[512,128]{1,0:T(8,128)S(1)}) custom-call(f32[8,1152]{1,0:T(8,128)S(1)} %mask.1.bias_ref, bf16[512,128]{1,0:T(8,128)(2,1)S(1)} %collective-permute-done.6.query_ref, bf16[128,256]{1,0:T(8,128)(2,1)S(1)} %get-tuple-element.31.refs_0_, bf16[128,256]{1,0:T(8,128)(2,1)S(1)} %get-tuple-element.33.refs_1_, ...), custom_call_target="tpu_custom_call" | custom-call | flops 603979776 | bytes 2228224 | tf_op jit(solution)/shard_map/attend/pallas_call | solution.py:267
  31.6 1.8 %collective-permute-start.9 = (bf16[544,128]{1,0:T(8,128)(2,1)S(1)}, bf16[544,128]{1,0:T(8,128)(2,1)S(1)}, u32[]{:S(2)}, u32[]{:S(2)}) collective-permute-start(bf16[544,128]{1,0:T(8,128)(2,1)S(1)} %merge.2), channel_id=1, source_target_pairs={{0,2},{1,3},{2,0},{3,1},{4,6},{5,7},{6,4},{7,5},{8,10},{9,11},{10,... | collective-permute-start | bytes 417800 | tf_op jit(solution)/shard_map/ppermute | solution.py:28
  33.5 2.0 %attend.7 = bf16[544,128]{1,0:T(8,128)(2,1)S(1)} custom-call(f32[8,1152]{1,0:T(8,128)S(1)} %mask.1.bias_ref, bf16[512,128]{1,0:T(8,128)(2,1)S(1)} %get-tuple-element.42.query_ref, bf16[128,256]{1,0:T(8,128)(2,1)S(1)} %get-tuple-element.31.refs_0_, bf16[128,256]{1,0:T(8,128)(2,1)S(1)} %get-tuple-element.33.refs_1_, ...), custom_call_target="tpu_custom_call" | custom-call | flops 603979776 | bytes 2228224 | tf_op jit(solution)/shard_map/attend/pallas_call | solution.py:267
  35.5 1.8 %attend.4 = (f32[512,128]{1,0:T(8,128)S(1)}, f32[512,128]{1,0:T(8,128)S(1)}) custom-call(f32[8,1152]{1,0:T(8,128)S(1)} %mask.1.bias_ref, bf16[512,128]{1,0:T(8,128)(2,1)S(1)} %constant_dynamic-slice_fusion.query_ref, bf16[128,256]{1,0:T(8,128)(2,1)S(1)} %get-tuple-element.31.refs_0_, bf16[128,256]{1,0:T(8,128)(2,1)S(1)} %get-tuple-element.33.refs_1_, ...), custom_call_target="tpu_custom_call" | custom-call | flops 2415919104 | bytes 2228224 | tf_op jit(solution)/shard_map/attend/pallas_call | solution.py:267
  38.0 3.6 %collective-permute-start.11 = (bf16[512,128]{1,0:T(8,128)(2,1)S(1)}, bf16[512,128]{1,0:T(8,128)(2,1)S(1)}, u32[]{:S(2)}, u32[]{:S(2)}) collective-permute-start(bf16[512,128]{1,0:T(8,128)(2,1)S(1)} %merge.3.refs_0_), channel_id=1, source_target_pairs={{0,24},{4,28},{8,16},{12,20},{16,8},{20,12},{24,0},{28,4},{1,25},{... | collective-permute-start | bytes 393224 | tf_op jit(solution)/shard_map/ppermute | solution.py:28
  42.7 2.4 %collective-permute-start.18 = (bf16[512,128]{1,0:T(8,128)(2,1)S(1)}, bf16[512,128]{1,0:T(8,128)(2,1)S(1)}, u32[]{:S(2)}, u32[]{:S(2)}) collective-permute-start(bf16[512,128]{1,0:T(8,128)(2,1)S(1)} %merge.3.refs_0_), channel_id=1, source_target_pairs={{0,12},{4,8},{8,4},{12,0},{16,28},{20,24},{24,20},{28,16},{1,13},{... | collective-permute-start | bytes 393224 | tf_op jit(solution)/shard_map/ppermute | solution.py:28
  45.7 2.3 %collective-permute-start.12 = (bf16[512,128]{1,0:T(8,128)(2,1)S(1)}, bf16[512,128]{1,0:T(8,128)(2,1)S(1)}, u32[]{:S(2)}, u32[]{:S(2)}) collective-permute-start(bf16[512,128]{1,0:T(8,128)(2,1)S(1)} %collective-permute-done.11.refs_2_), channel_id=1, source_target_pairs={{0,8},{4,12},{8,0},{12,4},{16,24},{20,28},{24,16},{28,20},{1,9},{5... | collective-permute-start | bytes 393224 | tf_op jit(solution)/shard_map/ppermute | solution.py:28
  48.1 1.7 %collective-permute-start.13 = (bf16[512,128]{1,0:T(8,128)(2,1)S(1)}, bf16[512,128]{1,0:T(8,128)(2,1)S(1)}, u32[]{:S(2)}, u32[]{:S(2)}) collective-permute-start(bf16[512,128]{1,0:T(8,128)(2,1)S(1)} %collective-permute-done.11.refs_2_), channel_id=1, source_target_pairs={{0,12},{4,8},{8,4},{12,0},{16,28},{20,24},{24,20},{28,16},{1,13},{... | collective-permute-start | bytes 393224 | tf_op jit(solution)/shard_map/ppermute | solution.py:28
  50.6 1.7 %collective-permute-done.18.refs_3_ = bf16[512,128]{1,0:T(8,128)(2,1)S(1)} collective-permute-done((bf16[512,128]{1,0:T(8,128)(2,1)S(1)}, bf16[512,128]{1,0:T(8,128)(2,1)S(1)}, u32[]{:S(2)}, u32[]{:S(2)}) %collective-permute-start.18) | collective-permute-done | bytes 131104 | tf_op jit(solution)/shard_map/ppermute | solution.py:28
  53.1 1.1 %collective-permute-done.12.refs_0_ = bf16[512,128]{1,0:T(8,128)(2,1)S(1)} collective-permute-done((bf16[512,128]{1,0:T(8,128)(2,1)S(1)}, bf16[512,128]{1,0:T(8,128)(2,1)S(1)}, u32[]{:S(2)}, u32[]{:S(2)}) %collective-permute-start.12) | collective-permute-done | bytes 131104 | tf_op jit(solution)/shard_map/ppermute | solution.py:28
  54.2 3.6 %collective-permute-done.13.refs_1_ = bf16[512,128]{1,0:T(8,128)(2,1)S(1)} collective-permute-done((bf16[512,128]{1,0:T(8,128)(2,1)S(1)}, bf16[512,128]{1,0:T(8,128)(2,1)S(1)}, u32[]{:S(2)}, u32[]{:S(2)}) %collective-permute-start.13) | collective-permute-done | bytes 131104 | tf_op jit(solution)/shard_map/ppermute | solution.py:28
  57.8 1.5 %project_late.1 = bf16[512,1024]{1,0:T(8,128)(2,1)} custom-call(bf16[512,1024]{1,0:T(8,128)(2,1)S(1)} %get-tuple-element.26.weight_ref, bf16[512,128]{1,0:T(8,128)(2,1)S(1)} %collective-permute-done.12.refs_0_, bf16[512,128]{1,0:T(8,128)(2,1)S(1)} %collective-permute-done.13.refs_1_, bf16[512,128]{1,0:T(8,128)(2,1)S(1)} %collective-permute-done.11.refs_2_, ...), custom_call_target="tpu_custom_call" | custom-call | flops 536870912 | bytes 2097152 | tf_op jit(solution)/shard_map/project_late/pallas_call | solution.py:424
  (52 shorter events, 7.4 us)
Async XLA Ops:
  0.6 13.5 %copy-start.2 = (bf16[8,2,64,256]{3,2,1,0:T(8,128)(2,1)S(1)}, bf16[8,2,64,256]{3,2,1,0:T(8,128)(2,1)}, u32[]{:S(2)}) copy-start(bf16[8,2,64,256]{3,2,1,0:T(8,128)(2,1)} %raw_ref.2) | copy-start | bytes 1572868
  1.8 16.0 %copy-start.5 = (bf16[27,256]{1,0:T(8,128)(2,1)S(1)}, bf16[27,256]{1,0:T(8,128)(2,1)}, u32[]{:S(2)}) copy-start(bf16[27,256]{1,0:T(8,128)(2,1)} %weight_ref.3) | copy-start | bytes 41476
  2.0 17.7 %copy-start.6 = (s32[9]{0:T(128)S(1)}, s32[9]{0:T(128)}, u32[]{:S(2)}) copy-start(s32[9]{0:T(128)} %valid_ref) | copy-start | bytes 112
  2.0 6.5 %collective-permute-start = (bf16[256,256]{1,0:T(8,128)(2,1)S(1)}, bf16[256,256]{1,0:T(8,128)(2,1)S(1)}, u32[]{:S(2)}, u32[]{:S(2)}) collective-permute-start(bf16[256,256]{1,0:T(8,128)(2,1)S(1)} %get-tuple-element.28), channel_id=1, source_target_pairs={{0,4},{4,0},{8,12},{12,8},{16,20},{20,16},{24,28},{28,24},{1,5},{5... | collective-permute-start | bytes 393224 | tf_op jit(solution)/shard_map/ppermute | solution.py:28
  5.1 9.0 %collective-permute-start.6 = (bf16[512,128]{1,0:T(8,128)(2,1)S(1)}, bf16[512,128]{1,0:T(8,128)(2,1)S(1)}, u32[]{:S(2)}, u32[]{:S(2)}) collective-permute-start(bf16[512,128]{1,0:T(8,128)(2,1)S(1)} %constant_dynamic-slice_fusion.query_ref), channel_id=1, source_target_pairs={{0,2},{1,3},{2,0},{3,1},{4,6},{5,7},{6,4},{7,5},{8,10},{9,11},{10,... | collective-permute-start | bytes 393224 | tf_op jit(solution)/shard_map/ppermute | solution.py:28
  8.5 15.5 %copy-start.4 = (bf16[1,4,1,32,2048]{4,3,2,1,0:T(8,128)(2,1)S(1)}, bf16[1,4,1,32,2048]{4,3,2,1,0:T(8,128)(2,1)}, u32[]{:S(2)}) copy-start(bf16[1,4,1,32,2048]{4,3,2,1,0:T(8,128)(2,1)} %param.9) | copy-start | bytes 1572868
  8.5 5.6 %collective-permute-start.1 = (bf16[256,256]{1,0:T(8,128)(2,1)S(1)}, bf16[256,256]{1,0:T(8,128)(2,1)S(1)}, u32[]{:S(2)}, u32[]{:S(2)}) collective-permute-start(bf16[256,256]{1,0:T(8,128)(2,1)S(1)} %get-tuple-element.29), channel_id=1, source_target_pairs={{0,4},{4,0},{8,12},{12,8},{16,20},{20,16},{24,28},{28,24},{1,5},{5... | collective-permute-start | bytes 393224 | tf_op jit(solution)/shard_map/ppermute | solution.py:28
  10.3 7.5 %collective-permute-start.5 = (bf16[256,256]{1,0:T(8,128)(2,1)S(1)}, bf16[256,256]{1,0:T(8,128)(2,1)S(1)}, u32[]{:S(2)}, u32[]{:S(2)}) collective-permute-start(bf16[256,256]{1,0:T(8,128)(2,1)S(1)} %pad_maximum_fusion.3), channel_id=1, source_target_pairs={{0,24},{4,28},{8,16},{12,20},{16,8},{20,12},{24,0},{28,4},{1,25},{... | collective-permute-start | bytes 393224 | tf_op jit(solution)/shard_map/ppermute | solution.py:28
  14.0 10.0 %collective-permute-start.4 = (bf16[256,256]{1,0:T(8,128)(2,1)S(1)}, bf16[256,256]{1,0:T(8,128)(2,1)S(1)}, u32[]{:S(2)}, u32[]{:S(2)}) collective-permute-start(bf16[256,256]{1,0:T(8,128)(2,1)S(1)} %pad_maximum_fusion.2), channel_id=1, source_target_pairs={{0,16},{4,20},{8,24},{12,28},{16,0},{20,4},{24,8},{28,12},{1,17},{... | collective-permute-start | bytes 393224 | tf_op jit(solution)/shard_map/ppermute | solution.py:28
  14.2 3.7 %collective-permute-start.2 = (bf16[8,1,64,256]{3,2,1,0:T(8,128)(2,1)S(1)}, bf16[8,1,64,256]{3,2,1,0:T(8,128)(2,1)S(1)}, u32[]{:S(2)}, u32[]{:S(2)}) collective-permute-start(bf16[8,1,64,256]{3,2,1,0:T(8,128)(2,1)S(1)} %edge.1), channel_id=1, source_target_pairs={{0,1},{1,2},{2,3},{4,5},{5,6},{6,7},{8,9},{9,10},{10,11},{12,13},{... | collective-permute-start | bytes 786440 | tf_op jit(solution)/shard_map/ppermute | solution.py:33
  15.5 8.5 %collective-permute-start.3 = (bf16[256,256]{1,0:T(8,128)(2,1)S(1)}, bf16[256,256]{1,0:T(8,128)(2,1)S(1)}, u32[]{:S(2)}, u32[]{:S(2)}) collective-permute-start(bf16[256,256]{1,0:T(8,128)(2,1)S(1)} %pad_maximum_fusion.1), channel_id=1, source_target_pairs={{0,8},{4,12},{8,0},{12,4},{16,24},{20,28},{24,16},{28,20},{1,9},{5... | collective-permute-start | bytes 393224 | tf_op jit(solution)/shard_map/ppermute | solution.py:28
  20.3 6.8 %collective-permute-start.7 = (bf16[1024,128]{1,0:T(8,128)(2,1)S(1)}, bf16[1024,128]{1,0:T(8,128)(2,1)S(1)}, u32[]{:S(2)}, u32[]{:S(2)}) collective-permute-start(bf16[1024,128]{1,0:T(8,128)(2,1)S(1)} %pad_maximum_fusion), channel_id=1, source_target_pairs={{0,1},{1,0},{2,3},{3,2},{4,5},{5,4},{6,7},{7,6},{8,9},{9,8},{10,11... | collective-permute-start | bytes 786440 | tf_op jit(solution)/shard_map/ppermute | solution.py:28
  24.1 17.5 %collective-permute-start.15 = (bf16[1,4,1,32,2048]{4,3,2,1,0:T(8,128)(2,1)S(1)}, bf16[1,4,1,32,2048]{4,3,2,1,0:T(8,128)(2,1)S(1)}, u32[]{:S(2)}, u32[]{:S(2)}) collective-permute-start(bf16[1,4,1,32,2048]{4,3,2,1,0:T(8,128)(2,1)S(1)} %copy-done.4), channel_id=1, source_target_pairs={{0,4},{4,8},{8,12},{12,16},{16,20},{20,24},{24,28},{1,5},{5,9},{9,... | collective-permute-start | bytes 1572872 | tf_op jit(solution)/shard_map/ppermute | solution.py:33
  29.1 2.3 %collective-permute-start.8 = (bf16[544,128]{1,0:T(8,128)(2,1)S(1)}, bf16[544,128]{1,0:T(8,128)(2,1)S(1)}, u32[]{:S(2)}, u32[]{:S(2)}) collective-permute-start(bf16[544,128]{1,0:T(8,128)(2,1)S(1)} %attend.6), channel_id=1, source_target_pairs={{0,1},{1,0},{2,3},{3,2},{4,5},{5,4},{6,7},{7,6},{8,9},{9,8},{10,11... | collective-permute-start | bytes 417800 | tf_op jit(solution)/shard_map/ppermute | solution.py:28
  31.6 6.0 %collective-permute-start.9 = (bf16[544,128]{1,0:T(8,128)(2,1)S(1)}, bf16[544,128]{1,0:T(8,128)(2,1)S(1)}, u32[]{:S(2)}, u32[]{:S(2)}) collective-permute-start(bf16[544,128]{1,0:T(8,128)(2,1)S(1)} %merge.2), channel_id=1, source_target_pairs={{0,2},{1,3},{2,0},{3,1},{4,6},{5,7},{6,4},{7,5},{8,10},{9,11},{10,... | collective-permute-start | bytes 417800 | tf_op jit(solution)/shard_map/ppermute | solution.py:28
  35.4 1.9 %collective-permute-start.10 = (bf16[544,128]{1,0:T(8,128)(2,1)S(1)}, bf16[544,128]{1,0:T(8,128)(2,1)S(1)}, u32[]{:S(2)}, u32[]{:S(2)}) collective-permute-start(bf16[544,128]{1,0:T(8,128)(2,1)S(1)} %attend.7), channel_id=1, source_target_pairs={{0,1},{1,0},{2,3},{3,2},{4,5},{5,4},{6,7},{7,6},{8,9},{9,8},{10,11... | collective-permute-start | bytes 417800 | tf_op jit(solution)/shard_map/ppermute | solution.py:28
  35.5 14.8 %copy-start.1 = (bf16[1024,1024]{1,0:T(8,128)(2,1)S(1)}, bf16[1024,1024]{1,0:T(8,128)(2,1)}, u32[]{:S(2)}) copy-start(bf16[1024,1024]{1,0:T(8,128)(2,1)} %weight_ref.2) | copy-start | bytes 6291460
  38.0 7.8 %collective-permute-start.11 = (bf16[512,128]{1,0:T(8,128)(2,1)S(1)}, bf16[512,128]{1,0:T(8,128)(2,1)S(1)}, u32[]{:S(2)}, u32[]{:S(2)}) collective-permute-start(bf16[512,128]{1,0:T(8,128)(2,1)S(1)} %merge.3.refs_0_), channel_id=1, source_target_pairs={{0,24},{4,28},{8,16},{12,20},{16,8},{20,12},{24,0},{28,4},{1,25},{... | collective-permute-start | bytes 393224 | tf_op jit(solution)/shard_map/ppermute | solution.py:28
  41.6 8.1 %collective-permute-start.16 = (bf16[512,128]{1,0:T(8,128)(2,1)S(1)}, bf16[512,128]{1,0:T(8,128)(2,1)S(1)}, u32[]{:S(2)}, u32[]{:S(2)}) collective-permute-start(bf16[512,128]{1,0:T(8,128)(2,1)S(1)} %merge.3.refs_0_), channel_id=1, source_target_pairs={{0,4},{4,0},{8,12},{12,8},{16,20},{20,16},{24,28},{28,24},{1,5},{5... | collective-permute-start | bytes 393224 | tf_op jit(solution)/shard_map/ppermute | solution.py:28
  41.6 8.9 %collective-permute-start.17 = (bf16[512,128]{1,0:T(8,128)(2,1)S(1)}, bf16[512,128]{1,0:T(8,128)(2,1)S(1)}, u32[]{:S(2)}, u32[]{:S(2)}) collective-permute-start(bf16[512,128]{1,0:T(8,128)(2,1)S(1)} %merge.3.refs_0_), channel_id=1, source_target_pairs={{0,8},{4,12},{8,0},{12,4},{16,24},{20,28},{24,16},{28,20},{1,9},{5... | collective-permute-start | bytes 393224 | tf_op jit(solution)/shard_map/ppermute | solution.py:28
  42.7 9.6 %collective-permute-start.18 = (bf16[512,128]{1,0:T(8,128)(2,1)S(1)}, bf16[512,128]{1,0:T(8,128)(2,1)S(1)}, u32[]{:S(2)}, u32[]{:S(2)}) collective-permute-start(bf16[512,128]{1,0:T(8,128)(2,1)S(1)} %merge.3.refs_0_), channel_id=1, source_target_pairs={{0,12},{4,8},{8,4},{12,0},{16,28},{20,24},{24,20},{28,16},{1,13},{... | collective-permute-start | bytes 393224 | tf_op jit(solution)/shard_map/ppermute | solution.py:28
  45.7 8.4 %collective-permute-start.12 = (bf16[512,128]{1,0:T(8,128)(2,1)S(1)}, bf16[512,128]{1,0:T(8,128)(2,1)S(1)}, u32[]{:S(2)}, u32[]{:S(2)}) collective-permute-start(bf16[512,128]{1,0:T(8,128)(2,1)S(1)} %collective-permute-done.11.refs_2_), channel_id=1, source_target_pairs={{0,8},{4,12},{8,0},{12,4},{16,24},{20,28},{24,16},{28,20},{1,9},{5... | collective-permute-start | bytes 393224 | tf_op jit(solution)/shard_map/ppermute | solution.py:28
  48.1 9.7 %collective-permute-start.13 = (bf16[512,128]{1,0:T(8,128)(2,1)S(1)}, bf16[512,128]{1,0:T(8,128)(2,1)S(1)}, u32[]{:S(2)}, u32[]{:S(2)}) collective-permute-start(bf16[512,128]{1,0:T(8,128)(2,1)S(1)} %collective-permute-done.11.refs_2_), channel_id=1, source_target_pairs={{0,12},{4,8},{8,4},{12,0},{16,28},{20,24},{24,20},{28,16},{1,13},{... | collective-permute-start | bytes 393224 | tf_op jit(solution)/shard_map/ppermute | solution.py:28
  49.7 8.0 %collective-permute-start.14 = (bf16[512,128]{1,0:T(8,128)(2,1)S(1)}, bf16[512,128]{1,0:T(8,128)(2,1)S(1)}, u32[]{:S(2)}, u32[]{:S(2)}) collective-permute-start(bf16[512,128]{1,0:T(8,128)(2,1)S(1)} %collective-permute-done.11.refs_2_), channel_id=1, source_target_pairs={{0,4},{4,0},{8,12},{12,8},{16,20},{20,16},{24,28},{28,24},{1,5},{5... | collective-permute-start | bytes 393224 | tf_op jit(solution)/shard_map/ppermute | solution.py:28
  (2 other events, 5.6 us)

commit v7 on v6

--- a/solution.py
+++ b/solution.py
@@ -172,30 +172,41 @@
     wide = 2 * head_size
     lane = lanes_of((rows, wide))
     queries = query_ref[...].astype(jnp.float32) * head_size ** (-0.5)
+    groups = [sources[: len(sources) // 2 + 1], sources[len(sources) // 2 + 1 :]]
     memory, scores = [], []
     for h in range(heads):
         own = queries if h == 0 else pltpu.roll(queries, width - h * head_size, 1)
         if own.shape[1] < wide:
             own = jnp.concatenate([own, own], axis=1)
         own = jnp.where(lane < head_size, own, 0.0).astype(jnp.bfloat16)
-        memory.append(
-            jnp.concatenate([source[:, h * wide : (h + 1) * wide] for source in sources], axis=0)
-        )
-        product = lax.dot_general(
-            own, memory[h], (((1,), (1,)), ((), ())), preferred_element_type=jnp.float32
-        )
-        scores.append(product + bias_ref[:1])
+        memory.append([])
+        scores.append([])
+        at = 0
+        for group in groups:
+            held = [source[:, h * wide : (h + 1) * wide] for source in group]
+            memory[h].append(jnp.concatenate(held, axis=0))
+            product = lax.dot_general(
+                own, memory[h][-1], (((1,), (1,)), ((), ())), preferred_element_type=jnp.float32
+            )
+            count = product.shape[1]
+            scores[h].append(product + bias_ref[:1, at : at + count])
+            at += count
     weights, peaks = [], []
     for h in range(heads):
-        peaks.append(jnp.max(scores[h], axis=1, keepdims=True))
-        weights.append(jnp.exp(scores[h] - peaks[h]).astype(jnp.bfloat16))
+        peak = jnp.max(scores[h][0], axis=1, keepdims=True)
+        for part in scores[h][1:]:
+            peak = jnp.maximum(peak, jnp.max(part, axis=1, keepdims=True))
+        peaks.append(peak)
+        weights.append([jnp.exp(part - peak).astype(jnp.bfloat16) for part in scores[h]])
     totals = []
-    memory_lane = lanes_of(memory[0].shape)
     for h in range(heads):
-        ones_and_values = jnp.where(memory_lane < head_size, 1.0, memory[h].astype(jnp.float32))
-        total = jnp.dot(
-            weights[h], ones_and_values.astype(jnp.bfloat16), preferred_element_type=jnp.float32
-        )
+        total = None
+        for held, weight in zip(memory[h], weights[h]):
+            ones_and_values = jnp.where(lanes_of(held.shape) < head_size, 1.0, held.astype(jnp.float32))
+            term = jnp.dot(
+                weight, ones_and_values.astype(jnp.bfloat16), preferred_element_type=jnp.float32
+            )
+            total = term if total is None else total + term
         totals.append(total)
     if heads == 1:
         turned = pltpu.roll(totals[0], head_size, 1)
@@ -481,7 +492,8 @@
         both = jnp.concatenate([kept[d // 2], far_in[row : row + tokens]], axis=0)
         both = exchange(both, "slot", d)
         sources[d], sources[d + 1] = both[:tokens], both[tokens:]
-    behind = from_behind(edge(after(raw_clip, near_in)), "space", 1)
+    below = edge(raw_clip)
+    behind = from_behind(below.reshape(-1, below.shape[-1]), "space", 1).reshape(below.shape)
     fresh, fresh_rows = pool(raw_clip, behind, pool_weight, head_size)
     for d in range(2, half, 2):
         row = d // 2 * tokens
@@ -491,7 +503,8 @@
     order = (None,) + tuple(range(slots))
     bias = mask(place, after(valid_columns, fresh_rows), columns, tokens, order)
     far = exchange(after(near, bias), "space", 1)
-    aged_memory = from_behind(after(old_memory, *sources.values(), bias), "slot", 1)
+    aged_memory = from_behind(after(resident, *sources.values(), bias), "slot", 1)
+    aged_memory = aged_memory.reshape(old_memory.shape)
     call = partial(
         attend,
         bias,

time: 59.6 us -> 58.5 us (0.982)
  starting transfers between devices: 32.8 us -> 27.5 us
  waiting for transfers between devices: 10.8 us -> 15 us
  local copies, waits for them, and re-layouts: 1.29 us -> 2.33 us
  Pallas kernels: 13.4 us -> 12.4 us
    ppermute x17, starting transfers between devices: 28.5 us -> 22.5 us  [exchange(): return lax.ppermute(block, axis, [(i, i ^ distance) for i in range(size)])]
    ppermute x17, waiting for transfers between devices: 10.8 us -> 15 us  [exchange(): return lax.ppermute(block, axis, [(i, i ^ distance) for i in range(size)])]
    unnamed x14 -> x16, local copies, waits for them, and re-layouts: 1.18 us -> 2.22 us
    pallas_call x4, Pallas kernels: 7.62 us -> 6.68 us  [attend(): pl.pallas_call(partial(attend_kernel, head_size, travels), grid=(rows //...]
    ppermute x2, starting transfers between devices: 4.3 us -> 5.06 us  [from_behind(): lax.ppermute(block, axis, [(i - distance, i) for i in devices if i - dist...]
  transfers between devices with their start and end apart: 19 -> 19, of which waited for: 8 -> 7; matrix products, arithmetic and copies ran while one was open for 0% -> 0% of each run, Pallas kernels for 20% -> 18%
where the time goes in v7:
time: 58.5 us; the launch traced here: 58.3 us
  starting transfers between devices  27.5 us (47%)
  waiting for transfers between devices  15 us (26%)
  Pallas kernels  12.4 us (21%)
  local copies, waits for them, and re-layouts  2.33 us (4%)
  between operations  0.92 us (2%)
    ppermute x17, starting transfers between devices, exchange(): return lax.ppermute(block, axis, [(i, i ^ distance) for i in range(size)])  22.5 us
    ppermute x17, waiting for transfers between devices, exchange(): return lax.ppermute(block, axis, [(i, i ^ distance) for i in range(size)])  15 us
    pallas_call x4, Pallas kernels, attend(): pl.pallas_call(partial(attend_kernel, head_size, travels), grid=(rows //...  6.68 us
    ppermute x2, starting transfers between devices, from_behind(): lax.ppermute(block, axis, [(i - distance, i) for i in devices if i - dist...  5.06 us
    unnamed x16, local copies, waits for them, and re-layouts  2.22 us
    pallas_call x1, Pallas kernels, pool(): pl.pallas_call(partial(pool_kernel, head_size), out_shape=[jax.ShapeDtype...  1.83 us
    pallas_call x1, Pallas kernels, project_late(): pl.pallas_call(project_late_kernel, out_shape=jax.ShapeDtypeStruct((rows,...  1.5 us
  transfers between devices with their start and end apart: 19, of which 7 were waited for; matrix products, arithmetic and copies ran while one was open for 0% of the time, Pallas kernels for 18%

profile of v7, /device:TPU:0, one launch (start us, length us, event | category | flops | bytes accessed | tf_op | source)
XLA Modules:
  0.0 58.3 jit_solution(10238280069120192410)
XLA Ops:
  0.7 1.1 %copy-done.4 = bf16[1,4,1,32,2048]{4,3,2,1,0:T(8,128)(2,1)S(1)} copy-done((bf16[1,4,1,32,2048]{4,3,2,1,0:T(8,128)(2,1)S(1)}, bf16[1,4,1,32,2048]{4,3,2,1,0:T(8,128)(2,1)}, u32[]{:S(2)}) %copy-start.4) | copy-done | bytes 524312
  2.0 3.0 %collective-permute-start.1 = (bf16[256,256]{1,0:T(8,128)(2,1)S(1)}, bf16[256,256]{1,0:T(8,128)(2,1)S(1)}, u32[]{:S(2)}, u32[]{:S(2)}) collective-permute-start(bf16[256,256]{1,0:T(8,128)(2,1)S(1)} %get-tuple-element.30), channel_id=1, source_target_pairs={{0,4},{4,0},{8,12},{12,8},{16,20},{20,16},{24,28},{28,24},{1,5},{5... | collective-permute-start | bytes 393224 | tf_op jit(solution)/shard_map/ppermute | solution.py:28
  6.1 1.6 %collective-permute-start = (bf16[512,256]{1,0:T(8,128)(2,1)S(1)}, bf16[512,256]{1,0:T(8,128)(2,1)S(1)}, u32[]{:S(2)}, u32[]{:S(2)}) collective-permute-start(bf16[512,256]{1,0:T(8,128)(2,1)S(1)} %bitcast.9), channel_id=1, source_target_pairs={{0,1},{1,2},{2,3},{4,5},{5,6},{6,7},{8,9},{9,10},{10,11},{12,13},{... | collective-permute-start | bytes 786440 | tf_op jit(solution)/shard_map/ppermute | solution.py:33
  7.8 2.0 %collective-permute-start.6 = (bf16[512,128]{1,0:T(8,128)(2,1)S(1)}, bf16[512,128]{1,0:T(8,128)(2,1)S(1)}, u32[]{:S(2)}, u32[]{:S(2)}) collective-permute-start(bf16[512,128]{1,0:T(8,128)(2,1)S(1)} %constant_dynamic-slice_fusion.query_ref), channel_id=1, source_target_pairs={{0,2},{1,3},{2,0},{3,1},{4,6},{5,7},{6,4},{7,5},{8,10},{9,11},{10,... | collective-permute-start | bytes 393224 | tf_op jit(solution)/shard_map/ppermute | solution.py:28
  10.3 3.7 %collective-permute-start.5 = (bf16[256,256]{1,0:T(8,128)(2,1)S(1)}, bf16[256,256]{1,0:T(8,128)(2,1)S(1)}, u32[]{:S(2)}, u32[]{:S(2)}) collective-permute-start(bf16[256,256]{1,0:T(8,128)(2,1)S(1)} %pad_maximum_fusion.3), channel_id=1, source_target_pairs={{0,24},{4,28},{8,16},{12,20},{16,8},{20,12},{24,0},{28,4},{1,25},{... | collective-permute-start | bytes 393224 | tf_op jit(solution)/shard_map/ppermute | solution.py:28
  14.1 1.3 %collective-permute-done.2 = bf16[256,256]{1,0:T(8,128)(2,1)S(1)} collective-permute-done((bf16[256,256]{1,0:T(8,128)(2,1)S(1)}, bf16[256,256]{1,0:T(8,128)(2,1)S(1)}, u32[]{:S(2)}, u32[]{:S(2)}) %collective-permute-start.2) | collective-permute-done | bytes 131104 | tf_op jit(solution)/shard_map/ppermute | solution.py:28
  15.4 1.6 %collective-permute-start.3 = (bf16[256,256]{1,0:T(8,128)(2,1)S(1)}, bf16[256,256]{1,0:T(8,128)(2,1)S(1)}, u32[]{:S(2)}, u32[]{:S(2)}) collective-permute-start(bf16[256,256]{1,0:T(8,128)(2,1)S(1)} %pad_maximum_fusion.1), channel_id=1, source_target_pairs={{0,8},{4,12},{8,0},{12,4},{16,24},{20,28},{24,16},{28,20},{1,9},{5... | collective-permute-start | bytes 393224 | tf_op jit(solution)/shard_map/ppermute | solution.py:28
  17.1 1.8 %pool.1 = (bf16[4,1,32,256]{3,2,1,0:T(8,128)(2,1)}, bf16[128,256]{1,0:T(8,128)(2,1)S(1)}) custom-call(bf16[8,2,64,256]{3,2,1,0:T(8,128)(2,1)S(1)} %copy-done.3, bf16[8,1,64,256]{3,2,1,0:T(8,128)(2,1)S(1)} %bitcast.8, bf16[27,256]{1,0:T(8,128)(2,1)S(1)} %copy-done.6), custom_call_target="tpu_custom_call" | custom-call | tf_op jit(solution)/shard_map/pool/pallas_call | solution.py:98
  19.8 5.4 %collective-permute-done.4 = bf16[256,256]{1,0:T(8,128)(2,1)S(1)} collective-permute-done((bf16[256,256]{1,0:T(8,128)(2,1)S(1)}, bf16[256,256]{1,0:T(8,128)(2,1)S(1)}, u32[]{:S(2)}, u32[]{:S(2)}) %collective-permute-start.4) | collective-permute-done | bytes 131104 | tf_op jit(solution)/shard_map/ppermute | solution.py:28
  25.2 3.5 %collective-permute-start.15 = (bf16[128,2048]{1,0:T(8,128)(2,1)S(1)}, bf16[128,2048]{1,0:T(8,128)(2,1)S(1)}, u32[]{:S(2)}, u32[]{:S(2)}) collective-permute-start(bf16[128,2048]{1,0:T(8,128)(2,1)S(1)} %bitcast.6), channel_id=1, source_target_pairs={{0,4},{4,8},{8,12},{12,16},{16,20},{20,24},{24,28},{1,5},{5,9},{9,... | collective-permute-start | bytes 1572872 | tf_op jit(solution)/shard_map/ppermute | solution.py:33
  28.7 1.7 %attend.6 = bf16[544,128]{1,0:T(8,128)(2,1)S(1)} custom-call(f32[8,1152]{1,0:T(8,128)S(1)} %mask.1.bias_ref, bf16[512,128]{1,0:T(8,128)(2,1)S(1)} %get-tuple-element.48.query_ref, bf16[128,256]{1,0:T(8,128)(2,1)S(1)} %get-tuple-element.26.refs_0_, bf16[128,256]{1,0:T(8,128)(2,1)S(1)} %get-tuple-element.28.refs_1_, ...), custom_call_target="tpu_custom_call" | custom-call | flops 603979776 | bytes 2228224 | tf_op jit(solution)/shard_map/attend/pallas_call | solution.py:278
  30.5 1.6 %attend.5 = (f32[512,128]{1,0:T(8,128)S(1)}, f32[512,128]{1,0:T(8,128)S(1)}) custom-call(f32[8,1152]{1,0:T(8,128)S(1)} %mask.1.bias_ref, bf16[512,128]{1,0:T(8,128)(2,1)S(1)} %collective-permute-done.6.query_ref, bf16[128,256]{1,0:T(8,128)(2,1)S(1)} %get-tuple-element.26.refs_0_, bf16[128,256]{1,0:T(8,128)(2,1)S(1)} %get-tuple-element.28.refs_1_, ...), custom_call_target="tpu_custom_call" | custom-call | flops 603979776 | bytes 2228224 | tf_op jit(solution)/shard_map/attend/pallas_call | solution.py:278
  32.5 1.4 %collective-permute-start.9 = (bf16[544,128]{1,0:T(8,128)(2,1)S(1)}, bf16[544,128]{1,0:T(8,128)(2,1)S(1)}, u32[]{:S(2)}, u32[]{:S(2)}) collective-permute-start(bf16[544,128]{1,0:T(8,128)(2,1)S(1)} %merge.2), channel_id=1, source_target_pairs={{0,2},{1,3},{2,0},{3,1},{4,6},{5,7},{6,4},{7,5},{8,10},{9,11},{10,... | collective-permute-start | bytes 417800 | tf_op jit(solution)/shard_map/ppermute | solution.py:28
  33.9 1.7 %attend.7 = bf16[544,128]{1,0:T(8,128)(2,1)S(1)} custom-call(f32[8,1152]{1,0:T(8,128)S(1)} %mask.1.bias_ref, bf16[512,128]{1,0:T(8,128)(2,1)S(1)} %get-tuple-element.40.query_ref, bf16[128,256]{1,0:T(8,128)(2,1)S(1)} %get-tuple-element.26.refs_0_, bf16[128,256]{1,0:T(8,128)(2,1)S(1)} %get-tuple-element.28.refs_1_, ...), custom_call_target="tpu_custom_call" | custom-call | flops 603979776 | bytes 2228224 | tf_op jit(solution)/shard_map/attend/pallas_call | solution.py:278
  35.9 1.6 %attend.4 = (f32[512,128]{1,0:T(8,128)S(1)}, f32[512,128]{1,0:T(8,128)S(1)}) custom-call(f32[8,1152]{1,0:T(8,128)S(1)} %mask.1.bias_ref, bf16[512,128]{1,0:T(8,128)(2,1)S(1)} %constant_dynamic-slice_fusion.query_ref, bf16[128,256]{1,0:T(8,128)(2,1)S(1)} %get-tuple-element.26.refs_0_, bf16[128,256]{1,0:T(8,128)(2,1)S(1)} %get-tuple-element.28.refs_1_, ...), custom_call_target="tpu_custom_call" | custom-call | flops 2415919104 | bytes 2228224 | tf_op jit(solution)/shard_map/attend/pallas_call | solution.py:278
  38.9 2.5 %collective-permute-start.11 = (bf16[512,128]{1,0:T(8,128)(2,1)S(1)}, bf16[512,128]{1,0:T(8,128)(2,1)S(1)}, u32[]{:S(2)}, u32[]{:S(2)}) collective-permute-start(bf16[512,128]{1,0:T(8,128)(2,1)S(1)} %merge.3.refs_0_), channel_id=1, source_target_pairs={{0,24},{4,28},{8,16},{12,20},{16,8},{20,12},{24,0},{28,4},{1,25},{... | collective-permute-start | bytes 393224 | tf_op jit(solution)/shard_map/ppermute | solution.py:28
  42.6 2.3 %collective-permute-start.18 = (bf16[512,128]{1,0:T(8,128)(2,1)S(1)}, bf16[512,128]{1,0:T(8,128)(2,1)S(1)}, u32[]{:S(2)}, u32[]{:S(2)}) collective-permute-start(bf16[512,128]{1,0:T(8,128)(2,1)S(1)} %merge.3.refs_0_), channel_id=1, source_target_pairs={{0,12},{4,8},{8,4},{12,0},{16,28},{20,24},{24,20},{28,16},{1,13},{... | collective-permute-start | bytes 393224 | tf_op jit(solution)/shard_map/ppermute | solution.py:28
  44.9 2.3 %collective-permute-done.11.refs_2_ = bf16[512,128]{1,0:T(8,128)(2,1)S(1)} collective-permute-done((bf16[512,128]{1,0:T(8,128)(2,1)S(1)}, bf16[512,128]{1,0:T(8,128)(2,1)S(1)}, u32[]{:S(2)}, u32[]{:S(2)}) %collective-permute-start.11) | collective-permute-done | bytes 131104 | tf_op jit(solution)/shard_map/ppermute | solution.py:28
  47.2 1.3 %collective-permute-start.13 = (bf16[512,128]{1,0:T(8,128)(2,1)S(1)}, bf16[512,128]{1,0:T(8,128)(2,1)S(1)}, u32[]{:S(2)}, u32[]{:S(2)}) collective-permute-start(bf16[512,128]{1,0:T(8,128)(2,1)S(1)} %collective-permute-done.11.refs_2_), channel_id=1, source_target_pairs={{0,12},{4,8},{8,4},{12,0},{16,28},{20,24},{24,20},{28,16},{1,13},{... | collective-permute-start | bytes 393224 | tf_op jit(solution)/shard_map/ppermute | solution.py:28
  48.5 2.2 %collective-permute-start.14 = (bf16[512,128]{1,0:T(8,128)(2,1)S(1)}, bf16[512,128]{1,0:T(8,128)(2,1)S(1)}, u32[]{:S(2)}, u32[]{:S(2)}) collective-permute-start(bf16[512,128]{1,0:T(8,128)(2,1)S(1)} %collective-permute-done.11.refs_2_), channel_id=1, source_target_pairs={{0,4},{4,0},{8,12},{12,8},{16,20},{20,16},{24,28},{28,24},{1,5},{5... | collective-permute-start | bytes 393224 | tf_op jit(solution)/shard_map/ppermute | solution.py:28
  51.0 1.2 %collective-permute-done.18.refs_3_ = bf16[512,128]{1,0:T(8,128)(2,1)S(1)} collective-permute-done((bf16[512,128]{1,0:T(8,128)(2,1)S(1)}, bf16[512,128]{1,0:T(8,128)(2,1)S(1)}, u32[]{:S(2)}, u32[]{:S(2)}) %collective-permute-start.18) | collective-permute-done | bytes 131104 | tf_op jit(solution)/shard_map/ppermute | solution.py:28
  53.0 1.7 %collective-permute-done.12.refs_0_ = bf16[512,128]{1,0:T(8,128)(2,1)S(1)} collective-permute-done((bf16[512,128]{1,0:T(8,128)(2,1)S(1)}, bf16[512,128]{1,0:T(8,128)(2,1)S(1)}, u32[]{:S(2)}, u32[]{:S(2)}) %collective-permute-start.12) | collective-permute-done | bytes 131104 | tf_op jit(solution)/shard_map/ppermute | solution.py:28
  54.7 2.1 %collective-permute-done.13.refs_1_ = bf16[512,128]{1,0:T(8,128)(2,1)S(1)} collective-permute-done((bf16[512,128]{1,0:T(8,128)(2,1)S(1)}, bf16[512,128]{1,0:T(8,128)(2,1)S(1)}, u32[]{:S(2)}, u32[]{:S(2)}) %collective-permute-start.13) | collective-permute-done | bytes 131104 | tf_op jit(solution)/shard_map/ppermute | solution.py:28
  56.8 1.5 %project_late.1 = bf16[512,1024]{1,0:T(8,128)(2,1)} custom-call(bf16[512,1024]{1,0:T(8,128)(2,1)S(1)} %get-tuple-element.25.weight_ref, bf16[512,128]{1,0:T(8,128)(2,1)S(1)} %collective-permute-done.12.refs_0_, bf16[512,128]{1,0:T(8,128)(2,1)S(1)} %collective-permute-done.13.refs_1_, bf16[512,128]{1,0:T(8,128)(2,1)S(1)} %collective-permute-done.11.refs_2_, ...), custom_call_target="tpu_custom_call" | custom-call | flops 536870912 | bytes 2097152 | tf_op jit(solution)/shard_map/project_late/pallas_call | solution.py:435
  (54 shorter events, 7.2 us)
Async XLA Ops:
  0.6 16.4 %copy-start.3 = (bf16[8,2,64,256]{3,2,1,0:T(8,128)(2,1)S(1)}, bf16[8,2,64,256]{3,2,1,0:T(8,128)(2,1)}, u32[]{:S(2)}) copy-start(bf16[8,2,64,256]{3,2,1,0:T(8,128)(2,1)} %raw_ref.3) | copy-start | bytes 1572868
  1.8 17.1 %copy-start.7 = (s32[9]{0:T(128)S(1)}, s32[9]{0:T(128)}, u32[]{:S(2)}) copy-start(s32[9]{0:T(128)} %valid_ref) | copy-start | bytes 112
  2.0 7.8 %collective-permute-start.1 = (bf16[256,256]{1,0:T(8,128)(2,1)S(1)}, bf16[256,256]{1,0:T(8,128)(2,1)S(1)}, u32[]{:S(2)}, u32[]{:S(2)}) collective-permute-start(bf16[256,256]{1,0:T(8,128)(2,1)S(1)} %get-tuple-element.30), channel_id=1, source_target_pairs={{0,4},{4,0},{8,12},{12,8},{16,20},{20,16},{24,28},{28,24},{1,5},{5... | collective-permute-start | bytes 393224 | tf_op jit(solution)/shard_map/ppermute | solution.py:28
  6.1 11.0 %copy-start.6 = (bf16[27,256]{1,0:T(8,128)(2,1)S(1)}, bf16[27,256]{1,0:T(8,128)(2,1)}, u32[]{:S(2)}) copy-start(bf16[27,256]{1,0:T(8,128)(2,1)} %weight_ref.3) | copy-start | bytes 41476
  6.1 19.1 %copy-start.5 = (bf16[1,4,1,32,2048]{4,3,2,1,0:T(8,128)(2,1)S(1)}, bf16[1,4,1,32,2048]{4,3,2,1,0:T(8,128)(2,1)}, u32[]{:S(2)}) copy-start(bf16[1,4,1,32,2048]{4,3,2,1,0:T(8,128)(2,1)} %param.9) | copy-start | bytes 1572868
  6.1 11.0 %collective-permute-start = (bf16[512,256]{1,0:T(8,128)(2,1)S(1)}, bf16[512,256]{1,0:T(8,128)(2,1)S(1)}, u32[]{:S(2)}, u32[]{:S(2)}) collective-permute-start(bf16[512,256]{1,0:T(8,128)(2,1)S(1)} %bitcast.9), channel_id=1, source_target_pairs={{0,1},{1,2},{2,3},{4,5},{5,6},{6,7},{8,9},{9,10},{10,11},{12,13},{... | collective-permute-start | bytes 786440 | tf_op jit(solution)/shard_map/ppermute | solution.py:33
  7.8 6.3 %collective-permute-start.6 = (bf16[512,128]{1,0:T(8,128)(2,1)S(1)}, bf16[512,128]{1,0:T(8,128)(2,1)S(1)}, u32[]{:S(2)}, u32[]{:S(2)}) collective-permute-start(bf16[512,128]{1,0:T(8,128)(2,1)S(1)} %constant_dynamic-slice_fusion.query_ref), channel_id=1, source_target_pairs={{0,2},{1,3},{2,0},{3,1},{4,6},{5,7},{6,4},{7,5},{8,10},{9,11},{10,... | collective-permute-start | bytes 393224 | tf_op jit(solution)/shard_map/ppermute | solution.py:28
  9.8 5.6 %collective-permute-start.2 = (bf16[256,256]{1,0:T(8,128)(2,1)S(1)}, bf16[256,256]{1,0:T(8,128)(2,1)S(1)}, u32[]{:S(2)}, u32[]{:S(2)}) collective-permute-start(bf16[256,256]{1,0:T(8,128)(2,1)S(1)} %get-tuple-element.31), channel_id=1, source_target_pairs={{0,4},{4,0},{8,12},{12,8},{16,20},{20,16},{24,28},{28,24},{1,5},{5... | collective-permute-start | bytes 393224 | tf_op jit(solution)/shard_map/ppermute | solution.py:28
  10.3 9.4 %collective-permute-start.5 = (bf16[256,256]{1,0:T(8,128)(2,1)S(1)}, bf16[256,256]{1,0:T(8,128)(2,1)S(1)}, u32[]{:S(2)}, u32[]{:S(2)}) collective-permute-start(bf16[256,256]{1,0:T(8,128)(2,1)S(1)} %pad_maximum_fusion.3), channel_id=1, source_target_pairs={{0,24},{4,28},{8,16},{12,20},{16,8},{20,12},{24,0},{28,4},{1,25},{... | collective-permute-start | bytes 393224 | tf_op jit(solution)/shard_map/ppermute | solution.py:28
  14.0 11.1 %collective-permute-start.4 = (bf16[256,256]{1,0:T(8,128)(2,1)S(1)}, bf16[256,256]{1,0:T(8,128)(2,1)S(1)}, u32[]{:S(2)}, u32[]{:S(2)}) collective-permute-start(bf16[256,256]{1,0:T(8,128)(2,1)S(1)} %pad_maximum_fusion.2), channel_id=1, source_target_pairs={{0,16},{4,20},{8,24},{12,28},{16,0},{20,4},{24,8},{28,12},{1,17},{... | collective-permute-start | bytes 393224 | tf_op jit(solution)/shard_map/ppermute | solution.py:28
  15.4 9.7 %collective-permute-start.3 = (bf16[256,256]{1,0:T(8,128)(2,1)S(1)}, bf16[256,256]{1,0:T(8,128)(2,1)S(1)}, u32[]{:S(2)}, u32[]{:S(2)}) collective-permute-start(bf16[256,256]{1,0:T(8,128)(2,1)S(1)} %pad_maximum_fusion.1), channel_id=1, source_target_pairs={{0,8},{4,12},{8,0},{12,4},{16,24},{20,28},{24,16},{28,20},{1,9},{5... | collective-permute-start | bytes 393224 | tf_op jit(solution)/shard_map/ppermute | solution.py:28
  19.5 9.2 %collective-permute-start.7 = (bf16[1024,128]{1,0:T(8,128)(2,1)S(1)}, bf16[1024,128]{1,0:T(8,128)(2,1)S(1)}, u32[]{:S(2)}, u32[]{:S(2)}) collective-permute-start(bf16[1024,128]{1,0:T(8,128)(2,1)S(1)} %pad_maximum_fusion), channel_id=1, source_target_pairs={{0,1},{1,0},{2,3},{3,2},{4,5},{5,4},{6,7},{7,6},{8,9},{9,8},{10,11... | collective-permute-start | bytes 786440 | tf_op jit(solution)/shard_map/ppermute | solution.py:28
  25.2 16.2 %collective-permute-start.15 = (bf16[128,2048]{1,0:T(8,128)(2,1)S(1)}, bf16[128,2048]{1,0:T(8,128)(2,1)S(1)}, u32[]{:S(2)}, u32[]{:S(2)}) collective-permute-start(bf16[128,2048]{1,0:T(8,128)(2,1)S(1)} %bitcast.6), channel_id=1, source_target_pairs={{0,4},{4,8},{8,12},{12,16},{16,20},{20,24},{24,28},{1,5},{5,9},{9,... | collective-permute-start | bytes 1572872 | tf_op jit(solution)/shard_map/ppermute | solution.py:33
  30.4 1.7 %collective-permute-start.8 = (bf16[544,128]{1,0:T(8,128)(2,1)S(1)}, bf16[544,128]{1,0:T(8,128)(2,1)S(1)}, u32[]{:S(2)}, u32[]{:S(2)}) collective-permute-start(bf16[544,128]{1,0:T(8,128)(2,1)S(1)} %attend.6), channel_id=1, source_target_pairs={{0,1},{1,0},{2,3},{3,2},{4,5},{5,4},{6,7},{7,6},{8,9},{9,8},{10,11... | collective-permute-start | bytes 417800 | tf_op jit(solution)/shard_map/ppermute | solution.py:28
  32.5 6.1 %collective-permute-start.9 = (bf16[544,128]{1,0:T(8,128)(2,1)S(1)}, bf16[544,128]{1,0:T(8,128)(2,1)S(1)}, u32[]{:S(2)}, u32[]{:S(2)}) collective-permute-start(bf16[544,128]{1,0:T(8,128)(2,1)S(1)} %merge.2), channel_id=1, source_target_pairs={{0,2},{1,3},{2,0},{3,1},{4,6},{5,7},{6,4},{7,5},{8,10},{9,11},{10,... | collective-permute-start | bytes 417800 | tf_op jit(solution)/shard_map/ppermute | solution.py:28
  35.6 1.9 %collective-permute-start.10 = (bf16[544,128]{1,0:T(8,128)(2,1)S(1)}, bf16[544,128]{1,0:T(8,128)(2,1)S(1)}, u32[]{:S(2)}, u32[]{:S(2)}) collective-permute-start(bf16[544,128]{1,0:T(8,128)(2,1)S(1)} %attend.7), channel_id=1, source_target_pairs={{0,1},{1,0},{2,3},{3,2},{4,5},{5,4},{6,7},{7,6},{8,9},{9,8},{10,11... | collective-permute-start | bytes 417800 | tf_op jit(solution)/shard_map/ppermute | solution.py:28
  35.9 14.8 %copy-start.1 = (bf16[1024,1024]{1,0:T(8,128)(2,1)S(1)}, bf16[1024,1024]{1,0:T(8,128)(2,1)}, u32[]{:S(2)}) copy-start(bf16[1024,1024]{1,0:T(8,128)(2,1)} %weight_ref.2) | copy-start | bytes 6291460
  38.9 8.3 %collective-permute-start.11 = (bf16[512,128]{1,0:T(8,128)(2,1)S(1)}, bf16[512,128]{1,0:T(8,128)(2,1)S(1)}, u32[]{:S(2)}, u32[]{:S(2)}) collective-permute-start(bf16[512,128]{1,0:T(8,128)(2,1)S(1)} %merge.3.refs_0_), channel_id=1, source_target_pairs={{0,24},{4,28},{8,16},{12,20},{16,8},{20,12},{24,0},{28,4},{1,25},{... | collective-permute-start | bytes 393224 | tf_op jit(solution)/shard_map/ppermute | solution.py:28
  41.5 7.0 %collective-permute-start.16 = (bf16[512,128]{1,0:T(8,128)(2,1)S(1)}, bf16[512,128]{1,0:T(8,128)(2,1)S(1)}, u32[]{:S(2)}, u32[]{:S(2)}) collective-permute-start(bf16[512,128]{1,0:T(8,128)(2,1)S(1)} %merge.3.refs_0_), channel_id=1, source_target_pairs={{0,4},{4,0},{8,12},{12,8},{16,20},{20,16},{24,28},{28,24},{1,5},{5... | collective-permute-start | bytes 393224 | tf_op jit(solution)/shard_map/ppermute | solution.py:28
  41.6 9.3 %collective-permute-start.17 = (bf16[512,128]{1,0:T(8,128)(2,1)S(1)}, bf16[512,128]{1,0:T(8,128)(2,1)S(1)}, u32[]{:S(2)}, u32[]{:S(2)}) collective-permute-start(bf16[512,128]{1,0:T(8,128)(2,1)S(1)} %merge.3.refs_0_), channel_id=1, source_target_pairs={{0,8},{4,12},{8,0},{12,4},{16,24},{20,28},{24,16},{28,20},{1,9},{5... | collective-permute-start | bytes 393224 | tf_op jit(solution)/shard_map/ppermute | solution.py:28
  42.6 9.6 %collective-permute-start.18 = (bf16[512,128]{1,0:T(8,128)(2,1)S(1)}, bf16[512,128]{1,0:T(8,128)(2,1)S(1)}, u32[]{:S(2)}, u32[]{:S(2)}) collective-permute-start(bf16[512,128]{1,0:T(8,128)(2,1)S(1)} %merge.3.refs_0_), channel_id=1, source_target_pairs={{0,12},{4,8},{8,4},{12,0},{16,28},{20,24},{24,20},{28,16},{1,13},{... | collective-permute-start | bytes 393224 | tf_op jit(solution)/shard_map/ppermute | solution.py:28
  47.2 7.5 %collective-permute-start.12 = (bf16[512,128]{1,0:T(8,128)(2,1)S(1)}, bf16[512,128]{1,0:T(8,128)(2,1)S(1)}, u32[]{:S(2)}, u32[]{:S(2)}) collective-permute-start(bf16[512,128]{1,0:T(8,128)(2,1)S(1)} %collective-permute-done.11.refs_2_), channel_id=1, source_target_pairs={{0,8},{4,12},{8,0},{12,4},{16,24},{20,28},{24,16},{28,20},{1,9},{5... | collective-permute-start | bytes 393224 | tf_op jit(solution)/shard_map/ppermute | solution.py:28
  47.2 9.6 %collective-permute-start.13 = (bf16[512,128]{1,0:T(8,128)(2,1)S(1)}, bf16[512,128]{1,0:T(8,128)(2,1)S(1)}, u32[]{:S(2)}, u32[]{:S(2)}) collective-permute-start(bf16[512,128]{1,0:T(8,128)(2,1)S(1)} %collective-permute-done.11.refs_2_), channel_id=1, source_target_pairs={{0,12},{4,8},{8,4},{12,0},{16,28},{20,24},{24,20},{28,16},{1,13},{... | collective-permute-start | bytes 393224 | tf_op jit(solution)/shard_map/ppermute | solution.py:28
  48.5 8.3 %collective-permute-start.14 = (bf16[512,128]{1,0:T(8,128)(2,1)S(1)}, bf16[512,128]{1,0:T(8,128)(2,1)S(1)}, u32[]{:S(2)}, u32[]{:S(2)}) collective-permute-start(bf16[512,128]{1,0:T(8,128)(2,1)S(1)} %collective-permute-done.11.refs_2_), channel_id=1, source_target_pairs={{0,4},{4,0},{8,12},{12,8},{16,20},{20,16},{24,28},{28,24},{1,5},{5... | collective-permute-start | bytes 393224 | tf_op jit(solution)/shard_map/ppermute | solution.py:28
  (3 other events, 9.3 us)

commit v8 on v7

--- a/solution.py
+++ b/solution.py
@@ -451,7 +451,7 @@
 def gather(mixed, slots, aged):
     half, top = slots // 2, slots - 2
     blocks = {0: mixed, top: exchange(mixed, "slot", top)}
-    late = after(mixed, aged)
+    late = after(mixed, *aged)
     blocks[2] = exchange(late, "slot", 2)
     blocks[1] = exchange(late, "slot", 1)
     for d in range(3, half):
@@ -503,8 +503,10 @@
     order = (None,) + tuple(range(slots))
     bias = mask(place, after(valid_columns, fresh_rows), columns, tokens, order)
     far = exchange(after(near, bias), "space", 1)
-    aged_memory = from_behind(after(resident, *sources.values(), bias), "slot", 1)
-    aged_memory = aged_memory.reshape(old_memory.shape)
+    inside = [(i, i + 1) for i in range(0, slots, 2)]
+    onward = [(i, i + 1) for i in range(1, slots - 1, 2)]
+    inside = lax.ppermute(after(resident, near_in), "slot", inside)
+    onward = lax.ppermute(after(resident, *sources.values(), bias), "slot", onward)
     call = partial(
         attend,
         bias,
@@ -525,7 +527,8 @@
     value, level = call(queries=own_queries, travels=False, weight=4)
     mixed = merge(value, level, parts, head_size, False)
 
-    blocks = gather(mixed, slots, aged_memory)
+    blocks = gather(mixed, slots, (inside, onward))
+    aged_memory = jnp.where(slot_index % 2 == 1, inside, onward).reshape(old_memory.shape)
     early_weight, late_weight = arrange(place, out_weight, slots)
     total, aged_memory = project_early(early_weight, [blocks[d] for d in range(half)], aged_memory)
     attended = project_late(late_weight, [blocks[d] for d in range(half, slots)], total)

time: 58.5 us -> 58.3 us (level)
  waiting for transfers between devices: 15 us -> 12.2 us
  starting transfers between devices: 27.5 us -> 28.6 us
  Pallas kernels: 12.4 us -> 13.4 us
    ppermute x2 -> x1, starting transfers between devices: 5.06 us -> 1.47 us  [from_behind(): lax.ppermute(block, axis, [(i - distance, i) for i in devices if i - dist...]
    ppermute x0 -> x2, starting transfers between devices: none -> 3.14 us  [the longest x1 2.45 us: local(): inside = lax.ppermute(after(resident, near_in), 'slot', inside)]
    ppermute x17, waiting for transfers between devices: 15 us -> 12.2 us  [exchange(): return lax.ppermute(block, axis, [(i, i ^ distance) for i in range(size)])]
    ppermute x17, starting transfers between devices: 22.5 us -> 23.9 us  [exchange(): return lax.ppermute(block, axis, [(i, i ^ distance) for i in range(size)])]
    pallas_call x1, Pallas kernels: 0.17 us -> 1.25 us  [cut(): pl.pallas_call(partial(cut_kernel, width, groups), out_shape=[jax.ShapeDt...]
    unnamed x16 -> x20, local copies, waits for them, and re-layouts: 2.22 us -> 2.66 us
  transfers between devices with their start and end apart: 19 -> 20, of which waited for: 7 -> 8; matrix products, arithmetic and copies ran while one was open for 0% -> 0% of each run, Pallas kernels for 18% -> 18%
where the time goes in v8:
time: 58.3 us; the launch traced here: 58 us
  starting transfers between devices  28.6 us (49%)
  Pallas kernels  13.4 us (23%)
  waiting for transfers between devices  12.2 us (21%)
  local copies, waits for them, and re-layouts  2.77 us (5%)
  between operations  0.94 us (2%)
    ppermute x17, starting transfers between devices, exchange(): return lax.ppermute(block, axis, [(i, i ^ distance) for i in range(size)])  23.9 us
    ppermute x17, waiting for transfers between devices, exchange(): return lax.ppermute(block, axis, [(i, i ^ distance) for i in range(size)])  12.2 us
    pallas_call x4, Pallas kernels, attend(): pl.pallas_call(partial(attend_kernel, head_size, travels), grid=(rows //...  6.64 us
    unnamed x20, local copies, waits for them, and re-layouts  2.66 us
    ppermute x1, starting transfers between devices, local(): inside = lax.ppermute(after(resident, near_in), 'slot', inside)  2.45 us
    pallas_call x1, Pallas kernels, pool(): pl.pallas_call(partial(pool_kernel, head_size), out_shape=[jax.ShapeDtype...  1.83 us
    ppermute x1, starting transfers between devices, from_behind(): lax.ppermute(block, axis, [(i - distance, i) for i in devices if i - dist...  1.47 us
    pallas_call x1, Pallas kernels, project_late(): pl.pallas_call(project_late_kernel, out_shape=jax.ShapeDtypeStruct((rows,...  1.47 us
  transfers between devices with their start and end apart: 20, of which 8 were waited for; matrix products, arithmetic and copies ran while one was open for 0% of the time, Pallas kernels for 18%

profile of v8, /device:TPU:0, one launch (start us, length us, event | category | flops | bytes accessed | tf_op | source)
XLA Modules:
  0.0 58.0 jit_solution(103868149856376414)
XLA Ops:
  0.7 1.3 %cut.1 = (bf16[256,256]{1,0:T(8,128)(2,1)S(1)}, bf16[256,256]{1,0:T(8,128)(2,1)S(1)}, bf16[128,256]{1,0:T(8,128)(2,1)S(1)}, bf16[128,256]{1,0:T(8,128)(2,1)S(1)}...) custom-call(s32[1]{0:T(128)} %bitcast.place_ref, bf16[128,2048]{1,0:T(8,128)(2,1)} %bitcast.3.memory_ref), custom_call_target="tpu_custom_call" | custom-call | tf_op jit(solution)/shard_map/cut/pallas_call | solution.py:134
  1.9 3.0 %collective-permute-start.1 = (bf16[256,256]{1,0:T(8,128)(2,1)S(1)}, bf16[256,256]{1,0:T(8,128)(2,1)S(1)}, u32[]{:S(2)}, u32[]{:S(2)}) collective-permute-start(bf16[256,256]{1,0:T(8,128)(2,1)S(1)} %get-tuple-element.31), channel_id=1, source_target_pairs={{0,4},{4,0},{8,12},{12,8},{16,20},{20,16},{24,28},{28,24},{1,5},{5... | collective-permute-start | bytes 393224 | tf_op jit(solution)/shard_map/ppermute | solution.py:28
  5.0 1.0 %copy-done.2 = bf16[8,2,64,256]{3,2,1,0:T(8,128)(2,1)S(1)} copy-done((bf16[8,2,64,256]{3,2,1,0:T(8,128)(2,1)S(1)}, bf16[8,2,64,256]{3,2,1,0:T(8,128)(2,1)}, u32[]{:S(2)}) %copy-start.2) | copy-done | bytes 524312
  6.0 1.5 %collective-permute-start = (bf16[512,256]{1,0:T(8,128)(2,1)S(1)}, bf16[512,256]{1,0:T(8,128)(2,1)S(1)}, u32[]{:S(2)}, u32[]{:S(2)}) collective-permute-start(bf16[512,256]{1,0:T(8,128)(2,1)S(1)} %bitcast.7), channel_id=1, source_target_pairs={{0,1},{1,2},{2,3},{4,5},{5,6},{6,7},{8,9},{9,10},{10,11},{12,13},{... | collective-permute-start | bytes 786440 | tf_op jit(solution)/shard_map/ppermute | solution.py:33
  7.6 2.0 %collective-permute-start.6 = (bf16[512,128]{1,0:T(8,128)(2,1)S(1)}, bf16[512,128]{1,0:T(8,128)(2,1)S(1)}, u32[]{:S(2)}, u32[]{:S(2)}) collective-permute-start(bf16[512,128]{1,0:T(8,128)(2,1)S(1)} %constant_dynamic-slice_fusion.query_ref), channel_id=1, source_target_pairs={{0,2},{1,3},{2,0},{3,1},{4,6},{5,7},{6,4},{7,5},{8,10},{9,11},{10,... | collective-permute-start | bytes 393224 | tf_op jit(solution)/shard_map/ppermute | solution.py:28
  10.2 3.7 %collective-permute-start.5 = (bf16[256,256]{1,0:T(8,128)(2,1)S(1)}, bf16[256,256]{1,0:T(8,128)(2,1)S(1)}, u32[]{:S(2)}, u32[]{:S(2)}) collective-permute-start(bf16[256,256]{1,0:T(8,128)(2,1)S(1)} %pad_maximum_fusion.3), channel_id=1, source_target_pairs={{0,24},{4,28},{8,16},{12,20},{16,8},{20,12},{24,0},{28,4},{1,25},{... | collective-permute-start | bytes 393224 | tf_op jit(solution)/shard_map/ppermute | solution.py:28
  14.0 1.2 %collective-permute-done.2 = bf16[256,256]{1,0:T(8,128)(2,1)S(1)} collective-permute-done((bf16[256,256]{1,0:T(8,128)(2,1)S(1)}, bf16[256,256]{1,0:T(8,128)(2,1)S(1)}, u32[]{:S(2)}, u32[]{:S(2)}) %collective-permute-start.2) | collective-permute-done | bytes 131104 | tf_op jit(solution)/shard_map/ppermute | solution.py:28
  15.2 1.6 %collective-permute-start.3 = (bf16[256,256]{1,0:T(8,128)(2,1)S(1)}, bf16[256,256]{1,0:T(8,128)(2,1)S(1)}, u32[]{:S(2)}, u32[]{:S(2)}) collective-permute-start(bf16[256,256]{1,0:T(8,128)(2,1)S(1)} %pad_maximum_fusion.1), channel_id=1, source_target_pairs={{0,8},{4,12},{8,0},{12,4},{16,24},{20,28},{24,16},{28,20},{1,9},{5... | collective-permute-start | bytes 393224 | tf_op jit(solution)/shard_map/ppermute | solution.py:28
  16.9 1.8 %pool.1 = (bf16[4,1,32,256]{3,2,1,0:T(8,128)(2,1)}, bf16[128,256]{1,0:T(8,128)(2,1)S(1)}) custom-call(bf16[8,2,64,256]{3,2,1,0:T(8,128)(2,1)S(1)} %copy-done.3, bf16[8,1,64,256]{3,2,1,0:T(8,128)(2,1)S(1)} %bitcast.6, bf16[27,256]{1,0:T(8,128)(2,1)S(1)} %copy-done.4), custom_call_target="tpu_custom_call" | custom-call | tf_op jit(solution)/shard_map/pool/pallas_call | solution.py:98
  19.3 2.4 %collective-permute-start.15 = (bf16[128,2048]{1,0:T(8,128)(2,1)}, bf16[128,2048]{1,0:T(8,128)(2,1)S(1)}, u32[]{:S(2)}, u32[]{:S(2)}) collective-permute-start(bf16[128,2048]{1,0:T(8,128)(2,1)} %bitcast.3.memory_ref), channel_id=1, source_target_pairs={{0,4},{8,12},{16,20},{24,28},{1,5},{9,13},{17,21},{25,29},{2,6},{1... | collective-permute-start | bytes 1572872 | tf_op jit(solution)/shard_map/ppermute | solution.py:508
  21.8 3.1 %collective-permute-done.4 = bf16[256,256]{1,0:T(8,128)(2,1)S(1)} collective-permute-done((bf16[256,256]{1,0:T(8,128)(2,1)S(1)}, bf16[256,256]{1,0:T(8,128)(2,1)S(1)}, u32[]{:S(2)}, u32[]{:S(2)}) %collective-permute-start.4) | collective-permute-done | bytes 131104 | tf_op jit(solution)/shard_map/ppermute | solution.py:28
  25.7 1.7 %attend.6 = bf16[544,128]{1,0:T(8,128)(2,1)S(1)} custom-call(f32[8,1152]{1,0:T(8,128)S(1)} %mask.1.bias_ref, bf16[512,128]{1,0:T(8,128)(2,1)S(1)} %get-tuple-element.50.query_ref, bf16[128,256]{1,0:T(8,128)(2,1)S(1)} %get-tuple-element.27.refs_0_, bf16[128,256]{1,0:T(8,128)(2,1)S(1)} %get-tuple-element.29.refs_1_, ...), custom_call_target="tpu_custom_call" | custom-call | flops 603979776 | bytes 2228224 | tf_op jit(solution)/shard_map/attend/pallas_call | solution.py:278
  27.5 1.6 %attend.5 = (f32[512,128]{1,0:T(8,128)S(1)}, f32[512,128]{1,0:T(8,128)S(1)}) custom-call(f32[8,1152]{1,0:T(8,128)S(1)} %mask.1.bias_ref, bf16[512,128]{1,0:T(8,128)(2,1)S(1)} %collective-permute-done.6.query_ref, bf16[128,256]{1,0:T(8,128)(2,1)S(1)} %get-tuple-element.27.refs_0_, bf16[128,256]{1,0:T(8,128)(2,1)S(1)} %get-tuple-element.29.refs_1_, ...), custom_call_target="tpu_custom_call" | custom-call | flops 603979776 | bytes 2228224 | tf_op jit(solution)/shard_map/attend/pallas_call | solution.py:278
  29.5 1.7 %collective-permute-start.9 = (bf16[544,128]{1,0:T(8,128)(2,1)S(1)}, bf16[544,128]{1,0:T(8,128)(2,1)S(1)}, u32[]{:S(2)}, u32[]{:S(2)}) collective-permute-start(bf16[544,128]{1,0:T(8,128)(2,1)S(1)} %merge.2), channel_id=1, source_target_pairs={{0,2},{1,3},{2,0},{3,1},{4,6},{5,7},{6,4},{7,5},{8,10},{9,11},{10,... | collective-permute-start | bytes 417800 | tf_op jit(solution)/shard_map/ppermute | solution.py:28
  31.2 1.7 %attend.7 = bf16[544,128]{1,0:T(8,128)(2,1)S(1)} custom-call(f32[8,1152]{1,0:T(8,128)S(1)} %mask.1.bias_ref, bf16[512,128]{1,0:T(8,128)(2,1)S(1)} %get-tuple-element.41.query_ref, bf16[128,256]{1,0:T(8,128)(2,1)S(1)} %get-tuple-element.27.refs_0_, bf16[128,256]{1,0:T(8,128)(2,1)S(1)} %get-tuple-element.29.refs_1_, ...), custom_call_target="tpu_custom_call" | custom-call | flops 603979776 | bytes 2228224 | tf_op jit(solution)/shard_map/attend/pallas_call | solution.py:278
  33.2 1.6 %attend.4 = (f32[512,128]{1,0:T(8,128)S(1)}, f32[512,128]{1,0:T(8,128)S(1)}) custom-call(f32[8,1152]{1,0:T(8,128)S(1)} %mask.1.bias_ref, bf16[512,128]{1,0:T(8,128)(2,1)S(1)} %constant_dynamic-slice_fusion.query_ref, bf16[128,256]{1,0:T(8,128)(2,1)S(1)} %get-tuple-element.27.refs_0_, bf16[128,256]{1,0:T(8,128)(2,1)S(1)} %get-tuple-element.29.refs_1_, ...), custom_call_target="tpu_custom_call" | custom-call | flops 2415919104 | bytes 2228224 | tf_op jit(solution)/shard_map/attend/pallas_call | solution.py:278
  35.9 3.2 %collective-permute-start.11 = (bf16[512,128]{1,0:T(8,128)(2,1)S(1)}, bf16[512,128]{1,0:T(8,128)(2,1)S(1)}, u32[]{:S(2)}, u32[]{:S(2)}) collective-permute-start(bf16[512,128]{1,0:T(8,128)(2,1)S(1)} %merge.3.refs_0_), channel_id=1, source_target_pairs={{0,24},{4,28},{8,16},{12,20},{16,8},{20,12},{24,0},{28,4},{1,25},{... | collective-permute-start | bytes 393224 | tf_op jit(solution)/shard_map/ppermute | solution.py:28
  41.9 2.5 %collective-permute-start.18 = (bf16[512,128]{1,0:T(8,128)(2,1)S(1)}, bf16[512,128]{1,0:T(8,128)(2,1)S(1)}, u32[]{:S(2)}, u32[]{:S(2)}) collective-permute-start(bf16[512,128]{1,0:T(8,128)(2,1)S(1)} %merge.3.refs_0_), channel_id=1, source_target_pairs={{0,8},{4,12},{8,0},{12,4},{16,24},{20,28},{24,16},{28,20},{1,9},{5... | collective-permute-start | bytes 393224 | tf_op jit(solution)/shard_map/ppermute | solution.py:28
  44.6 1.2 %collective-permute-start.12 = (bf16[512,128]{1,0:T(8,128)(2,1)S(1)}, bf16[512,128]{1,0:T(8,128)(2,1)S(1)}, u32[]{:S(2)}, u32[]{:S(2)}) collective-permute-start(bf16[512,128]{1,0:T(8,128)(2,1)S(1)} %collective-permute-done.11.refs_2_), channel_id=1, source_target_pairs={{0,8},{4,12},{8,0},{12,4},{16,24},{20,28},{24,16},{28,20},{1,9},{5... | collective-permute-start | bytes 393224 | tf_op jit(solution)/shard_map/ppermute | solution.py:28
  45.8 2.2 %collective-permute-start.13 = (bf16[512,128]{1,0:T(8,128)(2,1)S(1)}, bf16[512,128]{1,0:T(8,128)(2,1)S(1)}, u32[]{:S(2)}, u32[]{:S(2)}) collective-permute-start(bf16[512,128]{1,0:T(8,128)(2,1)S(1)} %collective-permute-done.11.refs_2_), channel_id=1, source_target_pairs={{0,12},{4,8},{8,4},{12,0},{16,28},{20,24},{24,20},{28,16},{1,13},{... | collective-permute-start | bytes 393224 | tf_op jit(solution)/shard_map/ppermute | solution.py:28
  48.7 3.0 %collective-permute-done.19.refs_3_ = bf16[512,128]{1,0:T(8,128)(2,1)S(1)} collective-permute-done((bf16[512,128]{1,0:T(8,128)(2,1)S(1)}, bf16[512,128]{1,0:T(8,128)(2,1)S(1)}, u32[]{:S(2)}, u32[]{:S(2)}) %collective-permute-start.19) | collective-permute-done | bytes 131104 | tf_op jit(solution)/shard_map/ppermute | solution.py:28
  52.5 1.7 %collective-permute-done.12.refs_0_ = bf16[512,128]{1,0:T(8,128)(2,1)S(1)} collective-permute-done((bf16[512,128]{1,0:T(8,128)(2,1)S(1)}, bf16[512,128]{1,0:T(8,128)(2,1)S(1)}, u32[]{:S(2)}, u32[]{:S(2)}) %collective-permute-start.12) | collective-permute-done | bytes 131104 | tf_op jit(solution)/shard_map/ppermute | solution.py:28
  54.1 2.2 %collective-permute-done.13.refs_1_ = bf16[512,128]{1,0:T(8,128)(2,1)S(1)} collective-permute-done((bf16[512,128]{1,0:T(8,128)(2,1)S(1)}, bf16[512,128]{1,0:T(8,128)(2,1)S(1)}, u32[]{:S(2)}, u32[]{:S(2)}) %collective-permute-start.13) | collective-permute-done | bytes 131104 | tf_op jit(solution)/shard_map/ppermute | solution.py:28
  56.5 1.5 %project_late.1 = bf16[512,1024]{1,0:T(8,128)(2,1)} custom-call(bf16[512,1024]{1,0:T(8,128)(2,1)S(1)} %get-tuple-element.26.weight_ref, bf16[512,128]{1,0:T(8,128)(2,1)S(1)} %collective-permute-done.12.refs_0_, bf16[512,128]{1,0:T(8,128)(2,1)S(1)} %collective-permute-done.13.refs_1_, bf16[512,128]{1,0:T(8,128)(2,1)S(1)} %collective-permute-done.11.refs_2_, ...), custom_call_target="tpu_custom_call" | custom-call | flops 536870912 | bytes 2097152 | tf_op jit(solution)/shard_map/project_late/pallas_call | solution.py:435
  (61 shorter events, 8.6 us)
Async XLA Ops:
  0.6 16.2 %copy-start.3 = (bf16[8,2,64,256]{3,2,1,0:T(8,128)(2,1)S(1)}, bf16[8,2,64,256]{3,2,1,0:T(8,128)(2,1)}, u32[]{:S(2)}) copy-start(bf16[8,2,64,256]{3,2,1,0:T(8,128)(2,1)} %raw_ref.3) | copy-start | bytes 1572868
  0.7 18.0 %copy-start.5 = (s32[9]{0:T(128)S(1)}, s32[9]{0:T(128)}, u32[]{:S(2)}) copy-start(s32[9]{0:T(128)} %valid_ref) | copy-start | bytes 112
  1.9 7.7 %collective-permute-start.1 = (bf16[256,256]{1,0:T(8,128)(2,1)S(1)}, bf16[256,256]{1,0:T(8,128)(2,1)S(1)}, u32[]{:S(2)}, u32[]{:S(2)}) collective-permute-start(bf16[256,256]{1,0:T(8,128)(2,1)S(1)} %get-tuple-element.31), channel_id=1, source_target_pairs={{0,4},{4,0},{8,12},{12,8},{16,20},{20,16},{24,28},{28,24},{1,5},{5... | collective-permute-start | bytes 393224 | tf_op jit(solution)/shard_map/ppermute | solution.py:28
  6.0 10.9 %copy-start.4 = (bf16[27,256]{1,0:T(8,128)(2,1)S(1)}, bf16[27,256]{1,0:T(8,128)(2,1)}, u32[]{:S(2)}) copy-start(bf16[27,256]{1,0:T(8,128)(2,1)} %weight_ref.3) | copy-start | bytes 41476
  6.0 10.8 %collective-permute-start = (bf16[512,256]{1,0:T(8,128)(2,1)S(1)}, bf16[512,256]{1,0:T(8,128)(2,1)S(1)}, u32[]{:S(2)}, u32[]{:S(2)}) collective-permute-start(bf16[512,256]{1,0:T(8,128)(2,1)S(1)} %bitcast.7), channel_id=1, source_target_pairs={{0,1},{1,2},{2,3},{4,5},{5,6},{6,7},{8,9},{9,10},{10,11},{12,13},{... | collective-permute-start | bytes 786440 | tf_op jit(solution)/shard_map/ppermute | solution.py:33
  7.6 6.4 %collective-permute-start.6 = (bf16[512,128]{1,0:T(8,128)(2,1)S(1)}, bf16[512,128]{1,0:T(8,128)(2,1)S(1)}, u32[]{:S(2)}, u32[]{:S(2)}) collective-permute-start(bf16[512,128]{1,0:T(8,128)(2,1)S(1)} %constant_dynamic-slice_fusion.query_ref), channel_id=1, source_target_pairs={{0,2},{1,3},{2,0},{3,1},{4,6},{5,7},{6,4},{7,5},{8,10},{9,11},{10,... | collective-permute-start | bytes 393224 | tf_op jit(solution)/shard_map/ppermute | solution.py:28
  9.6 5.6 %collective-permute-start.2 = (bf16[256,256]{1,0:T(8,128)(2,1)S(1)}, bf16[256,256]{1,0:T(8,128)(2,1)S(1)}, u32[]{:S(2)}, u32[]{:S(2)}) collective-permute-start(bf16[256,256]{1,0:T(8,128)(2,1)S(1)} %get-tuple-element.32), channel_id=1, source_target_pairs={{0,4},{4,0},{8,12},{12,8},{16,20},{20,16},{24,28},{28,24},{1,5},{5... | collective-permute-start | bytes 393224 | tf_op jit(solution)/shard_map/ppermute | solution.py:28
  10.2 11.6 %collective-permute-start.5 = (bf16[256,256]{1,0:T(8,128)(2,1)S(1)}, bf16[256,256]{1,0:T(8,128)(2,1)S(1)}, u32[]{:S(2)}, u32[]{:S(2)}) collective-permute-start(bf16[256,256]{1,0:T(8,128)(2,1)S(1)} %pad_maximum_fusion.3), channel_id=1, source_target_pairs={{0,24},{4,28},{8,16},{12,20},{16,8},{20,12},{24,0},{28,4},{1,25},{... | collective-permute-start | bytes 393224 | tf_op jit(solution)/shard_map/ppermute | solution.py:28
  13.9 11.0 %collective-permute-start.4 = (bf16[256,256]{1,0:T(8,128)(2,1)S(1)}, bf16[256,256]{1,0:T(8,128)(2,1)S(1)}, u32[]{:S(2)}, u32[]{:S(2)}) collective-permute-start(bf16[256,256]{1,0:T(8,128)(2,1)S(1)} %pad_maximum_fusion.2), channel_id=1, source_target_pairs={{0,16},{4,20},{8,24},{12,28},{16,0},{20,4},{24,8},{28,12},{1,17},{... | collective-permute-start | bytes 393224 | tf_op jit(solution)/shard_map/ppermute | solution.py:28
  15.2 9.7 %collective-permute-start.3 = (bf16[256,256]{1,0:T(8,128)(2,1)S(1)}, bf16[256,256]{1,0:T(8,128)(2,1)S(1)}, u32[]{:S(2)}, u32[]{:S(2)}) collective-permute-start(bf16[256,256]{1,0:T(8,128)(2,1)S(1)} %pad_maximum_fusion.1), channel_id=1, source_target_pairs={{0,8},{4,12},{8,0},{12,4},{16,24},{20,28},{24,16},{28,20},{1,9},{5... | collective-permute-start | bytes 393224 | tf_op jit(solution)/shard_map/ppermute | solution.py:28
  19.3 19.9 %collective-permute-start.15 = (bf16[128,2048]{1,0:T(8,128)(2,1)}, bf16[128,2048]{1,0:T(8,128)(2,1)S(1)}, u32[]{:S(2)}, u32[]{:S(2)}) collective-permute-start(bf16[128,2048]{1,0:T(8,128)(2,1)} %bitcast.3.memory_ref), channel_id=1, source_target_pairs={{0,4},{8,12},{16,20},{24,28},{1,5},{9,13},{17,21},{25,29},{2,6},{1... | collective-permute-start | bytes 1572872 | tf_op jit(solution)/shard_map/ppermute | solution.py:508
  21.7 4.0 %collective-permute-start.7 = (bf16[1024,128]{1,0:T(8,128)(2,1)S(1)}, bf16[1024,128]{1,0:T(8,128)(2,1)S(1)}, u32[]{:S(2)}, u32[]{:S(2)}) collective-permute-start(bf16[1024,128]{1,0:T(8,128)(2,1)S(1)} %pad_maximum_fusion), channel_id=1, source_target_pairs={{0,1},{1,0},{2,3},{3,2},{4,5},{5,4},{6,7},{7,6},{8,9},{9,8},{10,11... | collective-permute-start | bytes 786440 | tf_op jit(solution)/shard_map/ppermute | solution.py:28
  25.0 15.0 %collective-permute-start.16 = (bf16[128,2048]{1,0:T(8,128)(2,1)}, bf16[128,2048]{1,0:T(8,128)(2,1)S(1)}, u32[]{:S(2)}, u32[]{:S(2)}) collective-permute-start(bf16[128,2048]{1,0:T(8,128)(2,1)} %bitcast.3.memory_ref), channel_id=1, source_target_pairs={{4,8},{12,16},{20,24},{5,9},{13,17},{21,25},{6,10},{14,18},{22,26}... | collective-permute-start | bytes 1572872 | tf_op jit(solution)/shard_map/ppermute | solution.py:509
  27.4 1.7 %collective-permute-start.8 = (bf16[544,128]{1,0:T(8,128)(2,1)S(1)}, bf16[544,128]{1,0:T(8,128)(2,1)S(1)}, u32[]{:S(2)}, u32[]{:S(2)}) collective-permute-start(bf16[544,128]{1,0:T(8,128)(2,1)S(1)} %attend.6), channel_id=1, source_target_pairs={{0,1},{1,0},{2,3},{3,2},{4,5},{5,4},{6,7},{7,6},{8,9},{9,8},{10,11... | collective-permute-start | bytes 417800 | tf_op jit(solution)/shard_map/ppermute | solution.py:28
  29.5 6.1 %collective-permute-start.9 = (bf16[544,128]{1,0:T(8,128)(2,1)S(1)}, bf16[544,128]{1,0:T(8,128)(2,1)S(1)}, u32[]{:S(2)}, u32[]{:S(2)}) collective-permute-start(bf16[544,128]{1,0:T(8,128)(2,1)S(1)} %merge.2), channel_id=1, source_target_pairs={{0,2},{1,3},{2,0},{3,1},{4,6},{5,7},{6,4},{7,5},{8,10},{9,11},{10,... | collective-permute-start | bytes 417800 | tf_op jit(solution)/shard_map/ppermute | solution.py:28
  32.9 1.9 %collective-permute-start.10 = (bf16[544,128]{1,0:T(8,128)(2,1)S(1)}, bf16[544,128]{1,0:T(8,128)(2,1)S(1)}, u32[]{:S(2)}, u32[]{:S(2)}) collective-permute-start(bf16[544,128]{1,0:T(8,128)(2,1)S(1)} %attend.7), channel_id=1, source_target_pairs={{0,1},{1,0},{2,3},{3,2},{4,5},{5,4},{6,7},{7,6},{8,9},{9,8},{10,11... | collective-permute-start | bytes 417800 | tf_op jit(solution)/shard_map/ppermute | solution.py:28
  33.2 8.4 %copy-start.1 = (bf16[1024,1024]{1,0:T(8,128)(2,1)S(1)}, bf16[1024,1024]{1,0:T(8,128)(2,1)}, u32[]{:S(2)}) copy-start(bf16[1024,1024]{1,0:T(8,128)(2,1)} %weight_ref.2) | copy-start | bytes 6291460
  35.9 8.6 %collective-permute-start.11 = (bf16[512,128]{1,0:T(8,128)(2,1)S(1)}, bf16[512,128]{1,0:T(8,128)(2,1)S(1)}, u32[]{:S(2)}, u32[]{:S(2)}) collective-permute-start(bf16[512,128]{1,0:T(8,128)(2,1)S(1)} %merge.3.refs_0_), channel_id=1, source_target_pairs={{0,24},{4,28},{8,16},{12,20},{16,8},{20,12},{24,0},{28,4},{1,25},{... | collective-permute-start | bytes 393224 | tf_op jit(solution)/shard_map/ppermute | solution.py:28
  40.8 7.3 %collective-permute-start.17 = (bf16[512,128]{1,0:T(8,128)(2,1)S(1)}, bf16[512,128]{1,0:T(8,128)(2,1)S(1)}, u32[]{:S(2)}, u32[]{:S(2)}) collective-permute-start(bf16[512,128]{1,0:T(8,128)(2,1)S(1)} %merge.3.refs_0_), channel_id=1, source_target_pairs={{0,4},{4,0},{8,12},{12,8},{16,20},{20,16},{24,28},{28,24},{1,5},{5... | collective-permute-start | bytes 393224 | tf_op jit(solution)/shard_map/ppermute | solution.py:28
  41.9 6.9 %collective-permute-start.18 = (bf16[512,128]{1,0:T(8,128)(2,1)S(1)}, bf16[512,128]{1,0:T(8,128)(2,1)S(1)}, u32[]{:S(2)}, u32[]{:S(2)}) collective-permute-start(bf16[512,128]{1,0:T(8,128)(2,1)S(1)} %merge.3.refs_0_), channel_id=1, source_target_pairs={{0,8},{4,12},{8,0},{12,4},{16,24},{20,28},{24,16},{28,20},{1,9},{5... | collective-permute-start | bytes 393224 | tf_op jit(solution)/shard_map/ppermute | solution.py:28
  44.3 7.3 %collective-permute-start.19 = (bf16[512,128]{1,0:T(8,128)(2,1)S(1)}, bf16[512,128]{1,0:T(8,128)(2,1)S(1)}, u32[]{:S(2)}, u32[]{:S(2)}) collective-permute-start(bf16[512,128]{1,0:T(8,128)(2,1)S(1)} %merge.3.refs_0_), channel_id=1, source_target_pairs={{0,12},{4,8},{8,4},{12,0},{16,28},{20,24},{24,20},{28,16},{1,13},{... | collective-permute-start | bytes 393224 | tf_op jit(solution)/shard_map/ppermute | solution.py:28
  44.6 9.6 %collective-permute-start.12 = (bf16[512,128]{1,0:T(8,128)(2,1)S(1)}, bf16[512,128]{1,0:T(8,128)(2,1)S(1)}, u32[]{:S(2)}, u32[]{:S(2)}) collective-permute-start(bf16[512,128]{1,0:T(8,128)(2,1)S(1)} %collective-permute-done.11.refs_2_), channel_id=1, source_target_pairs={{0,8},{4,12},{8,0},{12,4},{16,24},{20,28},{24,16},{28,20},{1,9},{5... | collective-permute-start | bytes 393224 | tf_op jit(solution)/shard_map/ppermute | solution.py:28
  45.8 10.5 %collective-permute-start.13 = (bf16[512,128]{1,0:T(8,128)(2,1)S(1)}, bf16[512,128]{1,0:T(8,128)(2,1)S(1)}, u32[]{:S(2)}, u32[]{:S(2)}) collective-permute-start(bf16[512,128]{1,0:T(8,128)(2,1)S(1)} %collective-permute-done.11.refs_2_), channel_id=1, source_target_pairs={{0,12},{4,8},{8,4},{12,0},{16,28},{20,24},{24,20},{28,16},{1,13},{... | collective-permute-start | bytes 393224 | tf_op jit(solution)/shard_map/ppermute | solution.py:28
  48.0 8.5 %collective-permute-start.14 = (bf16[512,128]{1,0:T(8,128)(2,1)S(1)}, bf16[512,128]{1,0:T(8,128)(2,1)S(1)}, u32[]{:S(2)}, u32[]{:S(2)}) collective-permute-start(bf16[512,128]{1,0:T(8,128)(2,1)S(1)} %collective-permute-done.11.refs_2_), channel_id=1, source_target_pairs={{0,4},{4,0},{8,12},{12,8},{16,20},{20,16},{24,28},{28,24},{1,5},{5... | collective-permute-start | bytes 393224 | tf_op jit(solution)/shard_map/ppermute | solution.py:28
  (6 other events, 23.5 us)

commit v9 on v8

--- a/solution.py
+++ b/solution.py
@@ -453,7 +453,7 @@
     blocks = {0: mixed, top: exchange(mixed, "slot", top)}
     late = after(mixed, *aged)
     blocks[2] = exchange(late, "slot", 2)
-    blocks[1] = exchange(late, "slot", 1)
+    blocks[1] = exchange(mixed, "slot", 1)
     for d in range(3, half):
         blocks[d] = exchange(late, "slot", d)
     for d in range(1, half):

time: 58.3 us -> 63.4 us (1.087)
  starting transfers between devices: 28.6 us -> 32.9 us
  local copies, waits for them, and re-layouts: 2.77 us -> 1.18 us
  other arithmetic: 0.11 us -> 1.15 us
  waiting for transfers between devices: 12.2 us -> 13 us
    ppermute x1, starting transfers between devices: 2.45 us -> 4.22 us  [local(): inside = lax.ppermute(after(resident, near_in), 'slot', inside)]
    ppermute x17, starting transfers between devices: 23.9 us -> 25.7 us  [exchange(): return lax.ppermute(block, axis, [(i, i ^ distance) for i in range(size)])]
    unnamed x20 -> x12, local copies, waits for them, and re-layouts: 2.66 us -> 1.07 us
    select_n x1, other arithmetic: 0.06 us -> 1.1 us  [local(): jnp.where(slot_index % 2 == 1, inside, onward).reshape(old_memory.shape)]
    ppermute x17, waiting for transfers between devices: 12.2 us -> 13 us  [exchange(): return lax.ppermute(block, axis, [(i, i ^ distance) for i in range(size)])]
    ppermute x1, starting transfers between devices: 0.69 us -> 1.46 us  [local(): lax.ppermute(after(resident, *sources.values(), bias), 'slot', onward)]
  transfers between devices with their start and end apart: 20 -> 20, of which waited for: 8 -> 6; matrix products, arithmetic and copies ran while one was open for 0% -> 2% of each run, Pallas kernels for 18% -> 14%
where the time goes in v9:
time: 63.4 us; the launch traced here: 62.6 us
  starting transfers between devices  32.9 us (52%)
  Pallas kernels  13.4 us (21%)
  waiting for transfers between devices  13 us (21%)
  local copies, waits for them, and re-layouts  1.18 us (2%)
  other arithmetic  1.15 us (2%)
  between operations  0.94 us (1%)
    ppermute x17, starting transfers between devices, exchange(): return lax.ppermute(block, axis, [(i, i ^ distance) for i in range(size)])  25.7 us
    ppermute x17, waiting for transfers between devices, exchange(): return lax.ppermute(block, axis, [(i, i ^ distance) for i in range(size)])  13 us
    pallas_call x4, Pallas kernels, attend(): pl.pallas_call(partial(attend_kernel, head_size, travels), grid=(rows //...  6.64 us
    ppermute x1, starting transfers between devices, local(): inside = lax.ppermute(after(resident, near_in), 'slot', inside)  4.22 us
    pallas_call x1, Pallas kernels, pool(): pl.pallas_call(partial(pool_kernel, head_size), out_shape=[jax.ShapeDtype...  1.83 us
    ppermute x1, starting transfers between devices, from_behind(): lax.ppermute(block, axis, [(i - distance, i) for i in devices if i - dist...  1.47 us
    pallas_call x1, Pallas kernels, project_late(): pl.pallas_call(project_late_kernel, out_shape=jax.ShapeDtypeStruct((rows,...  1.46 us
    ppermute x1, starting transfers between devices, local(): lax.ppermute(after(resident, *sources.values(), bias), 'slot', onward)  1.46 us
  transfers between devices with their start and end apart: 20, of which 6 were waited for; matrix products, arithmetic and copies ran while one was open for 2% of the time, Pallas kernels for 14%

profile of v9, /device:TPU:0, one launch (start us, length us, event | category | flops | bytes accessed | tf_op | source)
XLA Modules:
  0.0 62.6 jit_solution(9657301739703393122)
XLA Ops:
  0.7 1.3 %cut.1 = (bf16[256,256]{1,0:T(8,128)(2,1)S(1)}, bf16[256,256]{1,0:T(8,128)(2,1)S(1)}, bf16[128,256]{1,0:T(8,128)(2,1)S(1)}, bf16[128,256]{1,0:T(8,128)(2,1)S(1)}...) custom-call(s32[1]{0:T(128)} %bitcast.place_ref, bf16[128,2048]{1,0:T(8,128)(2,1)} %bitcast.3.memory_ref), custom_call_target="tpu_custom_call" | custom-call | tf_op jit(solution)/shard_map/cut/pallas_call | solution.py:134
  1.9 3.0 %collective-permute-start.1 = (bf16[256,256]{1,0:T(8,128)(2,1)S(1)}, bf16[256,256]{1,0:T(8,128)(2,1)S(1)}, u32[]{:S(2)}, u32[]{:S(2)}) collective-permute-start(bf16[256,256]{1,0:T(8,128)(2,1)S(1)} %get-tuple-element.31), channel_id=1, source_target_pairs={{0,4},{4,0},{8,12},{12,8},{16,20},{20,16},{24,28},{28,24},{1,5},{5... | collective-permute-start | bytes 393224 | tf_op jit(solution)/shard_map/ppermute | solution.py:28
  6.0 1.5 %collective-permute-start = (bf16[512,256]{1,0:T(8,128)(2,1)S(1)}, bf16[512,256]{1,0:T(8,128)(2,1)S(1)}, u32[]{:S(2)}, u32[]{:S(2)}) collective-permute-start(bf16[512,256]{1,0:T(8,128)(2,1)S(1)} %bitcast.7), channel_id=1, source_target_pairs={{0,1},{1,2},{2,3},{4,5},{5,6},{6,7},{8,9},{9,10},{10,11},{12,13},{... | collective-permute-start | bytes 786440 | tf_op jit(solution)/shard_map/ppermute | solution.py:33
  7.6 2.0 %collective-permute-start.6 = (bf16[512,128]{1,0:T(8,128)(2,1)S(1)}, bf16[512,128]{1,0:T(8,128)(2,1)S(1)}, u32[]{:S(2)}, u32[]{:S(2)}) collective-permute-start(bf16[512,128]{1,0:T(8,128)(2,1)S(1)} %constant_dynamic-slice_fusion.query_ref), channel_id=1, source_target_pairs={{0,2},{1,3},{2,0},{3,1},{4,6},{5,7},{6,4},{7,5},{8,10},{9,11},{10,... | collective-permute-start | bytes 393224 | tf_op jit(solution)/shard_map/ppermute | solution.py:28
  10.2 3.7 %collective-permute-start.5 = (bf16[256,256]{1,0:T(8,128)(2,1)S(1)}, bf16[256,256]{1,0:T(8,128)(2,1)S(1)}, u32[]{:S(2)}, u32[]{:S(2)}) collective-permute-start(bf16[256,256]{1,0:T(8,128)(2,1)S(1)} %pad_maximum_fusion.3), channel_id=1, source_target_pairs={{0,24},{4,28},{8,16},{12,20},{16,8},{20,12},{24,0},{28,4},{1,25},{... | collective-permute-start | bytes 393224 | tf_op jit(solution)/shard_map/ppermute | solution.py:28
  14.0 1.2 %collective-permute-done.2 = bf16[256,256]{1,0:T(8,128)(2,1)S(1)} collective-permute-done((bf16[256,256]{1,0:T(8,128)(2,1)S(1)}, bf16[256,256]{1,0:T(8,128)(2,1)S(1)}, u32[]{:S(2)}, u32[]{:S(2)}) %collective-permute-start.2) | collective-permute-done | bytes 131104 | tf_op jit(solution)/shard_map/ppermute | solution.py:28
  15.2 1.6 %collective-permute-start.3 = (bf16[256,256]{1,0:T(8,128)(2,1)S(1)}, bf16[256,256]{1,0:T(8,128)(2,1)S(1)}, u32[]{:S(2)}, u32[]{:S(2)}) collective-permute-start(bf16[256,256]{1,0:T(8,128)(2,1)S(1)} %pad_maximum_fusion.1), channel_id=1, source_target_pairs={{0,8},{4,12},{8,0},{12,4},{16,24},{20,28},{24,16},{28,20},{1,9},{5... | collective-permute-start | bytes 393224 | tf_op jit(solution)/shard_map/ppermute | solution.py:28
  16.9 1.8 %pool.1 = (bf16[4,1,32,256]{3,2,1,0:T(8,128)(2,1)}, bf16[128,256]{1,0:T(8,128)(2,1)S(1)}) custom-call(bf16[8,2,64,256]{3,2,1,0:T(8,128)(2,1)S(1)} %copy-done.3, bf16[8,1,64,256]{3,2,1,0:T(8,128)(2,1)S(1)} %bitcast.6, bf16[27,256]{1,0:T(8,128)(2,1)S(1)} %copy-done.4), custom_call_target="tpu_custom_call" | custom-call | tf_op jit(solution)/shard_map/pool/pallas_call | solution.py:98
  19.6 5.4 %collective-permute-done.4 = bf16[256,256]{1,0:T(8,128)(2,1)S(1)} collective-permute-done((bf16[256,256]{1,0:T(8,128)(2,1)S(1)}, bf16[256,256]{1,0:T(8,128)(2,1)S(1)}, u32[]{:S(2)}, u32[]{:S(2)}) %collective-permute-start.4) | collective-permute-done | bytes 131104 | tf_op jit(solution)/shard_map/ppermute | solution.py:28
  25.0 1.7 %attend.6 = bf16[544,128]{1,0:T(8,128)(2,1)S(1)} custom-call(f32[8,1152]{1,0:T(8,128)S(1)} %mask.1.bias_ref, bf16[512,128]{1,0:T(8,128)(2,1)S(1)} %get-tuple-element.50.query_ref, bf16[128,256]{1,0:T(8,128)(2,1)S(1)} %get-tuple-element.27.refs_0_, bf16[128,256]{1,0:T(8,128)(2,1)S(1)} %get-tuple-element.29.refs_1_, ...), custom_call_target="tpu_custom_call" | custom-call | flops 603979776 | bytes 2228224 | tf_op jit(solution)/shard_map/attend/pallas_call | solution.py:278
  26.8 4.2 %collective-permute-start.16 = (bf16[128,2048]{1,0:T(8,128)(2,1)}, bf16[128,2048]{1,0:T(8,128)(2,1)}, u32[]{:S(2)}, u32[]{:S(2)}) collective-permute-start(bf16[128,2048]{1,0:T(8,128)(2,1)} %bitcast.3.memory_ref), channel_id=1, source_target_pairs={{0,4},{8,12},{16,20},{24,28},{1,5},{9,13},{17,21},{25,29},{2,6},{1... | collective-permute-start | bytes 1572872 | tf_op jit(solution)/shard_map/ppermute | solution.py:508
  31.0 1.5 %collective-permute-start.17 = (bf16[128,2048]{1,0:T(8,128)(2,1)}, bf16[128,2048]{1,0:T(8,128)(2,1)}, u32[]{:S(2)}, u32[]{:S(2)}) collective-permute-start(bf16[128,2048]{1,0:T(8,128)(2,1)} %bitcast.3.memory_ref), channel_id=1, source_target_pairs={{4,8},{12,16},{20,24},{5,9},{13,17},{21,25},{6,10},{14,18},{22,26}... | collective-permute-start | bytes 1572872 | tf_op jit(solution)/shard_map/ppermute | solution.py:509
  32.5 1.6 %attend.5 = (f32[512,128]{1,0:T(8,128)S(1)}, f32[512,128]{1,0:T(8,128)S(1)}) custom-call(f32[8,1152]{1,0:T(8,128)S(1)} %mask.1.bias_ref, bf16[512,128]{1,0:T(8,128)(2,1)S(1)} %collective-permute-done.6.query_ref, bf16[128,256]{1,0:T(8,128)(2,1)S(1)} %get-tuple-element.27.refs_0_, bf16[128,256]{1,0:T(8,128)(2,1)S(1)} %get-tuple-element.29.refs_1_, ...), custom_call_target="tpu_custom_call" | custom-call | flops 603979776 | bytes 2228224 | tf_op jit(solution)/shard_map/attend/pallas_call | solution.py:278
  34.4 1.8 %collective-permute-start.9 = (bf16[544,128]{1,0:T(8,128)(2,1)S(1)}, bf16[544,128]{1,0:T(8,128)(2,1)S(1)}, u32[]{:S(2)}, u32[]{:S(2)}) collective-permute-start(bf16[544,128]{1,0:T(8,128)(2,1)S(1)} %merge.2), channel_id=1, source_target_pairs={{0,2},{1,3},{2,0},{3,1},{4,6},{5,7},{6,4},{7,5},{8,10},{9,11},{10,... | collective-permute-start | bytes 417800 | tf_op jit(solution)/shard_map/ppermute | solution.py:28
  36.2 1.7 %attend.7 = bf16[544,128]{1,0:T(8,128)(2,1)S(1)} custom-call(f32[8,1152]{1,0:T(8,128)S(1)} %mask.1.bias_ref, bf16[512,128]{1,0:T(8,128)(2,1)S(1)} %get-tuple-element.41.query_ref, bf16[128,256]{1,0:T(8,128)(2,1)S(1)} %get-tuple-element.27.refs_0_, bf16[128,256]{1,0:T(8,128)(2,1)S(1)} %get-tuple-element.29.refs_1_, ...), custom_call_target="tpu_custom_call" | custom-call | flops 603979776 | bytes 2228224 | tf_op jit(solution)/shard_map/attend/pallas_call | solution.py:278
  38.0 1.6 %attend.4 = (f32[512,128]{1,0:T(8,128)S(1)}, f32[512,128]{1,0:T(8,128)S(1)}) custom-call(f32[8,1152]{1,0:T(8,128)S(1)} %mask.1.bias_ref, bf16[512,128]{1,0:T(8,128)(2,1)S(1)} %constant_dynamic-slice_fusion.query_ref, bf16[128,256]{1,0:T(8,128)(2,1)S(1)} %get-tuple-element.27.refs_0_, bf16[128,256]{1,0:T(8,128)(2,1)S(1)} %get-tuple-element.29.refs_1_, ...), custom_call_target="tpu_custom_call" | custom-call | flops 2415919104 | bytes 2228224 | tf_op jit(solution)/shard_map/attend/pallas_call | solution.py:278
  40.6 2.4 %collective-permute-start.11 = (bf16[512,128]{1,0:T(8,128)(2,1)S(1)}, bf16[512,128]{1,0:T(8,128)(2,1)S(1)}, u32[]{:S(2)}, u32[]{:S(2)}) collective-permute-start(bf16[512,128]{1,0:T(8,128)(2,1)S(1)} %merge.3.refs_0_), channel_id=1, source_target_pairs={{0,24},{4,28},{8,16},{12,20},{16,8},{20,12},{24,0},{28,4},{1,25},{... | collective-permute-start | bytes 393224 | tf_op jit(solution)/shard_map/ppermute | solution.py:28
  43.3 5.4 %collective-permute-start.18 = (bf16[512,128]{1,0:T(8,128)(2,1)S(1)}, bf16[512,128]{1,0:T(8,128)(2,1)S(1)}, u32[]{:S(2)}, u32[]{:S(2)}) collective-permute-start(bf16[512,128]{1,0:T(8,128)(2,1)S(1)} %merge.3.refs_0_), channel_id=1, source_target_pairs={{0,8},{4,12},{8,0},{12,4},{16,24},{20,28},{24,16},{28,20},{1,9},{5... | collective-permute-start | bytes 393224 | tf_op jit(solution)/shard_map/ppermute | solution.py:28
  48.8 4.0 %collective-permute-start.13 = (bf16[512,128]{1,0:T(8,128)(2,1)S(1)}, bf16[512,128]{1,0:T(8,128)(2,1)S(1)}, u32[]{:S(2)}, u32[]{:S(2)}) collective-permute-start(bf16[512,128]{1,0:T(8,128)(2,1)S(1)} %collective-permute-done.11.refs_2_), channel_id=1, source_target_pairs={{0,12},{4,8},{8,4},{12,0},{16,28},{20,24},{24,20},{28,16},{1,13},{... | collective-permute-start | bytes 393224 | tf_op jit(solution)/shard_map/ppermute | solution.py:28
  53.4 1.1 %broadcast_select_fusion = bf16[128,2048]{1,0:T(8,128)(2,1)S(1)} fusion(bf16[128,2048]{1,0:T(8,128)(2,1)} %collective-permute-done.16, bf16[128,2048]{1,0:T(8,128)(2,1)} %collective-permute-done.17, pred[]{:T(512)S(6)} %eq.5), kind=kLoop, calls=%fused_computation | loop fusion | flops 262144 | bytes 1572865 | tf_op jit(solution)/shard_map/jit(_where)/select_n | solution.py:531
  54.5 1.6 %collective-permute-done.19.refs_3_ = bf16[512,128]{1,0:T(8,128)(2,1)S(1)} collective-permute-done((bf16[512,128]{1,0:T(8,128)(2,1)S(1)}, bf16[512,128]{1,0:T(8,128)(2,1)S(1)}, u32[]{:S(2)}, u32[]{:S(2)}) %collective-permute-start.19) | collective-permute-done | bytes 131104 | tf_op jit(solution)/shard_map/ppermute | solution.py:28
  56.8 1.2 %collective-permute-done.12.refs_0_ = bf16[512,128]{1,0:T(8,128)(2,1)S(1)} collective-permute-done((bf16[512,128]{1,0:T(8,128)(2,1)S(1)}, bf16[512,128]{1,0:T(8,128)(2,1)S(1)}, u32[]{:S(2)}, u32[]{:S(2)}) %collective-permute-start.12) | collective-permute-done | bytes 131104 | tf_op jit(solution)/shard_map/ppermute | solution.py:28
  58.0 3.1 %collective-permute-done.13.refs_1_ = bf16[512,128]{1,0:T(8,128)(2,1)S(1)} collective-permute-done((bf16[512,128]{1,0:T(8,128)(2,1)S(1)}, bf16[512,128]{1,0:T(8,128)(2,1)S(1)}, u32[]{:S(2)}, u32[]{:S(2)}) %collective-permute-start.13) | collective-permute-done | bytes 131104 | tf_op jit(solution)/shard_map/ppermute | solution.py:28
  61.1 1.5 %project_late.1 = bf16[512,1024]{1,0:T(8,128)(2,1)} custom-call(bf16[512,1024]{1,0:T(8,128)(2,1)S(1)} %get-tuple-element.26.weight_ref, bf16[512,128]{1,0:T(8,128)(2,1)S(1)} %collective-permute-done.12.refs_0_, bf16[512,128]{1,0:T(8,128)(2,1)S(1)} %collective-permute-done.13.refs_1_, bf16[512,128]{1,0:T(8,128)(2,1)S(1)} %collective-permute-done.11.refs_2_, ...), custom_call_target="tpu_custom_call" | custom-call | flops 536870912 | bytes 2097152 | tf_op jit(solution)/shard_map/project_late/pallas_call | solution.py:435
  (53 shorter events, 5.9 us)
Async XLA Ops:
  0.6 6.9 %copy-start = (bf16[512,1024]{1,0:T(8,128)(2,1)S(1)}, bf16[512,1024]{1,0:T(8,128)(2,1)}, u32[]{:S(2)}) copy-start(bf16[512,1024]{1,0:T(8,128)(2,1)} %param.6) | copy-start | bytes 3145732
  0.6 16.2 %copy-start.3 = (bf16[8,2,64,256]{3,2,1,0:T(8,128)(2,1)S(1)}, bf16[8,2,64,256]{3,2,1,0:T(8,128)(2,1)}, u32[]{:S(2)}) copy-start(bf16[8,2,64,256]{3,2,1,0:T(8,128)(2,1)} %raw_ref.3) | copy-start | bytes 1572868
  0.7 18.0 %copy-start.5 = (s32[9]{0:T(128)S(1)}, s32[9]{0:T(128)}, u32[]{:S(2)}) copy-start(s32[9]{0:T(128)} %valid_ref) | copy-start | bytes 112
  1.9 7.7 %collective-permute-start.1 = (bf16[256,256]{1,0:T(8,128)(2,1)S(1)}, bf16[256,256]{1,0:T(8,128)(2,1)S(1)}, u32[]{:S(2)}, u32[]{:S(2)}) collective-permute-start(bf16[256,256]{1,0:T(8,128)(2,1)S(1)} %get-tuple-element.31), channel_id=1, source_target_pairs={{0,4},{4,0},{8,12},{12,8},{16,20},{20,16},{24,28},{28,24},{1,5},{5... | collective-permute-start | bytes 393224 | tf_op jit(solution)/shard_map/ppermute | solution.py:28
  6.0 10.9 %copy-start.4 = (bf16[27,256]{1,0:T(8,128)(2,1)S(1)}, bf16[27,256]{1,0:T(8,128)(2,1)}, u32[]{:S(2)}) copy-start(bf16[27,256]{1,0:T(8,128)(2,1)} %weight_ref.3) | copy-start | bytes 41476
  6.0 10.8 %collective-permute-start = (bf16[512,256]{1,0:T(8,128)(2,1)S(1)}, bf16[512,256]{1,0:T(8,128)(2,1)S(1)}, u32[]{:S(2)}, u32[]{:S(2)}) collective-permute-start(bf16[512,256]{1,0:T(8,128)(2,1)S(1)} %bitcast.7), channel_id=1, source_target_pairs={{0,1},{1,2},{2,3},{4,5},{5,6},{6,7},{8,9},{9,10},{10,11},{12,13},{... | collective-permute-start | bytes 786440 | tf_op jit(solution)/shard_map/ppermute | solution.py:33
  7.6 6.4 %collective-permute-start.6 = (bf16[512,128]{1,0:T(8,128)(2,1)S(1)}, bf16[512,128]{1,0:T(8,128)(2,1)S(1)}, u32[]{:S(2)}, u32[]{:S(2)}) collective-permute-start(bf16[512,128]{1,0:T(8,128)(2,1)S(1)} %constant_dynamic-slice_fusion.query_ref), channel_id=1, source_target_pairs={{0,2},{1,3},{2,0},{3,1},{4,6},{5,7},{6,4},{7,5},{8,10},{9,11},{10,... | collective-permute-start | bytes 393224 | tf_op jit(solution)/shard_map/ppermute | solution.py:28
  9.6 5.6 %collective-permute-start.2 = (bf16[256,256]{1,0:T(8,128)(2,1)S(1)}, bf16[256,256]{1,0:T(8,128)(2,1)S(1)}, u32[]{:S(2)}, u32[]{:S(2)}) collective-permute-start(bf16[256,256]{1,0:T(8,128)(2,1)S(1)} %get-tuple-element.32), channel_id=1, source_target_pairs={{0,4},{4,0},{8,12},{12,8},{16,20},{20,16},{24,28},{28,24},{1,5},{5... | collective-permute-start | bytes 393224 | tf_op jit(solution)/shard_map/ppermute | solution.py:28
  10.2 9.3 %collective-permute-start.5 = (bf16[256,256]{1,0:T(8,128)(2,1)S(1)}, bf16[256,256]{1,0:T(8,128)(2,1)S(1)}, u32[]{:S(2)}, u32[]{:S(2)}) collective-permute-start(bf16[256,256]{1,0:T(8,128)(2,1)S(1)} %pad_maximum_fusion.3), channel_id=1, source_target_pairs={{0,24},{4,28},{8,16},{12,20},{16,8},{20,12},{24,0},{28,4},{1,25},{... | collective-permute-start | bytes 393224 | tf_op jit(solution)/shard_map/ppermute | solution.py:28
  13.9 11.0 %collective-permute-start.4 = (bf16[256,256]{1,0:T(8,128)(2,1)S(1)}, bf16[256,256]{1,0:T(8,128)(2,1)S(1)}, u32[]{:S(2)}, u32[]{:S(2)}) collective-permute-start(bf16[256,256]{1,0:T(8,128)(2,1)S(1)} %pad_maximum_fusion.2), channel_id=1, source_target_pairs={{0,16},{4,20},{8,24},{12,28},{16,0},{20,4},{24,8},{28,12},{1,17},{... | collective-permute-start | bytes 393224 | tf_op jit(solution)/shard_map/ppermute | solution.py:28
  15.2 9.7 %collective-permute-start.3 = (bf16[256,256]{1,0:T(8,128)(2,1)S(1)}, bf16[256,256]{1,0:T(8,128)(2,1)S(1)}, u32[]{:S(2)}, u32[]{:S(2)}) collective-permute-start(bf16[256,256]{1,0:T(8,128)(2,1)S(1)} %pad_maximum_fusion.1), channel_id=1, source_target_pairs={{0,8},{4,12},{8,0},{12,4},{16,24},{20,28},{24,16},{28,20},{1,9},{5... | collective-permute-start | bytes 393224 | tf_op jit(solution)/shard_map/ppermute | solution.py:28
  19.3 5.7 %collective-permute-start.7 = (bf16[1024,128]{1,0:T(8,128)(2,1)S(1)}, bf16[1024,128]{1,0:T(8,128)(2,1)S(1)}, u32[]{:S(2)}, u32[]{:S(2)}) collective-permute-start(bf16[1024,128]{1,0:T(8,128)(2,1)S(1)} %pad_maximum_fusion), channel_id=1, source_target_pairs={{0,1},{1,0},{2,3},{3,2},{4,5},{5,4},{6,7},{7,6},{8,9},{9,8},{10,11... | collective-permute-start | bytes 786440 | tf_op jit(solution)/shard_map/ppermute | solution.py:28
  26.7 7.4 %collective-permute-start.8 = (bf16[544,128]{1,0:T(8,128)(2,1)S(1)}, bf16[544,128]{1,0:T(8,128)(2,1)S(1)}, u32[]{:S(2)}, u32[]{:S(2)}) collective-permute-start(bf16[544,128]{1,0:T(8,128)(2,1)S(1)} %attend.6), channel_id=1, source_target_pairs={{0,1},{1,0},{2,3},{3,2},{4,5},{5,4},{6,7},{7,6},{8,9},{9,8},{10,11... | collective-permute-start | bytes 417800 | tf_op jit(solution)/shard_map/ppermute | solution.py:28
  26.8 16.5 %collective-permute-start.16 = (bf16[128,2048]{1,0:T(8,128)(2,1)}, bf16[128,2048]{1,0:T(8,128)(2,1)}, u32[]{:S(2)}, u32[]{:S(2)}) collective-permute-start(bf16[128,2048]{1,0:T(8,128)(2,1)} %bitcast.3.memory_ref), channel_id=1, source_target_pairs={{0,4},{8,12},{16,20},{24,28},{1,5},{9,13},{17,21},{25,29},{2,6},{1... | collective-permute-start | bytes 1572872 | tf_op jit(solution)/shard_map/ppermute | solution.py:508
  31.0 12.2 %collective-permute-start.17 = (bf16[128,2048]{1,0:T(8,128)(2,1)}, bf16[128,2048]{1,0:T(8,128)(2,1)}, u32[]{:S(2)}, u32[]{:S(2)}) collective-permute-start(bf16[128,2048]{1,0:T(8,128)(2,1)} %bitcast.3.memory_ref), channel_id=1, source_target_pairs={{4,8},{12,16},{20,24},{5,9},{13,17},{21,25},{6,10},{14,18},{22,26}... | collective-permute-start | bytes 1572872 | tf_op jit(solution)/shard_map/ppermute | solution.py:509
  34.4 5.8 %collective-permute-start.9 = (bf16[544,128]{1,0:T(8,128)(2,1)S(1)}, bf16[544,128]{1,0:T(8,128)(2,1)S(1)}, u32[]{:S(2)}, u32[]{:S(2)}) collective-permute-start(bf16[544,128]{1,0:T(8,128)(2,1)S(1)} %merge.2), channel_id=1, source_target_pairs={{0,2},{1,3},{2,0},{3,1},{4,6},{5,7},{6,4},{7,5},{8,10},{9,11},{10,... | collective-permute-start | bytes 417800 | tf_op jit(solution)/shard_map/ppermute | solution.py:28
  37.9 1.7 %collective-permute-start.10 = (bf16[544,128]{1,0:T(8,128)(2,1)S(1)}, bf16[544,128]{1,0:T(8,128)(2,1)S(1)}, u32[]{:S(2)}, u32[]{:S(2)}) collective-permute-start(bf16[544,128]{1,0:T(8,128)(2,1)S(1)} %attend.7), channel_id=1, source_target_pairs={{0,1},{1,0},{2,3},{3,2},{4,5},{5,4},{6,7},{7,6},{8,9},{9,8},{10,11... | collective-permute-start | bytes 417800 | tf_op jit(solution)/shard_map/ppermute | solution.py:28
  40.6 8.1 %collective-permute-start.11 = (bf16[512,128]{1,0:T(8,128)(2,1)S(1)}, bf16[512,128]{1,0:T(8,128)(2,1)S(1)}, u32[]{:S(2)}, u32[]{:S(2)}) collective-permute-start(bf16[512,128]{1,0:T(8,128)(2,1)S(1)} %merge.3.refs_0_), channel_id=1, source_target_pairs={{0,24},{4,28},{8,16},{12,20},{16,8},{20,12},{24,0},{28,4},{1,25},{... | collective-permute-start | bytes 393224 | tf_op jit(solution)/shard_map/ppermute | solution.py:28
  43.0 9.8 %collective-permute-start.15 = (bf16[512,128]{1,0:T(8,128)(2,1)S(1)}, bf16[512,128]{1,0:T(8,128)(2,1)S(1)}, u32[]{:S(2)}, u32[]{:S(2)}) collective-permute-start(bf16[512,128]{1,0:T(8,128)(2,1)S(1)} %merge.3.refs_0_), channel_id=1, source_target_pairs={{0,4},{4,0},{8,12},{12,8},{16,20},{20,16},{24,28},{28,24},{1,5},{5... | collective-permute-start | bytes 393224 | tf_op jit(solution)/shard_map/ppermute | solution.py:28
  43.3 11.2 %collective-permute-start.18 = (bf16[512,128]{1,0:T(8,128)(2,1)S(1)}, bf16[512,128]{1,0:T(8,128)(2,1)S(1)}, u32[]{:S(2)}, u32[]{:S(2)}) collective-permute-start(bf16[512,128]{1,0:T(8,128)(2,1)S(1)} %merge.3.refs_0_), channel_id=1, source_target_pairs={{0,8},{4,12},{8,0},{12,4},{16,24},{20,28},{24,16},{28,20},{1,9},{5... | collective-permute-start | bytes 393224 | tf_op jit(solution)/shard_map/ppermute | solution.py:28
  48.7 7.3 %collective-permute-start.19 = (bf16[512,128]{1,0:T(8,128)(2,1)S(1)}, bf16[512,128]{1,0:T(8,128)(2,1)S(1)}, u32[]{:S(2)}, u32[]{:S(2)}) collective-permute-start(bf16[512,128]{1,0:T(8,128)(2,1)S(1)} %merge.3.refs_0_), channel_id=1, source_target_pairs={{0,12},{4,8},{8,4},{12,0},{16,28},{20,24},{24,20},{28,16},{1,13},{... | collective-permute-start | bytes 393224 | tf_op jit(solution)/shard_map/ppermute | solution.py:28
  48.7 9.3 %collective-permute-start.12 = (bf16[512,128]{1,0:T(8,128)(2,1)S(1)}, bf16[512,128]{1,0:T(8,128)(2,1)S(1)}, u32[]{:S(2)}, u32[]{:S(2)}) collective-permute-start(bf16[512,128]{1,0:T(8,128)(2,1)S(1)} %collective-permute-done.11.refs_2_), channel_id=1, source_target_pairs={{0,8},{4,12},{8,0},{12,4},{16,24},{20,28},{24,16},{28,20},{1,9},{5... | collective-permute-start | bytes 393224 | tf_op jit(solution)/shard_map/ppermute | solution.py:28
  48.8 12.3 %collective-permute-start.13 = (bf16[512,128]{1,0:T(8,128)(2,1)S(1)}, bf16[512,128]{1,0:T(8,128)(2,1)S(1)}, u32[]{:S(2)}, u32[]{:S(2)}) collective-permute-start(bf16[512,128]{1,0:T(8,128)(2,1)S(1)} %collective-permute-done.11.refs_2_), channel_id=1, source_target_pairs={{0,12},{4,8},{8,4},{12,0},{16,28},{20,24},{24,20},{28,16},{1,13},{... | collective-permute-start | bytes 393224 | tf_op jit(solution)/shard_map/ppermute | solution.py:28
  52.8 8.3 %collective-permute-start.14 = (bf16[512,128]{1,0:T(8,128)(2,1)S(1)}, bf16[512,128]{1,0:T(8,128)(2,1)S(1)}, u32[]{:S(2)}, u32[]{:S(2)}) collective-permute-start(bf16[512,128]{1,0:T(8,128)(2,1)S(1)} %collective-permute-done.11.refs_2_), channel_id=1, source_target_pairs={{0,4},{4,0},{8,12},{12,8},{16,20},{20,16},{24,28},{28,24},{1,5},{5... | collective-permute-start | bytes 393224 | tf_op jit(solution)/shard_map/ppermute | solution.py:28
  (2 other events, 6.1 us)
